TPU v7x, 32 devices: a whole 2x2x4 slice. The times are simulated.
32 devices in a mesh: parts: 2 (over y), gx: 4 (over z), gy: 2 (over x), gz: 2 (over core).
Axes of the slice: x: 2, y: 2, z: 4, core: 2. Of those that a mesh axis runs over, the one named last changes fastest.
Arguments:
- embeds: bfloat16 [8192, 512], P(('parts', 'gx', 'gy', 'gz')), parts along dimension 0, may hold values from -6 to 6
- cluster: int32 [8192], P(('parts', 'gx', 'gy', 'gz')), parts along dimension 0, may hold values from 0 to 127, as said below
Outputs:
- nearest: float32 [8192], P(('parts', 'gx', 'gy', 'gz')), parts along dimension 0
There are 2 independent parts, one for each index of `parts`. A program takes and returns all parts, laid end to end along the dimension named above; each array names one. Nothing has to cross between parts.
Inputs may be any that keep to these rules, and one draw needn't show every extreme that they name: `cluster`: cluster c belongs to owner c // 16. Among the 256 embeddings of one device, at most 64 lie in clusters of any one owner, and on every device some owner has exactly 64.
All inputs are finite; a program needn't handle non-finite values.
Results may differ from a plain program's by a relative error of at most 0.0018.
Values may be sent and summed in bfloat16 or wider, within the bound.
No kernel may reach another device: no remote copies, remote signals or barrier semaphores. Data moves between devices by JAX's collectives and lax.ppermute only.
A program may use at most 64 MiB of HBM per device.

v0:
```python
import jax
import jax.numpy as jnp
from jax import lax
from jax.sharding import PartitionSpec as P

CLU_OWN = 16


EPS = 1e-06


def masked_sims(queries, query_labels, query_ids, keys, key_labels, key_ids):
    sims = jnp.einsum("qd,kd->qk", queries, keys, preferred_element_type=jnp.float32)
    keep = (
        (query_labels[:, None] == key_labels[None, :])
        & (query_labels[:, None] >= 0)
        & (query_ids[:, None] != key_ids[None, :])
    )
    return jnp.where(keep, sims, -1.0)


def on_device(embeds, cluster):
    rows, width = embeds.shape
    size_x = lax.axis_size("gx")
    size_y = lax.axis_size("gy")
    owners = size_x * size_y
    cap = 2 * rows // owners
    total = owners * cap
    vecs = embeds.astype(jnp.float32)
    unit = (vecs * lax.rsqrt(jnp.sum(vecs * vecs, axis=1, keepdims=True) + EPS)).astype(
        jnp.bfloat16
    )
    target = cluster // CLU_OWN
    onehot = (target[:, None] == jnp.arange(owners, dtype=jnp.int32)[None, :]).astype(jnp.int32)
    before = jnp.cumsum(onehot, axis=0) - onehot
    slot = jnp.sum(before * onehot, axis=1)
    place = target * cap + slot
    outgoing = jnp.zeros((total, width), jnp.bfloat16).at[place].set(unit)
    out_labels = jnp.full((total,), -1, jnp.int32).at[place].set(cluster)
    got, got_labels = (
        lax.all_to_all(
            outgoing.reshape(owners, cap, width),
            ("gx", "gy"),
            split_axis=0,
            concat_axis=0,
            tiled=True,
        ),
        lax.all_to_all(
            out_labels.reshape(owners, cap), ("gx", "gy"), split_axis=0, concat_axis=0, tiled=True
        ),
    )
    members = got.reshape(total, width)
    labels = got_labels.reshape(total)
    core = lax.axis_index("gz")
    query_ids = core * total + jnp.arange(total, dtype=jnp.int32)
    keys = lax.all_gather(members, "gz", axis=0, tiled=True)
    key_labels = lax.all_gather(labels, "gz", axis=0, tiled=True)
    key_ids = jnp.arange(keys.shape[0], dtype=jnp.int32)
    best = jnp.maximum(
        jnp.full((total,), -1.0, jnp.float32),
        jnp.max(masked_sims(members, labels, query_ids, keys, key_labels, key_ids), axis=1),
    )
    back = lax.all_to_all(
        best.reshape(owners, cap), ("gx", "gy"), split_axis=0, concat_axis=0, tiled=True
    )
    return back.reshape(total)[place]


def solution(mesh):
    placed = (P(("parts", "gx", "gy", "gz"), None), P(("parts", "gx", "gy", "gz")))
    return jax.shard_map(
        on_device,
        mesh=mesh,
        in_specs=placed,
        out_specs=P(("parts", "gx", "gy", "gz")),
        check_vma=False,
    )
```

profile of v0, /device:TPU:0, one launch (start us, length us, event | category | flops | bytes accessed | tf_op | source)
XLA Modules:
  0.0 73.4 jit_solution(2999316740347399555)
XLA Ops:
  6.5 0.0 all-gather.3.cloned.1.call-start
  6.5 0.7 fusion.14
  7.2 0.7 and_select_fusion
  7.9 0.6 reduce-window.6
  8.5 0.2 slice_reduce_fusion
  8.8 0.1 fusion.8
  8.9 0.7 compare_select_fusion
  9.6 1.1 %fusion.1 = f32[256]{0:T(256)S(1)} fusion(bf16[256,512]{1,0:T(8,128)(2,1)} %param.2), kind=kLoop, calls=%fused_computation.8 | loop fusion | flops 392960 | bytes 263168 | tf_op jit(solution)/shard_map/reduce_sum | solution.py:30
  10.6 2.1 %scatter_custom_fusion.1 = bf16[512,512]{1,0:T(8,128)(2,1)S(1)} fusion(s32[256]{0:T(256)S(1)} %compare_select_fusion, bf16[256,512]{1,0:T(8,128)(2,1)} %param.2, f32[256]{0:T(256)S(1)} %add_rsqrt_fusion, bf16[]{:T(256)} %constant.39.clone.1), kind=kCustom, calls=%fused_computation.10 | custom fusion | flops 393216 | bytes 787458 | tf_op jit(solution)/shard_map/scatter | solution.py:38
  12.8 21.7 %all_to_all.20 = bf16[8,64,512]{2,1,0:T(8,128)(2,1)} all-to-all(bf16[8,64,512]{2,1,0:T(8,128)(2,1)S(1)} %bitcast.18), channel_id=1, replica_groups=mesh['parts'=2,'gx'=4,'gy'=2,'gz'=2] {'gx','gy'}, dimensions={0} | all-to-all | bytes 1048576 | tf_op jit(solution)/shard_map/all_to_all | solution.py:41
  34.5 0.0 all-gather.3.cloned.1.call-update
  34.5 1.6 %scatter_custom_fusion = s32[512]{0:T(512)S(1)} fusion(s32[256]{0:T(256)S(1)} %compare_select_fusion, s32[256]{0:T(256)} %param.3, s32[]{:T(128)} %constant.13.clone.1), kind=kCustom, calls=%fused_computation.30 | custom fusion | bytes 2560 | tf_op jit(solution)/shard_map/scatter | solution.py:39
  36.1 0.7 all_to_all.13
  36.7 3.6 %all-to-all-start = ((s32[8,1,64]{2,1,0:T(1,128)}), s32[8,1,64]{2,1,0:T(1,128)S(1)}, u32[]{:S(2)}, u32[]{:S(2)}) async-start(s32[8,1,64]{2,1,0:T(1,128)} %all_to_all.13), calls=%async_computation | async-start | bytes 8192 | tf_op jit(solution)/shard_map/all_to_all | solution.py:48
  40.3 6.5 %all-to-all-done = s32[8,1,64]{2,1,0:T(1,128)S(1)} async-done(((s32[8,1,64]{2,1,0:T(1,128)}), s32[8,1,64]{2,1,0:T(1,128)S(1)}, u32[]{:S(2)}, u32[]{:S(2)}) %all-to-all-start) | async-done | bytes 2080 | tf_op jit(solution)/shard_map/all_to_all | solution.py:48
  46.8 0.5 broadcast.73
  47.3 0.7 reduce.10
  48.0 0.1 eq.45
  48.0 0.1 reshape.100
  48.1 1.8 %all-gather = s32[2,1,512]{2,1,0:T(1,128)S(1)} all-gather(s32[1,1,512]{2,1,0:T(1,128)S(1)} %reshape.100), channel_id=1, replica_groups=mesh['parts'=2,'gx'=4,'gy'=2,'gz'=2] {'gz'}, dimensions={0}, use_global_device_ids=true | all-gather | bytes 6144 | tf_op jit(solution)/shard_map/all_gather | solution.py:57
  49.9 0.0 all-gather.3.cloned.1.call-done
  49.9 2.4 %select_reduce_fusion = f32[512]{0:T(512)S(1)} fusion(bf16[512,512]{1,0:T(8,128)(2,1)} %bitcast.17, bf16[1024,512]{1,0:T(8,128)(2,1)} %all-gather.3.cloned.1.call-done, s32[512]{0:T(512)S(1)} %iota_add_fusion, s32[1024]{0:T(1024)S(1)} %bitcast.20, s32[512]{0:T(512)S(1)} %eq.45, pred[512]{0:T(512)(128)(4,1)S(1)} %broadcast_compare_fusion), kind=kOutput, calls=%fused_computation.3 | convolution fusion | flops 540016128 | bytes 1583616 | tf_op jit(solution)/shard_map/qd,kd->qk/dot_general | solution.py:13
  52.4 0.7 max_broadcast_in_dim.15
  53.0 3.3 %all-to-all-start.2 = ((f32[8,1,64]{2,1,0:T(1,128)}), f32[8,1,64]{2,1,0:T(1,128)S(1)}, u32[]{:S(2)}, u32[]{:S(2)}) async-start(f32[8,1,64]{2,1,0:T(1,128)} %max_broadcast_in_dim.15), calls=%async_computation.2 | async-start | bytes 8192 | tf_op jit(solution)/shard_map/all_to_all | solution.py:63
  56.4 6.4 %all-to-all-done.2 = f32[8,1,64]{2,1,0:T(1,128)S(1)} async-done(((f32[8,1,64]{2,1,0:T(1,128)}), f32[8,1,64]{2,1,0:T(1,128)S(1)}, u32[]{:S(2)}, u32[]{:S(2)}) %all-to-all-start.2) | async-done | bytes 2080 | tf_op jit(solution)/shard_map/all_to_all | solution.py:63
  62.8 0.5 broadcast.74
  63.3 0.7 reduce.11
  64.0 0.1 reshape.72
  64.0 2.5 %gather_fusion = f32[256]{0:T(256)} fusion(f32[512]{0:T(512)S(1)} %reshape.72, s32[1024]{0:T(1024)S(1)} %pad_clamp_fusion), kind=kCustom, calls=%fused_computation | custom fusion | bytes 3072 | tf_op jit(solution)/shard_map/gather | solution.py:66
  (8 shorter events, 0.1 us)
Async XLA Ops:
  6.5 43.4 %all-gather.3.cloned.1.call-start = ((), (), s32[]{:S(2)}) async-start(), calls=%async_computation.3 | async-start | bytes 1572864 | tf_op jit(solution)/shard_map/all_gather | solution.py:56
  36.7 10.0 %all-to-all-start = ((s32[8,1,64]{2,1,0:T(1,128)}), s32[8,1,64]{2,1,0:T(1,128)S(1)}, u32[]{:S(2)}, u32[]{:S(2)}) async-start(s32[8,1,64]{2,1,0:T(1,128)} %all_to_all.13), calls=%async_computation | async-start | bytes 8192 | tf_op jit(solution)/shard_map/all_to_all | solution.py:48
  53.0 9.7 %all-to-all-start.2 = ((f32[8,1,64]{2,1,0:T(1,128)}), f32[8,1,64]{2,1,0:T(1,128)S(1)}, u32[]{:S(2)}, u32[]{:S(2)}) async-start(f32[8,1,64]{2,1,0:T(1,128)} %max_broadcast_in_dim.15), calls=%async_computation.2 | async-start | bytes 8192 | tf_op jit(solution)/shard_map/all_to_all | solution.py:63
Sparse Core Ops, SparseCore 0:
  34.6 8.0 all-gather.2
where the time goes:
time: 73.8 us; the launch traced here: 73.4 us
  blocking collectives  23.5 us (32%)
  between operations  13.5 us (18%)
  waiting for transfers between devices  12.9 us (17%)
  other arithmetic  7.35 us (10%)
  starting transfers between devices  6.92 us (9%)
  local copies, waits for them, and re-layouts  6.87 us (9%)
  matrix products  2.44 us (3%)
    all_to_all x1, blocking collectives, on_device(): lax.all_to_all(outgoing.reshape(owners, cap, width), ('gx', 'gy'), split_...  21.7 us
    all_to_all x1, waiting for transfers between devices, on_device(): lax.all_to_all(out_labels.reshape(owners, cap), ('gx', 'gy'), split_axis=...  6.45 us
    all_to_all x1, waiting for transfers between devices, on_device(): lax.all_to_all(best.reshape(owners, cap), ('gx', 'gy'), split_axis=0, con...  6.39 us
    all_to_all x1, starting transfers between devices, on_device(): lax.all_to_all(out_labels.reshape(owners, cap), ('gx', 'gy'), split_axis=...  3.59 us
    all_to_all x1, starting transfers between devices, on_device(): lax.all_to_all(best.reshape(owners, cap), ('gx', 'gy'), split_axis=0, con...  3.33 us
    gather x1, local copies, waits for them, and re-layouts, on_device(): return back.reshape(total)[place]  2.5 us
    dot_general x1, matrix products, masked_sims(): jnp.einsum('qd,kd->qk', queries, keys, preferred_element_type=jnp.float32)  2.44 us
    scatter x1, other arithmetic, on_device(): outgoing = jnp.zeros((total, width), jnp.bfloat16).at[place].set(unit)  2.14 us
  transfers between devices with their start and end apart: 3, of which 2 were waited for; matrix products, arithmetic and copies ran while one was open for 4% of the time, Pallas kernels for 0%

commit v1 on v0

--- a/solution.py
+++ b/solution.py
@@ -1,12 +1,183 @@
 import jax
 import jax.numpy as jnp
 from jax import lax
+from jax.experimental import pallas as pl
+from jax.experimental.pallas import tpu as pltpu
 from jax.sharding import PartitionSpec as P
 
 CLU_OWN = 16
 
 
 EPS = 1e-06
+
+GROUP = ("gx", "gy", "gz")
+
+
+def normalised(block):
+    vecs = block.astype(jnp.float32)
+    return (vecs * lax.rsqrt(jnp.sum(vecs * vecs, axis=1, keepdims=True) + EPS)).astype(
+        jnp.bfloat16
+    )
+
+
+def as_column(labels):
+    rows = labels.shape[1]
+    return jnp.transpose(jnp.broadcast_to(labels, (128, rows)))
+
+
+def best_of(queries, query_labels, keys, key_column, own=False):
+    sims = lax.dot_general(
+        keys, queries, (((1,), (1,)), ((), ())), preferred_element_type=jnp.float32
+    )
+    halves = []
+    for start in range(0, sims.shape[1], 128):
+        keep = key_column == query_labels[:, start : start + 128]
+        if own:
+            row = lax.broadcasted_iota(jnp.int32, keep.shape, 0)
+            column = lax.broadcasted_iota(jnp.int32, keep.shape, 1) + start
+            keep = keep & (row != column)
+        halves.append(
+            jnp.max(
+                jnp.where(keep, sims[:, start : start + 128], -1.0), axis=0, keepdims=True
+            )
+        )
+    return jnp.concatenate(halves, axis=1)
+
+
+def near_kernel(blocks, labels, best_ref, unit_ref):
+    query_labels = labels[0][...]
+    best = None
+    for at, (block, label) in enumerate(zip(blocks, labels)):
+        unit_ref[at] = normalised(block[...])
+        found = best_of(
+            unit_ref[0], query_labels, unit_ref[at], as_column(label[...]), own=at == 0
+        )
+        best = found if best is None else jnp.maximum(best, found)
+    best_ref[...] = best
+
+
+def far_kernel(unit_ref, back, ahead, labels, near_ref, mine, sibling, to_back, to_ahead):
+    own, other, prev, prev_other, succ, succ_other, l_back, l_ahead = [r[...] for r in labels]
+    u_back = normalised(back[...])
+    u_ahead = normalised(ahead[...])
+    c_back = as_column(l_back)
+    c_ahead = as_column(l_ahead)
+    mine[...] = jnp.maximum(
+        near_ref[...],
+        jnp.maximum(
+            best_of(unit_ref[0], own, u_back, c_back),
+            best_of(unit_ref[0], own, u_ahead, c_ahead),
+        ),
+    )
+    sibling[...] = jnp.maximum(
+        best_of(unit_ref[1], other, u_back, c_back),
+        best_of(unit_ref[1], other, u_ahead, c_ahead),
+    )
+    to_ahead[...] = jnp.maximum(
+        best_of(u_ahead, l_ahead, u_back, c_back),
+        jnp.maximum(
+            best_of(u_ahead, l_ahead, unit_ref[2], as_column(prev)),
+            best_of(u_ahead, l_ahead, unit_ref[3], as_column(prev_other)),
+        ),
+    )
+    to_back[...] = jnp.maximum(
+        best_of(u_back, l_back, u_ahead, c_ahead),
+        jnp.maximum(
+            best_of(u_back, l_back, unit_ref[4], as_column(succ)),
+            best_of(u_back, l_back, unit_ref[5], as_column(succ_other)),
+        ),
+    )
+
+
+def ring_perms(size_x, size_y, size_z):
+    chips = size_x * size_y
+    half = chips // 2
+
+    def device(place, core):
+        place = place % chips
+        x, y = (place, 0) if place < size_x else (chips - 1 - place, 1)
+        return (x * size_y + y) * size_z + core
+
+    def perm(to):
+        return [
+            (device(p, k), device(*to(p, k))) for p in range(chips) for k in range(size_z)
+        ]
+
+    def swapped(place, core):
+        return core if place % chips < half else 1 - core
+
+    return {
+        "sibling": perm(lambda p, k: (p, 1 - k)),
+        "next": perm(lambda p, k: (p + 1, k)),
+        "prev": perm(lambda p, k: (p - 1, k)),
+        "next_sibling": perm(lambda p, k: (p + 1, 1 - k)),
+        "prev_sibling": perm(lambda p, k: (p - 1, 1 - k)),
+        "relay_next": perm(lambda p, k: (p + 1, swapped(p + 1, k))),
+        "two_next": perm(lambda p, k: (p + 2, swapped(p + 2, k))),
+        "two_prev": perm(lambda p, k: (p - 2, k)),
+        "back_two_next": perm(lambda p, k: (p + 2, k)),
+        "back_two_prev": perm(lambda p, k: (p - 2, swapped(p, k))),
+    }
+
+
+def on_ring(embeds, cluster):
+    rows, width = embeds.shape
+    perms = ring_perms(*(lax.axis_size(a) for a in GROUP))
+
+    def send(value, name):
+        return lax.ppermute(value, GROUP, perms[name])
+
+    label = cluster.reshape(1, rows)
+    prev = send(embeds, "next")
+    succ = send(embeds, "prev")
+    other = send(embeds, "sibling")
+    labels = [label] + [
+        send(label, name)
+        for name in (
+            "sibling",
+            "next",
+            "next_sibling",
+            "prev",
+            "prev_sibling",
+            "two_next",
+            "two_prev",
+        )
+    ]
+    back = send(prev, "relay_next")
+    ahead = send(succ, "prev")
+    prev_other = send(prev, "sibling")
+    succ_other = send(succ, "sibling")
+
+    vmem = pl.BlockSpec(memory_space=pltpu.VMEM)
+    line = jax.ShapeDtypeStruct((1, rows), jnp.float32)
+    blocks = [embeds, other, prev, prev_other, succ, succ_other]
+    near, units = pl.pallas_call(
+        lambda *refs: near_kernel(refs[:6], refs[6:12], refs[12], refs[13]),
+        out_shape=[line, jax.ShapeDtypeStruct((6, rows, width), jnp.bfloat16)],
+        in_specs=[vmem] * 12,
+        out_specs=[vmem] * 2,
+        compiler_params=pltpu.CompilerParams(vmem_limit_bytes=32 * 2**20),
+        cost_estimate=pl.CostEstimate(
+            flops=12 * rows * rows * width, bytes_accessed=24 * rows * width, transcendentals=0
+        ),
+        name="near",
+    )(*blocks, *labels[:6])
+    mine, sibling, to_back, to_ahead = pl.pallas_call(
+        lambda *refs: far_kernel(refs[0], refs[1], refs[2], refs[3:11], *refs[11:]),
+        out_shape=[line] * 4,
+        in_specs=[vmem] * 12,
+        out_specs=[vmem] * 4,
+        compiler_params=pltpu.CompilerParams(vmem_limit_bytes=32 * 2**20),
+        cost_estimate=pl.CostEstimate(
+            flops=20 * rows * rows * width, bytes_accessed=16 * rows * width, transcendentals=0
+        ),
+        name="far",
+    )(units, back, ahead, *labels, near)
+    best = jnp.maximum(
+        jnp.maximum(mine, send(sibling, "sibling")),
+        jnp.maximum(send(to_back, "back_two_prev"), send(to_ahead, "back_two_next")),
+    )
+    return best.reshape(rows)
 
 
 def masked_sims(queries, query_labels, query_ids, keys, key_labels, key_ids):
@@ -19,17 +190,14 @@
     return jnp.where(keep, sims, -1.0)
 
 
-def on_device(embeds, cluster):
+def by_owner(embeds, cluster):
     rows, width = embeds.shape
     size_x = lax.axis_size("gx")
     size_y = lax.axis_size("gy")
     owners = size_x * size_y
     cap = 2 * rows // owners
     total = owners * cap
-    vecs = embeds.astype(jnp.float32)
-    unit = (vecs * lax.rsqrt(jnp.sum(vecs * vecs, axis=1, keepdims=True) + EPS)).astype(
-        jnp.bfloat16
-    )
+    unit = normalised(embeds)
     target = cluster // CLU_OWN
     onehot = (target[:, None] == jnp.arange(owners, dtype=jnp.int32)[None, :]).astype(jnp.int32)
     before = jnp.cumsum(onehot, axis=0) - onehot
@@ -67,9 +235,11 @@
 
 
 def solution(mesh):
+    shape = mesh.shape
+    ring = shape["gx"] * shape["gy"] == 8 and shape["gy"] == 2 and shape["gz"] == 2
     placed = (P(("parts", "gx", "gy", "gz"), None), P(("parts", "gx", "gy", "gz")))
     return jax.shard_map(
-        on_device,
+        on_ring if ring else by_owner,
         mesh=mesh,
         in_specs=placed,
         out_specs=P(("parts", "gx", "gy", "gz")),

time: 73.8 us -> 36.3 us (0.49)
  blocking collectives: 23.5 us -> 0 us
  between operations: 13.5 us -> 0.04 us
  starting transfers between devices: 6.92 us -> 14.6 us
  other arithmetic: 7.35 us -> 0.57 us
  local copies, waits for them, and re-layouts: 6.87 us -> 1.63 us
  waiting for transfers between devices: 12.9 us -> 17.4 us
  matrix products: 2.44 us -> 0 us
  Pallas kernels: 0 us -> 1.91 us
    all_to_all x1 -> x0, blocking collectives: 21.7 us -> none  [on_device(): lax.all_to_all(outgoing.reshape(owners, cap, width), ('gx', 'gy'), split_...]
    ppermute x0 -> x17, waiting for transfers between devices: none -> 17.4 us  [send(): return lax.ppermute(value, GROUP, perms[name])]
    ppermute x0 -> x17, starting transfers between devices: none -> 14.6 us  [send(): return lax.ppermute(value, GROUP, perms[name])]
    all_to_all x2 -> x0, waiting for transfers between devices: 12.8 us -> none  [the longest x1 6.45 us: on_device(): lax.all_to_all(out_labels.reshape(owners, cap), ('gx', 'gy'), split_axis=...]
    all_to_all x2 -> x0, starting transfers between devices: 6.92 us -> none  [the longest x1 3.59 us: on_device(): lax.all_to_all(out_labels.reshape(owners, cap), ('gx', 'gy'), split_axis=...]
    gather x1 -> x0, local copies, waits for them, and re-layouts: 2.5 us -> none  [on_device(): return back.reshape(total)[place]]
    dot_general x1 -> x0, matrix products: 2.44 us -> none  [masked_sims(): jnp.einsum('qd,kd->qk', queries, keys, preferred_element_type=jnp.float32)]
    scatter x1 -> x0, other arithmetic: 2.14 us -> none  [on_device(): outgoing = jnp.zeros((total, width), jnp.bfloat16).at[place].set(unit)]
  transfers between devices with their start and end apart: 3 -> 17, of which waited for: 2 -> 9; matrix products, arithmetic and copies ran while one was open for 4% -> 0% of each run, Pallas kernels for 0% -> 3%
where the time goes in v1:
time: 36.3 us; the launch traced here: 36.2 us
  waiting for transfers between devices  17.4 us (48%)
  starting transfers between devices  14.6 us (40%)
  Pallas kernels  1.91 us (5%)
  local copies, waits for them, and re-layouts  1.63 us (4%)
  other arithmetic  0.57 us (2%)
    ppermute x17, waiting for transfers between devices, send(): return lax.ppermute(value, GROUP, perms[name])  17.4 us
    ppermute x17, starting transfers between devices, send(): return lax.ppermute(value, GROUP, perms[name])  14.6 us
    unnamed x6, local copies, waits for them, and re-layouts  1.63 us
    pallas_call x1, Pallas kernels, on_ring(): pl.pallas_call(lambda *refs: far_kernel(refs[0], refs[1], refs[2], refs[3...  0.97 us
    pallas_call x1, Pallas kernels, on_ring(): pl.pallas_call(lambda *refs: near_kernel(refs[:6], refs[6:12], refs[12],...  0.95 us
  transfers between devices with their start and end apart: 17, of which 9 were waited for; matrix products, arithmetic and copies ran while one was open for 0% of the time, Pallas kernels for 3%

profile of v1, /device:TPU:0, one launch (start us, length us, event | category | flops | bytes accessed | tf_op | source)
XLA Modules:
  0.0 36.2 jit_solution(17714118115844623083)
XLA Ops:
  0.0 3.0 %collective-permute-start.1 = (bf16[256,512]{1,0:T(8,128)(2,1)}, bf16[256,512]{1,0:T(8,128)(2,1)S(1)}, u32[]{:S(2)}, u32[]{:S(2)}) collective-permute-start(bf16[256,512]{1,0:T(8,128)(2,1)} %refs_0_.1), channel_id=1, source_target_pairs={{0,4},{1,5},{4,8},{5,9},{8,12},{9,13},{12,14},{13,15},{14,10},{15,... | collective-permute-start | bytes 786440 | tf_op jit(solution)/shard_map/ppermute | solution.py:128
  3.0 0.0 collective-permute-start.3
  3.0 0.0 collective-permute-start
  3.0 6.4 %collective-permute-done.1.refs_2_ = bf16[256,512]{1,0:T(8,128)(2,1)S(1)} collective-permute-done((bf16[256,512]{1,0:T(8,128)(2,1)}, bf16[256,512]{1,0:T(8,128)(2,1)S(1)}, u32[]{:S(2)}, u32[]{:S(2)}) %collective-permute-start.1) | collective-permute-done | bytes 262176 | tf_op jit(solution)/shard_map/ppermute | solution.py:128
  9.5 0.0 collective-permute-start.2
  9.5 1.5 %collective-permute-done.3.refs_4_ = bf16[256,512]{1,0:T(8,128)(2,1)S(1)} collective-permute-done((bf16[256,512]{1,0:T(8,128)(2,1)}, bf16[256,512]{1,0:T(8,128)(2,1)S(1)}, u32[]{:S(2)}, u32[]{:S(2)}) %collective-permute-start.3) | collective-permute-done | bytes 262176 | tf_op jit(solution)/shard_map/ppermute | solution.py:128
  11.0 0.0 collective-permute-start.4
  11.0 0.5 %collective-permute-start.5 = (s32[1,256]{1,0:T(1,128)}, s32[1,256]{1,0:T(1,128)S(1)}, u32[]{:S(2)}, u32[]{:S(2)}) collective-permute-start(s32[1,256]{1,0:T(1,128)} %bitcast.2), channel_id=1, source_target_pairs={{0,1},{1,0},{4,5},{5,4},{8,9},{9,8},{12,13},{13,12},{14,15},{15,14... | collective-permute-start | bytes 3080 | tf_op jit(solution)/shard_map/ppermute | solution.py:128
  11.5 1.6 %collective-permute-start.6 = (s32[1,256]{1,0:T(1,128)}, s32[1,256]{1,0:T(1,128)S(1)}, u32[]{:S(2)}, u32[]{:S(2)}) collective-permute-start(s32[1,256]{1,0:T(1,128)} %bitcast.3), channel_id=1, source_target_pairs={{0,4},{1,5},{4,8},{5,9},{8,12},{9,13},{12,14},{13,15},{14,10},{15,... | collective-permute-start | bytes 3080 | tf_op jit(solution)/shard_map/ppermute | solution.py:128
  13.1 0.0 collective-permute-done.5.refs_7_.refs_4_
  13.1 1.0 %collective-permute-start.7 = (s32[1,256]{1,0:T(1,128)}, s32[1,256]{1,0:T(1,128)S(1)}, u32[]{:S(2)}, u32[]{:S(2)}) collective-permute-start(s32[1,256]{1,0:T(1,128)} %bitcast.4), channel_id=1, source_target_pairs={{0,5},{1,4},{4,9},{5,8},{8,13},{9,12},{12,15},{13,14},{14,11},{15,... | collective-permute-start | bytes 3080 | tf_op jit(solution)/shard_map/ppermute | solution.py:128
  14.0 1.2 %collective-permute-done.6.refs_8_.refs_5_ = s32[1,256]{1,0:T(1,128)S(1)} collective-permute-done((s32[1,256]{1,0:T(1,128)}, s32[1,256]{1,0:T(1,128)S(1)}, u32[]{:S(2)}, u32[]{:S(2)}) %collective-permute-start.6) | collective-permute-done | bytes 1056 | tf_op jit(solution)/shard_map/ppermute | solution.py:128
  15.3 0.3 collective-permute-start.8
  15.6 0.7 %collective-permute-done.7.refs_9_.refs_6_ = s32[1,256]{1,0:T(1,128)S(1)} collective-permute-done((s32[1,256]{1,0:T(1,128)}, s32[1,256]{1,0:T(1,128)S(1)}, u32[]{:S(2)}, u32[]{:S(2)}) %collective-permute-start.7) | collective-permute-done | bytes 1056 | tf_op jit(solution)/shard_map/ppermute | solution.py:128
  16.3 0.2 collective-permute-start.9
  16.5 2.6 %collective-permute-done.8.refs_10_.refs_7_ = s32[1,256]{1,0:T(1,128)S(1)} collective-permute-done((s32[1,256]{1,0:T(1,128)}, s32[1,256]{1,0:T(1,128)S(1)}, u32[]{:S(2)}, u32[]{:S(2)}) %collective-permute-start.8) | collective-permute-done | bytes 1056 | tf_op jit(solution)/shard_map/ppermute | solution.py:128
  19.1 1.6 %collective-permute-start.10 = (bf16[256,512]{1,0:T(8,128)(2,1)S(1)}, bf16[256,512]{1,0:T(8,128)(2,1)S(1)}, u32[]{:S(2)}, u32[]{:S(2)}) collective-permute-start(bf16[256,512]{1,0:T(8,128)(2,1)S(1)} %collective-permute-done.1.refs_2_), channel_id=1, source_target_pairs={{0,4},{1,5},{4,8},{5,9},{8,12},{9,13},{12,15},{13,14},{14,11},{15,... | collective-permute-start | bytes 786440 | tf_op jit(solution)/shard_map/ppermute | solution.py:128
  20.7 0.5 %collective-permute-start.11 = (bf16[256,512]{1,0:T(8,128)(2,1)S(1)}, bf16[256,512]{1,0:T(8,128)(2,1)S(1)}, u32[]{:S(2)}, u32[]{:S(2)}) collective-permute-start(bf16[256,512]{1,0:T(8,128)(2,1)S(1)} %collective-permute-done.3.refs_4_), channel_id=1, source_target_pairs={{0,2},{1,3},{4,0},{5,1},{8,4},{9,5},{12,8},{13,9},{14,12},{15,13},... | collective-permute-start | bytes 786440 | tf_op jit(solution)/shard_map/ppermute | solution.py:128
  21.1 2.6 %collective-permute-start.12 = (s32[1,256]{1,0:T(1,128)}, s32[1,256]{1,0:T(1,128)S(1)}, u32[]{:S(2)}, u32[]{:S(2)}) collective-permute-start(s32[1,256]{1,0:T(1,128)} %bitcast.7), channel_id=1, source_target_pairs={{0,8},{1,9},{4,12},{5,13},{8,15},{9,14},{12,11},{13,10},{14,7},{15... | collective-permute-start | bytes 3080 | tf_op jit(solution)/shard_map/ppermute | solution.py:128
  23.7 0.3 collective-permute-start.13
  24.0 0.9 %copy-done = bf16[256,512]{1,0:T(8,128)(2,1)S(1)} copy-done((bf16[256,512]{1,0:T(8,128)(2,1)S(1)}, bf16[256,512]{1,0:T(8,128)(2,1)}, u32[]{:S(2)}) %copy-start) | copy-done | bytes 262168
  25.0 0.7 %copy-done.1 = s32[256]{0:T(256)S(1)} copy-done((s32[256]{0:T(256)S(1)}, s32[256]{0:T(256)}, u32[]{:S(2)}) %copy-start.1) | copy-done | bytes 1048
  25.7 0.9 %near.1 = (f32[1,256]{1,0:T(1,128)S(1)}, bf16[6,256,512]{2,1,0:T(8,128)(2,1)S(1)}) custom-call(bf16[256,512]{1,0:T(8,128)(2,1)S(1)} %copy-done, bf16[256,512]{1,0:T(8,128)(2,1)S(1)} %collective-permute-done.refs_1_, bf16[256,512]{1,0:T(8,128)(2,1)S(1)} %collective-permute-done.1.refs_2_, bf16[256,512]{1,0:T(8,128)(2,1)S(1)} %collective-permute-done.2.refs_3_, ...), custom_call_target="tpu_custom_call" | custom-call | flops 402653184 | bytes 3145728 | tf_op jit(solution)/shard_map/near/pallas_call | solution.py:154
  26.6 0.9 %collective-permute-done.12.refs_9_ = s32[1,256]{1,0:T(1,128)S(1)} collective-permute-done((s32[1,256]{1,0:T(1,128)}, s32[1,256]{1,0:T(1,128)S(1)}, u32[]{:S(2)}, u32[]{:S(2)}) %collective-permute-start.12) | collective-permute-done | bytes 1056 | tf_op jit(solution)/shard_map/ppermute | solution.py:128
  27.5 1.4 %collective-permute-done.13.refs_10_ = s32[1,256]{1,0:T(1,128)S(1)} collective-permute-done((s32[1,256]{1,0:T(1,128)}, s32[1,256]{1,0:T(1,128)S(1)}, u32[]{:S(2)}, u32[]{:S(2)}) %collective-permute-start.13) | collective-permute-done | bytes 1056 | tf_op jit(solution)/shard_map/ppermute | solution.py:128
  28.9 1.0 %far.1 = (f32[1,256]{1,0:T(1,128)S(1)}, f32[1,256]{1,0:T(1,128)S(1)}, f32[1,256]{1,0:T(1,128)S(1)}, f32[1,256]{1,0:T(1,128)S(1)}) custom-call(bf16[6,256,512]{2,1,0:T(8,128)(2,1)S(1)} %get-tuple-element.11.refs_0_, bf16[256,512]{1,0:T(8,128)(2,1)S(1)} %collective-permute-done.10.refs_1_, bf16[256,512]{1,0:T(8,128)(2,1)S(1)} %collective-permute-done.11.refs_2_, ...), custom_call_target="tpu_custom_call" | custom-call | flops 671088640 | bytes 2097152 | tf_op jit(solution)/shard_map/far/pallas_call | solution.py:165
  29.9 0.1 collective-permute-start.14
  29.9 1.2 %collective-permute-start.15 = (f32[1,256]{1,0:T(1,128)S(1)}, f32[1,256]{1,0:T(1,128)S(1)}, u32[]{:S(2)}, u32[]{:S(2)}) collective-permute-start(f32[1,256]{1,0:T(1,128)S(1)} %get-tuple-element.15), channel_id=1, source_target_pairs={{0,6},{1,7},{4,2},{5,3},{8,0},{9,1},{12,4},{13,5},{14,9},{15,8},{1... | collective-permute-start | bytes 3080 | tf_op jit(solution)/shard_map/ppermute | solution.py:128
  31.1 1.8 %collective-permute-start.16 = (f32[1,256]{1,0:T(1,128)S(1)}, f32[1,256]{1,0:T(1,128)S(1)}, u32[]{:S(2)}, u32[]{:S(2)}) collective-permute-start(f32[1,256]{1,0:T(1,128)S(1)} %get-tuple-element.16), channel_id=1, source_target_pairs={{0,8},{1,9},{4,12},{5,13},{8,14},{9,15},{12,10},{13,11},{14,6},{15... | collective-permute-start | bytes 3080 | tf_op jit(solution)/shard_map/ppermute | solution.py:128
  32.9 1.5 %collective-permute-done.15 = f32[1,256]{1,0:T(1,128)S(1)} collective-permute-done((f32[1,256]{1,0:T(1,128)S(1)}, f32[1,256]{1,0:T(1,128)S(1)}, u32[]{:S(2)}, u32[]{:S(2)}) %collective-permute-start.15) | collective-permute-done | bytes 1056 | tf_op jit(solution)/shard_map/ppermute | solution.py:128
  34.5 1.1 %collective-permute-done.16 = f32[1,256]{1,0:T(1,128)S(1)} collective-permute-done((f32[1,256]{1,0:T(1,128)S(1)}, f32[1,256]{1,0:T(1,128)S(1)}, u32[]{:S(2)}, u32[]{:S(2)}) %collective-permute-start.16) | collective-permute-done | bytes 1056 | tf_op jit(solution)/shard_map/ppermute | solution.py:128
  35.6 0.6 %maximum_maximum_fusion = f32[1,256]{1,0:T(1,128)} fusion(f32[1,256]{1,0:T(1,128)S(1)} %collective-permute-done.15, f32[1,256]{1,0:T(1,128)S(1)} %collective-permute-done.16, f32[1,256]{1,0:T(1,128)S(1)} %get-tuple-element.13, f32[1,256]{1,0:T(1,128)S(1)} %collective-permute-done.14), kind=kLoop, calls=%fused_computation | loop fusion | flops 768 | bytes 5120 | tf_op jit(solution)/shard_map/max | solution.py:176
  (11 shorter events, 0.0 us)
Async XLA Ops:
  0.0 28.9 %copy-start.2 = (s32[256]{0:T(256)S(1)}, s32[256]{0:T(256)}, u32[]{:S(2)}) copy-start(s32[256]{0:T(256)} %param.3) | copy-start | bytes 3076
  0.0 9.5 %collective-permute-start.1 = (bf16[256,512]{1,0:T(8,128)(2,1)}, bf16[256,512]{1,0:T(8,128)(2,1)S(1)}, u32[]{:S(2)}, u32[]{:S(2)}) collective-permute-start(bf16[256,512]{1,0:T(8,128)(2,1)} %refs_0_.1), channel_id=1, source_target_pairs={{0,4},{1,5},{4,8},{5,9},{8,12},{9,13},{12,14},{13,15},{14,10},{15,... | collective-permute-start | bytes 786440 | tf_op jit(solution)/shard_map/ppermute | solution.py:128
  3.0 8.0 %collective-permute-start.3 = (bf16[256,512]{1,0:T(8,128)(2,1)}, bf16[256,512]{1,0:T(8,128)(2,1)S(1)}, u32[]{:S(2)}, u32[]{:S(2)}) collective-permute-start(bf16[256,512]{1,0:T(8,128)(2,1)} %refs_0_.1), channel_id=1, source_target_pairs={{0,2},{1,3},{4,0},{5,1},{8,4},{9,5},{12,8},{13,9},{14,12},{15,13},... | collective-permute-start | bytes 786440 | tf_op jit(solution)/shard_map/ppermute | solution.py:128
  3.0 18.1 %collective-permute-start = (bf16[256,512]{1,0:T(8,128)(2,1)}, bf16[256,512]{1,0:T(8,128)(2,1)S(1)}, u32[]{:S(2)}, u32[]{:S(2)}) collective-permute-start(bf16[256,512]{1,0:T(8,128)(2,1)} %refs_0_.1), channel_id=1, source_target_pairs={{0,1},{1,0},{4,5},{5,4},{8,9},{9,8},{12,13},{13,12},{14,15},{15,14... | collective-permute-start | bytes 786440 | tf_op jit(solution)/shard_map/ppermute | solution.py:128
  9.5 14.2 %collective-permute-start.2 = (bf16[256,512]{1,0:T(8,128)(2,1)S(1)}, bf16[256,512]{1,0:T(8,128)(2,1)S(1)}, u32[]{:S(2)}, u32[]{:S(2)}) collective-permute-start(bf16[256,512]{1,0:T(8,128)(2,1)S(1)} %collective-permute-done.1.refs_2_), channel_id=1, source_target_pairs={{0,1},{1,0},{4,5},{5,4},{8,9},{9,8},{12,13},{13,12},{14,15},{15,14... | collective-permute-start | bytes 786440 | tf_op jit(solution)/shard_map/ppermute | solution.py:128
  11.0 13.0 %collective-permute-start.4 = (bf16[256,512]{1,0:T(8,128)(2,1)S(1)}, bf16[256,512]{1,0:T(8,128)(2,1)S(1)}, u32[]{:S(2)}, u32[]{:S(2)}) collective-permute-start(bf16[256,512]{1,0:T(8,128)(2,1)S(1)} %collective-permute-done.3.refs_4_), channel_id=1, source_target_pairs={{0,1},{1,0},{4,5},{5,4},{8,9},{9,8},{12,13},{13,12},{14,15},{15,14... | collective-permute-start | bytes 786440 | tf_op jit(solution)/shard_map/ppermute | solution.py:128
  11.0 2.1 %collective-permute-start.5 = (s32[1,256]{1,0:T(1,128)}, s32[1,256]{1,0:T(1,128)S(1)}, u32[]{:S(2)}, u32[]{:S(2)}) collective-permute-start(s32[1,256]{1,0:T(1,128)} %bitcast.2), channel_id=1, source_target_pairs={{0,1},{1,0},{4,5},{5,4},{8,9},{9,8},{12,13},{13,12},{14,15},{15,14... | collective-permute-start | bytes 3080 | tf_op jit(solution)/shard_map/ppermute | solution.py:128
  11.5 3.8 %collective-permute-start.6 = (s32[1,256]{1,0:T(1,128)}, s32[1,256]{1,0:T(1,128)S(1)}, u32[]{:S(2)}, u32[]{:S(2)}) collective-permute-start(s32[1,256]{1,0:T(1,128)} %bitcast.3), channel_id=1, source_target_pairs={{0,4},{1,5},{4,8},{5,9},{8,12},{9,13},{12,14},{13,15},{14,10},{15,... | collective-permute-start | bytes 3080 | tf_op jit(solution)/shard_map/ppermute | solution.py:128
  13.1 3.2 %collective-permute-start.7 = (s32[1,256]{1,0:T(1,128)}, s32[1,256]{1,0:T(1,128)S(1)}, u32[]{:S(2)}, u32[]{:S(2)}) collective-permute-start(s32[1,256]{1,0:T(1,128)} %bitcast.4), channel_id=1, source_target_pairs={{0,5},{1,4},{4,9},{5,8},{8,13},{9,12},{12,15},{13,14},{14,11},{15,... | collective-permute-start | bytes 3080 | tf_op jit(solution)/shard_map/ppermute | solution.py:128
  15.3 3.8 %collective-permute-start.8 = (s32[1,256]{1,0:T(1,128)}, s32[1,256]{1,0:T(1,128)S(1)}, u32[]{:S(2)}, u32[]{:S(2)}) collective-permute-start(s32[1,256]{1,0:T(1,128)} %bitcast.5), channel_id=1, source_target_pairs={{0,2},{1,3},{4,0},{5,1},{8,4},{9,5},{12,8},{13,9},{14,12},{15,13},... | collective-permute-start | bytes 3080 | tf_op jit(solution)/shard_map/ppermute | solution.py:128
  16.3 4.4 %collective-permute-start.9 = (s32[1,256]{1,0:T(1,128)}, s32[1,256]{1,0:T(1,128)S(1)}, u32[]{:S(2)}, u32[]{:S(2)}) collective-permute-start(s32[1,256]{1,0:T(1,128)} %bitcast.6), channel_id=1, source_target_pairs={{0,3},{1,2},{4,1},{5,0},{8,5},{9,4},{12,9},{13,8},{14,13},{15,12},... | collective-permute-start | bytes 3080 | tf_op jit(solution)/shard_map/ppermute | solution.py:128
  19.1 9.8 %collective-permute-start.10 = (bf16[256,512]{1,0:T(8,128)(2,1)S(1)}, bf16[256,512]{1,0:T(8,128)(2,1)S(1)}, u32[]{:S(2)}, u32[]{:S(2)}) collective-permute-start(bf16[256,512]{1,0:T(8,128)(2,1)S(1)} %collective-permute-done.1.refs_2_), channel_id=1, source_target_pairs={{0,4},{1,5},{4,8},{5,9},{8,12},{9,13},{12,15},{13,14},{14,11},{15,... | collective-permute-start | bytes 786440 | tf_op jit(solution)/shard_map/ppermute | solution.py:128
  20.7 8.2 %collective-permute-start.11 = (bf16[256,512]{1,0:T(8,128)(2,1)S(1)}, bf16[256,512]{1,0:T(8,128)(2,1)S(1)}, u32[]{:S(2)}, u32[]{:S(2)}) collective-permute-start(bf16[256,512]{1,0:T(8,128)(2,1)S(1)} %collective-permute-done.3.refs_4_), channel_id=1, source_target_pairs={{0,2},{1,3},{4,0},{5,1},{8,4},{9,5},{12,8},{13,9},{14,12},{15,13},... | collective-permute-start | bytes 786440 | tf_op jit(solution)/shard_map/ppermute | solution.py:128
  21.1 6.4 %collective-permute-start.12 = (s32[1,256]{1,0:T(1,128)}, s32[1,256]{1,0:T(1,128)S(1)}, u32[]{:S(2)}, u32[]{:S(2)}) collective-permute-start(s32[1,256]{1,0:T(1,128)} %bitcast.7), channel_id=1, source_target_pairs={{0,8},{1,9},{4,12},{5,13},{8,15},{9,14},{12,11},{13,10},{14,7},{15... | collective-permute-start | bytes 3080 | tf_op jit(solution)/shard_map/ppermute | solution.py:128
  23.7 5.2 %collective-permute-start.13 = (s32[1,256]{1,0:T(1,128)}, s32[1,256]{1,0:T(1,128)S(1)}, u32[]{:S(2)}, u32[]{:S(2)}) collective-permute-start(s32[1,256]{1,0:T(1,128)} %bitcast.8), channel_id=1, source_target_pairs={{0,6},{1,7},{4,2},{5,3},{8,0},{9,1},{12,4},{13,5},{14,8},{15,9},{1... | collective-permute-start | bytes 3080 | tf_op jit(solution)/shard_map/ppermute | solution.py:128
  24.0 1.0 %copy-start = (bf16[256,512]{1,0:T(8,128)(2,1)S(1)}, bf16[256,512]{1,0:T(8,128)(2,1)}, u32[]{:S(2)}) copy-start(bf16[256,512]{1,0:T(8,128)(2,1)} %refs_0_.1) | copy-start | bytes 786436
  25.0 0.7 %copy-start.1 = (s32[256]{0:T(256)S(1)}, s32[256]{0:T(256)}, u32[]{:S(2)}) copy-start(s32[256]{0:T(256)} %param.3) | copy-start | bytes 3076
  29.9 3.1 %collective-permute-start.14 = (f32[1,256]{1,0:T(1,128)S(1)}, f32[1,256]{1,0:T(1,128)S(1)}, u32[]{:S(2)}, u32[]{:S(2)}) collective-permute-start(f32[1,256]{1,0:T(1,128)S(1)} %get-tuple-element.14), channel_id=1, source_target_pairs={{0,1},{1,0},{4,5},{5,4},{8,9},{9,8},{12,13},{13,12},{14,15},{15,14... | collective-permute-start | bytes 3080 | tf_op jit(solution)/shard_map/ppermute | solution.py:128
  29.9 4.5 %collective-permute-start.15 = (f32[1,256]{1,0:T(1,128)S(1)}, f32[1,256]{1,0:T(1,128)S(1)}, u32[]{:S(2)}, u32[]{:S(2)}) collective-permute-start(f32[1,256]{1,0:T(1,128)S(1)} %get-tuple-element.15), channel_id=1, source_target_pairs={{0,6},{1,7},{4,2},{5,3},{8,0},{9,1},{12,4},{13,5},{14,9},{15,8},{1... | collective-permute-start | bytes 3080 | tf_op jit(solution)/shard_map/ppermute | solution.py:128
  31.1 4.5 %collective-permute-start.16 = (f32[1,256]{1,0:T(1,128)S(1)}, f32[1,256]{1,0:T(1,128)S(1)}, u32[]{:S(2)}, u32[]{:S(2)}) collective-permute-start(f32[1,256]{1,0:T(1,128)S(1)} %get-tuple-element.16), channel_id=1, source_target_pairs={{0,8},{1,9},{4,12},{5,13},{8,14},{9,15},{12,10},{13,11},{14,6},{15... | collective-permute-start | bytes 3080 | tf_op jit(solution)/shard_map/ppermute | solution.py:128

commit v2 on v0

--- a/solution.py
+++ b/solution.py
@@ -1,12 +1,194 @@
 import jax
 import jax.numpy as jnp
 from jax import lax
+from jax.experimental import pallas as pl
+from jax.experimental.pallas import tpu as pltpu
 from jax.sharding import PartitionSpec as P
 
 CLU_OWN = 16
 
 
 EPS = 1e-06
+
+GROUP = ("gx", "gy", "gz")
+
+
+def normalised(block):
+    vecs = block.astype(jnp.float32)
+    return (vecs * lax.rsqrt(jnp.sum(vecs * vecs, axis=1, keepdims=True) + EPS)).astype(
+        jnp.bfloat16
+    )
+
+
+LABEL_ROWS = 16
+CHUNKS = 4
+
+
+def pack_kernel(embeds, label, packed, raw, line, sems):
+    rows, width = embeds.shape
+    step = rows // CHUNKS
+    line_copy = pltpu.make_async_copy(label, line, sems.at[CHUNKS])
+    line_copy.start()
+    copies = []
+    for i in range(CHUNKS):
+        part = pl.ds(i * step, step)
+        copies.append(pltpu.make_async_copy(embeds.at[part], raw.at[part], sems.at[i]))
+        copies[-1].start()
+    line_copy.wait()
+    lines = jnp.broadcast_to(line[...].astype(jnp.float32), (LABEL_ROWS, rows))
+    packed[rows:, :rows] = lines.astype(jnp.bfloat16)
+    packed[rows:, rows:] = jnp.zeros((LABEL_ROWS, width - rows), jnp.bfloat16)
+    for i in range(CHUNKS):
+        part = pl.ds(i * step, step)
+        copies[i].wait()
+        packed[part, :] = normalised(raw[part, :])
+
+
+class Block:
+    def __init__(self, ref):
+        self.rows = ref.shape[0] - LABEL_ROWS
+        self.unit = ref[: self.rows, :]
+        self.label = ref[self.rows :, : self.rows].astype(jnp.float32)[:1]
+
+    def column(self):
+        return jnp.transpose(jnp.broadcast_to(self.label, (128, self.rows)))
+
+
+def best_of(queries, keys, key_column, own=False):
+    sims = lax.dot_general(
+        keys.unit, queries.unit, (((1,), (1,)), ((), ())), preferred_element_type=jnp.float32
+    )
+    halves = []
+    for start in range(0, sims.shape[1], 128):
+        keep = key_column == queries.label[:, start : start + 128]
+        if own:
+            row = lax.broadcasted_iota(jnp.int32, keep.shape, 0)
+            column = lax.broadcasted_iota(jnp.int32, keep.shape, 1) + start
+            keep = keep & (row != column)
+        halves.append(
+            jnp.max(
+                jnp.where(keep, sims[:, start : start + 128], -1.0), axis=0, keepdims=True
+            )
+        )
+    return jnp.concatenate(halves, axis=1)
+
+
+def near_kernel(*refs):
+    *blocks, best_ref = refs
+    mine = Block(blocks[0])
+    best = best_of(mine, mine, mine.column(), own=True)
+    for ref in blocks[1:]:
+        keys = Block(ref)
+        best = jnp.maximum(best, best_of(mine, keys, keys.column()))
+    best_ref[...] = best
+
+
+def far_kernel(
+    own, prev, prev_other, succ, succ_other, back, ahead, near, mine, to_back, to_ahead
+):
+    own, back, ahead = Block(own), Block(back), Block(ahead)
+    c_own, c_back, c_ahead = own.column(), back.column(), ahead.column()
+    mine[...] = jnp.maximum(
+        near[...], jnp.maximum(best_of(own, back, c_back), best_of(own, ahead, c_ahead))
+    )
+    found = jnp.maximum(best_of(ahead, back, c_back), best_of(ahead, own, c_own))
+    for ref in (prev, prev_other):
+        keys = Block(ref)
+        found = jnp.maximum(found, best_of(ahead, keys, keys.column()))
+    to_ahead[...] = found
+    found = jnp.maximum(best_of(back, ahead, c_ahead), best_of(back, own, c_own))
+    for ref in (succ, succ_other):
+        keys = Block(ref)
+        found = jnp.maximum(found, best_of(back, keys, keys.column()))
+    to_back[...] = found
+
+
+def ring_perms(size_x, size_y, size_z):
+    chips = size_x * size_y
+
+    def device(place, core):
+        place = place % chips
+        x, y = (place, 0) if place < size_x else (chips - 1 - place, 1)
+        return (x * size_y + y) * size_z + core
+
+    def perm(to):
+        return [
+            (device(p, k), device(*to(p, k))) for p in range(chips) for k in range(size_z)
+        ]
+
+    def from_back(place, core):
+        return core ^ (place % chips in (0, 1))
+
+    def from_ahead(place, core):
+        return core ^ (place % chips not in (chips - 2, chips - 1))
+
+    return {
+        "sibling": perm(lambda p, k: (p, 1 - k)),
+        "next": perm(lambda p, k: (p + 1, k)),
+        "prev": perm(lambda p, k: (p - 1, k)),
+        "on_next": perm(lambda p, k: (p + 1, from_back(p + 1, k))),
+        "on_prev": perm(lambda p, k: (p - 1, from_ahead(p - 1, k))),
+        "home_back": perm(lambda p, k: (p - 2, from_back(p, k))),
+        "home_ahead": perm(lambda p, k: (p + 2, from_ahead(p, k))),
+    }
+
+
+def on_ring(embeds, cluster):
+    rows, width = embeds.shape
+    perms = ring_perms(*(lax.axis_size(a) for a in GROUP))
+
+    def send(value, name):
+        return lax.ppermute(value, GROUP, perms[name])
+
+    vmem = pl.BlockSpec(memory_space=pltpu.VMEM)
+    line = jax.ShapeDtypeStruct((1, rows), jnp.float32)
+    own = pl.pallas_call(
+        pack_kernel,
+        out_shape=jax.ShapeDtypeStruct((rows + LABEL_ROWS, width), jnp.bfloat16),
+        in_specs=[pl.BlockSpec(memory_space=pl.ANY)] * 2,
+        out_specs=vmem,
+        scratch_shapes=[
+            pltpu.VMEM((rows, width), jnp.bfloat16),
+            pltpu.VMEM((1, rows), jnp.int32),
+            pltpu.SemaphoreType.DMA((CHUNKS + 1,)),
+        ],
+        compiler_params=pltpu.CompilerParams(vmem_limit_bytes=60 * 2**20),
+        name="pack",
+    )(embeds, cluster.reshape(1, rows))
+    prev = send(own, "next")
+    succ = send(own, "prev")
+    other = send(own, "sibling")
+    back = send(prev, "on_next")
+    ahead = send(succ, "on_prev")
+    prev_other = send(prev, "sibling")
+    succ_other = send(succ, "sibling")
+    params = pltpu.CompilerParams(vmem_limit_bytes=32 * 2**20)
+    near = pl.pallas_call(
+        near_kernel,
+        out_shape=line,
+        in_specs=[vmem] * 6,
+        out_specs=vmem,
+        compiler_params=params,
+        cost_estimate=pl.CostEstimate(
+            flops=12 * rows * rows * width, bytes_accessed=12 * rows * width, transcendentals=0
+        ),
+        name="near",
+    )(own, other, prev, prev_other, succ, succ_other)
+    mine, to_back, to_ahead = pl.pallas_call(
+        far_kernel,
+        out_shape=[line] * 3,
+        in_specs=[vmem] * 8,
+        out_specs=[vmem] * 3,
+        compiler_params=params,
+        cost_estimate=pl.CostEstimate(
+            flops=20 * rows * rows * width, bytes_accessed=14 * rows * width, transcendentals=0
+        ),
+        name="far",
+    )(own, prev, prev_other, succ, succ_other, back, ahead, near)
+    best = jnp.maximum(
+        mine, jnp.maximum(send(to_back, "home_back"), send(to_ahead, "home_ahead"))
+    )
+    return best.reshape(rows)
 
 
 def masked_sims(queries, query_labels, query_ids, keys, key_labels, key_ids):
@@ -19,17 +201,14 @@
     return jnp.where(keep, sims, -1.0)
 
 
-def on_device(embeds, cluster):
+def by_owner(embeds, cluster):
     rows, width = embeds.shape
     size_x = lax.axis_size("gx")
     size_y = lax.axis_size("gy")
     owners = size_x * size_y
     cap = 2 * rows // owners
     total = owners * cap
-    vecs = embeds.astype(jnp.float32)
-    unit = (vecs * lax.rsqrt(jnp.sum(vecs * vecs, axis=1, keepdims=True) + EPS)).astype(
-        jnp.bfloat16
-    )
+    unit = normalised(embeds)
     target = cluster // CLU_OWN
     onehot = (target[:, None] == jnp.arange(owners, dtype=jnp.int32)[None, :]).astype(jnp.int32)
     before = jnp.cumsum(onehot, axis=0) - onehot
@@ -67,9 +246,11 @@
 
 
 def solution(mesh):
+    shape = mesh.shape
+    ring = shape["gx"] * shape["gy"] == 8 and shape["gy"] == 2 and shape["gz"] == 2
     placed = (P(("parts", "gx", "gy", "gz"), None), P(("parts", "gx", "gy", "gz")))
     return jax.shard_map(
-        on_device,
+        on_ring if ring else by_owner,
         mesh=mesh,
         in_specs=placed,
         out_specs=P(("parts", "gx", "gy", "gz")),

time: 73.8 us -> 30.3 us (0.41)
  blocking collectives: 23.5 us -> 0 us
  between operations: 13.5 us -> 0.05 us
  other arithmetic: 7.35 us -> 0.57 us
  local copies, waits for them, and re-layouts: 6.87 us -> 0.95 us
  waiting for transfers between devices: 12.9 us -> 17.4 us
  Pallas kernels: 0 us -> 3.52 us
  matrix products: 2.44 us -> 0 us
    all_to_all x1 -> x0, blocking collectives: 21.7 us -> none  [on_device(): lax.all_to_all(outgoing.reshape(owners, cap, width), ('gx', 'gy'), split_...]
    ppermute x0 -> x9, waiting for transfers between devices: none -> 17.4 us  [send(): return lax.ppermute(value, GROUP, perms[name])]
    all_to_all x2 -> x0, waiting for transfers between devices: 12.8 us -> none  [the longest x1 6.45 us: on_device(): lax.all_to_all(out_labels.reshape(owners, cap), ('gx', 'gy'), split_axis=...]
    ppermute x0 -> x9, starting transfers between devices: none -> 7.64 us  [send(): return lax.ppermute(value, GROUP, perms[name])]
    all_to_all x2 -> x0, starting transfers between devices: 6.92 us -> none  [the longest x1 3.59 us: on_device(): lax.all_to_all(out_labels.reshape(owners, cap), ('gx', 'gy'), split_axis=...]
    pallas_call x0 -> x3, Pallas kernels: none -> 3.52 us  [the longest x1 2.01 us: on_ring(): pl.pallas_call(pack_kernel, out_shape=jax.ShapeDtypeStruct((rows + LABEL_...]
    gather x1 -> x0, local copies, waits for them, and re-layouts: 2.5 us -> none  [on_device(): return back.reshape(total)[place]]
    dot_general x1 -> x0, matrix products: 2.44 us -> none  [masked_sims(): jnp.einsum('qd,kd->qk', queries, keys, preferred_element_type=jnp.float32)]
  transfers between devices with their start and end apart: 3 -> 9, of which waited for: 2 -> 6; matrix products, arithmetic and copies ran while one was open for 4% -> 0% of each run, Pallas kernels for 0% -> 2%
where the time goes in v2:
time: 30.3 us; the launch traced here: 30.1 us
  waiting for transfers between devices  17.4 us (57%)
  starting transfers between devices  7.64 us (25%)
  Pallas kernels  3.52 us (12%)
  local copies, waits for them, and re-layouts  0.95 us (3%)
  other arithmetic  0.57 us (2%)
    ppermute x9, waiting for transfers between devices, send(): return lax.ppermute(value, GROUP, perms[name])  17.4 us
    ppermute x9, starting transfers between devices, send(): return lax.ppermute(value, GROUP, perms[name])  7.64 us
    pallas_call x1, Pallas kernels, on_ring(): pl.pallas_call(pack_kernel, out_shape=jax.ShapeDtypeStruct((rows + LABEL_...  2.01 us
    unnamed x4, local copies, waits for them, and re-layouts  0.95 us
    pallas_call x1, Pallas kernels, on_ring(): pl.pallas_call(far_kernel, out_shape=[line] * 3, in_specs=[vmem] * 8, out...  0.89 us
    pallas_call x1, Pallas kernels, on_ring(): pl.pallas_call(near_kernel, out_shape=line, in_specs=[vmem] * 6, out_spec...  0.62 us
  transfers between devices with their start and end apart: 9, of which 6 were waited for; matrix products, arithmetic and copies ran while one was open for 0% of the time, Pallas kernels for 2%

profile of v2, /device:TPU:0, one launch (start us, length us, event | category | flops | bytes accessed | tf_op | source)
XLA Modules:
  0.0 30.1 jit_solution(898053185193881697)
XLA Ops:
  0.0 2.0 %pack.1.refs_0_.own = bf16[272,512]{1,0:T(8,128)(2,1)} custom-call(bf16[256,512]{1,0:T(8,128)(2,1)} %embeds.1, s32[1,256]{1,0:T(1,128)} %bitcast.2), custom_call_target="tpu_custom_call" | custom-call | tf_op jit(solution)/shard_map/pack/pallas_call | solution.py:145
  2.0 3.1 %collective-permute-start = (bf16[272,512]{1,0:T(8,128)(2,1)}, bf16[272,512]{1,0:T(8,128)(2,1)S(1)}, u32[]{:S(2)}, u32[]{:S(2)}) collective-permute-start(bf16[272,512]{1,0:T(8,128)(2,1)} %pack.1.refs_0_.own), channel_id=1, source_target_pairs={{0,4},{1,5},{4,8},{5,9},{8,12},{9,13},{12,14},{13,15},{14,10},{15,... | collective-permute-start | bytes 835592 | tf_op jit(solution)/shard_map/ppermute | solution.py:141
  5.1 0.0 collective-permute-start.2
  5.1 0.0 collective-permute-start.6
  5.1 6.8 %collective-permute-done.refs_2_.prev = bf16[272,512]{1,0:T(8,128)(2,1)S(1)} collective-permute-done((bf16[272,512]{1,0:T(8,128)(2,1)}, bf16[272,512]{1,0:T(8,128)(2,1)S(1)}, u32[]{:S(2)}, u32[]{:S(2)}) %collective-permute-start) | collective-permute-done | bytes 278560 | tf_op jit(solution)/shard_map/ppermute | solution.py:141
  11.9 0.0 collective-permute-start.1
  11.9 1.5 %collective-permute-done.2.refs_4_.succ = bf16[272,512]{1,0:T(8,128)(2,1)S(1)} collective-permute-done((bf16[272,512]{1,0:T(8,128)(2,1)}, bf16[272,512]{1,0:T(8,128)(2,1)S(1)}, u32[]{:S(2)}, u32[]{:S(2)}) %collective-permute-start.2) | collective-permute-done | bytes 278560 | tf_op jit(solution)/shard_map/ppermute | solution.py:141
  13.4 0.0 collective-permute-start.3
  13.4 1.7 %collective-permute-start.4 = (bf16[272,512]{1,0:T(8,128)(2,1)S(1)}, bf16[272,512]{1,0:T(8,128)(2,1)S(1)}, u32[]{:S(2)}, u32[]{:S(2)}) collective-permute-start(bf16[272,512]{1,0:T(8,128)(2,1)S(1)} %collective-permute-done.refs_2_.prev), channel_id=1, source_target_pairs={{0,5},{1,4},{4,8},{5,9},{8,12},{9,13},{12,14},{13,15},{14,10},{15,... | collective-permute-start | bytes 835592 | tf_op jit(solution)/shard_map/ppermute | solution.py:141
  15.1 0.4 %collective-permute-start.5 = (bf16[272,512]{1,0:T(8,128)(2,1)S(1)}, bf16[272,512]{1,0:T(8,128)(2,1)S(1)}, u32[]{:S(2)}, u32[]{:S(2)}) collective-permute-start(bf16[272,512]{1,0:T(8,128)(2,1)S(1)} %collective-permute-done.2.refs_4_.succ), channel_id=1, source_target_pairs={{0,2},{1,3},{4,1},{5,0},{8,5},{9,4},{12,9},{13,8},{14,13},{15,12},... | collective-permute-start | bytes 835592 | tf_op jit(solution)/shard_map/ppermute | solution.py:141
  15.6 0.0 collective-permute-done.6.refs_1_
  15.6 0.0 collective-permute-done.1.refs_3_.prev_other
  15.6 0.0 collective-permute-done.3.refs_5_.succ_other
  15.6 0.0 copy-start
  15.6 0.9 %copy-done = bf16[272,512]{1,0:T(8,128)(2,1)S(1)} copy-done((bf16[272,512]{1,0:T(8,128)(2,1)S(1)}, bf16[272,512]{1,0:T(8,128)(2,1)}, u32[]{:S(2)}) %copy-start) | copy-done | bytes 278552
  16.5 0.0 copy-start.1
  16.5 0.6 %near.1 = f32[1,256]{1,0:T(1,128)S(1)} custom-call(bf16[272,512]{1,0:T(8,128)(2,1)S(1)} %copy-done, bf16[272,512]{1,0:T(8,128)(2,1)S(1)} %collective-permute-done.6.refs_1_, bf16[272,512]{1,0:T(8,128)(2,1)S(1)} %collective-permute-done.refs_2_.prev, bf16[272,512]{1,0:T(8,128)(2,1)S(1)} %collective-permute-done.1.refs_3_.prev_other, ...), custom_call_target="tpu_custom_call" | custom-call | flops 402653184 | bytes 1572864 | tf_op jit(solution)/shard_map/near/pallas_call | solution.py:166
  17.2 4.6 %collective-permute-done.4.back = bf16[272,512]{1,0:T(8,128)(2,1)S(1)} collective-permute-done((bf16[272,512]{1,0:T(8,128)(2,1)S(1)}, bf16[272,512]{1,0:T(8,128)(2,1)S(1)}, u32[]{:S(2)}, u32[]{:S(2)}) %collective-permute-start.4) | collective-permute-done | bytes 278560 | tf_op jit(solution)/shard_map/ppermute | solution.py:141
  21.7 2.1 %collective-permute-done.5.ahead = bf16[272,512]{1,0:T(8,128)(2,1)S(1)} collective-permute-done((bf16[272,512]{1,0:T(8,128)(2,1)S(1)}, bf16[272,512]{1,0:T(8,128)(2,1)S(1)}, u32[]{:S(2)}, u32[]{:S(2)}) %collective-permute-start.5) | collective-permute-done | bytes 278560 | tf_op jit(solution)/shard_map/ppermute | solution.py:141
  23.9 0.0 copy-done.1
  23.9 0.9 %far.1 = (f32[1,256]{1,0:T(1,128)S(1)}, f32[1,256]{1,0:T(1,128)S(1)}, f32[1,256]{1,0:T(1,128)S(1)}) custom-call(bf16[272,512]{1,0:T(8,128)(2,1)S(1)} %copy-done.1, bf16[272,512]{1,0:T(8,128)(2,1)S(1)} %collective-permute-done.refs_2_.prev, bf16[272,512]{1,0:T(8,128)(2,1)S(1)} %collective-permute-done.1.refs_3_.prev_other, ...), custom_call_target="tpu_custom_call" | custom-call | flops 671088640 | bytes 1835008 | tf_op jit(solution)/shard_map/far/pallas_call | solution.py:177
  24.8 0.1 collective-permute-start.7
  24.9 2.3 %collective-permute-start.8 = (f32[1,256]{1,0:T(1,128)S(1)}, f32[1,256]{1,0:T(1,128)S(1)}, u32[]{:S(2)}, u32[]{:S(2)}) collective-permute-start(f32[1,256]{1,0:T(1,128)S(1)} %get-tuple-element.10), channel_id=1, source_target_pairs={{0,9},{1,8},{4,13},{5,12},{8,15},{9,14},{12,11},{13,10},{14,7},{15... | collective-permute-start | bytes 3080 | tf_op jit(solution)/shard_map/ppermute | solution.py:141
  27.2 2.1 %collective-permute-done.7 = f32[1,256]{1,0:T(1,128)S(1)} collective-permute-done((f32[1,256]{1,0:T(1,128)S(1)}, f32[1,256]{1,0:T(1,128)S(1)}, u32[]{:S(2)}, u32[]{:S(2)}) %collective-permute-start.7) | collective-permute-done | bytes 1056 | tf_op jit(solution)/shard_map/ppermute | solution.py:141
  29.3 0.3 collective-permute-done.8
  29.6 0.6 %maximum_maximum_fusion = f32[1,256]{1,0:T(1,128)} fusion(f32[1,256]{1,0:T(1,128)S(1)} %get-tuple-element.8, f32[1,256]{1,0:T(1,128)S(1)} %collective-permute-done.7, f32[1,256]{1,0:T(1,128)S(1)} %collective-permute-done.8), kind=kLoop, calls=%fused_computation | loop fusion | flops 512 | bytes 4096 | tf_op jit(solution)/shard_map/max | solution.py:188
Async XLA Ops:
  2.0 9.9 %collective-permute-start = (bf16[272,512]{1,0:T(8,128)(2,1)}, bf16[272,512]{1,0:T(8,128)(2,1)S(1)}, u32[]{:S(2)}, u32[]{:S(2)}) collective-permute-start(bf16[272,512]{1,0:T(8,128)(2,1)} %pack.1.refs_0_.own), channel_id=1, source_target_pairs={{0,4},{1,5},{4,8},{5,9},{8,12},{9,13},{12,14},{13,15},{14,10},{15,... | collective-permute-start | bytes 835592 | tf_op jit(solution)/shard_map/ppermute | solution.py:141
  5.1 8.3 %collective-permute-start.2 = (bf16[272,512]{1,0:T(8,128)(2,1)}, bf16[272,512]{1,0:T(8,128)(2,1)S(1)}, u32[]{:S(2)}, u32[]{:S(2)}) collective-permute-start(bf16[272,512]{1,0:T(8,128)(2,1)} %pack.1.refs_0_.own), channel_id=1, source_target_pairs={{0,2},{1,3},{4,0},{5,1},{8,4},{9,5},{12,8},{13,9},{14,12},{15,13},... | collective-permute-start | bytes 835592 | tf_op jit(solution)/shard_map/ppermute | solution.py:141
  5.1 10.5 %collective-permute-start.6 = (bf16[272,512]{1,0:T(8,128)(2,1)}, bf16[272,512]{1,0:T(8,128)(2,1)S(1)}, u32[]{:S(2)}, u32[]{:S(2)}) collective-permute-start(bf16[272,512]{1,0:T(8,128)(2,1)} %pack.1.refs_0_.own), channel_id=1, source_target_pairs={{0,1},{1,0},{4,5},{5,4},{8,9},{9,8},{12,13},{13,12},{14,15},{15,14... | collective-permute-start | bytes 835592 | tf_op jit(solution)/shard_map/ppermute | solution.py:141
  11.9 3.7 %collective-permute-start.1 = (bf16[272,512]{1,0:T(8,128)(2,1)S(1)}, bf16[272,512]{1,0:T(8,128)(2,1)S(1)}, u32[]{:S(2)}, u32[]{:S(2)}) collective-permute-start(bf16[272,512]{1,0:T(8,128)(2,1)S(1)} %collective-permute-done.refs_2_.prev), channel_id=1, source_target_pairs={{0,1},{1,0},{4,5},{5,4},{8,9},{9,8},{12,13},{13,12},{14,15},{15,14... | collective-permute-start | bytes 835592 | tf_op jit(solution)/shard_map/ppermute | solution.py:141
  13.4 2.2 %collective-permute-start.3 = (bf16[272,512]{1,0:T(8,128)(2,1)S(1)}, bf16[272,512]{1,0:T(8,128)(2,1)S(1)}, u32[]{:S(2)}, u32[]{:S(2)}) collective-permute-start(bf16[272,512]{1,0:T(8,128)(2,1)S(1)} %collective-permute-done.2.refs_4_.succ), channel_id=1, source_target_pairs={{0,1},{1,0},{4,5},{5,4},{8,9},{9,8},{12,13},{13,12},{14,15},{15,14... | collective-permute-start | bytes 835592 | tf_op jit(solution)/shard_map/ppermute | solution.py:141
  13.4 8.3 %collective-permute-start.4 = (bf16[272,512]{1,0:T(8,128)(2,1)S(1)}, bf16[272,512]{1,0:T(8,128)(2,1)S(1)}, u32[]{:S(2)}, u32[]{:S(2)}) collective-permute-start(bf16[272,512]{1,0:T(8,128)(2,1)S(1)} %collective-permute-done.refs_2_.prev), channel_id=1, source_target_pairs={{0,5},{1,4},{4,8},{5,9},{8,12},{9,13},{12,14},{13,15},{14,10},{15,... | collective-permute-start | bytes 835592 | tf_op jit(solution)/shard_map/ppermute | solution.py:141
  15.1 8.8 %collective-permute-start.5 = (bf16[272,512]{1,0:T(8,128)(2,1)S(1)}, bf16[272,512]{1,0:T(8,128)(2,1)S(1)}, u32[]{:S(2)}, u32[]{:S(2)}) collective-permute-start(bf16[272,512]{1,0:T(8,128)(2,1)S(1)} %collective-permute-done.2.refs_4_.succ), channel_id=1, source_target_pairs={{0,2},{1,3},{4,1},{5,0},{8,5},{9,4},{12,9},{13,8},{14,13},{15,12},... | collective-permute-start | bytes 835592 | tf_op jit(solution)/shard_map/ppermute | solution.py:141
  15.6 1.0 %copy-start = (bf16[272,512]{1,0:T(8,128)(2,1)S(1)}, bf16[272,512]{1,0:T(8,128)(2,1)}, u32[]{:S(2)}) copy-start(bf16[272,512]{1,0:T(8,128)(2,1)} %pack.1.refs_0_.own) | copy-start | bytes 835588
  16.5 7.4 %copy-start.1 = (bf16[272,512]{1,0:T(8,128)(2,1)S(1)}, bf16[272,512]{1,0:T(8,128)(2,1)}, u32[]{:S(2)}) copy-start(bf16[272,512]{1,0:T(8,128)(2,1)} %pack.1.refs_0_.own) | copy-start | bytes 835588
  24.8 4.5 %collective-permute-start.7 = (f32[1,256]{1,0:T(1,128)S(1)}, f32[1,256]{1,0:T(1,128)S(1)}, u32[]{:S(2)}, u32[]{:S(2)}) collective-permute-start(f32[1,256]{1,0:T(1,128)S(1)} %get-tuple-element.9), channel_id=1, source_target_pairs={{0,7},{1,6},{4,3},{5,2},{8,0},{9,1},{12,4},{13,5},{14,8},{15,9},{1... | collective-permute-start | bytes 3080 | tf_op jit(solution)/shard_map/ppermute | solution.py:141
  24.9 4.7 %collective-permute-start.8 = (f32[1,256]{1,0:T(1,128)S(1)}, f32[1,256]{1,0:T(1,128)S(1)}, u32[]{:S(2)}, u32[]{:S(2)}) collective-permute-start(f32[1,256]{1,0:T(1,128)S(1)} %get-tuple-element.10), channel_id=1, source_target_pairs={{0,9},{1,8},{4,13},{5,12},{8,15},{9,14},{12,11},{13,10},{14,7},{15... | collective-permute-start | bytes 3080 | tf_op jit(solution)/shard_map/ppermute | solution.py:141

commit v3 on v0

--- a/solution.py
+++ b/solution.py
@@ -1,12 +1,285 @@
 import jax
 import jax.numpy as jnp
 from jax import lax
+from jax.experimental import pallas as pl
+from jax.experimental.pallas import tpu as pltpu
 from jax.sharding import PartitionSpec as P
 
 CLU_OWN = 16
 
 
 EPS = 1e-06
+
+GROUP = ("gx", "gy", "gz")
+
+
+def normalised(block):
+    vecs = block.astype(jnp.float32)
+    return (vecs * lax.rsqrt(jnp.sum(vecs * vecs, axis=1, keepdims=True) + EPS)).astype(
+        jnp.bfloat16
+    )
+
+
+LABEL_ROWS = 16
+VMEM_BYTES = 32 * 2**20
+NEAR_COST = 6
+FIRST_COST = 5
+SECOND_COST = 6
+
+
+def pack_first_kernel(embeds, label, first, raw, line, sems):
+    rows, width = embeds.shape
+    half = rows // 2
+    copies = [
+        pltpu.make_async_copy(label, line, sems.at[0]),
+        pltpu.make_async_copy(embeds.at[pl.ds(0, half)], raw, sems.at[1]),
+    ]
+    for copy in copies:
+        copy.start()
+    copies[0].wait()
+    lines = jnp.broadcast_to(line[...].astype(jnp.float32), (LABEL_ROWS, rows))
+    first[half:, :rows] = lines.astype(jnp.bfloat16)
+    first[half:, rows:] = jnp.zeros((LABEL_ROWS, width - rows), jnp.bfloat16)
+    copies[1].wait()
+    first[:half, :] = normalised(raw[...])
+
+
+def pack_second_kernel(embeds, first, second, both, raw, sem):
+    half = second.shape[0]
+    copy = pltpu.make_async_copy(embeds.at[pl.ds(half, half)], raw, sem)
+    copy.start()
+    both[:half, :] = first[:half, :]
+    both[2 * half :, :] = first[half:, :]
+    copy.wait()
+    unit = normalised(raw[...])
+    second[...] = unit
+    both[half : 2 * half, :] = unit
+
+
+class Block:
+    def __init__(self, unit, label):
+        self.unit = unit
+        self.label = label
+        self.rows = unit.shape[0]
+        self.along_rows = None
+
+    def column(self):
+        if self.along_rows is None:
+            self.along_rows = jnp.transpose(jnp.broadcast_to(self.label, (128, self.rows)))
+        return self.along_rows
+
+
+def labels_in(first):
+    half = first.shape[0] - LABEL_ROWS
+    return first[half:, : 2 * half].astype(jnp.float32)[:1]
+
+
+def packed(ref):
+    rows = ref.shape[0] - LABEL_ROWS
+    return Block(ref[:rows, :], ref[rows:, :rows].astype(jnp.float32)[:1])
+
+
+def whole(first, second):
+    half = second.shape[0]
+    return Block(jnp.concatenate([first[:half, :], second[...]], axis=0), labels_in(first))
+
+
+def first_half(first):
+    half = first.shape[0] - LABEL_ROWS
+    return Block(first[:half, :], labels_in(first)[:, :half])
+
+
+def second_half(first, second):
+    half = second.shape[0]
+    return Block(second[...], labels_in(first)[:, half:])
+
+
+def best_of(queries, *all_keys):
+    best = None
+    for keys in all_keys:
+        sims = lax.dot_general(
+            keys.unit, queries.unit, (((1,), (1,)), ((), ())), preferred_element_type=jnp.float32
+        )
+        pieces = []
+        for start in range(0, queries.rows, 128):
+            keep = keys.column() == queries.label[:, start : start + 128]
+            if keys is queries:
+                row = lax.broadcasted_iota(jnp.int32, keep.shape, 0)
+                column = lax.broadcasted_iota(jnp.int32, keep.shape, 1) + start
+                keep = keep & (row != column)
+            found = jnp.where(keep, sims[:, start : start + 128], -1.0)
+            pieces.append(jnp.max(found, axis=0, keepdims=True))
+        found = jnp.concatenate(pieces, axis=1)
+        best = found if best is None else jnp.maximum(best, found)
+    return best
+
+
+def near_kernel(
+    own, prev_a, prev_b, succ_a, succ_b, mine, to_prev, to_succ
+):
+    own = packed(own)
+    prev, succ = whole(prev_a, prev_b), whole(succ_a, succ_b)
+    mine[...] = best_of(own, own, prev, succ)
+    to_prev[...] = best_of(prev, own)
+    to_succ[...] = best_of(succ, own)
+
+
+def other_kernel(own, other, mine, mine_out):
+    mine_out[...] = jnp.maximum(mine[...], best_of(packed(own), packed(other)))
+
+
+def far_first_kernel(
+    own, prev_a, prev_b, succ_a, succ_b, back_a, ahead_a, *refs
+):
+    mine, to_prev, to_succ, mine_out, to_prev_out, to_succ_out, to_back, to_ahead = refs
+    own = packed(own)
+    prev, succ = whole(prev_a, prev_b), whole(succ_a, succ_b)
+    back, ahead = first_half(back_a), first_half(ahead_a)
+    mine_out[...] = jnp.maximum(mine[...], best_of(own, back, ahead))
+    to_prev_out[...] = jnp.maximum(to_prev[...], best_of(prev, ahead))
+    to_succ_out[...] = jnp.maximum(to_succ[...], best_of(succ, back))
+    to_back[...] = best_of(back, own, succ, ahead)
+    to_ahead[...] = best_of(ahead, own, prev, back)
+
+
+def far_second_kernel(
+    own, prev_a, prev_b, succ_a, succ_b, back_a, ahead_a, back_b, ahead_b, *refs
+):
+    mine, to_prev, to_succ, back_first, ahead_first, *out = refs
+    mine_out, to_prev_out, to_succ_out, to_back, to_ahead = out
+    own = packed(own)
+    prev, succ = whole(prev_a, prev_b), whole(succ_a, succ_b)
+    half = back_b.shape[0]
+    back, ahead = first_half(back_a), first_half(ahead_a)
+    back_rest, ahead_rest = second_half(back_a, back_b), second_half(ahead_a, ahead_b)
+    mine_out[...] = jnp.maximum(mine[...], best_of(own, back_rest, ahead_rest))
+    to_prev_out[...] = jnp.maximum(to_prev[...], best_of(prev, ahead_rest))
+    to_succ_out[...] = jnp.maximum(to_succ[...], best_of(succ, back_rest))
+    to_back[:, :half] = jnp.maximum(back_first[...], best_of(back, ahead_rest))
+    to_back[:, half:] = best_of(back_rest, own, succ, ahead, ahead_rest)
+    to_ahead[:, :half] = jnp.maximum(ahead_first[...], best_of(ahead, back_rest))
+    to_ahead[:, half:] = best_of(ahead_rest, own, prev, back, back_rest)
+
+
+ONE_BACK = (0, 0, 0, 1, 1, 0, 0, 1)
+TWO_BACK = (1, 1, 0, 0, 0, 0, 0, 0)
+
+
+def ring_perms(size_x, size_y, size_z):
+    chips = size_x * size_y
+
+    def device(place, core):
+        place = place % chips
+        x, y = (place, 0) if place < size_x else (chips - 1 - place, 1)
+        return (x * size_y + y) * size_z + core
+
+    def changed(place, step):
+        place = place % chips
+        if step == 0:
+            return 0
+        if step < 0:
+            return 1 - changed(place - step, -step)
+        return (ONE_BACK if step == 1 else TWO_BACK)[place]
+
+    def perm(held, step):
+        pairs = []
+        for place in range(chips):
+            for core in range(size_z):
+                source = core ^ changed(place, held)
+                target = source ^ changed(place + step, held + step)
+                pairs.append((device(place, core), device(place + step, target)))
+        return pairs
+
+    return {
+        "sibling": [(d, d ^ 1) for d in range(chips * size_z)],
+        "next": perm(0, 1),
+        "prev": perm(0, -1),
+        "on_next": perm(1, 1),
+        "on_prev": perm(-1, -1),
+        "home_prev": perm(1, -1),
+        "home_succ": perm(-1, 1),
+        "home_back": perm(2, -2),
+        "home_ahead": perm(-2, 2),
+    }
+
+
+def kernel_call(kernel, inputs, outputs, matmuls):
+    vmem = pl.BlockSpec(memory_space=pltpu.VMEM)
+    return pl.pallas_call(
+        kernel,
+        out_shape=outputs,
+        in_specs=[vmem] * len(inputs),
+        out_specs=[vmem] * len(outputs),
+        compiler_params=pltpu.CompilerParams(vmem_limit_bytes=VMEM_BYTES),
+        cost_estimate=pl.CostEstimate(
+            flops=matmuls * 2**26, bytes_accessed=2**20, transcendentals=0
+        ),
+        name=kernel.__name__,
+    )(*inputs)
+
+
+def on_ring(embeds, cluster):
+    rows, width = embeds.shape
+    half = rows // 2
+    perms = ring_perms(*(lax.axis_size(a) for a in GROUP))
+
+    def send(value, name):
+        return lax.ppermute(value, GROUP, perms[name])
+
+    line = jax.ShapeDtypeStruct((1, rows), jnp.float32)
+    half_line = jax.ShapeDtypeStruct((1, half), jnp.float32)
+    anywhere = pl.BlockSpec(memory_space=pl.ANY)
+    vmem = pl.BlockSpec(memory_space=pltpu.VMEM)
+    params = pltpu.CompilerParams(vmem_limit_bytes=VMEM_BYTES)
+    own_a = pl.pallas_call(
+        pack_first_kernel,
+        out_shape=jax.ShapeDtypeStruct((half + LABEL_ROWS, width), jnp.bfloat16),
+        in_specs=[anywhere] * 2,
+        out_specs=vmem,
+        scratch_shapes=[
+            pltpu.VMEM((half, width), jnp.bfloat16),
+            pltpu.VMEM((1, rows), jnp.int32),
+            pltpu.SemaphoreType.DMA((2,)),
+        ],
+        compiler_params=params,
+        name="pack_first",
+    )(embeds, cluster.reshape(1, rows))
+    own_b, own = pl.pallas_call(
+        pack_second_kernel,
+        out_shape=[
+            jax.ShapeDtypeStruct((half, width), jnp.bfloat16),
+            jax.ShapeDtypeStruct((rows + LABEL_ROWS, width), jnp.bfloat16),
+        ],
+        in_specs=[anywhere, vmem],
+        out_specs=[vmem] * 2,
+        scratch_shapes=[pltpu.VMEM((half, width), jnp.bfloat16), pltpu.SemaphoreType.DMA],
+        compiler_params=params,
+        name="pack_second",
+    )(embeds, own_a)
+    prev_a, succ_a = send(own_a, "next"), send(own_a, "prev")
+    prev_b, succ_b = send(own_b, "next"), send(own_b, "prev")
+    other = send(own, "sibling")
+    back_a, ahead_a = send(prev_a, "on_next"), send(succ_a, "on_prev")
+    back_b, ahead_b = send(prev_b, "on_next"), send(succ_b, "on_prev")
+    blocks = [own, prev_a, prev_b, succ_a, succ_b]
+    near = kernel_call(near_kernel, blocks, [line] * 3, NEAR_COST)
+    parts = kernel_call(
+        far_first_kernel,
+        [*blocks, back_a, ahead_a, *near],
+        [line] * 3 + [half_line] * 2,
+        FIRST_COST,
+    )
+    mine, *found = kernel_call(
+        far_second_kernel,
+        [*blocks, back_a, ahead_a, back_b, ahead_b, *parts],
+        [line] * 5,
+        SECOND_COST,
+    )
+    (mine,) = kernel_call(other_kernel, [own, other, mine], [line], 1)
+    homes = ("home_prev", "home_succ", "home_back", "home_ahead")
+    for value, home in zip(found[::-1], homes[::-1]):
+        mine = jnp.maximum(mine, send(value, home))
+    return mine.reshape(rows)
 
 
 def masked_sims(queries, query_labels, query_ids, keys, key_labels, key_ids):
@@ -19,17 +292,14 @@
     return jnp.where(keep, sims, -1.0)
 
 
-def on_device(embeds, cluster):
+def by_owner(embeds, cluster):
     rows, width = embeds.shape
     size_x = lax.axis_size("gx")
     size_y = lax.axis_size("gy")
     owners = size_x * size_y
     cap = 2 * rows // owners
     total = owners * cap
-    vecs = embeds.astype(jnp.float32)
-    unit = (vecs * lax.rsqrt(jnp.sum(vecs * vecs, axis=1, keepdims=True) + EPS)).astype(
-        jnp.bfloat16
-    )
+    unit = normalised(embeds)
     target = cluster // CLU_OWN
     onehot = (target[:, None] == jnp.arange(owners, dtype=jnp.int32)[None, :]).astype(jnp.int32)
     before = jnp.cumsum(onehot, axis=0) - onehot
@@ -67,9 +337,11 @@
 
 
 def solution(mesh):
+    shape = mesh.shape
+    ring = shape["gx"] * shape["gy"] == 8 and shape["gy"] == 2 and shape["gz"] == 2
     placed = (P(("parts", "gx", "gy", "gz"), None), P(("parts", "gx", "gy", "gz")))
     return jax.shard_map(
-        on_device,
+        on_ring if ring else by_owner,
         mesh=mesh,
         in_specs=placed,
         out_specs=P(("parts", "gx", "gy", "gz")),

time: 73.8 us -> 29.3 us (0.40)
  blocking collectives: 23.5 us -> 0 us
  between operations: 13.5 us -> 0.07 us
  other arithmetic: 7.35 us -> 0.57 us
  local copies, waits for them, and re-layouts: 6.87 us -> 1.63 us
  starting transfers between devices: 6.92 us -> 11.3 us
  Pallas kernels: 0 us -> 3.18 us
  matrix products: 2.44 us -> 0 us
    all_to_all x1 -> x0, blocking collectives: 21.7 us -> none  [on_device(): lax.all_to_all(outgoing.reshape(owners, cap, width), ('gx', 'gy'), split_...]
    all_to_all x2 -> x0, waiting for transfers between devices: 12.8 us -> none  [the longest x1 6.45 us: on_device(): lax.all_to_all(out_labels.reshape(owners, cap), ('gx', 'gy'), split_axis=...]
    ppermute x0 -> x13, waiting for transfers between devices: none -> 12.4 us  [send(): return lax.ppermute(value, GROUP, perms[name])]
    ppermute x0 -> x13, starting transfers between devices: none -> 11.3 us  [send(): return lax.ppermute(value, GROUP, perms[name])]
    all_to_all x2 -> x0, starting transfers between devices: 6.92 us -> none  [the longest x1 3.59 us: on_device(): lax.all_to_all(out_labels.reshape(owners, cap), ('gx', 'gy'), split_axis=...]
    pallas_call x0 -> x6, Pallas kernels: none -> 3.18 us  [the longest x4 2.62 us: kernel_call(): pl.pallas_call(kernel, out_shape=outputs, in_specs=[vmem] * len(inputs),...]
    gather x1 -> x0, local copies, waits for them, and re-layouts: 2.5 us -> none  [on_device(): return back.reshape(total)[place]]
    dot_general x1 -> x0, matrix products: 2.44 us -> none  [masked_sims(): jnp.einsum('qd,kd->qk', queries, keys, preferred_element_type=jnp.float32)]
  transfers between devices with their start and end apart: 3 -> 13, of which waited for: 2 -> 9; matrix products, arithmetic and copies ran while one was open for 4% -> 0% of each run, Pallas kernels for 0% -> 10%
where the time goes in v3:
time: 29.3 us; the launch traced here: 29.1 us
  waiting for transfers between devices  12.4 us (42%)
  starting transfers between devices  11.3 us (39%)
  Pallas kernels  3.18 us (11%)
  local copies, waits for them, and re-layouts  1.63 us (6%)
  other arithmetic  0.57 us (2%)
    ppermute x13, waiting for transfers between devices, send(): return lax.ppermute(value, GROUP, perms[name])  12.4 us
    ppermute x13, starting transfers between devices, send(): return lax.ppermute(value, GROUP, perms[name])  11.3 us
    pallas_call x4, Pallas kernels, kernel_call(): pl.pallas_call(kernel, out_shape=outputs, in_specs=[vmem] * len(inputs),...  2.62 us
    unnamed x4, local copies, waits for them, and re-layouts  1.63 us
  transfers between devices with their start and end apart: 13, of which 9 were waited for; matrix products, arithmetic and copies ran while one was open for 0% of the time, Pallas kernels for 10%

profile of v3, /device:TPU:0, one launch (start us, length us, event | category | flops | bytes accessed | tf_op | source)
XLA Modules:
  0.0 29.1 jit_solution(8305948654530014893)
XLA Ops:
  0.0 0.7 %copy-done.1 = s32[256]{0:T(256)S(1)} copy-done((s32[256]{0:T(256)S(1)}, s32[256]{0:T(256)}, u32[]{:S(2)}) %copy-start.1) | copy-done | bytes 1048
  0.7 0.9 %copy-done = bf16[256,512]{1,0:T(8,128)(2,1)S(1)} copy-done((bf16[256,512]{1,0:T(8,128)(2,1)S(1)}, bf16[256,512]{1,0:T(8,128)(2,1)}, u32[]{:S(2)}) %copy-start) | copy-done | bytes 262168
  1.6 0.3 pack_first.1.first
  1.9 3.1 %collective-permute-start.1 = (bf16[144,512]{1,0:T(8,128)(2,1)S(1)}, bf16[144,512]{1,0:T(8,128)(2,1)S(1)}, u32[]{:S(2)}, u32[]{:S(2)}) collective-permute-start(bf16[144,512]{1,0:T(8,128)(2,1)S(1)} %pack_first.1.first), channel_id=1, source_target_pairs={{0,4},{1,5},{4,8},{5,9},{8,13},{9,12},{12,15},{13,14},{14,10},{15,... | collective-permute-start | bytes 442376 | tf_op jit(solution)/shard_map/ppermute | solution.py:227
  5.0 0.0 collective-permute-start.3
  5.0 0.3 pack_second.1
  5.3 1.6 %collective-permute-start.2 = (bf16[128,512]{1,0:T(8,128)(2,1)S(1)}, bf16[128,512]{1,0:T(8,128)(2,1)S(1)}, u32[]{:S(2)}, u32[]{:S(2)}) collective-permute-start(bf16[128,512]{1,0:T(8,128)(2,1)S(1)} %get-tuple-element.21), channel_id=1, source_target_pairs={{0,4},{1,5},{4,8},{5,9},{8,13},{9,12},{12,15},{13,14},{14,10},{15,... | collective-permute-start | bytes 393224 | tf_op jit(solution)/shard_map/ppermute | solution.py:227
  6.9 0.0 collective-permute-start.4
  6.9 0.6 %collective-permute-start = (bf16[272,512]{1,0:T(8,128)(2,1)S(1)}, bf16[272,512]{1,0:T(8,128)(2,1)S(1)}, u32[]{:S(2)}, u32[]{:S(2)}) collective-permute-start(bf16[272,512]{1,0:T(8,128)(2,1)S(1)} %get-tuple-element.20.own), channel_id=1, source_target_pairs={{0,1},{1,0},{2,3},{3,2},{4,5},{5,4},{6,7},{7,6},{8,9},{9,8},{10,11... | collective-permute-start | bytes 835592 | tf_op jit(solution)/shard_map/ppermute | solution.py:227
  7.5 1.9 %collective-permute-done.1.prev_a = bf16[144,512]{1,0:T(8,128)(2,1)S(1)} collective-permute-done((bf16[144,512]{1,0:T(8,128)(2,1)S(1)}, bf16[144,512]{1,0:T(8,128)(2,1)S(1)}, u32[]{:S(2)}, u32[]{:S(2)}) %collective-permute-start.1) | collective-permute-done | bytes 147488 | tf_op jit(solution)/shard_map/ppermute | solution.py:227
  9.4 0.0 collective-permute-start.5
  9.4 1.6 %collective-permute-done.3.succ_a = bf16[144,512]{1,0:T(8,128)(2,1)S(1)} collective-permute-done((bf16[144,512]{1,0:T(8,128)(2,1)S(1)}, bf16[144,512]{1,0:T(8,128)(2,1)S(1)}, u32[]{:S(2)}, u32[]{:S(2)}) %collective-permute-start.3) | collective-permute-done | bytes 147488 | tf_op jit(solution)/shard_map/ppermute | solution.py:227
  11.0 0.4 %collective-permute-start.6 = (bf16[144,512]{1,0:T(8,128)(2,1)S(1)}, bf16[144,512]{1,0:T(8,128)(2,1)S(1)}, u32[]{:S(2)}, u32[]{:S(2)}) collective-permute-start(bf16[144,512]{1,0:T(8,128)(2,1)S(1)} %collective-permute-done.3.succ_a), channel_id=1, source_target_pairs={{0,3},{1,2},{4,0},{5,1},{8,5},{9,4},{12,9},{13,8},{14,12},{15,13},... | collective-permute-start | bytes 442376 | tf_op jit(solution)/shard_map/ppermute | solution.py:227
  11.4 0.2 collective-permute-done.2.prev_b
  11.6 1.2 %collective-permute-start.7 = (bf16[128,512]{1,0:T(8,128)(2,1)S(1)}, bf16[128,512]{1,0:T(8,128)(2,1)S(1)}, u32[]{:S(2)}, u32[]{:S(2)}) collective-permute-start(bf16[128,512]{1,0:T(8,128)(2,1)S(1)} %collective-permute-done.2.prev_b), channel_id=1, source_target_pairs={{0,5},{1,4},{4,8},{5,9},{8,12},{9,13},{12,15},{13,14},{14,11},{15,... | collective-permute-start | bytes 393224 | tf_op jit(solution)/shard_map/ppermute | solution.py:227
  12.7 1.1 %collective-permute-done.4.succ_b = bf16[128,512]{1,0:T(8,128)(2,1)S(1)} collective-permute-done((bf16[128,512]{1,0:T(8,128)(2,1)S(1)}, bf16[128,512]{1,0:T(8,128)(2,1)S(1)}, u32[]{:S(2)}, u32[]{:S(2)}) %collective-permute-start.4) | collective-permute-done | bytes 131104 | tf_op jit(solution)/shard_map/ppermute | solution.py:227
  13.8 0.0 collective-permute-start.8
  13.8 0.6 %near_kernel.1 = (f32[1,256]{1,0:T(1,128)S(1)}, f32[1,256]{1,0:T(1,128)S(1)}, f32[1,256]{1,0:T(1,128)S(1)}) custom-call(bf16[272,512]{1,0:T(8,128)(2,1)S(1)} %get-tuple-element.20.own, bf16[144,512]{1,0:T(8,128)(2,1)S(1)} %collective-permute-done.1.prev_a, bf16[128,512]{1,0:T(8,128)(2,1)S(1)} %collective-permute-done.2.prev_b, ...), custom_call_target="tpu_custom_call" | custom-call | flops 402653184 | bytes 1048576 | tf_op jit(solution)/shard_map/near_kernel/pallas_call | solution.py:208
  14.4 1.5 %collective-permute-done.5.back_a = bf16[144,512]{1,0:T(8,128)(2,1)S(1)} collective-permute-done((bf16[144,512]{1,0:T(8,128)(2,1)S(1)}, bf16[144,512]{1,0:T(8,128)(2,1)S(1)}, u32[]{:S(2)}, u32[]{:S(2)}) %collective-permute-start.5) | collective-permute-done | bytes 147488 | tf_op jit(solution)/shard_map/ppermute | solution.py:227
  15.9 1.7 %collective-permute-done.6.ahead_a = bf16[144,512]{1,0:T(8,128)(2,1)S(1)} collective-permute-done((bf16[144,512]{1,0:T(8,128)(2,1)S(1)}, bf16[144,512]{1,0:T(8,128)(2,1)S(1)}, u32[]{:S(2)}, u32[]{:S(2)}) %collective-permute-start.6) | collective-permute-done | bytes 147488 | tf_op jit(solution)/shard_map/ppermute | solution.py:227
  17.6 0.8 %far_first_kernel.1 = (f32[1,256]{1,0:T(1,128)S(1)}, f32[1,256]{1,0:T(1,128)S(1)}, f32[1,256]{1,0:T(1,128)S(1)}, f32[1,128]{1,0:T(1,128)S(1)}, f32[1,128]{1,0:T(1,128)S(1)}) custom-call(bf16[272,512]{1,0:T(8,128)(2,1)S(1)} %get-tuple-element.20.own, bf16[144,512]{1,0:T(8,128)(2,1)S(1)} %collective-permute-done.1.prev_a, ...), custom_call_target="tpu_custom_call" | custom-call | flops 335544320 | bytes 1048576 | tf_op jit(solution)/shard_map/far_first_kernel/pallas_call | solution.py:208
  18.4 0.0 collective-permute-done.7.back_b
  18.4 1.6 %collective-permute-done.8.ahead_b = bf16[128,512]{1,0:T(8,128)(2,1)S(1)} collective-permute-done((bf16[128,512]{1,0:T(8,128)(2,1)S(1)}, bf16[128,512]{1,0:T(8,128)(2,1)S(1)}, u32[]{:S(2)}, u32[]{:S(2)}) %collective-permute-start.8) | collective-permute-done | bytes 131104 | tf_op jit(solution)/shard_map/ppermute | solution.py:227
  20.0 1.0 %far_second_kernel.1 = (f32[1,256]{1,0:T(1,128)S(1)}, f32[1,256]{1,0:T(1,128)S(1)}, f32[1,256]{1,0:T(1,128)S(1)}, f32[1,256]{1,0:T(1,128)S(1)}, f32[1,256]{1,0:T(1,128)S(1)}) custom-call(bf16[272,512]{1,0:T(8,128)(2,1)S(1)} %get-tuple-element.20.own, bf16[144,512]{1,0:T(8,128)(2,1)S(1)} %collective-permute-done.1.prev_a, ...), custom_call_target="tpu_custom_call" | custom-call | flops 402653184 | bytes 1048576 | tf_op jit(solution)/shard_map/far_second_kernel/pallas_call | solution.py:208
  20.9 0.1 collective-permute-start.12
  21.0 1.3 %collective-permute-start.11 = (f32[1,256]{1,0:T(1,128)S(1)}, f32[1,256]{1,0:T(1,128)S(1)}, u32[]{:S(2)}, u32[]{:S(2)}) collective-permute-start(f32[1,256]{1,0:T(1,128)S(1)} %get-tuple-element.33), channel_id=1, source_target_pairs={{0,5},{1,4},{4,9},{5,8},{8,12},{9,13},{12,14},{13,15},{14,11},{15,... | collective-permute-start | bytes 3080 | tf_op jit(solution)/shard_map/ppermute | solution.py:227
  22.4 1.7 %collective-permute-start.10 = (f32[1,256]{1,0:T(1,128)S(1)}, f32[1,256]{1,0:T(1,128)S(1)}, u32[]{:S(2)}, u32[]{:S(2)}) collective-permute-start(f32[1,256]{1,0:T(1,128)S(1)} %get-tuple-element.32), channel_id=1, source_target_pairs={{0,7},{1,6},{4,3},{5,2},{8,0},{9,1},{12,4},{13,5},{14,8},{15,9},{1... | collective-permute-start | bytes 3080 | tf_op jit(solution)/shard_map/ppermute | solution.py:227
  24.1 1.3 %collective-permute-start.9 = (f32[1,256]{1,0:T(1,128)S(1)}, f32[1,256]{1,0:T(1,128)S(1)}, u32[]{:S(2)}, u32[]{:S(2)}) collective-permute-start(f32[1,256]{1,0:T(1,128)S(1)} %get-tuple-element.31), channel_id=1, source_target_pairs={{0,9},{1,8},{4,13},{5,12},{8,15},{9,14},{12,11},{13,10},{14,7},{15... | collective-permute-start | bytes 3080 | tf_op jit(solution)/shard_map/ppermute | solution.py:227
  25.4 0.3 other_kernel.1
  25.7 1.3 %collective-permute-done.10 = f32[1,256]{1,0:T(1,128)S(1)} collective-permute-done((f32[1,256]{1,0:T(1,128)S(1)}, f32[1,256]{1,0:T(1,128)S(1)}, u32[]{:S(2)}, u32[]{:S(2)}) %collective-permute-start.10) | collective-permute-done | bytes 1056 | tf_op jit(solution)/shard_map/ppermute | solution.py:227
  27.0 1.6 %collective-permute-done.9 = f32[1,256]{1,0:T(1,128)S(1)} collective-permute-done((f32[1,256]{1,0:T(1,128)S(1)}, f32[1,256]{1,0:T(1,128)S(1)}, u32[]{:S(2)}, u32[]{:S(2)}) %collective-permute-start.9) | collective-permute-done | bytes 1056 | tf_op jit(solution)/shard_map/ppermute | solution.py:227
  28.6 0.6 %maximum_maximum_fusion = f32[1,256]{1,0:T(1,128)} fusion(f32[1,256]{1,0:T(1,128)S(1)} %collective-permute-done.12, f32[1,256]{1,0:T(1,128)S(1)} %collective-permute-done.11, f32[1,256]{1,0:T(1,128)S(1)} %collective-permute-done.10, f32[1,256]{1,0:T(1,128)S(1)} %other_kernel.1, f32[1,256]{1,0:T(1,128)S(1)} %collective-permute-done.9), kind=kLoop, calls=%fused_computation | loop fusion | flops 1024 | bytes 6144 | tf_op jit(solution)/shard_map/max | solution.py:281
  (5 shorter events, 0.0 us)
Async XLA Ops:
  0.0 0.7 %copy-start.1 = (s32[256]{0:T(256)S(1)}, s32[256]{0:T(256)}, u32[]{:S(2)}) copy-start(s32[256]{0:T(256)} %param.3) | copy-start | bytes 3076
  0.7 0.9 %copy-start = (bf16[256,512]{1,0:T(8,128)(2,1)S(1)}, bf16[256,512]{1,0:T(8,128)(2,1)}, u32[]{:S(2)}) copy-start(bf16[256,512]{1,0:T(8,128)(2,1)} %embeds.3) | copy-start | bytes 786436
  1.9 7.5 %collective-permute-start.1 = (bf16[144,512]{1,0:T(8,128)(2,1)S(1)}, bf16[144,512]{1,0:T(8,128)(2,1)S(1)}, u32[]{:S(2)}, u32[]{:S(2)}) collective-permute-start(bf16[144,512]{1,0:T(8,128)(2,1)S(1)} %pack_first.1.first), channel_id=1, source_target_pairs={{0,4},{1,5},{4,8},{5,9},{8,13},{9,12},{12,15},{13,14},{14,10},{15,... | collective-permute-start | bytes 442376 | tf_op jit(solution)/shard_map/ppermute | solution.py:227
  5.0 6.0 %collective-permute-start.3 = (bf16[144,512]{1,0:T(8,128)(2,1)S(1)}, bf16[144,512]{1,0:T(8,128)(2,1)S(1)}, u32[]{:S(2)}, u32[]{:S(2)}) collective-permute-start(bf16[144,512]{1,0:T(8,128)(2,1)S(1)} %pack_first.1.first), channel_id=1, source_target_pairs={{0,3},{1,2},{4,1},{5,0},{8,5},{9,4},{12,8},{13,9},{14,12},{15,13},... | collective-permute-start | bytes 442376 | tf_op jit(solution)/shard_map/ppermute | solution.py:227
  5.3 6.3 %collective-permute-start.2 = (bf16[128,512]{1,0:T(8,128)(2,1)S(1)}, bf16[128,512]{1,0:T(8,128)(2,1)S(1)}, u32[]{:S(2)}, u32[]{:S(2)}) collective-permute-start(bf16[128,512]{1,0:T(8,128)(2,1)S(1)} %get-tuple-element.21), channel_id=1, source_target_pairs={{0,4},{1,5},{4,8},{5,9},{8,13},{9,12},{12,15},{13,14},{14,10},{15,... | collective-permute-start | bytes 393224 | tf_op jit(solution)/shard_map/ppermute | solution.py:227
  6.9 6.9 %collective-permute-start.4 = (bf16[128,512]{1,0:T(8,128)(2,1)S(1)}, bf16[128,512]{1,0:T(8,128)(2,1)S(1)}, u32[]{:S(2)}, u32[]{:S(2)}) collective-permute-start(bf16[128,512]{1,0:T(8,128)(2,1)S(1)} %get-tuple-element.21), channel_id=1, source_target_pairs={{0,3},{1,2},{4,1},{5,0},{8,5},{9,4},{12,8},{13,9},{14,12},{15,13},... | collective-permute-start | bytes 393224 | tf_op jit(solution)/shard_map/ppermute | solution.py:227
  6.9 18.4 %collective-permute-start = (bf16[272,512]{1,0:T(8,128)(2,1)S(1)}, bf16[272,512]{1,0:T(8,128)(2,1)S(1)}, u32[]{:S(2)}, u32[]{:S(2)}) collective-permute-start(bf16[272,512]{1,0:T(8,128)(2,1)S(1)} %get-tuple-element.20.own), channel_id=1, source_target_pairs={{0,1},{1,0},{2,3},{3,2},{4,5},{5,4},{6,7},{7,6},{8,9},{9,8},{10,11... | collective-permute-start | bytes 835592 | tf_op jit(solution)/shard_map/ppermute | solution.py:227
  9.4 6.4 %collective-permute-start.5 = (bf16[144,512]{1,0:T(8,128)(2,1)S(1)}, bf16[144,512]{1,0:T(8,128)(2,1)S(1)}, u32[]{:S(2)}, u32[]{:S(2)}) collective-permute-start(bf16[144,512]{1,0:T(8,128)(2,1)S(1)} %collective-permute-done.1.prev_a), channel_id=1, source_target_pairs={{0,5},{1,4},{4,8},{5,9},{8,12},{9,13},{12,15},{13,14},{14,11},{15,... | collective-permute-start | bytes 442376 | tf_op jit(solution)/shard_map/ppermute | solution.py:227
  11.0 6.5 %collective-permute-start.6 = (bf16[144,512]{1,0:T(8,128)(2,1)S(1)}, bf16[144,512]{1,0:T(8,128)(2,1)S(1)}, u32[]{:S(2)}, u32[]{:S(2)}) collective-permute-start(bf16[144,512]{1,0:T(8,128)(2,1)S(1)} %collective-permute-done.3.succ_a), channel_id=1, source_target_pairs={{0,3},{1,2},{4,0},{5,1},{8,5},{9,4},{12,9},{13,8},{14,12},{15,13},... | collective-permute-start | bytes 442376 | tf_op jit(solution)/shard_map/ppermute | solution.py:227
  11.6 6.8 %collective-permute-start.7 = (bf16[128,512]{1,0:T(8,128)(2,1)S(1)}, bf16[128,512]{1,0:T(8,128)(2,1)S(1)}, u32[]{:S(2)}, u32[]{:S(2)}) collective-permute-start(bf16[128,512]{1,0:T(8,128)(2,1)S(1)} %collective-permute-done.2.prev_b), channel_id=1, source_target_pairs={{0,5},{1,4},{4,8},{5,9},{8,12},{9,13},{12,15},{13,14},{14,11},{15,... | collective-permute-start | bytes 393224 | tf_op jit(solution)/shard_map/ppermute | solution.py:227
  13.8 6.1 %collective-permute-start.8 = (bf16[128,512]{1,0:T(8,128)(2,1)S(1)}, bf16[128,512]{1,0:T(8,128)(2,1)S(1)}, u32[]{:S(2)}, u32[]{:S(2)}) collective-permute-start(bf16[128,512]{1,0:T(8,128)(2,1)S(1)} %collective-permute-done.4.succ_b), channel_id=1, source_target_pairs={{0,3},{1,2},{4,0},{5,1},{8,5},{9,4},{12,9},{13,8},{14,12},{15,13},... | collective-permute-start | bytes 393224 | tf_op jit(solution)/shard_map/ppermute | solution.py:227
  20.9 4.7 %collective-permute-start.12 = (f32[1,256]{1,0:T(1,128)S(1)}, f32[1,256]{1,0:T(1,128)S(1)}, u32[]{:S(2)}, u32[]{:S(2)}) collective-permute-start(f32[1,256]{1,0:T(1,128)S(1)} %get-tuple-element.34), channel_id=1, source_target_pairs={{0,2},{1,3},{4,0},{5,1},{8,4},{9,5},{12,9},{13,8},{14,13},{15,12},... | collective-permute-start | bytes 3080 | tf_op jit(solution)/shard_map/ppermute | solution.py:227
  21.0 4.7 %collective-permute-start.11 = (f32[1,256]{1,0:T(1,128)S(1)}, f32[1,256]{1,0:T(1,128)S(1)}, u32[]{:S(2)}, u32[]{:S(2)}) collective-permute-start(f32[1,256]{1,0:T(1,128)S(1)} %get-tuple-element.33), channel_id=1, source_target_pairs={{0,5},{1,4},{4,9},{5,8},{8,12},{9,13},{12,14},{13,15},{14,11},{15,... | collective-permute-start | bytes 3080 | tf_op jit(solution)/shard_map/ppermute | solution.py:227
  22.4 4.7 %collective-permute-start.10 = (f32[1,256]{1,0:T(1,128)S(1)}, f32[1,256]{1,0:T(1,128)S(1)}, u32[]{:S(2)}, u32[]{:S(2)}) collective-permute-start(f32[1,256]{1,0:T(1,128)S(1)} %get-tuple-element.32), channel_id=1, source_target_pairs={{0,7},{1,6},{4,3},{5,2},{8,0},{9,1},{12,4},{13,5},{14,8},{15,9},{1... | collective-permute-start | bytes 3080 | tf_op jit(solution)/shard_map/ppermute | solution.py:227
  24.1 4.5 %collective-permute-start.9 = (f32[1,256]{1,0:T(1,128)S(1)}, f32[1,256]{1,0:T(1,128)S(1)}, u32[]{:S(2)}, u32[]{:S(2)}) collective-permute-start(f32[1,256]{1,0:T(1,128)S(1)} %get-tuple-element.31), channel_id=1, source_target_pairs={{0,9},{1,8},{4,13},{5,12},{8,15},{9,14},{12,11},{13,10},{14,7},{15... | collective-permute-start | bytes 3080 | tf_op jit(solution)/shard_map/ppermute | solution.py:227

commit v4 on v3

--- a/solution.py
+++ b/solution.py
@@ -22,9 +22,10 @@
 
 LABEL_ROWS = 16
 VMEM_BYTES = 32 * 2**20
-NEAR_COST = 6
+PACK_BYTES = 32 * 2**20
+NEAR_COST = 1
 FIRST_COST = 5
-SECOND_COST = 6
+SECOND_COST = 200
 
 
 def pack_first_kernel(embeds, label, first, raw, line, sems):
@@ -114,55 +115,48 @@
     return best
 
 
-def near_kernel(
-    own, prev_a, prev_b, succ_a, succ_b, mine, to_prev, to_succ
-):
+def near_kernel(own, prev_a, prev_b, succ_a, succ_b, mine, bundle):
+    half = prev_b.shape[0]
+    for at, (first, second) in enumerate(((prev_a, prev_b), (succ_a, succ_b))):
+        bundle[at, :half, :] = first[:half, :]
+        bundle[at, half : 2 * half, :] = second[...]
+        bundle[at, 2 * half :, :] = first[half:, :]
+    bundle[2] = own[...]
     own = packed(own)
-    prev, succ = whole(prev_a, prev_b), whole(succ_a, succ_b)
-    mine[...] = best_of(own, own, prev, succ)
-    to_prev[...] = best_of(prev, own)
-    to_succ[...] = best_of(succ, own)
-
-
-def other_kernel(own, other, mine, mine_out):
-    mine_out[...] = jnp.maximum(mine[...], best_of(packed(own), packed(other)))
-
-
-def far_first_kernel(
-    own, prev_a, prev_b, succ_a, succ_b, back_a, ahead_a, *refs
-):
-    mine, to_prev, to_succ, mine_out, to_prev_out, to_succ_out, to_back, to_ahead = refs
-    own = packed(own)
-    prev, succ = whole(prev_a, prev_b), whole(succ_a, succ_b)
+    mine[...] = best_of(own, own, whole(prev_a, prev_b), whole(succ_a, succ_b))
+
+
+def far_first_kernel(own, bundle, back_a, ahead_a, near, mine, to_back, to_ahead):
+    own, prev, succ = packed(own), packed(bundle.at[0]), packed(bundle.at[1])
     back, ahead = first_half(back_a), first_half(ahead_a)
-    mine_out[...] = jnp.maximum(mine[...], best_of(own, back, ahead))
-    to_prev_out[...] = jnp.maximum(to_prev[...], best_of(prev, ahead))
-    to_succ_out[...] = jnp.maximum(to_succ[...], best_of(succ, back))
+    mine[...] = jnp.maximum(near[...], best_of(own, back, ahead))
     to_back[...] = best_of(back, own, succ, ahead)
     to_ahead[...] = best_of(ahead, own, prev, back)
 
 
-def far_second_kernel(
-    own, prev_a, prev_b, succ_a, succ_b, back_a, ahead_a, back_b, ahead_b, *refs
-):
-    mine, to_prev, to_succ, back_first, ahead_first, *out = refs
-    mine_out, to_prev_out, to_succ_out, to_back, to_ahead = out
-    own = packed(own)
-    prev, succ = whole(prev_a, prev_b), whole(succ_a, succ_b)
+def far_second_kernel(own, bundle, back_a, ahead_a, back_b, ahead_b, *refs):
+    near, back_first, ahead_first, mine, to_back, to_ahead = refs
+    own, prev, succ = packed(own), packed(bundle.at[0]), packed(bundle.at[1])
     half = back_b.shape[0]
     back, ahead = first_half(back_a), first_half(ahead_a)
     back_rest, ahead_rest = second_half(back_a, back_b), second_half(ahead_a, ahead_b)
-    mine_out[...] = jnp.maximum(mine[...], best_of(own, back_rest, ahead_rest))
-    to_prev_out[...] = jnp.maximum(to_prev[...], best_of(prev, ahead_rest))
-    to_succ_out[...] = jnp.maximum(to_succ[...], best_of(succ, back_rest))
+    mine[...] = jnp.maximum(near[...], best_of(own, back_rest, ahead_rest))
     to_back[:, :half] = jnp.maximum(back_first[...], best_of(back, ahead_rest))
     to_back[:, half:] = best_of(back_rest, own, succ, ahead, ahead_rest)
     to_ahead[:, :half] = jnp.maximum(ahead_first[...], best_of(ahead, back_rest))
     to_ahead[:, half:] = best_of(ahead_rest, own, prev, back, back_rest)
 
 
-ONE_BACK = (0, 0, 0, 1, 1, 0, 0, 1)
-TWO_BACK = (1, 1, 0, 0, 0, 0, 0, 0)
+def far_other_kernel(others, back_a, ahead_a, back_b, ahead_b, *refs):
+    back_found, ahead_found, to_back, to_ahead = refs
+    back, ahead = whole(back_a, back_b), whole(ahead_a, ahead_b)
+    to_back[...] = jnp.maximum(back_found[...], best_of(back, packed(others.at[1])))
+    to_ahead[...] = jnp.maximum(ahead_found[...], best_of(ahead, packed(others.at[0])))
+
+
+def other_kernel(own, others, found, mine):
+    keys = (packed(others.at[at]) for at in range(3))
+    mine[...] = jnp.maximum(found[...], best_of(packed(own), *keys))
 
 
 def ring_perms(size_x, size_y, size_z):
@@ -173,33 +167,25 @@
         x, y = (place, 0) if place < size_x else (chips - 1 - place, 1)
         return (x * size_y + y) * size_z + core
 
-    def changed(place, step):
-        place = place % chips
-        if step == 0:
-            return 0
-        if step < 0:
-            return 1 - changed(place - step, -step)
-        return (ONE_BACK if step == 1 else TWO_BACK)[place]
-
-    def perm(held, step):
-        pairs = []
-        for place in range(chips):
-            for core in range(size_z):
-                source = core ^ changed(place, held)
-                target = source ^ changed(place + step, held + step)
-                pairs.append((device(place, core), device(place + step, target)))
-        return pairs
+    def perm(to):
+        return [
+            (device(p, k), device(*to(p, k))) for p in range(chips) for k in range(size_z)
+        ]
+
+    def from_back(place, core):
+        return core ^ (place % chips in (0, 1))
+
+    def from_ahead(place, core):
+        return core ^ (place % chips not in (chips - 2, chips - 1))
 
     return {
-        "sibling": [(d, d ^ 1) for d in range(chips * size_z)],
-        "next": perm(0, 1),
-        "prev": perm(0, -1),
-        "on_next": perm(1, 1),
-        "on_prev": perm(-1, -1),
-        "home_prev": perm(1, -1),
-        "home_succ": perm(-1, 1),
-        "home_back": perm(2, -2),
-        "home_ahead": perm(-2, 2),
+        "sibling": perm(lambda p, k: (p, 1 - k)),
+        "next": perm(lambda p, k: (p + 1, k)),
+        "prev": perm(lambda p, k: (p - 1, k)),
+        "on_next": perm(lambda p, k: (p + 1, from_back(p + 1, k))),
+        "on_prev": perm(lambda p, k: (p - 1, from_ahead(p - 1, k))),
+        "home_back": perm(lambda p, k: (p - 2, from_back(p, k))),
+        "home_ahead": perm(lambda p, k: (p + 2, from_ahead(p, k))),
     }
 
 
@@ -230,7 +216,7 @@
     half_line = jax.ShapeDtypeStruct((1, half), jnp.float32)
     anywhere = pl.BlockSpec(memory_space=pl.ANY)
     vmem = pl.BlockSpec(memory_space=pltpu.VMEM)
-    params = pltpu.CompilerParams(vmem_limit_bytes=VMEM_BYTES)
+    params = pltpu.CompilerParams(vmem_limit_bytes=PACK_BYTES)
     own_a = pl.pallas_call(
         pack_first_kernel,
         out_shape=jax.ShapeDtypeStruct((half + LABEL_ROWS, width), jnp.bfloat16),
@@ -258,28 +244,38 @@
     )(embeds, own_a)
     prev_a, succ_a = send(own_a, "next"), send(own_a, "prev")
     prev_b, succ_b = send(own_b, "next"), send(own_b, "prev")
-    other = send(own, "sibling")
     back_a, ahead_a = send(prev_a, "on_next"), send(succ_a, "on_prev")
     back_b, ahead_b = send(prev_b, "on_next"), send(succ_b, "on_prev")
-    blocks = [own, prev_a, prev_b, succ_a, succ_b]
-    near = kernel_call(near_kernel, blocks, [line] * 3, NEAR_COST)
+    mine, bundle = kernel_call(
+        near_kernel,
+        [own, prev_a, prev_b, succ_a, succ_b],
+        [line, jax.ShapeDtypeStruct((3, rows + LABEL_ROWS, width), jnp.bfloat16)],
+        NEAR_COST,
+    )
+    others = send(bundle, "sibling")
     parts = kernel_call(
         far_first_kernel,
-        [*blocks, back_a, ahead_a, *near],
-        [line] * 3 + [half_line] * 2,
+        [own, bundle, back_a, ahead_a, mine],
+        [line, half_line, half_line],
         FIRST_COST,
     )
-    mine, *found = kernel_call(
+    mine, to_back, to_ahead = kernel_call(
         far_second_kernel,
-        [*blocks, back_a, ahead_a, back_b, ahead_b, *parts],
-        [line] * 5,
+        [own, bundle, back_a, ahead_a, back_b, ahead_b, *parts],
+        [line] * 3,
         SECOND_COST,
     )
-    (mine,) = kernel_call(other_kernel, [own, other, mine], [line], 1)
-    homes = ("home_prev", "home_succ", "home_back", "home_ahead")
-    for value, home in zip(found[::-1], homes[::-1]):
-        mine = jnp.maximum(mine, send(value, home))
-    return mine.reshape(rows)
+    to_back, to_ahead = kernel_call(
+        far_other_kernel,
+        [others, back_a, ahead_a, back_b, ahead_b, to_back, to_ahead],
+        [line] * 2,
+        2,
+    )
+    (mine,) = kernel_call(other_kernel, [own, others, mine], [line], 3)
+    best = jnp.maximum(
+        mine, jnp.maximum(send(to_back, "home_back"), send(to_ahead, "home_ahead"))
+    )
+    return best.reshape(rows)
 
 
 def masked_sims(queries, query_labels, query_ids, keys, key_labels, key_ids):

time: 29.3 us -> 28.3 us (0.966)
  waiting for transfers between devices: 12.4 us -> 10.5 us
  starting transfers between devices: 11.3 us -> 12.2 us
    ppermute x13 -> x11, waiting for transfers between devices: 12.4 us -> 10.5 us  [send(): return lax.ppermute(value, GROUP, perms[name])]
    ppermute x13 -> x11, starting transfers between devices: 11.3 us -> 12.2 us  [send(): return lax.ppermute(value, GROUP, perms[name])]
    pallas_call x4 -> x5, Pallas kernels: 2.62 us -> 2.67 us  [kernel_call(): pl.pallas_call(kernel, out_shape=outputs, in_specs=[vmem] * len(inputs),...]
  transfers between devices with their start and end apart: 13 -> 11, of which waited for: 9 -> 7; matrix products, arithmetic and copies ran while one was open for 0% -> 0% of each run, Pallas kernels for 10% -> 9%
where the time goes in v4:
time: 28.3 us; the launch traced here: 28.1 us
  starting transfers between devices  12.2 us (43%)
  waiting for transfers between devices  10.5 us (37%)
  Pallas kernels  3.21 us (11%)
  local copies, waits for them, and re-layouts  1.63 us (6%)
  other arithmetic  0.57 us (2%)
    ppermute x11, starting transfers between devices, send(): return lax.ppermute(value, GROUP, perms[name])  12.2 us
    ppermute x11, waiting for transfers between devices, send(): return lax.ppermute(value, GROUP, perms[name])  10.5 us
    pallas_call x5, Pallas kernels, kernel_call(): pl.pallas_call(kernel, out_shape=outputs, in_specs=[vmem] * len(inputs),...  2.67 us
    unnamed x4, local copies, waits for them, and re-layouts  1.63 us
  transfers between devices with their start and end apart: 11, of which 7 were waited for; matrix products, arithmetic and copies ran while one was open for 0% of the time, Pallas kernels for 9%

profile of v4, /device:TPU:0, one launch (start us, length us, event | category | flops | bytes accessed | tf_op | source)
XLA Modules:
  0.0 28.1 jit_solution(4050155501439573193)
XLA Ops:
  0.0 0.7 %copy-done.1 = s32[256]{0:T(256)S(1)} copy-done((s32[256]{0:T(256)S(1)}, s32[256]{0:T(256)}, u32[]{:S(2)}) %copy-start.1) | copy-done | bytes 1048
  0.7 0.9 %copy-done = bf16[256,512]{1,0:T(8,128)(2,1)S(1)} copy-done((bf16[256,512]{1,0:T(8,128)(2,1)S(1)}, bf16[256,512]{1,0:T(8,128)(2,1)}, u32[]{:S(2)}) %copy-start) | copy-done | bytes 262168
  1.6 0.3 pack_first.1.first
  1.9 3.0 %collective-permute-start.2 = (bf16[144,512]{1,0:T(8,128)(2,1)S(1)}, bf16[144,512]{1,0:T(8,128)(2,1)S(1)}, u32[]{:S(2)}, u32[]{:S(2)}) collective-permute-start(bf16[144,512]{1,0:T(8,128)(2,1)S(1)} %pack_first.1.first), channel_id=1, source_target_pairs={{0,2},{1,3},{4,0},{5,1},{8,4},{9,5},{12,8},{13,9},{14,12},{15,13},... | collective-permute-start | bytes 442376 | tf_op jit(solution)/shard_map/ppermute | solution.py:213
  4.9 0.2 collective-permute-start
  5.1 0.3 pack_second.1
  5.3 1.9 %collective-permute-start.3 = (bf16[128,512]{1,0:T(8,128)(2,1)S(1)}, bf16[128,512]{1,0:T(8,128)(2,1)S(1)}, u32[]{:S(2)}, u32[]{:S(2)}) collective-permute-start(bf16[128,512]{1,0:T(8,128)(2,1)S(1)} %get-tuple-element.18), channel_id=1, source_target_pairs={{0,2},{1,3},{4,0},{5,1},{8,4},{9,5},{12,8},{13,9},{14,12},{15,13},... | collective-permute-start | bytes 393224 | tf_op jit(solution)/shard_map/ppermute | solution.py:213
  7.3 0.2 collective-permute-start.1
  7.4 2.3 %collective-permute-done.2.succ_a = bf16[144,512]{1,0:T(8,128)(2,1)S(1)} collective-permute-done((bf16[144,512]{1,0:T(8,128)(2,1)S(1)}, bf16[144,512]{1,0:T(8,128)(2,1)S(1)}, u32[]{:S(2)}, u32[]{:S(2)}) %collective-permute-start.2) | collective-permute-done | bytes 147488 | tf_op jit(solution)/shard_map/ppermute | solution.py:213
  9.7 2.0 %collective-permute-start.6 = (bf16[144,512]{1,0:T(8,128)(2,1)S(1)}, bf16[144,512]{1,0:T(8,128)(2,1)S(1)}, u32[]{:S(2)}, u32[]{:S(2)}) collective-permute-start(bf16[144,512]{1,0:T(8,128)(2,1)S(1)} %collective-permute-done.2.succ_a), channel_id=1, source_target_pairs={{0,2},{1,3},{4,1},{5,0},{8,5},{9,4},{12,9},{13,8},{14,13},{15,12},... | collective-permute-start | bytes 442376 | tf_op jit(solution)/shard_map/ppermute | solution.py:213
  11.6 0.0 collective-permute-done.prev_a
  11.6 0.0 collective-permute-start.5
  11.7 0.3 %collective-permute-done.3.succ_b = bf16[128,512]{1,0:T(8,128)(2,1)S(1)} collective-permute-done((bf16[128,512]{1,0:T(8,128)(2,1)S(1)}, bf16[128,512]{1,0:T(8,128)(2,1)S(1)}, u32[]{:S(2)}, u32[]{:S(2)}) %collective-permute-start.3) | collective-permute-done | bytes 131104 | tf_op jit(solution)/shard_map/ppermute | solution.py:213
  12.0 2.5 %collective-permute-start.8 = (bf16[128,512]{1,0:T(8,128)(2,1)S(1)}, bf16[128,512]{1,0:T(8,128)(2,1)S(1)}, u32[]{:S(2)}, u32[]{:S(2)}) collective-permute-start(bf16[128,512]{1,0:T(8,128)(2,1)S(1)} %collective-permute-done.3.succ_b), channel_id=1, source_target_pairs={{0,2},{1,3},{4,1},{5,0},{8,5},{9,4},{12,9},{13,8},{14,13},{15,12},... | collective-permute-start | bytes 393224 | tf_op jit(solution)/shard_map/ppermute | solution.py:213
  14.5 0.0 collective-permute-done.1.prev_b
  14.5 0.0 collective-permute-start.7
  14.5 0.4 %near_kernel.1 = (f32[1,256]{1,0:T(1,128)S(1)}, bf16[3,272,512]{2,1,0:T(8,128)(2,1)S(1)}) custom-call(bf16[272,512]{1,0:T(8,128)(2,1)S(1)} %get-tuple-element.17.own, bf16[144,512]{1,0:T(8,128)(2,1)S(1)} %collective-permute-done.prev_a, bf16[128,512]{1,0:T(8,128)(2,1)S(1)} %collective-permute-done.1.prev_b, ...), custom_call_target="tpu_custom_call" | custom-call | flops 67108864 | bytes 1048576 | tf_op jit(solution)/shard_map/near_kernel/pallas_call | solution.py:194
  14.9 0.1 collective-permute-start.4
  15.0 0.3 %collective-permute-done.6.ahead_a = bf16[144,512]{1,0:T(8,128)(2,1)S(1)} collective-permute-done((bf16[144,512]{1,0:T(8,128)(2,1)S(1)}, bf16[144,512]{1,0:T(8,128)(2,1)S(1)}, u32[]{:S(2)}, u32[]{:S(2)}) %collective-permute-start.6) | collective-permute-done | bytes 147488 | tf_op jit(solution)/shard_map/ppermute | solution.py:213
  15.3 2.4 %collective-permute-done.5.back_a = bf16[144,512]{1,0:T(8,128)(2,1)S(1)} collective-permute-done((bf16[144,512]{1,0:T(8,128)(2,1)S(1)}, bf16[144,512]{1,0:T(8,128)(2,1)S(1)}, u32[]{:S(2)}, u32[]{:S(2)}) %collective-permute-start.5) | collective-permute-done | bytes 147488 | tf_op jit(solution)/shard_map/ppermute | solution.py:213
  17.7 0.7 %far_first_kernel.1 = (f32[1,256]{1,0:T(1,128)S(1)}, f32[1,128]{1,0:T(1,128)S(1)}, f32[1,128]{1,0:T(1,128)S(1)}) custom-call(bf16[272,512]{1,0:T(8,128)(2,1)S(1)} %get-tuple-element.17.own, bf16[3,272,512]{2,1,0:T(8,128)(2,1)S(1)} %get-tuple-element.19.bundle, bf16[144,512]{1,0:T(8,128)(2,1)S(1)} %collective-permute-done.5.back_a, ...), custom_call_target="tpu_custom_call" | custom-call | flops 335544320 | bytes 1048576 | tf_op jit(solution)/shard_map/far_first_kernel/pallas_call | solution.py:194
  18.3 0.0 collective-permute-done.8.ahead_b
  18.3 2.1 %collective-permute-done.7.back_b = bf16[128,512]{1,0:T(8,128)(2,1)S(1)} collective-permute-done((bf16[128,512]{1,0:T(8,128)(2,1)S(1)}, bf16[128,512]{1,0:T(8,128)(2,1)S(1)}, u32[]{:S(2)}, u32[]{:S(2)}) %collective-permute-start.7) | collective-permute-done | bytes 131104 | tf_op jit(solution)/shard_map/ppermute | solution.py:213
  20.5 0.8 %far_second_kernel.1 = (f32[1,256]{1,0:T(1,128)S(1)}, f32[1,256]{1,0:T(1,128)S(1)}, f32[1,256]{1,0:T(1,128)S(1)}) custom-call(bf16[272,512]{1,0:T(8,128)(2,1)S(1)} %get-tuple-element.17.own, bf16[3,272,512]{2,1,0:T(8,128)(2,1)S(1)} %get-tuple-element.19.bundle, bf16[144,512]{1,0:T(8,128)(2,1)S(1)} %collective-permute-done.5.back_a, ...), custom_call_target="tpu_custom_call" | custom-call | flops 13421772800 | bytes 1048576 | tf_op jit(solution)/shard_map/far_second_kernel/pallas_call | solution.py:194
  21.3 0.0 collective-permute-done.4.others
  21.3 0.3 %far_other_kernel.1 = (f32[1,256]{1,0:T(1,128)S(1)}, f32[1,256]{1,0:T(1,128)S(1)}) custom-call(bf16[3,272,512]{2,1,0:T(8,128)(2,1)S(1)} %collective-permute-done.4.others, bf16[144,512]{1,0:T(8,128)(2,1)S(1)} %collective-permute-done.5.back_a, bf16[144,512]{1,0:T(8,128)(2,1)S(1)} %collective-permute-done.6.ahead_a, ...), custom_call_target="tpu_custom_call" | custom-call | flops 134217728 | bytes 1048576 | tf_op jit(solution)/shard_map/far_other_kernel/pallas_call | solution.py:194
  21.6 1.5 %collective-permute-start.9 = (f32[1,256]{1,0:T(1,128)S(1)}, f32[1,256]{1,0:T(1,128)S(1)}, u32[]{:S(2)}, u32[]{:S(2)}) collective-permute-start(f32[1,256]{1,0:T(1,128)S(1)} %get-tuple-element.27), channel_id=1, source_target_pairs={{0,7},{1,6},{4,3},{5,2},{8,0},{9,1},{12,4},{13,5},{14,8},{15,9},{1... | collective-permute-start | bytes 3080 | tf_op jit(solution)/shard_map/ppermute | solution.py:213
  23.1 1.0 %collective-permute-start.10 = (f32[1,256]{1,0:T(1,128)S(1)}, f32[1,256]{1,0:T(1,128)S(1)}, u32[]{:S(2)}, u32[]{:S(2)}) collective-permute-start(f32[1,256]{1,0:T(1,128)S(1)} %get-tuple-element.28), channel_id=1, source_target_pairs={{0,9},{1,8},{4,13},{5,12},{8,15},{9,14},{12,11},{13,10},{14,7},{15... | collective-permute-start | bytes 3080 | tf_op jit(solution)/shard_map/ppermute | solution.py:213
  24.1 0.4 %other_kernel.1 = f32[1,256]{1,0:T(1,128)S(1)} custom-call(bf16[272,512]{1,0:T(8,128)(2,1)S(1)} %get-tuple-element.17.own, bf16[3,272,512]{2,1,0:T(8,128)(2,1)S(1)} %collective-permute-done.4.others, f32[1,256]{1,0:T(1,128)S(1)} %get-tuple-element.24.found), custom_call_target="tpu_custom_call" | custom-call | flops 201326592 | bytes 1048576 | tf_op jit(solution)/shard_map/other_kernel/pallas_call | solution.py:194
  24.5 1.7 %collective-permute-done.9 = f32[1,256]{1,0:T(1,128)S(1)} collective-permute-done((f32[1,256]{1,0:T(1,128)S(1)}, f32[1,256]{1,0:T(1,128)S(1)}, u32[]{:S(2)}, u32[]{:S(2)}) %collective-permute-start.9) | collective-permute-done | bytes 1056 | tf_op jit(solution)/shard_map/ppermute | solution.py:213
  26.2 1.4 %collective-permute-done.10 = f32[1,256]{1,0:T(1,128)S(1)} collective-permute-done((f32[1,256]{1,0:T(1,128)S(1)}, f32[1,256]{1,0:T(1,128)S(1)}, u32[]{:S(2)}, u32[]{:S(2)}) %collective-permute-start.10) | collective-permute-done | bytes 1056 | tf_op jit(solution)/shard_map/ppermute | solution.py:213
  27.6 0.6 %maximum_maximum_fusion = f32[1,256]{1,0:T(1,128)} fusion(f32[1,256]{1,0:T(1,128)S(1)} %other_kernel.1, f32[1,256]{1,0:T(1,128)S(1)} %collective-permute-done.9, f32[1,256]{1,0:T(1,128)S(1)} %collective-permute-done.10), kind=kLoop, calls=%fused_computation | loop fusion | flops 512 | bytes 4096 | tf_op jit(solution)/shard_map/max | solution.py:275
  (2 shorter events, 0.0 us)
Async XLA Ops:
  0.0 0.7 %copy-start.1 = (s32[256]{0:T(256)S(1)}, s32[256]{0:T(256)}, u32[]{:S(2)}) copy-start(s32[256]{0:T(256)} %param.3) | copy-start | bytes 3076
  0.7 0.9 %copy-start = (bf16[256,512]{1,0:T(8,128)(2,1)S(1)}, bf16[256,512]{1,0:T(8,128)(2,1)}, u32[]{:S(2)}) copy-start(bf16[256,512]{1,0:T(8,128)(2,1)} %embeds.3) | copy-start | bytes 786436
  1.9 7.8 %collective-permute-start.2 = (bf16[144,512]{1,0:T(8,128)(2,1)S(1)}, bf16[144,512]{1,0:T(8,128)(2,1)S(1)}, u32[]{:S(2)}, u32[]{:S(2)}) collective-permute-start(bf16[144,512]{1,0:T(8,128)(2,1)S(1)} %pack_first.1.first), channel_id=1, source_target_pairs={{0,2},{1,3},{4,0},{5,1},{8,4},{9,5},{12,8},{13,9},{14,12},{15,13},... | collective-permute-start | bytes 442376 | tf_op jit(solution)/shard_map/ppermute | solution.py:213
  4.9 6.7 %collective-permute-start = (bf16[144,512]{1,0:T(8,128)(2,1)S(1)}, bf16[144,512]{1,0:T(8,128)(2,1)S(1)}, u32[]{:S(2)}, u32[]{:S(2)}) collective-permute-start(bf16[144,512]{1,0:T(8,128)(2,1)S(1)} %pack_first.1.first), channel_id=1, source_target_pairs={{0,4},{1,5},{4,8},{5,9},{8,12},{9,13},{12,14},{13,15},{14,10},{15,... | collective-permute-start | bytes 442376 | tf_op jit(solution)/shard_map/ppermute | solution.py:213
  5.3 6.6 %collective-permute-start.3 = (bf16[128,512]{1,0:T(8,128)(2,1)S(1)}, bf16[128,512]{1,0:T(8,128)(2,1)S(1)}, u32[]{:S(2)}, u32[]{:S(2)}) collective-permute-start(bf16[128,512]{1,0:T(8,128)(2,1)S(1)} %get-tuple-element.18), channel_id=1, source_target_pairs={{0,2},{1,3},{4,0},{5,1},{8,4},{9,5},{12,8},{13,9},{14,12},{15,13},... | collective-permute-start | bytes 393224 | tf_op jit(solution)/shard_map/ppermute | solution.py:213
  7.3 7.2 %collective-permute-start.1 = (bf16[128,512]{1,0:T(8,128)(2,1)S(1)}, bf16[128,512]{1,0:T(8,128)(2,1)S(1)}, u32[]{:S(2)}, u32[]{:S(2)}) collective-permute-start(bf16[128,512]{1,0:T(8,128)(2,1)S(1)} %get-tuple-element.18), channel_id=1, source_target_pairs={{0,4},{1,5},{4,8},{5,9},{8,12},{9,13},{12,14},{13,15},{14,10},{15,... | collective-permute-start | bytes 393224 | tf_op jit(solution)/shard_map/ppermute | solution.py:213
  9.7 5.6 %collective-permute-start.6 = (bf16[144,512]{1,0:T(8,128)(2,1)S(1)}, bf16[144,512]{1,0:T(8,128)(2,1)S(1)}, u32[]{:S(2)}, u32[]{:S(2)}) collective-permute-start(bf16[144,512]{1,0:T(8,128)(2,1)S(1)} %collective-permute-done.2.succ_a), channel_id=1, source_target_pairs={{0,2},{1,3},{4,1},{5,0},{8,5},{9,4},{12,9},{13,8},{14,13},{15,12},... | collective-permute-start | bytes 442376 | tf_op jit(solution)/shard_map/ppermute | solution.py:213
  11.6 6.0 %collective-permute-start.5 = (bf16[144,512]{1,0:T(8,128)(2,1)S(1)}, bf16[144,512]{1,0:T(8,128)(2,1)S(1)}, u32[]{:S(2)}, u32[]{:S(2)}) collective-permute-start(bf16[144,512]{1,0:T(8,128)(2,1)S(1)} %collective-permute-done.prev_a), channel_id=1, source_target_pairs={{0,5},{1,4},{4,8},{5,9},{8,12},{9,13},{12,14},{13,15},{14,10},{15,... | collective-permute-start | bytes 442376 | tf_op jit(solution)/shard_map/ppermute | solution.py:213
  12.0 6.4 %collective-permute-start.8 = (bf16[128,512]{1,0:T(8,128)(2,1)S(1)}, bf16[128,512]{1,0:T(8,128)(2,1)S(1)}, u32[]{:S(2)}, u32[]{:S(2)}) collective-permute-start(bf16[128,512]{1,0:T(8,128)(2,1)S(1)} %collective-permute-done.3.succ_b), channel_id=1, source_target_pairs={{0,2},{1,3},{4,1},{5,0},{8,5},{9,4},{12,9},{13,8},{14,13},{15,12},... | collective-permute-start | bytes 393224 | tf_op jit(solution)/shard_map/ppermute | solution.py:213
  14.5 6.0 %collective-permute-start.7 = (bf16[128,512]{1,0:T(8,128)(2,1)S(1)}, bf16[128,512]{1,0:T(8,128)(2,1)S(1)}, u32[]{:S(2)}, u32[]{:S(2)}) collective-permute-start(bf16[128,512]{1,0:T(8,128)(2,1)S(1)} %collective-permute-done.1.prev_b), channel_id=1, source_target_pairs={{0,5},{1,4},{4,8},{5,9},{8,12},{9,13},{12,14},{13,15},{14,10},{15,... | collective-permute-start | bytes 393224 | tf_op jit(solution)/shard_map/ppermute | solution.py:213
  14.9 6.4 %collective-permute-start.4 = (bf16[3,272,512]{2,1,0:T(8,128)(2,1)S(1)}, bf16[3,272,512]{2,1,0:T(8,128)(2,1)S(1)}, u32[]{:S(2)}, u32[]{:S(2)}) collective-permute-start(bf16[3,272,512]{2,1,0:T(8,128)(2,1)S(1)} %get-tuple-element.19.bundle), channel_id=1, source_target_pairs={{0,1},{1,0},{4,5},{5,4},{8,9},{9,8},{12,13},{13,12},{14,15},{15,14... | collective-permute-start | bytes 2506760 | tf_op jit(solution)/shard_map/ppermute | solution.py:213
  21.6 4.5 %collective-permute-start.9 = (f32[1,256]{1,0:T(1,128)S(1)}, f32[1,256]{1,0:T(1,128)S(1)}, u32[]{:S(2)}, u32[]{:S(2)}) collective-permute-start(f32[1,256]{1,0:T(1,128)S(1)} %get-tuple-element.27), channel_id=1, source_target_pairs={{0,7},{1,6},{4,3},{5,2},{8,0},{9,1},{12,4},{13,5},{14,8},{15,9},{1... | collective-permute-start | bytes 3080 | tf_op jit(solution)/shard_map/ppermute | solution.py:213
  23.1 4.5 %collective-permute-start.10 = (f32[1,256]{1,0:T(1,128)S(1)}, f32[1,256]{1,0:T(1,128)S(1)}, u32[]{:S(2)}, u32[]{:S(2)}) collective-permute-start(f32[1,256]{1,0:T(1,128)S(1)} %get-tuple-element.28), channel_id=1, source_target_pairs={{0,9},{1,8},{4,13},{5,12},{8,15},{9,14},{12,11},{13,10},{14,7},{15... | collective-permute-start | bytes 3080 | tf_op jit(solution)/shard_map/ppermute | solution.py:213

commit v5 on v4

--- a/solution.py
+++ b/solution.py
@@ -22,7 +22,6 @@
 
 LABEL_ROWS = 16
 VMEM_BYTES = 32 * 2**20
-PACK_BYTES = 32 * 2**20
 NEAR_COST = 1
 FIRST_COST = 5
 SECOND_COST = 200
@@ -93,6 +92,13 @@
 def second_half(first, second):
     half = second.shape[0]
     return Block(second[...], labels_in(first)[:, half:])
+
+
+def joined(*blocks):
+    return Block(
+        jnp.concatenate([block.unit for block in blocks], axis=0),
+        jnp.concatenate([block.label for block in blocks], axis=1),
+    )
 
 
 def best_of(queries, *all_keys):
@@ -126,25 +132,26 @@
     mine[...] = best_of(own, own, whole(prev_a, prev_b), whole(succ_a, succ_b))
 
 
-def far_first_kernel(own, bundle, back_a, ahead_a, near, mine, to_back, to_ahead):
-    own, prev, succ = packed(own), packed(bundle.at[0]), packed(bundle.at[1])
-    back, ahead = first_half(back_a), first_half(ahead_a)
-    mine[...] = jnp.maximum(near[...], best_of(own, back, ahead))
-    to_back[...] = best_of(back, own, succ, ahead)
-    to_ahead[...] = best_of(ahead, own, prev, back)
-
-
-def far_second_kernel(own, bundle, back_a, ahead_a, back_b, ahead_b, *refs):
-    near, back_first, ahead_first, mine, to_back, to_ahead = refs
-    own, prev, succ = packed(own), packed(bundle.at[0]), packed(bundle.at[1])
+def far_first_kernel(own, prev_a, prev_b, succ_a, succ_b, back_a, ahead_a, found):
+    near = packed(own), whole(prev_a, prev_b), whole(succ_a, succ_b)
+    rows = joined(first_half(back_a), first_half(ahead_a))
+    found[...] = best_of(rows, rows, *near)
+
+
+def far_second_kernel(
+    own, prev_a, prev_b, succ_a, succ_b, back_a, ahead_a, back_b, ahead_b, *refs
+):
+    first_found, to_back, to_ahead = refs
+    near = packed(own), whole(prev_a, prev_b), whole(succ_a, succ_b)
     half = back_b.shape[0]
-    back, ahead = first_half(back_a), first_half(ahead_a)
-    back_rest, ahead_rest = second_half(back_a, back_b), second_half(ahead_a, ahead_b)
-    mine[...] = jnp.maximum(near[...], best_of(own, back_rest, ahead_rest))
-    to_back[:, :half] = jnp.maximum(back_first[...], best_of(back, ahead_rest))
-    to_back[:, half:] = best_of(back_rest, own, succ, ahead, ahead_rest)
-    to_ahead[:, :half] = jnp.maximum(ahead_first[...], best_of(ahead, back_rest))
-    to_ahead[:, half:] = best_of(ahead_rest, own, prev, back, back_rest)
+    first = joined(first_half(back_a), first_half(ahead_a))
+    second = joined(second_half(back_a, back_b), second_half(ahead_a, ahead_b))
+    found = jnp.maximum(first_found[...], best_of(first, second))
+    found_second = best_of(second, second, first, *near)
+    to_back[:, :half] = found[:, :half]
+    to_back[:, half:] = found_second[:, :half]
+    to_ahead[:, :half] = found[:, half:]
+    to_ahead[:, half:] = found_second[:, half:]
 
 
 def far_other_kernel(others, back_a, ahead_a, back_b, ahead_b, *refs):
@@ -154,9 +161,10 @@
     to_ahead[...] = jnp.maximum(ahead_found[...], best_of(ahead, packed(others.at[0])))
 
 
-def other_kernel(own, others, found, mine):
-    keys = (packed(others.at[at]) for at in range(3))
-    mine[...] = jnp.maximum(found[...], best_of(packed(own), *keys))
+def own_kernel(own, others, back_a, ahead_a, back_b, ahead_b, near, mine):
+    keys = [packed(others.at[at]) for at in range(3)]
+    keys += [whole(back_a, back_b), whole(ahead_a, ahead_b)]
+    mine[...] = jnp.maximum(near[...], best_of(packed(own), *keys))
 
 
 def ring_perms(size_x, size_y, size_z):
@@ -172,20 +180,20 @@
             (device(p, k), device(*to(p, k))) for p in range(chips) for k in range(size_z)
         ]
 
-    def from_back(place, core):
+    def from_prev(place, core):
         return core ^ (place % chips in (0, 1))
 
-    def from_ahead(place, core):
-        return core ^ (place % chips not in (chips - 2, chips - 1))
+    def from_next(place, core):
+        return core ^ (place % chips not in (0, 1))
 
     return {
         "sibling": perm(lambda p, k: (p, 1 - k)),
-        "next": perm(lambda p, k: (p + 1, k)),
-        "prev": perm(lambda p, k: (p - 1, k)),
-        "on_next": perm(lambda p, k: (p + 1, from_back(p + 1, k))),
-        "on_prev": perm(lambda p, k: (p - 1, from_ahead(p - 1, k))),
-        "home_back": perm(lambda p, k: (p - 2, from_back(p, k))),
-        "home_ahead": perm(lambda p, k: (p + 2, from_ahead(p, k))),
+        "next": perm(lambda p, k: (p + 1, from_prev(p + 1, k))),
+        "prev": perm(lambda p, k: (p - 1, from_next(p - 1, k))),
+        "on_next": perm(lambda p, k: (p + 1, k)),
+        "on_prev": perm(lambda p, k: (p - 1, k)),
+        "home_back": perm(lambda p, k: (p - 2, from_prev(p - 1, k))),
+        "home_ahead": perm(lambda p, k: (p + 2, from_next(p + 1, k))),
     }
 
 
@@ -213,10 +221,11 @@
         return lax.ppermute(value, GROUP, perms[name])
 
     line = jax.ShapeDtypeStruct((1, rows), jnp.float32)
-    half_line = jax.ShapeDtypeStruct((1, half), jnp.float32)
     anywhere = pl.BlockSpec(memory_space=pl.ANY)
     vmem = pl.BlockSpec(memory_space=pltpu.VMEM)
-    params = pltpu.CompilerParams(vmem_limit_bytes=PACK_BYTES)
+    params = pltpu.CompilerParams(vmem_limit_bytes=VMEM_BYTES)
+    embeds = pltpu.with_memory_space_constraint(embeds, pltpu.HBM)
+    label = pltpu.with_memory_space_constraint(cluster.reshape(1, rows), pltpu.HBM)
     own_a = pl.pallas_call(
         pack_first_kernel,
         out_shape=jax.ShapeDtypeStruct((half + LABEL_ROWS, width), jnp.bfloat16),
@@ -229,7 +238,7 @@
         ],
         compiler_params=params,
         name="pack_first",
-    )(embeds, cluster.reshape(1, rows))
+    )(embeds, label)
     own_b, own = pl.pallas_call(
         pack_second_kernel,
         out_shape=[
@@ -253,25 +262,18 @@
         NEAR_COST,
     )
     others = send(bundle, "sibling")
-    parts = kernel_call(
-        far_first_kernel,
-        [own, bundle, back_a, ahead_a, mine],
-        [line, half_line, half_line],
-        FIRST_COST,
-    )
-    mine, to_back, to_ahead = kernel_call(
-        far_second_kernel,
-        [own, bundle, back_a, ahead_a, back_b, ahead_b, *parts],
-        [line] * 3,
-        SECOND_COST,
+    blocks = [own, prev_a, prev_b, succ_a, succ_b]
+    far = [back_a, ahead_a, back_b, ahead_b]
+    (first_found,) = kernel_call(
+        far_first_kernel, [*blocks, back_a, ahead_a], [line], FIRST_COST
     )
     to_back, to_ahead = kernel_call(
-        far_other_kernel,
-        [others, back_a, ahead_a, back_b, ahead_b, to_back, to_ahead],
-        [line] * 2,
-        2,
-    )
-    (mine,) = kernel_call(other_kernel, [own, others, mine], [line], 3)
+        far_second_kernel, [*blocks, *far, first_found], [line] * 2, SECOND_COST
+    )
+    to_back, to_ahead = kernel_call(
+        far_other_kernel, [others, *far, to_back, to_ahead], [line] * 2, 2
+    )
+    (mine,) = kernel_call(own_kernel, [own, others, *far, mine], [line], 5)
     best = jnp.maximum(
         mine, jnp.maximum(send(to_back, "home_back"), send(to_ahead, "home_ahead"))
     )

time: 28.3 us -> 25.8 us (0.912)
  waiting for transfers between devices: 10.5 us -> 7.71 us
  local copies, waits for them, and re-layouts: 1.63 us -> 0 us
  Pallas kernels: 3.21 us -> 4.5 us
  starting transfers between devices: 12.2 us -> 12.8 us
    ppermute x11, waiting for transfers between devices: 10.5 us -> 7.71 us  [send(): return lax.ppermute(value, GROUP, perms[name])]
    unnamed x4 -> x0, local copies, waits for them, and re-layouts: 1.63 us -> none
    pallas_call x1, Pallas kernels: 0.28 us -> 1.05 us  [on_ring(): pl.pallas_call(pack_first_kernel, out_shape=jax.ShapeDtypeStruct((half +...]
    pallas_call x1, Pallas kernels: 0.27 us -> 1.02 us  [on_ring(): pl.pallas_call(pack_second_kernel, out_shape=[jax.ShapeDtypeStruct((half,...]
    ppermute x11, starting transfers between devices: 12.2 us -> 12.8 us  [send(): return lax.ppermute(value, GROUP, perms[name])]
  transfers between devices with their start and end apart: 11 -> 11, of which waited for: 7 -> 8; matrix products, arithmetic and copies ran while one was open for 0% -> 0% of each run, Pallas kernels for 9% -> 12%
where the time goes in v5:
time: 25.8 us; the launch traced here: 25.7 us
  starting transfers between devices  12.8 us (50%)
  waiting for transfers between devices  7.71 us (30%)
  Pallas kernels  4.5 us (17%)
  other arithmetic  0.57 us (2%)
    ppermute x11, starting transfers between devices, send(): return lax.ppermute(value, GROUP, perms[name])  12.8 us
    ppermute x11, waiting for transfers between devices, send(): return lax.ppermute(value, GROUP, perms[name])  7.71 us
    pallas_call x5, Pallas kernels, kernel_call(): pl.pallas_call(kernel, out_shape=outputs, in_specs=[vmem] * len(inputs),...  2.43 us
    pallas_call x1, Pallas kernels, on_ring(): pl.pallas_call(pack_first_kernel, out_shape=jax.ShapeDtypeStruct((half +...  1.05 us
    pallas_call x1, Pallas kernels, on_ring(): pl.pallas_call(pack_second_kernel, out_shape=[jax.ShapeDtypeStruct((half,...  1.02 us
    max x1, other arithmetic, on_ring(): jnp.maximum(mine, jnp.maximum(send(to_back, 'home_back'), send(to_ahead,...  0.57 us
  transfers between devices with their start and end apart: 11, of which 8 were waited for; matrix products, arithmetic and copies ran while one was open for 0% of the time, Pallas kernels for 12%

profile of v5, /device:TPU:0, one launch (start us, length us, event | category | flops | bytes accessed | tf_op | source)
XLA Modules:
  0.0 25.7 jit_solution(8619877973833167551)
XLA Ops:
  0.0 1.0 %pack_first.1.first = bf16[144,512]{1,0:T(8,128)(2,1)S(1)} custom-call(bf16[256,512]{1,0:T(8,128)(2,1)} %embeds.3, s32[1,256]{1,0:T(1,128)} %bitcast.2), custom_call_target="tpu_custom_call" | custom-call | tf_op jit(solution)/shard_map/pack_first/pallas_call | solution.py:229
  1.1 2.5 %collective-permute-start = (bf16[144,512]{1,0:T(8,128)(2,1)S(1)}, bf16[144,512]{1,0:T(8,128)(2,1)S(1)}, u32[]{:S(2)}, u32[]{:S(2)}) collective-permute-start(bf16[144,512]{1,0:T(8,128)(2,1)S(1)} %pack_first.1.first), channel_id=1, source_target_pairs={{0,5},{1,4},{4,8},{5,9},{8,12},{9,13},{12,14},{13,15},{14,10},{15,... | collective-permute-start | bytes 442376 | tf_op jit(solution)/shard_map/ppermute | solution.py:221
  3.6 0.0 collective-permute-start.2
  3.6 1.0 %pack_second.1 = (bf16[128,512]{1,0:T(8,128)(2,1)S(1)}, bf16[272,512]{1,0:T(8,128)(2,1)S(1)}) custom-call(bf16[256,512]{1,0:T(8,128)(2,1)} %embeds.3, bf16[144,512]{1,0:T(8,128)(2,1)S(1)} %pack_first.1.first), custom_call_target="tpu_custom_call" | custom-call | tf_op jit(solution)/shard_map/pack_second/pallas_call | solution.py:242
  4.6 2.1 %collective-permute-start.1 = (bf16[128,512]{1,0:T(8,128)(2,1)S(1)}, bf16[128,512]{1,0:T(8,128)(2,1)S(1)}, u32[]{:S(2)}, u32[]{:S(2)}) collective-permute-start(bf16[128,512]{1,0:T(8,128)(2,1)S(1)} %get-tuple-element.14), channel_id=1, source_target_pairs={{0,5},{1,4},{4,8},{5,9},{8,12},{9,13},{12,14},{13,15},{14,10},{15,... | collective-permute-start | bytes 393224 | tf_op jit(solution)/shard_map/ppermute | solution.py:221
  6.7 0.3 %collective-permute-start.3 = (bf16[128,512]{1,0:T(8,128)(2,1)S(1)}, bf16[128,512]{1,0:T(8,128)(2,1)S(1)}, u32[]{:S(2)}, u32[]{:S(2)}) collective-permute-start(bf16[128,512]{1,0:T(8,128)(2,1)S(1)} %get-tuple-element.14), channel_id=1, source_target_pairs={{0,3},{1,2},{4,0},{5,1},{8,4},{9,5},{12,9},{13,8},{14,13},{15,12},... | collective-permute-start | bytes 393224 | tf_op jit(solution)/shard_map/ppermute | solution.py:221
  7.0 0.9 %collective-permute-done.prev_a = bf16[144,512]{1,0:T(8,128)(2,1)S(1)} collective-permute-done((bf16[144,512]{1,0:T(8,128)(2,1)S(1)}, bf16[144,512]{1,0:T(8,128)(2,1)S(1)}, u32[]{:S(2)}, u32[]{:S(2)}) %collective-permute-start) | collective-permute-done | bytes 147488 | tf_op jit(solution)/shard_map/ppermute | solution.py:221
  7.8 2.5 %collective-permute-start.5 = (bf16[144,512]{1,0:T(8,128)(2,1)S(1)}, bf16[144,512]{1,0:T(8,128)(2,1)S(1)}, u32[]{:S(2)}, u32[]{:S(2)}) collective-permute-start(bf16[144,512]{1,0:T(8,128)(2,1)S(1)} %collective-permute-done.prev_a), channel_id=1, source_target_pairs={{0,4},{1,5},{4,8},{5,9},{8,12},{9,13},{12,14},{13,15},{14,10},{15,... | collective-permute-start | bytes 442376 | tf_op jit(solution)/shard_map/ppermute | solution.py:221
  10.3 0.0 collective-permute-done.2.succ_a
  10.3 0.0 collective-permute-start.6
  10.3 0.3 %collective-permute-done.1.prev_b = bf16[128,512]{1,0:T(8,128)(2,1)S(1)} collective-permute-done((bf16[128,512]{1,0:T(8,128)(2,1)S(1)}, bf16[128,512]{1,0:T(8,128)(2,1)S(1)}, u32[]{:S(2)}, u32[]{:S(2)}) %collective-permute-start.1) | collective-permute-done | bytes 131104 | tf_op jit(solution)/shard_map/ppermute | solution.py:221
  10.7 2.4 %collective-permute-start.7 = (bf16[128,512]{1,0:T(8,128)(2,1)S(1)}, bf16[128,512]{1,0:T(8,128)(2,1)S(1)}, u32[]{:S(2)}, u32[]{:S(2)}) collective-permute-start(bf16[128,512]{1,0:T(8,128)(2,1)S(1)} %collective-permute-done.1.prev_b), channel_id=1, source_target_pairs={{0,4},{1,5},{4,8},{5,9},{8,12},{9,13},{12,14},{13,15},{14,10},{15,... | collective-permute-start | bytes 393224 | tf_op jit(solution)/shard_map/ppermute | solution.py:221
  13.1 0.0 collective-permute-done.3.succ_b
  13.1 0.0 collective-permute-start.8
  13.1 0.4 %near_kernel.1 = (f32[1,256]{1,0:T(1,128)S(1)}, bf16[3,272,512]{2,1,0:T(8,128)(2,1)S(1)}) custom-call(bf16[272,512]{1,0:T(8,128)(2,1)S(1)} %get-tuple-element.13.own, bf16[144,512]{1,0:T(8,128)(2,1)S(1)} %collective-permute-done.prev_a, bf16[128,512]{1,0:T(8,128)(2,1)S(1)} %collective-permute-done.1.prev_b, ...), custom_call_target="tpu_custom_call" | custom-call | flops 67108864 | bytes 1048576 | tf_op jit(solution)/shard_map/near_kernel/pallas_call | solution.py:202
  13.5 0.1 collective-permute-start.4
  13.6 0.6 %collective-permute-done.5.back_a = bf16[144,512]{1,0:T(8,128)(2,1)S(1)} collective-permute-done((bf16[144,512]{1,0:T(8,128)(2,1)S(1)}, bf16[144,512]{1,0:T(8,128)(2,1)S(1)}, u32[]{:S(2)}, u32[]{:S(2)}) %collective-permute-start.5) | collective-permute-done | bytes 147488 | tf_op jit(solution)/shard_map/ppermute | solution.py:221
  14.2 2.1 %collective-permute-done.6.ahead_a = bf16[144,512]{1,0:T(8,128)(2,1)S(1)} collective-permute-done((bf16[144,512]{1,0:T(8,128)(2,1)S(1)}, bf16[144,512]{1,0:T(8,128)(2,1)S(1)}, u32[]{:S(2)}, u32[]{:S(2)}) %collective-permute-start.6) | collective-permute-done | bytes 147488 | tf_op jit(solution)/shard_map/ppermute | solution.py:221
  16.3 0.5 %far_first_kernel.1.refs_0_ = f32[1,256]{1,0:T(1,128)S(1)} custom-call(bf16[272,512]{1,0:T(8,128)(2,1)S(1)} %get-tuple-element.13.own, bf16[144,512]{1,0:T(8,128)(2,1)S(1)} %collective-permute-done.prev_a, bf16[128,512]{1,0:T(8,128)(2,1)S(1)} %collective-permute-done.1.prev_b, bf16[144,512]{1,0:T(8,128)(2,1)S(1)} %collective-permute-done.2.succ_a, ...), custom_call_target="tpu_custom_call" | custom-call | flops 335544320 | bytes 1048576 | tf_op jit(solution)/shard_map/far_first_kernel/pallas_call | solution.py:202
  16.8 0.1 collective-permute-done.7.back_b
  16.9 1.9 %collective-permute-done.8.ahead_b = bf16[128,512]{1,0:T(8,128)(2,1)S(1)} collective-permute-done((bf16[128,512]{1,0:T(8,128)(2,1)S(1)}, bf16[128,512]{1,0:T(8,128)(2,1)S(1)}, u32[]{:S(2)}, u32[]{:S(2)}) %collective-permute-start.8) | collective-permute-done | bytes 131104 | tf_op jit(solution)/shard_map/ppermute | solution.py:221
  18.8 0.6 %far_second_kernel.1 = (f32[1,256]{1,0:T(1,128)S(1)}, f32[1,256]{1,0:T(1,128)S(1)}) custom-call(bf16[272,512]{1,0:T(8,128)(2,1)S(1)} %get-tuple-element.13.own, bf16[144,512]{1,0:T(8,128)(2,1)S(1)} %collective-permute-done.prev_a, bf16[128,512]{1,0:T(8,128)(2,1)S(1)} %collective-permute-done.1.prev_b, bf16[144,512]{1,0:T(8,128)(2,1)S(1)} %collective-permute-done.2.succ_a, ...), custom_call_target="tpu_custom_call" | custom-call | flops 13421772800 | bytes 1048576 | tf_op jit(solution)/shard_map/far_second_kernel/pallas_call | solution.py:202
  19.4 0.0 collective-permute-done.4.others
  19.4 0.3 %far_other_kernel.1 = (f32[1,256]{1,0:T(1,128)S(1)}, f32[1,256]{1,0:T(1,128)S(1)}) custom-call(bf16[3,272,512]{2,1,0:T(8,128)(2,1)S(1)} %collective-permute-done.4.others, bf16[144,512]{1,0:T(8,128)(2,1)S(1)} %collective-permute-done.5.back_a, bf16[144,512]{1,0:T(8,128)(2,1)S(1)} %collective-permute-done.6.ahead_a, ...), custom_call_target="tpu_custom_call" | custom-call | flops 134217728 | bytes 1048576 | tf_op jit(solution)/shard_map/far_other_kernel/pallas_call | solution.py:202
  19.8 1.5 %collective-permute-start.9 = (f32[1,256]{1,0:T(1,128)S(1)}, f32[1,256]{1,0:T(1,128)S(1)}, u32[]{:S(2)}, u32[]{:S(2)}) collective-permute-start(f32[1,256]{1,0:T(1,128)S(1)} %get-tuple-element.19), channel_id=1, source_target_pairs={{0,6},{1,7},{4,3},{5,2},{8,1},{9,0},{12,4},{13,5},{14,8},{15,9},{1... | collective-permute-start | bytes 3080 | tf_op jit(solution)/shard_map/ppermute | solution.py:221
  21.2 1.6 %collective-permute-start.10 = (f32[1,256]{1,0:T(1,128)S(1)}, f32[1,256]{1,0:T(1,128)S(1)}, u32[]{:S(2)}, u32[]{:S(2)}) collective-permute-start(f32[1,256]{1,0:T(1,128)S(1)} %get-tuple-element.20), channel_id=1, source_target_pairs={{0,8},{1,9},{4,13},{5,12},{8,15},{9,14},{12,11},{13,10},{14,7},{15... | collective-permute-start | bytes 3080 | tf_op jit(solution)/shard_map/ppermute | solution.py:221
  22.8 0.6 %own_kernel.1 = f32[1,256]{1,0:T(1,128)S(1)} custom-call(bf16[272,512]{1,0:T(8,128)(2,1)S(1)} %get-tuple-element.13.own, bf16[3,272,512]{2,1,0:T(8,128)(2,1)S(1)} %collective-permute-done.4.others, bf16[144,512]{1,0:T(8,128)(2,1)S(1)} %collective-permute-done.5.back_a, bf16[144,512]{1,0:T(8,128)(2,1)S(1)} %collective-permute-done.6.ahead_a, ...), custom_call_target="tpu_custom_call" | custom-call | flops 335544320 | bytes 1048576 | tf_op jit(solution)/shard_map/own_kernel/pallas_call | solution.py:202
  23.3 0.4 %collective-permute-done.9 = f32[1,256]{1,0:T(1,128)S(1)} collective-permute-done((f32[1,256]{1,0:T(1,128)S(1)}, f32[1,256]{1,0:T(1,128)S(1)}, u32[]{:S(2)}, u32[]{:S(2)}) %collective-permute-start.9) | collective-permute-done | bytes 1056 | tf_op jit(solution)/shard_map/ppermute | solution.py:221
  23.7 1.4 %collective-permute-done.10 = f32[1,256]{1,0:T(1,128)S(1)} collective-permute-done((f32[1,256]{1,0:T(1,128)S(1)}, f32[1,256]{1,0:T(1,128)S(1)}, u32[]{:S(2)}, u32[]{:S(2)}) %collective-permute-start.10) | collective-permute-done | bytes 1056 | tf_op jit(solution)/shard_map/ppermute | solution.py:221
  25.1 0.6 %maximum_maximum_fusion = f32[1,256]{1,0:T(1,128)} fusion(f32[1,256]{1,0:T(1,128)S(1)} %own_kernel.1, f32[1,256]{1,0:T(1,128)S(1)} %collective-permute-done.9, f32[1,256]{1,0:T(1,128)S(1)} %collective-permute-done.10), kind=kLoop, calls=%fused_computation | loop fusion | flops 512 | bytes 4096 | tf_op jit(solution)/shard_map/max | solution.py:277
Async XLA Ops:
  1.1 6.8 %collective-permute-start = (bf16[144,512]{1,0:T(8,128)(2,1)S(1)}, bf16[144,512]{1,0:T(8,128)(2,1)S(1)}, u32[]{:S(2)}, u32[]{:S(2)}) collective-permute-start(bf16[144,512]{1,0:T(8,128)(2,1)S(1)} %pack_first.1.first), channel_id=1, source_target_pairs={{0,5},{1,4},{4,8},{5,9},{8,12},{9,13},{12,14},{13,15},{14,10},{15,... | collective-permute-start | bytes 442376 | tf_op jit(solution)/shard_map/ppermute | solution.py:221
  3.6 6.7 %collective-permute-start.2 = (bf16[144,512]{1,0:T(8,128)(2,1)S(1)}, bf16[144,512]{1,0:T(8,128)(2,1)S(1)}, u32[]{:S(2)}, u32[]{:S(2)}) collective-permute-start(bf16[144,512]{1,0:T(8,128)(2,1)S(1)} %pack_first.1.first), channel_id=1, source_target_pairs={{0,3},{1,2},{4,0},{5,1},{8,4},{9,5},{12,9},{13,8},{14,13},{15,12},... | collective-permute-start | bytes 442376 | tf_op jit(solution)/shard_map/ppermute | solution.py:221
  4.6 6.0 %collective-permute-start.1 = (bf16[128,512]{1,0:T(8,128)(2,1)S(1)}, bf16[128,512]{1,0:T(8,128)(2,1)S(1)}, u32[]{:S(2)}, u32[]{:S(2)}) collective-permute-start(bf16[128,512]{1,0:T(8,128)(2,1)S(1)} %get-tuple-element.14), channel_id=1, source_target_pairs={{0,5},{1,4},{4,8},{5,9},{8,12},{9,13},{12,14},{13,15},{14,10},{15,... | collective-permute-start | bytes 393224 | tf_op jit(solution)/shard_map/ppermute | solution.py:221
  6.7 6.4 %collective-permute-start.3 = (bf16[128,512]{1,0:T(8,128)(2,1)S(1)}, bf16[128,512]{1,0:T(8,128)(2,1)S(1)}, u32[]{:S(2)}, u32[]{:S(2)}) collective-permute-start(bf16[128,512]{1,0:T(8,128)(2,1)S(1)} %get-tuple-element.14), channel_id=1, source_target_pairs={{0,3},{1,2},{4,0},{5,1},{8,4},{9,5},{12,9},{13,8},{14,13},{15,12},... | collective-permute-start | bytes 393224 | tf_op jit(solution)/shard_map/ppermute | solution.py:221
  7.8 6.4 %collective-permute-start.5 = (bf16[144,512]{1,0:T(8,128)(2,1)S(1)}, bf16[144,512]{1,0:T(8,128)(2,1)S(1)}, u32[]{:S(2)}, u32[]{:S(2)}) collective-permute-start(bf16[144,512]{1,0:T(8,128)(2,1)S(1)} %collective-permute-done.prev_a), channel_id=1, source_target_pairs={{0,4},{1,5},{4,8},{5,9},{8,12},{9,13},{12,14},{13,15},{14,10},{15,... | collective-permute-start | bytes 442376 | tf_op jit(solution)/shard_map/ppermute | solution.py:221
  10.3 6.0 %collective-permute-start.6 = (bf16[144,512]{1,0:T(8,128)(2,1)S(1)}, bf16[144,512]{1,0:T(8,128)(2,1)S(1)}, u32[]{:S(2)}, u32[]{:S(2)}) collective-permute-start(bf16[144,512]{1,0:T(8,128)(2,1)S(1)} %collective-permute-done.2.succ_a), channel_id=1, source_target_pairs={{0,2},{1,3},{4,0},{5,1},{8,4},{9,5},{12,8},{13,9},{14,12},{15,13},... | collective-permute-start | bytes 442376 | tf_op jit(solution)/shard_map/ppermute | solution.py:221
  10.7 6.3 %collective-permute-start.7 = (bf16[128,512]{1,0:T(8,128)(2,1)S(1)}, bf16[128,512]{1,0:T(8,128)(2,1)S(1)}, u32[]{:S(2)}, u32[]{:S(2)}) collective-permute-start(bf16[128,512]{1,0:T(8,128)(2,1)S(1)} %collective-permute-done.1.prev_b), channel_id=1, source_target_pairs={{0,4},{1,5},{4,8},{5,9},{8,12},{9,13},{12,14},{13,15},{14,10},{15,... | collective-permute-start | bytes 393224 | tf_op jit(solution)/shard_map/ppermute | solution.py:221
  13.1 5.7 %collective-permute-start.8 = (bf16[128,512]{1,0:T(8,128)(2,1)S(1)}, bf16[128,512]{1,0:T(8,128)(2,1)S(1)}, u32[]{:S(2)}, u32[]{:S(2)}) collective-permute-start(bf16[128,512]{1,0:T(8,128)(2,1)S(1)} %collective-permute-done.3.succ_b), channel_id=1, source_target_pairs={{0,2},{1,3},{4,0},{5,1},{8,4},{9,5},{12,8},{13,9},{14,12},{15,13},... | collective-permute-start | bytes 393224 | tf_op jit(solution)/shard_map/ppermute | solution.py:221
  13.5 5.9 %collective-permute-start.4 = (bf16[3,272,512]{2,1,0:T(8,128)(2,1)S(1)}, bf16[3,272,512]{2,1,0:T(8,128)(2,1)S(1)}, u32[]{:S(2)}, u32[]{:S(2)}) collective-permute-start(bf16[3,272,512]{2,1,0:T(8,128)(2,1)S(1)} %get-tuple-element.15), channel_id=1, source_target_pairs={{0,1},{1,0},{4,5},{5,4},{8,9},{9,8},{12,13},{13,12},{14,15},{15,14... | collective-permute-start | bytes 2506760 | tf_op jit(solution)/shard_map/ppermute | solution.py:221
  19.8 4.0 %collective-permute-start.9 = (f32[1,256]{1,0:T(1,128)S(1)}, f32[1,256]{1,0:T(1,128)S(1)}, u32[]{:S(2)}, u32[]{:S(2)}) collective-permute-start(f32[1,256]{1,0:T(1,128)S(1)} %get-tuple-element.19), channel_id=1, source_target_pairs={{0,6},{1,7},{4,3},{5,2},{8,1},{9,0},{12,4},{13,5},{14,8},{15,9},{1... | collective-permute-start | bytes 3080 | tf_op jit(solution)/shard_map/ppermute | solution.py:221
  21.2 3.9 %collective-permute-start.10 = (f32[1,256]{1,0:T(1,128)S(1)}, f32[1,256]{1,0:T(1,128)S(1)}, u32[]{:S(2)}, u32[]{:S(2)}) collective-permute-start(f32[1,256]{1,0:T(1,128)S(1)} %get-tuple-element.20), channel_id=1, source_target_pairs={{0,8},{1,9},{4,13},{5,12},{8,15},{9,14},{12,11},{13,10},{14,7},{15... | collective-permute-start | bytes 3080 | tf_op jit(solution)/shard_map/ppermute | solution.py:221

commit v6 on v0

--- a/solution.py
+++ b/solution.py
@@ -1,12 +1,184 @@
 import jax
 import jax.numpy as jnp
 from jax import lax
+from jax.experimental import pallas as pl
+from jax.experimental.pallas import tpu as pltpu
 from jax.sharding import PartitionSpec as P
 
 CLU_OWN = 16
 
 
 EPS = 1e-06
+
+GROUP = ("gx", "gy", "gz")
+
+
+def normalised(block):
+    vecs = block.astype(jnp.float32)
+    return (vecs * lax.rsqrt(jnp.sum(vecs * vecs, axis=1, keepdims=True) + EPS)).astype(
+        jnp.bfloat16
+    )
+
+
+LABEL_ROWS = 16
+VMEM_BYTES = 32 * 2**20
+OWN_COST = 100
+FIRST_COST = 5
+SECOND_COST = 5
+
+
+def pack_kernel(embeds, label, packed, raw, line, sems):
+    rows, width = embeds.shape
+    half = rows // 2
+    copies = [pltpu.make_async_copy(label, line, sems.at[0])]
+    for i in range(2):
+        part = pl.ds(i * half, half)
+        copies.append(pltpu.make_async_copy(embeds.at[part], raw.at[part], sems.at[1 + i]))
+    for copy in copies:
+        copy.start()
+    copies[0].wait()
+    lines = jnp.broadcast_to(line[...].astype(jnp.float32), (LABEL_ROWS, rows))
+    packed[rows:, :rows] = lines.astype(jnp.bfloat16)
+    packed[rows:, rows:] = jnp.zeros((LABEL_ROWS, width - rows), jnp.bfloat16)
+    for i in range(2):
+        part = pl.ds(i * half, half)
+        copies[1 + i].wait()
+        packed[part, :] = normalised(raw[part, :])
+
+
+class Block:
+    def __init__(self, unit, label):
+        self.unit = unit
+        self.label = label
+        self.rows = unit.shape[0]
+        self.along_rows = None
+
+    def column(self):
+        if self.along_rows is None:
+            self.along_rows = jnp.transpose(jnp.broadcast_to(self.label, (128, self.rows)))
+        return self.along_rows
+
+
+def unpacked(ref):
+    rows = ref.shape[0] - LABEL_ROWS
+    return Block(ref[:rows, :], ref[rows:, :rows].astype(jnp.float32)[:1])
+
+
+def best_of(queries, *all_keys):
+    best = None
+    for keys in all_keys:
+        sims = lax.dot_general(
+            keys.unit, queries.unit, (((1,), (1,)), ((), ())), preferred_element_type=jnp.float32
+        )
+        pieces = []
+        for start in range(0, queries.rows, 128):
+            keep = keys.column() == queries.label[:, start : start + 128]
+            if keys is queries:
+                row = lax.broadcasted_iota(jnp.int32, keep.shape, 0)
+                column = lax.broadcasted_iota(jnp.int32, keep.shape, 1) + start
+                keep = keep & (row != column)
+            found = jnp.where(keep, sims[:, start : start + 128], -1.0)
+            pieces.append(jnp.max(found, axis=0, keepdims=True))
+        found = jnp.concatenate(pieces, axis=1)
+        best = found if best is None else jnp.maximum(best, found)
+    return best
+
+
+def rows_kernel(rows, *refs):
+    *keys, best = refs
+    best[...] = best_of(unpacked(rows), *(unpacked(key) for key in keys))
+
+
+def last_kernel(rows, *refs):
+    *keys, _, best = refs
+    best[...] = best_of(unpacked(rows), *(unpacked(key) for key in keys))
+
+
+def own_kernel(rows, *refs):
+    *keys, best = refs
+    rows = unpacked(rows)
+    best[...] = best_of(rows, rows, *(unpacked(key) for key in keys))
+
+
+def ring_perms(size_x, size_y, size_z):
+    chips = size_x * size_y
+
+    def device(place, core):
+        place = place % chips
+        x, y = (place, 0) if place < size_x else (chips - 1 - place, 1)
+        return (x * size_y + y) * size_z + core
+
+    def perm(to):
+        return [
+            (device(p, k), device(*to(p, k))) for p in range(chips) for k in range(size_z)
+        ]
+
+    step = (1, -1)
+    return {
+        "sibling": perm(lambda p, k: (p, 1 - k)),
+        "lane": perm(lambda p, k: (p + step[k], k)),
+        "other_lane": perm(lambda p, k: (p + step[1 - k], 1 - k)),
+        "home": perm(lambda p, k: (p - 2 * step[k], k)),
+        "home_other": perm(lambda p, k: (p - 2 * step[k], 1 - k)),
+    }
+
+
+def kernel_call(kernel, blocks, cost, name):
+    vmem = pl.BlockSpec(memory_space=pltpu.VMEM)
+    rows = blocks[0].shape[0] - LABEL_ROWS
+    return pl.pallas_call(
+        kernel,
+        out_shape=jax.ShapeDtypeStruct((1, rows), jnp.float32),
+        in_specs=[vmem] * len(blocks),
+        out_specs=vmem,
+        compiler_params=pltpu.CompilerParams(vmem_limit_bytes=VMEM_BYTES),
+        cost_estimate=pl.CostEstimate(
+            flops=cost * 2**26, bytes_accessed=2**20, transcendentals=0
+        ),
+        name=name,
+    )(*blocks)
+
+
+def on_ring(embeds, cluster):
+    rows, width = embeds.shape
+    perms = ring_perms(*(lax.axis_size(a) for a in GROUP))
+
+    def send(value, name):
+        return lax.ppermute(value, GROUP, perms[name])
+
+    anywhere = pl.BlockSpec(memory_space=pl.ANY)
+    own = pl.pallas_call(
+        pack_kernel,
+        out_shape=jax.ShapeDtypeStruct((rows + LABEL_ROWS, width), jnp.bfloat16),
+        in_specs=[anywhere] * 2,
+        out_specs=pl.BlockSpec(memory_space=pltpu.VMEM),
+        scratch_shapes=[
+            pltpu.VMEM((rows, width), jnp.bfloat16),
+            pltpu.VMEM((1, rows), jnp.int32),
+            pltpu.SemaphoreType.DMA((3,)),
+        ],
+        compiler_params=pltpu.CompilerParams(vmem_limit_bytes=VMEM_BYTES),
+        name="pack",
+    )(
+        pltpu.with_memory_space_constraint(embeds, pltpu.HBM),
+        pltpu.with_memory_space_constraint(cluster.reshape(1, rows), pltpu.HBM),
+    )
+    one_first, one_second = send(own, "lane"), send(own, "other_lane")
+    two_first, two_second = send(one_first, "lane"), send(one_second, "lane")
+    other = send(own, "sibling")
+    beyond = [send(block, "sibling") for block in (one_first, one_second, two_first)]
+    chip = [own, other]
+    found_first = kernel_call(rows_kernel, [two_first, *chip, *beyond], FIRST_COST, "first")
+    mine = kernel_call(
+        own_kernel, [own, other, one_first, one_second, *beyond[:2]], OWN_COST, "own"
+    )
+    found_second = kernel_call(
+        last_kernel, [two_second, *chip, *beyond, mine], SECOND_COST, "second"
+    )
+    best = jnp.maximum(
+        mine, jnp.maximum(send(found_first, "home"), send(found_second, "home_other"))
+    )
+    return best.reshape(rows)
 
 
 def masked_sims(queries, query_labels, query_ids, keys, key_labels, key_ids):
@@ -19,17 +191,14 @@
     return jnp.where(keep, sims, -1.0)
 
 
-def on_device(embeds, cluster):
+def by_owner(embeds, cluster):
     rows, width = embeds.shape
     size_x = lax.axis_size("gx")
     size_y = lax.axis_size("gy")
     owners = size_x * size_y
     cap = 2 * rows // owners
     total = owners * cap
-    vecs = embeds.astype(jnp.float32)
-    unit = (vecs * lax.rsqrt(jnp.sum(vecs * vecs, axis=1, keepdims=True) + EPS)).astype(
-        jnp.bfloat16
-    )
+    unit = normalised(embeds)
     target = cluster // CLU_OWN
     onehot = (target[:, None] == jnp.arange(owners, dtype=jnp.int32)[None, :]).astype(jnp.int32)
     before = jnp.cumsum(onehot, axis=0) - onehot
@@ -67,9 +236,11 @@
 
 
 def solution(mesh):
+    shape = mesh.shape
+    ring = shape["gx"] * shape["gy"] == 8 and shape["gy"] == 2 and shape["gz"] == 2
     placed = (P(("parts", "gx", "gy", "gz"), None), P(("parts", "gx", "gy", "gz")))
     return jax.shard_map(
-        on_device,
+        on_ring if ring else by_owner,
         mesh=mesh,
         in_specs=placed,
         out_specs=P(("parts", "gx", "gy", "gz")),

time: 73.8 us -> 28.7 us (0.39)
  blocking collectives: 23.5 us -> 0 us
  between operations: 13.5 us -> 0.05 us
  local copies, waits for them, and re-layouts: 6.87 us -> 0 us
  other arithmetic: 7.35 us -> 0.57 us
  starting transfers between devices: 6.92 us -> 11.5 us
  Pallas kernels: 0 us -> 2.89 us
  matrix products: 2.44 us -> 0 us
    all_to_all x1 -> x0, blocking collectives: 21.7 us -> none  [on_device(): lax.all_to_all(outgoing.reshape(owners, cap, width), ('gx', 'gy'), split_...]
    ppermute x0 -> x10, waiting for transfers between devices: none -> 13.5 us  [send(): return lax.ppermute(value, GROUP, perms[name])]
    all_to_all x2 -> x0, waiting for transfers between devices: 12.8 us -> none  [the longest x1 6.45 us: on_device(): lax.all_to_all(out_labels.reshape(owners, cap), ('gx', 'gy'), split_axis=...]
    ppermute x0 -> x10, starting transfers between devices: none -> 11.5 us  [send(): return lax.ppermute(value, GROUP, perms[name])]
    all_to_all x2 -> x0, starting transfers between devices: 6.92 us -> none  [the longest x1 3.59 us: on_device(): lax.all_to_all(out_labels.reshape(owners, cap), ('gx', 'gy'), split_axis=...]
    pallas_call x0 -> x4, Pallas kernels: none -> 2.89 us  [the longest x3 1.72 us: kernel_call(): pl.pallas_call(kernel, out_shape=jax.ShapeDtypeStruct((1, rows), jnp.floa...]
    gather x1 -> x0, local copies, waits for them, and re-layouts: 2.5 us -> none  [on_device(): return back.reshape(total)[place]]
    dot_general x1 -> x0, matrix products: 2.44 us -> none  [masked_sims(): jnp.einsum('qd,kd->qk', queries, keys, preferred_element_type=jnp.float32)]
  transfers between devices with their start and end apart: 3 -> 10, of which waited for: 2 -> 5; matrix products, arithmetic and copies ran while one was open for 4% -> 0% of each run, Pallas kernels for 0% -> 6%
where the time goes in v6:
time: 28.7 us; the launch traced here: 28.5 us
  waiting for transfers between devices  13.5 us (47%)
  starting transfers between devices  11.5 us (40%)
  Pallas kernels  2.89 us (10%)
  other arithmetic  0.57 us (2%)
    ppermute x10, waiting for transfers between devices, send(): return lax.ppermute(value, GROUP, perms[name])  13.5 us
    ppermute x10, starting transfers between devices, send(): return lax.ppermute(value, GROUP, perms[name])  11.5 us
    pallas_call x3, Pallas kernels, kernel_call(): pl.pallas_call(kernel, out_shape=jax.ShapeDtypeStruct((1, rows), jnp.floa...  1.72 us
    pallas_call x1, Pallas kernels, on_ring(): pl.pallas_call(pack_kernel, out_shape=jax.ShapeDtypeStruct((rows + LABEL_...  1.17 us
  transfers between devices with their start and end apart: 10, of which 5 were waited for; matrix products, arithmetic and copies ran while one was open for 0% of the time, Pallas kernels for 6%

profile of v6, /device:TPU:0, one launch (start us, length us, event | category | flops | bytes accessed | tf_op | source)
XLA Modules:
  0.0 28.5 jit_solution(14169157394947193384)
XLA Ops:
  0.0 1.2 %pack.1.rows.refs_0_ = bf16[272,512]{1,0:T(8,128)(2,1)S(1)} custom-call(bf16[256,512]{1,0:T(8,128)(2,1)} %embeds.1, s32[1,256]{1,0:T(1,128)} %bitcast.2), custom_call_target="tpu_custom_call" | custom-call | tf_op jit(solution)/shard_map/pack/pallas_call | solution.py:150
  1.2 3.1 %collective-permute-start.1 = (bf16[272,512]{1,0:T(8,128)(2,1)S(1)}, bf16[272,512]{1,0:T(8,128)(2,1)S(1)}, u32[]{:S(2)}, u32[]{:S(2)}) collective-permute-start(bf16[272,512]{1,0:T(8,128)(2,1)S(1)} %pack.1.rows.refs_0_), channel_id=1, source_target_pairs={{0,4},{1,3},{4,8},{5,1},{8,12},{9,5},{12,14},{13,9},{14,10},{15,13... | collective-permute-start | bytes 835592 | tf_op jit(solution)/shard_map/ppermute | solution.py:147
  4.3 0.7 %collective-permute-start.2 = (bf16[272,512]{1,0:T(8,128)(2,1)S(1)}, bf16[272,512]{1,0:T(8,128)(2,1)S(1)}, u32[]{:S(2)}, u32[]{:S(2)}) collective-permute-start(bf16[272,512]{1,0:T(8,128)(2,1)S(1)} %pack.1.rows.refs_0_), channel_id=1, source_target_pairs={{0,3},{1,4},{4,1},{5,8},{8,5},{9,12},{12,9},{13,14},{14,13},{15,10... | collective-permute-start | bytes 835592 | tf_op jit(solution)/shard_map/ppermute | solution.py:147
  4.9 5.4 %collective-permute-done.1.refs_1_ = bf16[272,512]{1,0:T(8,128)(2,1)S(1)} collective-permute-done((bf16[272,512]{1,0:T(8,128)(2,1)S(1)}, bf16[272,512]{1,0:T(8,128)(2,1)S(1)}, u32[]{:S(2)}, u32[]{:S(2)}) %collective-permute-start.1) | collective-permute-done | bytes 278560 | tf_op jit(solution)/shard_map/ppermute | solution.py:147
  10.3 2.5 %collective-permute-start.5 = (bf16[272,512]{1,0:T(8,128)(2,1)S(1)}, bf16[272,512]{1,0:T(8,128)(2,1)S(1)}, u32[]{:S(2)}, u32[]{:S(2)}) collective-permute-start(bf16[272,512]{1,0:T(8,128)(2,1)S(1)} %collective-permute-done.1.refs_1_), channel_id=1, source_target_pairs={{0,4},{1,3},{4,8},{5,1},{8,12},{9,5},{12,14},{13,9},{14,10},{15,13... | collective-permute-start | bytes 835592 | tf_op jit(solution)/shard_map/ppermute | solution.py:147
  12.8 0.0 collective-permute-start
  12.8 0.5 %collective-permute-start.3 = (bf16[272,512]{1,0:T(8,128)(2,1)S(1)}, bf16[272,512]{1,0:T(8,128)(2,1)S(1)}, u32[]{:S(2)}, u32[]{:S(2)}) collective-permute-start(bf16[272,512]{1,0:T(8,128)(2,1)S(1)} %collective-permute-done.1.refs_1_), channel_id=1, source_target_pairs={{0,1},{1,0},{4,5},{5,4},{8,9},{9,8},{12,13},{13,12},{14,15},{15,14... | collective-permute-start | bytes 835592 | tf_op jit(solution)/shard_map/ppermute | solution.py:147
  13.3 0.0 collective-permute-done.2.refs_2_
  13.3 0.0 collective-permute-start.4
  13.3 1.6 %collective-permute-start.8 = (bf16[272,512]{1,0:T(8,128)(2,1)S(1)}, bf16[272,512]{1,0:T(8,128)(2,1)S(1)}, u32[]{:S(2)}, u32[]{:S(2)}) collective-permute-start(bf16[272,512]{1,0:T(8,128)(2,1)S(1)} %collective-permute-done.2.refs_2_), channel_id=1, source_target_pairs={{0,4},{1,3},{4,8},{5,1},{8,12},{9,5},{12,14},{13,9},{14,10},{15,13... | collective-permute-start | bytes 835592 | tf_op jit(solution)/shard_map/ppermute | solution.py:147
  14.9 3.3 %collective-permute-done.5.rows = bf16[272,512]{1,0:T(8,128)(2,1)S(1)} collective-permute-done((bf16[272,512]{1,0:T(8,128)(2,1)S(1)}, bf16[272,512]{1,0:T(8,128)(2,1)S(1)}, u32[]{:S(2)}, u32[]{:S(2)}) %collective-permute-start.5) | collective-permute-done | bytes 278560 | tf_op jit(solution)/shard_map/ppermute | solution.py:147
  18.2 0.0 collective-permute-start.6
  18.2 0.0 collective-permute-done.refs_0_.refs_1_
  18.2 0.0 collective-permute-done.3.refs_3_.refs_2_
  18.2 0.0 collective-permute-done.4.refs_4_.refs_3_
  18.2 0.6 %own.1.refs_5_ = f32[1,256]{1,0:T(1,128)S(1)} custom-call(bf16[272,512]{1,0:T(8,128)(2,1)S(1)} %pack.1.rows.refs_0_, bf16[272,512]{1,0:T(8,128)(2,1)S(1)} %collective-permute-done.refs_0_.refs_1_, bf16[272,512]{1,0:T(8,128)(2,1)S(1)} %collective-permute-done.1.refs_1_, bf16[272,512]{1,0:T(8,128)(2,1)S(1)} %collective-permute-done.2.refs_2_, ...), custom_call_target="tpu_custom_call" | custom-call | flops 6710886400 | bytes 1048576 | tf_op jit(solution)/shard_map/own/pallas_call | solution.py:129
  18.9 0.9 %collective-permute-done.6.refs_4_ = bf16[272,512]{1,0:T(8,128)(2,1)S(1)} collective-permute-done((bf16[272,512]{1,0:T(8,128)(2,1)S(1)}, bf16[272,512]{1,0:T(8,128)(2,1)S(1)}, u32[]{:S(2)}, u32[]{:S(2)}) %collective-permute-start.6) | collective-permute-done | bytes 278560 | tf_op jit(solution)/shard_map/ppermute | solution.py:147
  19.8 0.5 %first.1 = f32[1,256]{1,0:T(1,128)S(1)} custom-call(bf16[272,512]{1,0:T(8,128)(2,1)S(1)} %collective-permute-done.5.rows, bf16[272,512]{1,0:T(8,128)(2,1)S(1)} %pack.1.rows.refs_0_, bf16[272,512]{1,0:T(8,128)(2,1)S(1)} %collective-permute-done.refs_0_.refs_1_, bf16[272,512]{1,0:T(8,128)(2,1)S(1)} %collective-permute-done.3.refs_3_.refs_2_, ...), custom_call_target="tpu_custom_call" | custom-call | flops 335544320 | bytes 1048576 | tf_op jit(solution)/shard_map/first/pallas_call | solution.py:129
  20.3 3.1 %collective-permute-start.7 = (f32[1,256]{1,0:T(1,128)S(1)}, f32[1,256]{1,0:T(1,128)S(1)}, u32[]{:S(2)}, u32[]{:S(2)}) collective-permute-start(f32[1,256]{1,0:T(1,128)S(1)} %first.1), channel_id=1, source_target_pairs={{0,6},{1,9},{4,2},{5,13},{8,0},{9,15},{12,4},{13,11},{14,8},{15,7}... | collective-permute-start | bytes 3080 | tf_op jit(solution)/shard_map/ppermute | solution.py:147
  23.4 0.0 collective-permute-done.8.rows
  23.4 0.6 %second.1 = f32[1,256]{1,0:T(1,128)S(1)} custom-call(bf16[272,512]{1,0:T(8,128)(2,1)S(1)} %collective-permute-done.8.rows, bf16[272,512]{1,0:T(8,128)(2,1)S(1)} %pack.1.rows.refs_0_, bf16[272,512]{1,0:T(8,128)(2,1)S(1)} %collective-permute-done.refs_0_.refs_1_, bf16[272,512]{1,0:T(8,128)(2,1)S(1)} %collective-permute-done.3.refs_3_.refs_2_, ...), custom_call_target="tpu_custom_call" | custom-call | flops 335544320 | bytes 1048576 | tf_op jit(solution)/shard_map/second/pallas_call | solution.py:129
  24.0 0.1 collective-permute-start.9
  24.1 0.8 %collective-permute-done.7 = f32[1,256]{1,0:T(1,128)S(1)} collective-permute-done((f32[1,256]{1,0:T(1,128)S(1)}, f32[1,256]{1,0:T(1,128)S(1)}, u32[]{:S(2)}, u32[]{:S(2)}) %collective-permute-start.7) | collective-permute-done | bytes 1056 | tf_op jit(solution)/shard_map/ppermute | solution.py:147
  24.9 3.1 %collective-permute-done.9 = f32[1,256]{1,0:T(1,128)S(1)} collective-permute-done((f32[1,256]{1,0:T(1,128)S(1)}, f32[1,256]{1,0:T(1,128)S(1)}, u32[]{:S(2)}, u32[]{:S(2)}) %collective-permute-start.9) | collective-permute-done | bytes 1056 | tf_op jit(solution)/shard_map/ppermute | solution.py:147
  28.0 0.6 %maximum_maximum_fusion = f32[1,256]{1,0:T(1,128)} fusion(f32[1,256]{1,0:T(1,128)S(1)} %own.1.refs_5_, f32[1,256]{1,0:T(1,128)S(1)} %collective-permute-done.7, f32[1,256]{1,0:T(1,128)S(1)} %collective-permute-done.9), kind=kLoop, calls=%fused_computation | loop fusion | flops 512 | bytes 4096 | tf_op jit(solution)/shard_map/max | solution.py:178
Async XLA Ops:
  1.2 9.1 %collective-permute-start.1 = (bf16[272,512]{1,0:T(8,128)(2,1)S(1)}, bf16[272,512]{1,0:T(8,128)(2,1)S(1)}, u32[]{:S(2)}, u32[]{:S(2)}) collective-permute-start(bf16[272,512]{1,0:T(8,128)(2,1)S(1)} %pack.1.rows.refs_0_), channel_id=1, source_target_pairs={{0,4},{1,3},{4,8},{5,1},{8,12},{9,5},{12,14},{13,9},{14,10},{15,13... | collective-permute-start | bytes 835592 | tf_op jit(solution)/shard_map/ppermute | solution.py:147
  4.3 9.0 %collective-permute-start.2 = (bf16[272,512]{1,0:T(8,128)(2,1)S(1)}, bf16[272,512]{1,0:T(8,128)(2,1)S(1)}, u32[]{:S(2)}, u32[]{:S(2)}) collective-permute-start(bf16[272,512]{1,0:T(8,128)(2,1)S(1)} %pack.1.rows.refs_0_), channel_id=1, source_target_pairs={{0,3},{1,4},{4,1},{5,8},{8,5},{9,12},{12,9},{13,14},{14,13},{15,10... | collective-permute-start | bytes 835592 | tf_op jit(solution)/shard_map/ppermute | solution.py:147
  10.3 7.9 %collective-permute-start.5 = (bf16[272,512]{1,0:T(8,128)(2,1)S(1)}, bf16[272,512]{1,0:T(8,128)(2,1)S(1)}, u32[]{:S(2)}, u32[]{:S(2)}) collective-permute-start(bf16[272,512]{1,0:T(8,128)(2,1)S(1)} %collective-permute-done.1.refs_1_), channel_id=1, source_target_pairs={{0,4},{1,3},{4,8},{5,1},{8,12},{9,5},{12,14},{13,9},{14,10},{15,13... | collective-permute-start | bytes 835592 | tf_op jit(solution)/shard_map/ppermute | solution.py:147
  12.8 5.4 %collective-permute-start = (bf16[272,512]{1,0:T(8,128)(2,1)S(1)}, bf16[272,512]{1,0:T(8,128)(2,1)S(1)}, u32[]{:S(2)}, u32[]{:S(2)}) collective-permute-start(bf16[272,512]{1,0:T(8,128)(2,1)S(1)} %pack.1.rows.refs_0_), channel_id=1, source_target_pairs={{0,1},{1,0},{4,5},{5,4},{8,9},{9,8},{12,13},{13,12},{14,15},{15,14... | collective-permute-start | bytes 835592 | tf_op jit(solution)/shard_map/ppermute | solution.py:147
  12.8 5.4 %collective-permute-start.3 = (bf16[272,512]{1,0:T(8,128)(2,1)S(1)}, bf16[272,512]{1,0:T(8,128)(2,1)S(1)}, u32[]{:S(2)}, u32[]{:S(2)}) collective-permute-start(bf16[272,512]{1,0:T(8,128)(2,1)S(1)} %collective-permute-done.1.refs_1_), channel_id=1, source_target_pairs={{0,1},{1,0},{4,5},{5,4},{8,9},{9,8},{12,13},{13,12},{14,15},{15,14... | collective-permute-start | bytes 835592 | tf_op jit(solution)/shard_map/ppermute | solution.py:147
  13.3 4.9 %collective-permute-start.4 = (bf16[272,512]{1,0:T(8,128)(2,1)S(1)}, bf16[272,512]{1,0:T(8,128)(2,1)S(1)}, u32[]{:S(2)}, u32[]{:S(2)}) collective-permute-start(bf16[272,512]{1,0:T(8,128)(2,1)S(1)} %collective-permute-done.2.refs_2_), channel_id=1, source_target_pairs={{0,1},{1,0},{4,5},{5,4},{8,9},{9,8},{12,13},{13,12},{14,15},{15,14... | collective-permute-start | bytes 835592 | tf_op jit(solution)/shard_map/ppermute | solution.py:147
  13.3 10.1 %collective-permute-start.8 = (bf16[272,512]{1,0:T(8,128)(2,1)S(1)}, bf16[272,512]{1,0:T(8,128)(2,1)S(1)}, u32[]{:S(2)}, u32[]{:S(2)}) collective-permute-start(bf16[272,512]{1,0:T(8,128)(2,1)S(1)} %collective-permute-done.2.refs_2_), channel_id=1, source_target_pairs={{0,4},{1,3},{4,8},{5,1},{8,12},{9,5},{12,14},{13,9},{14,10},{15,13... | collective-permute-start | bytes 835592 | tf_op jit(solution)/shard_map/ppermute | solution.py:147
  18.2 1.6 %collective-permute-start.6 = (bf16[272,512]{1,0:T(8,128)(2,1)S(1)}, bf16[272,512]{1,0:T(8,128)(2,1)S(1)}, u32[]{:S(2)}, u32[]{:S(2)}) collective-permute-start(bf16[272,512]{1,0:T(8,128)(2,1)S(1)} %collective-permute-done.5.rows), channel_id=1, source_target_pairs={{0,1},{1,0},{4,5},{5,4},{8,9},{9,8},{12,13},{13,12},{14,15},{15,14... | collective-permute-start | bytes 835592 | tf_op jit(solution)/shard_map/ppermute | solution.py:147
  20.3 4.5 %collective-permute-start.7 = (f32[1,256]{1,0:T(1,128)S(1)}, f32[1,256]{1,0:T(1,128)S(1)}, u32[]{:S(2)}, u32[]{:S(2)}) collective-permute-start(f32[1,256]{1,0:T(1,128)S(1)} %first.1), channel_id=1, source_target_pairs={{0,6},{1,9},{4,2},{5,13},{8,0},{9,15},{12,4},{13,11},{14,8},{15,7}... | collective-permute-start | bytes 3080 | tf_op jit(solution)/shard_map/ppermute | solution.py:147
  24.0 4.0 %collective-permute-start.9 = (f32[1,256]{1,0:T(1,128)S(1)}, f32[1,256]{1,0:T(1,128)S(1)}, u32[]{:S(2)}, u32[]{:S(2)}) collective-permute-start(f32[1,256]{1,0:T(1,128)S(1)} %second.1), channel_id=1, source_target_pairs={{0,7},{1,8},{4,3},{5,12},{8,1},{9,14},{12,5},{13,10},{14,9},{15,6}... | collective-permute-start | bytes 3080 | tf_op jit(solution)/shard_map/ppermute | solution.py:147

commit v7 on v6

--- a/solution.py
+++ b/solution.py
@@ -21,7 +21,9 @@
 
 
 LABEL_ROWS = 16
+LANES = 128
 VMEM_BYTES = 32 * 2**20
+NEAR_COST = 2
 OWN_COST = 100
 FIRST_COST = 5
 SECOND_COST = 5
@@ -37,31 +39,33 @@
     for copy in copies:
         copy.start()
     copies[0].wait()
-    lines = jnp.broadcast_to(line[...].astype(jnp.float32), (LABEL_ROWS, rows))
-    packed[rows:, :rows] = lines.astype(jnp.bfloat16)
-    packed[rows:, rows:] = jnp.zeros((LABEL_ROWS, width - rows), jnp.bfloat16)
+    row = lax.broadcasted_iota(jnp.int32, (LABEL_ROWS, LANES), 0)
+    lines = jnp.zeros((LABEL_ROWS, LANES), jnp.float32)
+    for i in range(rows // LANES):
+        piece = line[:, i * LANES : (i + 1) * LANES].astype(jnp.float32)
+        lines = jnp.where(row == i, piece, lines)
+    packed[rows * width // LANES :, :] = lines.astype(jnp.bfloat16)
     for i in range(2):
-        part = pl.ds(i * half, half)
         copies[1 + i].wait()
-        packed[part, :] = normalised(raw[part, :])
+        unit = normalised(raw[pl.ds(i * half, half), :])
+        for j in range(width // LANES):
+            packed[pl.ds(j * rows + i * half, half), :] = unit[:, j * LANES : (j + 1) * LANES]
 
 
 class Block:
-    def __init__(self, unit, label):
-        self.unit = unit
-        self.label = label
-        self.rows = unit.shape[0]
+    def __init__(self, packed, rows):
+        labels_at = packed.shape[0] - LABEL_ROWS
+        columns = [packed[at : at + rows, :] for at in range(0, labels_at, rows)]
+        self.unit = jnp.concatenate(columns, axis=1)
+        lines = packed[labels_at:, :].astype(jnp.float32)
+        self.label = jnp.concatenate([lines[i : i + 1] for i in range(rows // LANES)], axis=1)
+        self.rows = rows
         self.along_rows = None
 
     def column(self):
         if self.along_rows is None:
-            self.along_rows = jnp.transpose(jnp.broadcast_to(self.label, (128, self.rows)))
+            self.along_rows = jnp.transpose(jnp.broadcast_to(self.label, (LANES, self.rows)))
         return self.along_rows
-
-
-def unpacked(ref):
-    rows = ref.shape[0] - LABEL_ROWS
-    return Block(ref[:rows, :], ref[rows:, :rows].astype(jnp.float32)[:1])
 
 
 def best_of(queries, *all_keys):
@@ -71,33 +75,40 @@
             keys.unit, queries.unit, (((1,), (1,)), ((), ())), preferred_element_type=jnp.float32
         )
         pieces = []
-        for start in range(0, queries.rows, 128):
-            keep = keys.column() == queries.label[:, start : start + 128]
+        for start in range(0, queries.rows, LANES):
+            keep = keys.column() == queries.label[:, start : start + LANES]
             if keys is queries:
                 row = lax.broadcasted_iota(jnp.int32, keep.shape, 0)
                 column = lax.broadcasted_iota(jnp.int32, keep.shape, 1) + start
                 keep = keep & (row != column)
-            found = jnp.where(keep, sims[:, start : start + 128], -1.0)
+            found = jnp.where(keep, sims[:, start : start + LANES], -1.0)
             pieces.append(jnp.max(found, axis=0, keepdims=True))
         found = jnp.concatenate(pieces, axis=1)
         best = found if best is None else jnp.maximum(best, found)
     return best
 
 
+def near_kernel(rows, other, best):
+    size = best.shape[1]
+    rows = Block(rows, size)
+    best[...] = best_of(rows, rows, Block(other, size))
+
+
 def rows_kernel(rows, *refs):
     *keys, best = refs
-    best[...] = best_of(unpacked(rows), *(unpacked(key) for key in keys))
+    size = best.shape[1]
+    best[...] = best_of(Block(rows, size), *(Block(key, size) for key in keys))
 
 
 def last_kernel(rows, *refs):
     *keys, _, best = refs
-    best[...] = best_of(unpacked(rows), *(unpacked(key) for key in keys))
-
-
-def own_kernel(rows, *refs):
-    *keys, best = refs
-    rows = unpacked(rows)
-    best[...] = best_of(rows, rows, *(unpacked(key) for key in keys))
+    rows_kernel(rows, *keys, best)
+
+
+def more_kernel(rows, *refs):
+    *keys, found, best = refs
+    rows_kernel(rows, *keys, best)
+    best[...] = jnp.maximum(best[...], found[...])
 
 
 def ring_perms(size_x, size_y, size_z):
@@ -123,9 +134,8 @@
     }
 
 
-def kernel_call(kernel, blocks, cost, name):
+def kernel_call(kernel, rows, blocks, cost, name):
     vmem = pl.BlockSpec(memory_space=pltpu.VMEM)
-    rows = blocks[0].shape[0] - LABEL_ROWS
     return pl.pallas_call(
         kernel,
         out_shape=jax.ShapeDtypeStruct((1, rows), jnp.float32),
@@ -149,7 +159,7 @@
     anywhere = pl.BlockSpec(memory_space=pl.ANY)
     own = pl.pallas_call(
         pack_kernel,
-        out_shape=jax.ShapeDtypeStruct((rows + LABEL_ROWS, width), jnp.bfloat16),
+        out_shape=jax.ShapeDtypeStruct((rows * width // LANES + LABEL_ROWS, LANES), jnp.bfloat16),
         in_specs=[anywhere] * 2,
         out_specs=pl.BlockSpec(memory_space=pltpu.VMEM),
         scratch_shapes=[
@@ -163,17 +173,21 @@
         pltpu.with_memory_space_constraint(embeds, pltpu.HBM),
         pltpu.with_memory_space_constraint(cluster.reshape(1, rows), pltpu.HBM),
     )
-    one_first, one_second = send(own, "lane"), send(own, "other_lane")
+    other = send(own, "sibling")
+    near = kernel_call(near_kernel, rows, [own, other], NEAR_COST, "near")
+    own_again, near = lax.optimization_barrier((own, near))
+    one_first, one_second = send(own, "lane"), send(own_again, "other_lane")
     two_first, two_second = send(one_first, "lane"), send(one_second, "lane")
-    other = send(own, "sibling")
     beyond = [send(block, "sibling") for block in (one_first, one_second, two_first)]
-    chip = [own, other]
-    found_first = kernel_call(rows_kernel, [two_first, *chip, *beyond], FIRST_COST, "first")
+    keys = [own, other, *beyond]
     mine = kernel_call(
-        own_kernel, [own, other, one_first, one_second, *beyond[:2]], OWN_COST, "own"
+        more_kernel, rows, [own, one_first, one_second, *beyond[:2], near], OWN_COST, "own"
+    )
+    found_first = kernel_call(
+        last_kernel, rows, [two_first, *keys, mine], FIRST_COST, "first"
     )
     found_second = kernel_call(
-        last_kernel, [two_second, *chip, *beyond, mine], SECOND_COST, "second"
+        last_kernel, rows, [two_second, *keys, found_first], SECOND_COST, "second"
     )
     best = jnp.maximum(
         mine, jnp.maximum(send(found_first, "home"), send(found_second, "home_other"))

time: 28.7 us -> 27.3 us (0.951)
  waiting for transfers between devices: 13.5 us -> 9.62 us
  starting transfers between devices: 11.5 us -> 13.8 us
    ppermute x10, waiting for transfers between devices: 13.5 us -> 9.62 us  [send(): return lax.ppermute(value, GROUP, perms[name])]
    ppermute x10, starting transfers between devices: 11.5 us -> 13.8 us  [send(): return lax.ppermute(value, GROUP, perms[name])]
    pallas_call x3 -> x4, Pallas kernels: 1.72 us -> 1.96 us  [kernel_call(): pl.pallas_call(kernel, out_shape=jax.ShapeDtypeStruct((1, rows), jnp.floa...]
  transfers between devices with their start and end apart: 10 -> 10, of which waited for: 5 -> 5; matrix products, arithmetic and copies ran while one was open for 0% -> 0% of each run, Pallas kernels for 6% -> 5%
where the time goes in v7:
time: 27.3 us; the launch traced here: 27.1 us
  starting transfers between devices  13.8 us (51%)
  waiting for transfers between devices  9.62 us (35%)
  Pallas kernels  3.13 us (11%)
  other arithmetic  0.57 us (2%)
    ppermute x10, starting transfers between devices, send(): return lax.ppermute(value, GROUP, perms[name])  13.8 us
    ppermute x10, waiting for transfers between devices, send(): return lax.ppermute(value, GROUP, perms[name])  9.62 us
    pallas_call x4, Pallas kernels, kernel_call(): pl.pallas_call(kernel, out_shape=jax.ShapeDtypeStruct((1, rows), jnp.floa...  1.96 us
    pallas_call x1, Pallas kernels, on_ring(): pl.pallas_call(pack_kernel, out_shape=jax.ShapeDtypeStruct((rows * width...  1.17 us
    max x1, other arithmetic, on_ring(): jnp.maximum(mine, jnp.maximum(send(found_first, 'home'), send(found_secon...  0.57 us
  transfers between devices with their start and end apart: 10, of which 5 were waited for; matrix products, arithmetic and copies ran while one was open for 0% of the time, Pallas kernels for 5%

profile of v7, /device:TPU:0, one launch (start us, length us, event | category | flops | bytes accessed | tf_op | source)
XLA Modules:
  0.0 27.1 jit_solution(756377605119106047)
XLA Ops:
  0.0 1.2 %pack.1.rows.refs_0_ = bf16[1040,128]{1,0:T(8,128)(2,1)S(1)} custom-call(bf16[256,512]{1,0:T(8,128)(2,1)} %embeds.1, s32[1,256]{1,0:T(1,128)} %bitcast.2), custom_call_target="tpu_custom_call" | custom-call | tf_op jit(solution)/shard_map/pack/pallas_call | solution.py:160
  1.2 0.5 %collective-permute-start.1 = (bf16[1040,128]{1,0:T(8,128)(2,1)S(1)}, bf16[1040,128]{1,0:T(8,128)(2,1)S(1)}, u32[]{:S(2)}, u32[]{:S(2)}) collective-permute-start(bf16[1040,128]{1,0:T(8,128)(2,1)S(1)} %pack.1.rows.refs_0_), channel_id=1, source_target_pairs={{0,1},{1,0},{4,5},{5,4},{8,9},{9,8},{12,13},{13,12},{14,15},{15,14... | collective-permute-start | bytes 798728 | tf_op jit(solution)/shard_map/ppermute | solution.py:157
  1.7 2.6 %collective-permute-start = (bf16[1040,128]{1,0:T(8,128)(2,1)S(1)}, bf16[1040,128]{1,0:T(8,128)(2,1)S(1)}, u32[]{:S(2)}, u32[]{:S(2)}) collective-permute-start(bf16[1040,128]{1,0:T(8,128)(2,1)S(1)} %pack.1.rows.refs_0_), channel_id=1, source_target_pairs={{0,4},{1,3},{4,8},{5,1},{8,12},{9,5},{12,14},{13,9},{14,10},{15,13... | collective-permute-start | bytes 798728 | tf_op jit(solution)/shard_map/ppermute | solution.py:157
  4.3 0.0 collective-permute-done.1.other.refs_1_
  4.3 0.3 %near.1.refs_4_ = f32[1,256]{1,0:T(1,128)S(1)} custom-call(bf16[1040,128]{1,0:T(8,128)(2,1)S(1)} %pack.1.rows.refs_0_, bf16[1040,128]{1,0:T(8,128)(2,1)S(1)} %collective-permute-done.1.other.refs_1_), custom_call_target="tpu_custom_call" | custom-call | flops 134217728 | bytes 1048576 | tf_op jit(solution)/shard_map/near/pallas_call | solution.py:139
  4.7 1.3 %collective-permute-start.2 = (bf16[1040,128]{1,0:T(8,128)(2,1)S(1)}, bf16[1040,128]{1,0:T(8,128)(2,1)S(1)}, u32[]{:S(2)}, u32[]{:S(2)}) collective-permute-start(bf16[1040,128]{1,0:T(8,128)(2,1)S(1)} %pack.1.rows.refs_0_), channel_id=1, source_target_pairs={{0,3},{1,4},{4,1},{5,8},{8,5},{9,12},{12,9},{13,14},{14,13},{15,10... | collective-permute-start | bytes 798728 | tf_op jit(solution)/shard_map/ppermute | solution.py:157
  6.0 3.6 %collective-permute-done.refs_0_ = bf16[1040,128]{1,0:T(8,128)(2,1)S(1)} collective-permute-done((bf16[1040,128]{1,0:T(8,128)(2,1)S(1)}, bf16[1040,128]{1,0:T(8,128)(2,1)S(1)}, u32[]{:S(2)}, u32[]{:S(2)}) %collective-permute-start) | collective-permute-done | bytes 266272 | tf_op jit(solution)/shard_map/ppermute | solution.py:157
  9.7 2.5 %collective-permute-start.5 = (bf16[1040,128]{1,0:T(8,128)(2,1)S(1)}, bf16[1040,128]{1,0:T(8,128)(2,1)S(1)}, u32[]{:S(2)}, u32[]{:S(2)}) collective-permute-start(bf16[1040,128]{1,0:T(8,128)(2,1)S(1)} %collective-permute-done.refs_0_), channel_id=1, source_target_pairs={{0,4},{1,3},{4,8},{5,1},{8,12},{9,5},{12,14},{13,9},{14,10},{15,13... | collective-permute-start | bytes 798728 | tf_op jit(solution)/shard_map/ppermute | solution.py:157
  12.1 0.0 collective-permute-start.3
  12.1 0.0 collective-permute-done.2.refs_1_
  12.1 0.5 %collective-permute-start.4 = (bf16[1040,128]{1,0:T(8,128)(2,1)S(1)}, bf16[1040,128]{1,0:T(8,128)(2,1)S(1)}, u32[]{:S(2)}, u32[]{:S(2)}) collective-permute-start(bf16[1040,128]{1,0:T(8,128)(2,1)S(1)} %collective-permute-done.2.refs_1_), channel_id=1, source_target_pairs={{0,1},{1,0},{4,5},{5,4},{8,9},{9,8},{12,13},{13,12},{14,15},{15,14... | collective-permute-start | bytes 798728 | tf_op jit(solution)/shard_map/ppermute | solution.py:157
  12.6 1.6 %collective-permute-start.8 = (bf16[1040,128]{1,0:T(8,128)(2,1)S(1)}, bf16[1040,128]{1,0:T(8,128)(2,1)S(1)}, u32[]{:S(2)}, u32[]{:S(2)}) collective-permute-start(bf16[1040,128]{1,0:T(8,128)(2,1)S(1)} %collective-permute-done.2.refs_1_), channel_id=1, source_target_pairs={{0,4},{1,3},{4,8},{5,1},{8,12},{9,5},{12,14},{13,9},{14,10},{15,13... | collective-permute-start | bytes 798728 | tf_op jit(solution)/shard_map/ppermute | solution.py:157
  14.2 2.3 %collective-permute-done.5.rows = bf16[1040,128]{1,0:T(8,128)(2,1)S(1)} collective-permute-done((bf16[1040,128]{1,0:T(8,128)(2,1)S(1)}, bf16[1040,128]{1,0:T(8,128)(2,1)S(1)}, u32[]{:S(2)}, u32[]{:S(2)}) %collective-permute-start.5) | collective-permute-done | bytes 266272 | tf_op jit(solution)/shard_map/ppermute | solution.py:157
  16.6 0.0 collective-permute-start.6
  16.6 0.0 collective-permute-done.3.refs_2_
  16.6 0.0 collective-permute-done.4.refs_3_
  16.6 0.5 %own.1.refs_5_ = f32[1,256]{1,0:T(1,128)S(1)} custom-call(bf16[1040,128]{1,0:T(8,128)(2,1)S(1)} %pack.1.rows.refs_0_, bf16[1040,128]{1,0:T(8,128)(2,1)S(1)} %collective-permute-done.refs_0_, bf16[1040,128]{1,0:T(8,128)(2,1)S(1)} %collective-permute-done.2.refs_1_, bf16[1040,128]{1,0:T(8,128)(2,1)S(1)} %collective-permute-done.3.refs_2_, ...), custom_call_target="tpu_custom_call" | custom-call | flops 6710886400 | bytes 1048576 | tf_op jit(solution)/shard_map/own/pallas_call | solution.py:139
  17.1 1.0 %collective-permute-done.6.refs_4_ = bf16[1040,128]{1,0:T(8,128)(2,1)S(1)} collective-permute-done((bf16[1040,128]{1,0:T(8,128)(2,1)S(1)}, bf16[1040,128]{1,0:T(8,128)(2,1)S(1)}, u32[]{:S(2)}, u32[]{:S(2)}) %collective-permute-start.6) | collective-permute-done | bytes 266272 | tf_op jit(solution)/shard_map/ppermute | solution.py:157
  18.1 0.6 %first.1.refs_5_ = f32[1,256]{1,0:T(1,128)S(1)} custom-call(bf16[1040,128]{1,0:T(8,128)(2,1)S(1)} %collective-permute-done.5.rows, bf16[1040,128]{1,0:T(8,128)(2,1)S(1)} %pack.1.rows.refs_0_, bf16[1040,128]{1,0:T(8,128)(2,1)S(1)} %collective-permute-done.1.other.refs_1_, bf16[1040,128]{1,0:T(8,128)(2,1)S(1)} %collective-permute-done.3.refs_2_, ...), custom_call_target="tpu_custom_call" | custom-call | flops 335544320 | bytes 1048576 | tf_op jit(solution)/shard_map/first/pallas_call | solution.py:139
  18.7 0.7 %collective-permute-done.8.rows = bf16[1040,128]{1,0:T(8,128)(2,1)S(1)} collective-permute-done((bf16[1040,128]{1,0:T(8,128)(2,1)S(1)}, bf16[1040,128]{1,0:T(8,128)(2,1)S(1)}, u32[]{:S(2)}, u32[]{:S(2)}) %collective-permute-start.8) | collective-permute-done | bytes 266272 | tf_op jit(solution)/shard_map/ppermute | solution.py:157
  19.4 0.6 %second.1 = f32[1,256]{1,0:T(1,128)S(1)} custom-call(bf16[1040,128]{1,0:T(8,128)(2,1)S(1)} %collective-permute-done.8.rows, bf16[1040,128]{1,0:T(8,128)(2,1)S(1)} %pack.1.rows.refs_0_, bf16[1040,128]{1,0:T(8,128)(2,1)S(1)} %collective-permute-done.1.other.refs_1_, bf16[1040,128]{1,0:T(8,128)(2,1)S(1)} %collective-permute-done.3.refs_2_, ...), custom_call_target="tpu_custom_call" | custom-call | flops 335544320 | bytes 1048576 | tf_op jit(solution)/shard_map/second/pallas_call | solution.py:139
  20.0 2.1 %collective-permute-start.9 = (f32[1,256]{1,0:T(1,128)S(1)}, f32[1,256]{1,0:T(1,128)S(1)}, u32[]{:S(2)}, u32[]{:S(2)}) collective-permute-start(f32[1,256]{1,0:T(1,128)S(1)} %second.1), channel_id=1, source_target_pairs={{0,7},{1,8},{4,3},{5,12},{8,1},{9,14},{12,5},{13,10},{14,9},{15,6}... | collective-permute-start | bytes 3080 | tf_op jit(solution)/shard_map/ppermute | solution.py:157
  22.1 2.6 %collective-permute-start.7 = (f32[1,256]{1,0:T(1,128)S(1)}, f32[1,256]{1,0:T(1,128)S(1)}, u32[]{:S(2)}, u32[]{:S(2)}) collective-permute-start(f32[1,256]{1,0:T(1,128)S(1)} %first.1.refs_5_), channel_id=1, source_target_pairs={{0,6},{1,9},{4,2},{5,13},{8,0},{9,15},{12,4},{13,11},{14,8},{15,7}... | collective-permute-start | bytes 3080 | tf_op jit(solution)/shard_map/ppermute | solution.py:157
  24.7 0.0 collective-permute-done.9
  24.7 1.9 %collective-permute-done.7 = f32[1,256]{1,0:T(1,128)S(1)} collective-permute-done((f32[1,256]{1,0:T(1,128)S(1)}, f32[1,256]{1,0:T(1,128)S(1)}, u32[]{:S(2)}, u32[]{:S(2)}) %collective-permute-start.7) | collective-permute-done | bytes 1056 | tf_op jit(solution)/shard_map/ppermute | solution.py:157
  26.5 0.6 %maximum_maximum_fusion = f32[1,256]{1,0:T(1,128)} fusion(f32[1,256]{1,0:T(1,128)S(1)} %own.1.refs_5_, f32[1,256]{1,0:T(1,128)S(1)} %collective-permute-done.7, f32[1,256]{1,0:T(1,128)S(1)} %collective-permute-done.9), kind=kLoop, calls=%fused_computation | loop fusion | flops 512 | bytes 4096 | tf_op jit(solution)/shard_map/max | solution.py:192
Async XLA Ops:
  1.2 3.2 %collective-permute-start.1 = (bf16[1040,128]{1,0:T(8,128)(2,1)S(1)}, bf16[1040,128]{1,0:T(8,128)(2,1)S(1)}, u32[]{:S(2)}, u32[]{:S(2)}) collective-permute-start(bf16[1040,128]{1,0:T(8,128)(2,1)S(1)} %pack.1.rows.refs_0_), channel_id=1, source_target_pairs={{0,1},{1,0},{4,5},{5,4},{8,9},{9,8},{12,13},{13,12},{14,15},{15,14... | collective-permute-start | bytes 798728 | tf_op jit(solution)/shard_map/ppermute | solution.py:157
  1.7 8.0 %collective-permute-start = (bf16[1040,128]{1,0:T(8,128)(2,1)S(1)}, bf16[1040,128]{1,0:T(8,128)(2,1)S(1)}, u32[]{:S(2)}, u32[]{:S(2)}) collective-permute-start(bf16[1040,128]{1,0:T(8,128)(2,1)S(1)} %pack.1.rows.refs_0_), channel_id=1, source_target_pairs={{0,4},{1,3},{4,8},{5,1},{8,12},{9,5},{12,14},{13,9},{14,10},{15,13... | collective-permute-start | bytes 798728 | tf_op jit(solution)/shard_map/ppermute | solution.py:157
  4.7 7.5 %collective-permute-start.2 = (bf16[1040,128]{1,0:T(8,128)(2,1)S(1)}, bf16[1040,128]{1,0:T(8,128)(2,1)S(1)}, u32[]{:S(2)}, u32[]{:S(2)}) collective-permute-start(bf16[1040,128]{1,0:T(8,128)(2,1)S(1)} %pack.1.rows.refs_0_), channel_id=1, source_target_pairs={{0,3},{1,4},{4,1},{5,8},{8,5},{9,12},{12,9},{13,14},{14,13},{15,10... | collective-permute-start | bytes 798728 | tf_op jit(solution)/shard_map/ppermute | solution.py:157
  9.7 6.9 %collective-permute-start.5 = (bf16[1040,128]{1,0:T(8,128)(2,1)S(1)}, bf16[1040,128]{1,0:T(8,128)(2,1)S(1)}, u32[]{:S(2)}, u32[]{:S(2)}) collective-permute-start(bf16[1040,128]{1,0:T(8,128)(2,1)S(1)} %collective-permute-done.refs_0_), channel_id=1, source_target_pairs={{0,4},{1,3},{4,8},{5,1},{8,12},{9,5},{12,14},{13,9},{14,10},{15,13... | collective-permute-start | bytes 798728 | tf_op jit(solution)/shard_map/ppermute | solution.py:157
  12.1 4.4 %collective-permute-start.3 = (bf16[1040,128]{1,0:T(8,128)(2,1)S(1)}, bf16[1040,128]{1,0:T(8,128)(2,1)S(1)}, u32[]{:S(2)}, u32[]{:S(2)}) collective-permute-start(bf16[1040,128]{1,0:T(8,128)(2,1)S(1)} %collective-permute-done.refs_0_), channel_id=1, source_target_pairs={{0,1},{1,0},{4,5},{5,4},{8,9},{9,8},{12,13},{13,12},{14,15},{15,14... | collective-permute-start | bytes 798728 | tf_op jit(solution)/shard_map/ppermute | solution.py:157
  12.1 4.4 %collective-permute-start.4 = (bf16[1040,128]{1,0:T(8,128)(2,1)S(1)}, bf16[1040,128]{1,0:T(8,128)(2,1)S(1)}, u32[]{:S(2)}, u32[]{:S(2)}) collective-permute-start(bf16[1040,128]{1,0:T(8,128)(2,1)S(1)} %collective-permute-done.2.refs_1_), channel_id=1, source_target_pairs={{0,1},{1,0},{4,5},{5,4},{8,9},{9,8},{12,13},{13,12},{14,15},{15,14... | collective-permute-start | bytes 798728 | tf_op jit(solution)/shard_map/ppermute | solution.py:157
  12.6 6.8 %collective-permute-start.8 = (bf16[1040,128]{1,0:T(8,128)(2,1)S(1)}, bf16[1040,128]{1,0:T(8,128)(2,1)S(1)}, u32[]{:S(2)}, u32[]{:S(2)}) collective-permute-start(bf16[1040,128]{1,0:T(8,128)(2,1)S(1)} %collective-permute-done.2.refs_1_), channel_id=1, source_target_pairs={{0,4},{1,3},{4,8},{5,1},{8,12},{9,5},{12,14},{13,9},{14,10},{15,13... | collective-permute-start | bytes 798728 | tf_op jit(solution)/shard_map/ppermute | solution.py:157
  16.6 1.5 %collective-permute-start.6 = (bf16[1040,128]{1,0:T(8,128)(2,1)S(1)}, bf16[1040,128]{1,0:T(8,128)(2,1)S(1)}, u32[]{:S(2)}, u32[]{:S(2)}) collective-permute-start(bf16[1040,128]{1,0:T(8,128)(2,1)S(1)} %collective-permute-done.5.rows), channel_id=1, source_target_pairs={{0,1},{1,0},{4,5},{5,4},{8,9},{9,8},{12,13},{13,12},{14,15},{15,14... | collective-permute-start | bytes 798728 | tf_op jit(solution)/shard_map/ppermute | solution.py:157
  20.0 4.7 %collective-permute-start.9 = (f32[1,256]{1,0:T(1,128)S(1)}, f32[1,256]{1,0:T(1,128)S(1)}, u32[]{:S(2)}, u32[]{:S(2)}) collective-permute-start(f32[1,256]{1,0:T(1,128)S(1)} %second.1), channel_id=1, source_target_pairs={{0,7},{1,8},{4,3},{5,12},{8,1},{9,14},{12,5},{13,10},{14,9},{15,6}... | collective-permute-start | bytes 3080 | tf_op jit(solution)/shard_map/ppermute | solution.py:157
  22.1 4.5 %collective-permute-start.7 = (f32[1,256]{1,0:T(1,128)S(1)}, f32[1,256]{1,0:T(1,128)S(1)}, u32[]{:S(2)}, u32[]{:S(2)}) collective-permute-start(f32[1,256]{1,0:T(1,128)S(1)} %first.1.refs_5_), channel_id=1, source_target_pairs={{0,6},{1,9},{4,2},{5,13},{8,0},{9,15},{12,4},{13,11},{14,8},{15,7}... | collective-permute-start | bytes 3080 | tf_op jit(solution)/shard_map/ppermute | solution.py:157

commit v8 on v5

--- a/solution.py
+++ b/solution.py
@@ -20,11 +20,19 @@
     )
 
 
+LANES = 128
 LABEL_ROWS = 16
 VMEM_BYTES = 32 * 2**20
 NEAR_COST = 1
 FIRST_COST = 5
+BACK_COST = 2
 SECOND_COST = 200
+
+
+def put_unit(unit, chunk, at, size):
+    count, width = unit.shape
+    for j in range(width // LANES):
+        chunk[j * size + at : j * size + at + count, :] = unit[:, j * LANES : (j + 1) * LANES]
 
 
 def pack_first_kernel(embeds, label, first, raw, line, sems):
@@ -37,23 +45,31 @@
     for copy in copies:
         copy.start()
     copies[0].wait()
-    lines = jnp.broadcast_to(line[...].astype(jnp.float32), (LABEL_ROWS, rows))
-    first[half:, :rows] = lines.astype(jnp.bfloat16)
-    first[half:, rows:] = jnp.zeros((LABEL_ROWS, width - rows), jnp.bfloat16)
+    row = lax.broadcasted_iota(jnp.int32, (LABEL_ROWS, LANES), 0)
+    lines = jnp.zeros((LABEL_ROWS, LANES), jnp.float32)
+    for i in range(rows // LANES):
+        piece = line[:, i * LANES : (i + 1) * LANES].astype(jnp.float32)
+        lines = jnp.where(row == i, piece, lines)
+    first[half * width // LANES :, :] = lines.astype(jnp.bfloat16)
     copies[1].wait()
-    first[:half, :] = normalised(raw[...])
-
-
-def pack_second_kernel(embeds, first, second, both, raw, sem):
-    half = second.shape[0]
-    copy = pltpu.make_async_copy(embeds.at[pl.ds(half, half)], raw, sem)
-    copy.start()
-    both[:half, :] = first[:half, :]
-    both[2 * half :, :] = first[half:, :]
-    copy.wait()
-    unit = normalised(raw[...])
-    second[...] = unit
-    both[half : 2 * half, :] = unit
+    put_unit(normalised(raw[...]), first, 0, half)
+
+
+def pack_second_kernel(embeds, first, second, both):
+    rows, width = embeds.shape
+    half = rows // 2
+    unit = normalised(embeds[half:, :])
+    put_unit(unit, second, 0, half)
+    put_chunks(first, second, both, rows)
+
+
+def put_chunks(first, second, both, rows):
+    size = second.shape[0]
+    half = rows // 2
+    for at in range(0, size, half):
+        both[2 * at : 2 * at + half, :] = first[at : at + half, :]
+        both[2 * at + half : 2 * (at + half), :] = second[at : at + half, :]
+    both[2 * size :, :] = first[size:, :]
 
 
 class Block:
@@ -65,33 +81,36 @@
 
     def column(self):
         if self.along_rows is None:
-            self.along_rows = jnp.transpose(jnp.broadcast_to(self.label, (128, self.rows)))
+            self.along_rows = jnp.transpose(jnp.broadcast_to(self.label, (LANES, self.rows)))
         return self.along_rows
 
 
-def labels_in(first):
-    half = first.shape[0] - LABEL_ROWS
-    return first[half:, : 2 * half].astype(jnp.float32)[:1]
-
-
-def packed(ref):
-    rows = ref.shape[0] - LABEL_ROWS
-    return Block(ref[:rows, :], ref[rows:, :rows].astype(jnp.float32)[:1])
-
-
-def whole(first, second):
-    half = second.shape[0]
-    return Block(jnp.concatenate([first[:half, :], second[...]], axis=0), labels_in(first))
-
-
-def first_half(first):
-    half = first.shape[0] - LABEL_ROWS
-    return Block(first[:half, :], labels_in(first)[:, :half])
-
-
-def second_half(first, second):
-    half = second.shape[0]
-    return Block(second[...], labels_in(first)[:, half:])
+def unit_in(chunk, rows, end):
+    return jnp.concatenate([chunk[at : at + rows, :] for at in range(0, end, rows)], axis=1)
+
+
+def labels_in(first, rows):
+    lines = first[first.shape[0] - LABEL_ROWS :, :].astype(jnp.float32)
+    return jnp.concatenate([lines[i : i + 1] for i in range(rows // LANES)], axis=1)
+
+
+def packed(both, rows):
+    return Block(unit_in(both, rows, both.shape[0] - LABEL_ROWS), labels_in(both, rows))
+
+
+def first_half(first, rows):
+    half = rows // 2
+    unit = unit_in(first, half, first.shape[0] - LABEL_ROWS)
+    return Block(unit, labels_in(first, rows)[:, :half])
+
+
+def second_half(first, second, rows):
+    half = rows // 2
+    return Block(unit_in(second, half, second.shape[0]), labels_in(first, rows)[:, half:])
+
+
+def whole(first, second, rows):
+    return joined(first_half(first, rows), second_half(first, second, rows))
 
 
 def joined(*blocks):
@@ -108,13 +127,13 @@
             keys.unit, queries.unit, (((1,), (1,)), ((), ())), preferred_element_type=jnp.float32
         )
         pieces = []
-        for start in range(0, queries.rows, 128):
-            keep = keys.column() == queries.label[:, start : start + 128]
+        for start in range(0, queries.rows, LANES):
+            keep = keys.column() == queries.label[:, start : start + LANES]
             if keys is queries:
                 row = lax.broadcasted_iota(jnp.int32, keep.shape, 0)
                 column = lax.broadcasted_iota(jnp.int32, keep.shape, 1) + start
                 keep = keep & (row != column)
-            found = jnp.where(keep, sims[:, start : start + 128], -1.0)
+            found = jnp.where(keep, sims[:, start : start + LANES], -1.0)
             pieces.append(jnp.max(found, axis=0, keepdims=True))
         found = jnp.concatenate(pieces, axis=1)
         best = found if best is None else jnp.maximum(best, found)
@@ -122,49 +141,54 @@
 
 
 def near_kernel(own, prev_a, prev_b, succ_a, succ_b, mine, bundle):
-    half = prev_b.shape[0]
-    for at, (first, second) in enumerate(((prev_a, prev_b), (succ_a, succ_b))):
-        bundle[at, :half, :] = first[:half, :]
-        bundle[at, half : 2 * half, :] = second[...]
-        bundle[at, 2 * half :, :] = first[half:, :]
+    rows = mine.shape[1]
+    put_chunks(prev_a, prev_b, bundle.at[0], rows)
+    put_chunks(succ_a, succ_b, bundle.at[1], rows)
     bundle[2] = own[...]
-    own = packed(own)
-    mine[...] = best_of(own, own, whole(prev_a, prev_b), whole(succ_a, succ_b))
+    own = packed(own, rows)
+    mine[...] = best_of(own, own, whole(prev_a, prev_b, rows), whole(succ_a, succ_b, rows))
 
 
 def far_first_kernel(own, prev_a, prev_b, succ_a, succ_b, back_a, ahead_a, found):
-    near = packed(own), whole(prev_a, prev_b), whole(succ_a, succ_b)
-    rows = joined(first_half(back_a), first_half(ahead_a))
-    found[...] = best_of(rows, rows, *near)
-
-
-def far_second_kernel(
-    own, prev_a, prev_b, succ_a, succ_b, back_a, ahead_a, back_b, ahead_b, *refs
-):
-    first_found, to_back, to_ahead = refs
-    near = packed(own), whole(prev_a, prev_b), whole(succ_a, succ_b)
-    half = back_b.shape[0]
-    first = joined(first_half(back_a), first_half(ahead_a))
-    second = joined(second_half(back_a, back_b), second_half(ahead_a, ahead_b))
-    found = jnp.maximum(first_found[...], best_of(first, second))
-    found_second = best_of(second, second, first, *near)
-    to_back[:, :half] = found[:, :half]
-    to_back[:, half:] = found_second[:, :half]
-    to_ahead[:, :half] = found[:, half:]
-    to_ahead[:, half:] = found_second[:, half:]
+    rows = found.shape[1]
+    near = packed(own, rows), whole(prev_a, prev_b, rows), whole(succ_a, succ_b, rows)
+    queries = joined(first_half(back_a, rows), first_half(ahead_a, rows))
+    found[...] = best_of(queries, queries, *near)
+
+
+def far_back_kernel(own, succ_a, succ_b, back_a, ahead_a, back_b, found, back, ahead):
+    rows = found.shape[1]
+    half = rows // 2
+    rest, first = second_half(back_a, back_b, rows), first_half(ahead_a, rows)
+    back[:, :half] = found[:, :half]
+    back[:, half:] = best_of(rest, packed(own, rows), whole(succ_a, succ_b, rows), first)
+    ahead[...] = jnp.maximum(found[:, half:], best_of(first, rest))
+
+
+def far_second_kernel(own, prev_a, prev_b, back_a, ahead_a, back_b, ahead_b, *refs):
+    back_found, ahead_found, to_back, to_ahead = refs
+    rows = to_back.shape[1]
+    half = rows // 2
+    back, rest = whole(back_a, back_b, rows), second_half(ahead_a, ahead_b, rows)
+    to_back[...] = jnp.maximum(back_found[...], best_of(back, rest))
+    to_ahead[:, :half] = ahead_found[...]
+    to_ahead[:, half:] = best_of(rest, packed(own, rows), whole(prev_a, prev_b, rows), back)
 
 
 def far_other_kernel(others, back_a, ahead_a, back_b, ahead_b, *refs):
     back_found, ahead_found, to_back, to_ahead = refs
-    back, ahead = whole(back_a, back_b), whole(ahead_a, ahead_b)
-    to_back[...] = jnp.maximum(back_found[...], best_of(back, packed(others.at[1])))
-    to_ahead[...] = jnp.maximum(ahead_found[...], best_of(ahead, packed(others.at[0])))
+    rows = to_back.shape[1]
+    back, ahead = whole(back_a, back_b, rows), whole(ahead_a, ahead_b, rows)
+    prev, succ = packed(others.at[0], rows), packed(others.at[1], rows)
+    to_back[...] = jnp.maximum(back_found[...], best_of(back, succ))
+    to_ahead[...] = jnp.maximum(ahead_found[...], best_of(ahead, prev))
 
 
 def own_kernel(own, others, back_a, ahead_a, back_b, ahead_b, near, mine):
-    keys = [packed(others.at[at]) for at in range(3)]
-    keys += [whole(back_a, back_b), whole(ahead_a, ahead_b)]
-    mine[...] = jnp.maximum(near[...], best_of(packed(own), *keys))
+    rows = mine.shape[1]
+    keys = [packed(others.at[at], rows) for at in range(3)]
+    keys += [whole(back_a, back_b, rows), whole(ahead_a, ahead_b, rows)]
+    mine[...] = jnp.maximum(near[...], best_of(packed(own, rows), *keys))
 
 
 def ring_perms(size_x, size_y, size_z):
@@ -221,14 +245,17 @@
         return lax.ppermute(value, GROUP, perms[name])
 
     line = jax.ShapeDtypeStruct((1, rows), jnp.float32)
+    half_line = jax.ShapeDtypeStruct((1, half), jnp.float32)
+
+    def chunk(count, labels):
+        size = count * width // LANES + labels * LABEL_ROWS
+        return jax.ShapeDtypeStruct((size, LANES), jnp.bfloat16)
+
     anywhere = pl.BlockSpec(memory_space=pl.ANY)
     vmem = pl.BlockSpec(memory_space=pltpu.VMEM)
-    params = pltpu.CompilerParams(vmem_limit_bytes=VMEM_BYTES)
-    embeds = pltpu.with_memory_space_constraint(embeds, pltpu.HBM)
-    label = pltpu.with_memory_space_constraint(cluster.reshape(1, rows), pltpu.HBM)
     own_a = pl.pallas_call(
         pack_first_kernel,
-        out_shape=jax.ShapeDtypeStruct((half + LABEL_ROWS, width), jnp.bfloat16),
+        out_shape=chunk(half, True),
         in_specs=[anywhere] * 2,
         out_specs=vmem,
         scratch_shapes=[
@@ -236,43 +263,31 @@
             pltpu.VMEM((1, rows), jnp.int32),
             pltpu.SemaphoreType.DMA((2,)),
         ],
-        compiler_params=params,
+        compiler_params=pltpu.CompilerParams(vmem_limit_bytes=VMEM_BYTES),
         name="pack_first",
-    )(embeds, label)
-    own_b, own = pl.pallas_call(
-        pack_second_kernel,
-        out_shape=[
-            jax.ShapeDtypeStruct((half, width), jnp.bfloat16),
-            jax.ShapeDtypeStruct((rows + LABEL_ROWS, width), jnp.bfloat16),
-        ],
-        in_specs=[anywhere, vmem],
-        out_specs=[vmem] * 2,
-        scratch_shapes=[pltpu.VMEM((half, width), jnp.bfloat16), pltpu.SemaphoreType.DMA],
-        compiler_params=params,
-        name="pack_second",
-    )(embeds, own_a)
+    )(
+        pltpu.with_memory_space_constraint(embeds, pltpu.HBM),
+        pltpu.with_memory_space_constraint(cluster.reshape(1, rows), pltpu.HBM),
+    )
+    own_b, own = kernel_call(
+        pack_second_kernel, [embeds, own_a], [chunk(half, False), chunk(rows, True)], 1
+    )
     prev_a, succ_a = send(own_a, "next"), send(own_a, "prev")
     prev_b, succ_b = send(own_b, "next"), send(own_b, "prev")
     back_a, ahead_a = send(prev_a, "on_next"), send(succ_a, "on_prev")
     back_b, ahead_b = send(prev_b, "on_next"), send(succ_b, "on_prev")
-    mine, bundle = kernel_call(
-        near_kernel,
-        [own, prev_a, prev_b, succ_a, succ_b],
-        [line, jax.ShapeDtypeStruct((3, rows + LABEL_ROWS, width), jnp.bfloat16)],
-        NEAR_COST,
-    )
+    prev, succ, far = [prev_a, prev_b], [succ_a, succ_b], [back_a, ahead_a, back_b, ahead_b]
+    bundle_shape = jax.ShapeDtypeStruct((3, *chunk(rows, True).shape), jnp.bfloat16)
+    mine, bundle = kernel_call(near_kernel, [own, *prev, *succ], [line, bundle_shape], NEAR_COST)
     others = send(bundle, "sibling")
-    blocks = [own, prev_a, prev_b, succ_a, succ_b]
-    far = [back_a, ahead_a, back_b, ahead_b]
-    (first_found,) = kernel_call(
-        far_first_kernel, [*blocks, back_a, ahead_a], [line], FIRST_COST
-    )
-    to_back, to_ahead = kernel_call(
-        far_second_kernel, [*blocks, *far, first_found], [line] * 2, SECOND_COST
-    )
-    to_back, to_ahead = kernel_call(
-        far_other_kernel, [others, *far, to_back, to_ahead], [line] * 2, 2
-    )
+    (found,) = kernel_call(
+        far_first_kernel, [own, *prev, *succ, back_a, ahead_a], [line], FIRST_COST
+    )
+    found = kernel_call(
+        far_back_kernel, [own, *succ, back_a, ahead_a, back_b, found], [line, half_line], BACK_COST
+    )
+    found = kernel_call(far_second_kernel, [own, *prev, *far, *found], [line] * 2, SECOND_COST)
+    to_back, to_ahead = kernel_call(far_other_kernel, [others, *far, *found], [line] * 2, 2)
     (mine,) = kernel_call(own_kernel, [own, others, *far, mine], [line], 5)
     best = jnp.maximum(
         mine, jnp.maximum(send(to_back, "home_back"), send(to_ahead, "home_ahead"))

time: 25.8 us -> 25.2 us (0.977)
  Pallas kernels: 4.5 us -> 3.92 us
    pallas_call x2 -> x1, Pallas kernels: 2.07 us -> 1.1 us  [on_ring(): pl.pallas_call(pack_first_kernel, out_shape=chunk(half, True), in_specs=[...]
    pallas_call x5 -> x7, Pallas kernels: 2.43 us -> 2.82 us  [kernel_call(): pl.pallas_call(kernel, out_shape=outputs, in_specs=[vmem] * len(inputs),...]
  transfers between devices with their start and end apart: 11 -> 11, of which waited for: 8 -> 8; matrix products, arithmetic and copies ran while one was open for 0% -> 0% of each run, Pallas kernels for 12% -> 10%
where the time goes in v8:
time: 25.2 us; the launch traced here: 25.1 us
  starting transfers between devices  12.9 us (51%)
  waiting for transfers between devices  7.63 us (30%)
  Pallas kernels  3.92 us (16%)
  other arithmetic  0.57 us (2%)
    ppermute x11, starting transfers between devices, send(): return lax.ppermute(value, GROUP, perms[name])  12.9 us
    ppermute x11, waiting for transfers between devices, send(): return lax.ppermute(value, GROUP, perms[name])  7.63 us
    pallas_call x7, Pallas kernels, kernel_call(): pl.pallas_call(kernel, out_shape=outputs, in_specs=[vmem] * len(inputs),...  2.82 us
    pallas_call x1, Pallas kernels, on_ring(): pl.pallas_call(pack_first_kernel, out_shape=chunk(half, True), in_specs=[...  1.1 us
    max x1, other arithmetic, on_ring(): jnp.maximum(mine, jnp.maximum(send(to_back, 'home_back'), send(to_ahead,...  0.57 us
  transfers between devices with their start and end apart: 11, of which 8 were waited for; matrix products, arithmetic and copies ran while one was open for 0% of the time, Pallas kernels for 10%

profile of v8, /device:TPU:0, one launch (start us, length us, event | category | flops | bytes accessed | tf_op | source)
XLA Modules:
  0.0 25.1 jit_solution(5871398931221575311)
XLA Ops:
  0.0 1.1 %pack_first.1.first = bf16[528,128]{1,0:T(8,128)(2,1)S(1)} custom-call(bf16[256,512]{1,0:T(8,128)(2,1)} %embeds.3, s32[1,256]{1,0:T(1,128)} %bitcast.2), custom_call_target="tpu_custom_call" | custom-call | tf_op jit(solution)/shard_map/pack_first/pallas_call | solution.py:256
  1.1 2.5 %collective-permute-start = (bf16[528,128]{1,0:T(8,128)(2,1)S(1)}, bf16[528,128]{1,0:T(8,128)(2,1)S(1)}, u32[]{:S(2)}, u32[]{:S(2)}) collective-permute-start(bf16[528,128]{1,0:T(8,128)(2,1)S(1)} %pack_first.1.first), channel_id=1, source_target_pairs={{0,5},{1,4},{4,8},{5,9},{8,12},{9,13},{12,14},{13,15},{14,10},{15,... | collective-permute-start | bytes 405512 | tf_op jit(solution)/shard_map/ppermute | solution.py:245
  3.6 0.0 collective-permute-start.2
  3.6 0.0 copy-done
  3.6 0.1 pack_second_kernel.1
  3.8 2.1 %collective-permute-start.1 = (bf16[512,128]{1,0:T(8,128)(2,1)S(1)}, bf16[512,128]{1,0:T(8,128)(2,1)S(1)}, u32[]{:S(2)}, u32[]{:S(2)}) collective-permute-start(bf16[512,128]{1,0:T(8,128)(2,1)S(1)} %get-tuple-element.16), channel_id=1, source_target_pairs={{0,5},{1,4},{4,8},{5,9},{8,12},{9,13},{12,14},{13,15},{14,10},{15,... | collective-permute-start | bytes 393224 | tf_op jit(solution)/shard_map/ppermute | solution.py:245
  5.9 0.3 %collective-permute-start.3 = (bf16[512,128]{1,0:T(8,128)(2,1)S(1)}, bf16[512,128]{1,0:T(8,128)(2,1)S(1)}, u32[]{:S(2)}, u32[]{:S(2)}) collective-permute-start(bf16[512,128]{1,0:T(8,128)(2,1)S(1)} %get-tuple-element.16), channel_id=1, source_target_pairs={{0,3},{1,2},{4,0},{5,1},{8,4},{9,5},{12,9},{13,8},{14,13},{15,12},... | collective-permute-start | bytes 393224 | tf_op jit(solution)/shard_map/ppermute | solution.py:245
  6.1 1.5 %collective-permute-done.prev_a = bf16[528,128]{1,0:T(8,128)(2,1)S(1)} collective-permute-done((bf16[528,128]{1,0:T(8,128)(2,1)S(1)}, bf16[528,128]{1,0:T(8,128)(2,1)S(1)}, u32[]{:S(2)}, u32[]{:S(2)}) %collective-permute-start) | collective-permute-done | bytes 135200 | tf_op jit(solution)/shard_map/ppermute | solution.py:245
  7.6 2.5 %collective-permute-start.5 = (bf16[528,128]{1,0:T(8,128)(2,1)S(1)}, bf16[528,128]{1,0:T(8,128)(2,1)S(1)}, u32[]{:S(2)}, u32[]{:S(2)}) collective-permute-start(bf16[528,128]{1,0:T(8,128)(2,1)S(1)} %collective-permute-done.prev_a), channel_id=1, source_target_pairs={{0,4},{1,5},{4,8},{5,9},{8,12},{9,13},{12,14},{13,15},{14,10},{15,... | collective-permute-start | bytes 405512 | tf_op jit(solution)/shard_map/ppermute | solution.py:245
  10.1 0.0 collective-permute-done.2.succ_a
  10.1 0.0 collective-permute-start.6
  10.1 0.3 %collective-permute-done.1.prev_b = bf16[512,128]{1,0:T(8,128)(2,1)S(1)} collective-permute-done((bf16[512,128]{1,0:T(8,128)(2,1)S(1)}, bf16[512,128]{1,0:T(8,128)(2,1)S(1)}, u32[]{:S(2)}, u32[]{:S(2)}) %collective-permute-start.1) | collective-permute-done | bytes 131104 | tf_op jit(solution)/shard_map/ppermute | solution.py:245
  10.4 2.5 %collective-permute-start.7 = (bf16[512,128]{1,0:T(8,128)(2,1)S(1)}, bf16[512,128]{1,0:T(8,128)(2,1)S(1)}, u32[]{:S(2)}, u32[]{:S(2)}) collective-permute-start(bf16[512,128]{1,0:T(8,128)(2,1)S(1)} %collective-permute-done.1.prev_b), channel_id=1, source_target_pairs={{0,4},{1,5},{4,8},{5,9},{8,12},{9,13},{12,14},{13,15},{14,10},{15,... | collective-permute-start | bytes 393224 | tf_op jit(solution)/shard_map/ppermute | solution.py:245
  12.9 0.0 collective-permute-done.3.succ_b
  12.9 0.0 collective-permute-start.8
  12.9 0.5 %near_kernel.1 = (f32[1,256]{1,0:T(1,128)S(1)}, bf16[3,1040,128]{2,1,0:T(8,128)(2,1)S(1)}) custom-call(bf16[1040,128]{1,0:T(8,128)(2,1)S(1)} %get-tuple-element.15.own, bf16[528,128]{1,0:T(8,128)(2,1)S(1)} %collective-permute-done.prev_a, bf16[512,128]{1,0:T(8,128)(2,1)S(1)} %collective-permute-done.1.prev_b, ...), custom_call_target="tpu_custom_call" | custom-call | flops 67108864 | bytes 1048576 | tf_op jit(solution)/shard_map/near_kernel/pallas_call | solution.py:226
  13.3 0.1 collective-permute-start.4
  13.4 0.6 %collective-permute-done.5.back_a = bf16[528,128]{1,0:T(8,128)(2,1)S(1)} collective-permute-done((bf16[528,128]{1,0:T(8,128)(2,1)S(1)}, bf16[528,128]{1,0:T(8,128)(2,1)S(1)}, u32[]{:S(2)}, u32[]{:S(2)}) %collective-permute-start.5) | collective-permute-done | bytes 135200 | tf_op jit(solution)/shard_map/ppermute | solution.py:245
  14.0 1.6 %collective-permute-done.6.ahead_a = bf16[528,128]{1,0:T(8,128)(2,1)S(1)} collective-permute-done((bf16[528,128]{1,0:T(8,128)(2,1)S(1)}, bf16[528,128]{1,0:T(8,128)(2,1)S(1)}, u32[]{:S(2)}, u32[]{:S(2)}) %collective-permute-start.6) | collective-permute-done | bytes 135200 | tf_op jit(solution)/shard_map/ppermute | solution.py:245
  15.6 0.5 %far_first_kernel.1.found = f32[1,256]{1,0:T(1,128)S(1)} custom-call(bf16[1040,128]{1,0:T(8,128)(2,1)S(1)} %get-tuple-element.15.own, bf16[528,128]{1,0:T(8,128)(2,1)S(1)} %collective-permute-done.prev_a, bf16[512,128]{1,0:T(8,128)(2,1)S(1)} %collective-permute-done.1.prev_b, bf16[528,128]{1,0:T(8,128)(2,1)S(1)} %collective-permute-done.2.succ_a, ...), custom_call_target="tpu_custom_call" | custom-call | flops 335544320 | bytes 1048576 | tf_op jit(solution)/shard_map/far_first_kernel/pallas_call | solution.py:226
  16.1 0.3 %collective-permute-done.7.back_b = bf16[512,128]{1,0:T(8,128)(2,1)S(1)} collective-permute-done((bf16[512,128]{1,0:T(8,128)(2,1)S(1)}, bf16[512,128]{1,0:T(8,128)(2,1)S(1)}, u32[]{:S(2)}, u32[]{:S(2)}) %collective-permute-start.7) | collective-permute-done | bytes 131104 | tf_op jit(solution)/shard_map/ppermute | solution.py:245
  16.4 0.4 %far_back_kernel.1 = (f32[1,256]{1,0:T(1,128)S(1)}, f32[1,128]{1,0:T(1,128)S(1)}) custom-call(bf16[1040,128]{1,0:T(8,128)(2,1)S(1)} %get-tuple-element.15.own, bf16[528,128]{1,0:T(8,128)(2,1)S(1)} %collective-permute-done.2.succ_a, bf16[512,128]{1,0:T(8,128)(2,1)S(1)} %collective-permute-done.3.succ_b, bf16[528,128]{1,0:T(8,128)(2,1)S(1)} %collective-permute-done.5.back_a, ...), custom_call_target="tpu_custom_call" | custom-call | flops 134217728 | bytes 1048576 | tf_op jit(solution)/shard_map/far_back_kernel/pallas_call | solution.py:226
  16.8 1.5 %collective-permute-done.8.ahead_b = bf16[512,128]{1,0:T(8,128)(2,1)S(1)} collective-permute-done((bf16[512,128]{1,0:T(8,128)(2,1)S(1)}, bf16[512,128]{1,0:T(8,128)(2,1)S(1)}, u32[]{:S(2)}, u32[]{:S(2)}) %collective-permute-start.8) | collective-permute-done | bytes 131104 | tf_op jit(solution)/shard_map/ppermute | solution.py:245
  18.3 0.4 %far_second_kernel.1 = (f32[1,256]{1,0:T(1,128)S(1)}, f32[1,256]{1,0:T(1,128)S(1)}) custom-call(bf16[1040,128]{1,0:T(8,128)(2,1)S(1)} %get-tuple-element.15.own, bf16[528,128]{1,0:T(8,128)(2,1)S(1)} %collective-permute-done.prev_a, bf16[512,128]{1,0:T(8,128)(2,1)S(1)} %collective-permute-done.1.prev_b, bf16[528,128]{1,0:T(8,128)(2,1)S(1)} %collective-permute-done.5.back_a, ...), custom_call_target="tpu_custom_call" | custom-call | flops 13421772800 | bytes 1048576 | tf_op jit(solution)/shard_map/far_second_kernel/pallas_call | solution.py:226
  18.8 0.0 collective-permute-done.4.others
  18.8 0.4 %far_other_kernel.1 = (f32[1,256]{1,0:T(1,128)S(1)}, f32[1,256]{1,0:T(1,128)S(1)}) custom-call(bf16[3,1040,128]{2,1,0:T(8,128)(2,1)S(1)} %collective-permute-done.4.others, bf16[528,128]{1,0:T(8,128)(2,1)S(1)} %collective-permute-done.5.back_a, bf16[528,128]{1,0:T(8,128)(2,1)S(1)} %collective-permute-done.6.ahead_a, ...), custom_call_target="tpu_custom_call" | custom-call | flops 134217728 | bytes 1048576 | tf_op jit(solution)/shard_map/far_other_kernel/pallas_call | solution.py:226
  19.1 1.5 %collective-permute-start.9 = (f32[1,256]{1,0:T(1,128)S(1)}, f32[1,256]{1,0:T(1,128)S(1)}, u32[]{:S(2)}, u32[]{:S(2)}) collective-permute-start(f32[1,256]{1,0:T(1,128)S(1)} %get-tuple-element.23), channel_id=1, source_target_pairs={{0,6},{1,7},{4,3},{5,2},{8,1},{9,0},{12,4},{13,5},{14,8},{15,9},{1... | collective-permute-start | bytes 3080 | tf_op jit(solution)/shard_map/ppermute | solution.py:245
  20.6 1.5 %collective-permute-start.10 = (f32[1,256]{1,0:T(1,128)S(1)}, f32[1,256]{1,0:T(1,128)S(1)}, u32[]{:S(2)}, u32[]{:S(2)}) collective-permute-start(f32[1,256]{1,0:T(1,128)S(1)} %get-tuple-element.24), channel_id=1, source_target_pairs={{0,8},{1,9},{4,13},{5,12},{8,15},{9,14},{12,11},{13,10},{14,7},{15... | collective-permute-start | bytes 3080 | tf_op jit(solution)/shard_map/ppermute | solution.py:245
  22.1 0.6 %own_kernel.1 = f32[1,256]{1,0:T(1,128)S(1)} custom-call(bf16[1040,128]{1,0:T(8,128)(2,1)S(1)} %get-tuple-element.15.own, bf16[3,1040,128]{2,1,0:T(8,128)(2,1)S(1)} %collective-permute-done.4.others, bf16[528,128]{1,0:T(8,128)(2,1)S(1)} %collective-permute-done.5.back_a, bf16[528,128]{1,0:T(8,128)(2,1)S(1)} %collective-permute-done.6.ahead_a, ...), custom_call_target="tpu_custom_call" | custom-call | flops 335544320 | bytes 1048576 | tf_op jit(solution)/shard_map/own_kernel/pallas_call | solution.py:226
  22.7 0.4 %collective-permute-done.9 = f32[1,256]{1,0:T(1,128)S(1)} collective-permute-done((f32[1,256]{1,0:T(1,128)S(1)}, f32[1,256]{1,0:T(1,128)S(1)}, u32[]{:S(2)}, u32[]{:S(2)}) %collective-permute-start.9) | collective-permute-done | bytes 1056 | tf_op jit(solution)/shard_map/ppermute | solution.py:245
  23.1 1.4 %collective-permute-done.10 = f32[1,256]{1,0:T(1,128)S(1)} collective-permute-done((f32[1,256]{1,0:T(1,128)S(1)}, f32[1,256]{1,0:T(1,128)S(1)}, u32[]{:S(2)}, u32[]{:S(2)}) %collective-permute-start.10) | collective-permute-done | bytes 1056 | tf_op jit(solution)/shard_map/ppermute | solution.py:245
  24.5 0.6 %maximum_maximum_fusion = f32[1,256]{1,0:T(1,128)} fusion(f32[1,256]{1,0:T(1,128)S(1)} %own_kernel.1, f32[1,256]{1,0:T(1,128)S(1)} %collective-permute-done.9, f32[1,256]{1,0:T(1,128)S(1)} %collective-permute-done.10), kind=kLoop, calls=%fused_computation | loop fusion | flops 512 | bytes 4096 | tf_op jit(solution)/shard_map/max | solution.py:292
  (1 shorter events, 0.0 us)
Async XLA Ops:
  0.0 3.6 %copy-start = (bf16[256,512]{1,0:T(8,128)(2,1)S(1)}, bf16[256,512]{1,0:T(8,128)(2,1)}, u32[]{:S(2)}) copy-start(bf16[256,512]{1,0:T(8,128)(2,1)} %embeds.3) | copy-start | bytes 786436
  1.1 6.5 %collective-permute-start = (bf16[528,128]{1,0:T(8,128)(2,1)S(1)}, bf16[528,128]{1,0:T(8,128)(2,1)S(1)}, u32[]{:S(2)}, u32[]{:S(2)}) collective-permute-start(bf16[528,128]{1,0:T(8,128)(2,1)S(1)} %pack_first.1.first), channel_id=1, source_target_pairs={{0,5},{1,4},{4,8},{5,9},{8,12},{9,13},{12,14},{13,15},{14,10},{15,... | collective-permute-start | bytes 405512 | tf_op jit(solution)/shard_map/ppermute | solution.py:245
  3.6 6.5 %collective-permute-start.2 = (bf16[528,128]{1,0:T(8,128)(2,1)S(1)}, bf16[528,128]{1,0:T(8,128)(2,1)S(1)}, u32[]{:S(2)}, u32[]{:S(2)}) collective-permute-start(bf16[528,128]{1,0:T(8,128)(2,1)S(1)} %pack_first.1.first), channel_id=1, source_target_pairs={{0,3},{1,2},{4,0},{5,1},{8,4},{9,5},{12,9},{13,8},{14,13},{15,12},... | collective-permute-start | bytes 405512 | tf_op jit(solution)/shard_map/ppermute | solution.py:245
  3.8 6.6 %collective-permute-start.1 = (bf16[512,128]{1,0:T(8,128)(2,1)S(1)}, bf16[512,128]{1,0:T(8,128)(2,1)S(1)}, u32[]{:S(2)}, u32[]{:S(2)}) collective-permute-start(bf16[512,128]{1,0:T(8,128)(2,1)S(1)} %get-tuple-element.16), channel_id=1, source_target_pairs={{0,5},{1,4},{4,8},{5,9},{8,12},{9,13},{12,14},{13,15},{14,10},{15,... | collective-permute-start | bytes 393224 | tf_op jit(solution)/shard_map/ppermute | solution.py:245
  5.9 7.0 %collective-permute-start.3 = (bf16[512,128]{1,0:T(8,128)(2,1)S(1)}, bf16[512,128]{1,0:T(8,128)(2,1)S(1)}, u32[]{:S(2)}, u32[]{:S(2)}) collective-permute-start(bf16[512,128]{1,0:T(8,128)(2,1)S(1)} %get-tuple-element.16), channel_id=1, source_target_pairs={{0,3},{1,2},{4,0},{5,1},{8,4},{9,5},{12,9},{13,8},{14,13},{15,12},... | collective-permute-start | bytes 393224 | tf_op jit(solution)/shard_map/ppermute | solution.py:245
  7.6 6.4 %collective-permute-start.5 = (bf16[528,128]{1,0:T(8,128)(2,1)S(1)}, bf16[528,128]{1,0:T(8,128)(2,1)S(1)}, u32[]{:S(2)}, u32[]{:S(2)}) collective-permute-start(bf16[528,128]{1,0:T(8,128)(2,1)S(1)} %collective-permute-done.prev_a), channel_id=1, source_target_pairs={{0,4},{1,5},{4,8},{5,9},{8,12},{9,13},{12,14},{13,15},{14,10},{15,... | collective-permute-start | bytes 405512 | tf_op jit(solution)/shard_map/ppermute | solution.py:245
  10.1 5.5 %collective-permute-start.6 = (bf16[528,128]{1,0:T(8,128)(2,1)S(1)}, bf16[528,128]{1,0:T(8,128)(2,1)S(1)}, u32[]{:S(2)}, u32[]{:S(2)}) collective-permute-start(bf16[528,128]{1,0:T(8,128)(2,1)S(1)} %collective-permute-done.2.succ_a), channel_id=1, source_target_pairs={{0,2},{1,3},{4,0},{5,1},{8,4},{9,5},{12,8},{13,9},{14,12},{15,13},... | collective-permute-start | bytes 405512 | tf_op jit(solution)/shard_map/ppermute | solution.py:245
  10.4 6.0 %collective-permute-start.7 = (bf16[512,128]{1,0:T(8,128)(2,1)S(1)}, bf16[512,128]{1,0:T(8,128)(2,1)S(1)}, u32[]{:S(2)}, u32[]{:S(2)}) collective-permute-start(bf16[512,128]{1,0:T(8,128)(2,1)S(1)} %collective-permute-done.1.prev_b), channel_id=1, source_target_pairs={{0,4},{1,5},{4,8},{5,9},{8,12},{9,13},{12,14},{13,15},{14,10},{15,... | collective-permute-start | bytes 393224 | tf_op jit(solution)/shard_map/ppermute | solution.py:245
  12.9 5.4 %collective-permute-start.8 = (bf16[512,128]{1,0:T(8,128)(2,1)S(1)}, bf16[512,128]{1,0:T(8,128)(2,1)S(1)}, u32[]{:S(2)}, u32[]{:S(2)}) collective-permute-start(bf16[512,128]{1,0:T(8,128)(2,1)S(1)} %collective-permute-done.3.succ_b), channel_id=1, source_target_pairs={{0,2},{1,3},{4,0},{5,1},{8,4},{9,5},{12,8},{13,9},{14,12},{15,13},... | collective-permute-start | bytes 393224 | tf_op jit(solution)/shard_map/ppermute | solution.py:245
  13.3 5.4 %collective-permute-start.4 = (bf16[3,1040,128]{2,1,0:T(8,128)(2,1)S(1)}, bf16[3,1040,128]{2,1,0:T(8,128)(2,1)S(1)}, u32[]{:S(2)}, u32[]{:S(2)}) collective-permute-start(bf16[3,1040,128]{2,1,0:T(8,128)(2,1)S(1)} %get-tuple-element.17), channel_id=1, source_target_pairs={{0,1},{1,0},{4,5},{5,4},{8,9},{9,8},{12,13},{13,12},{14,15},{15,14... | collective-permute-start | bytes 2396168 | tf_op jit(solution)/shard_map/ppermute | solution.py:245
  19.1 4.0 %collective-permute-start.9 = (f32[1,256]{1,0:T(1,128)S(1)}, f32[1,256]{1,0:T(1,128)S(1)}, u32[]{:S(2)}, u32[]{:S(2)}) collective-permute-start(f32[1,256]{1,0:T(1,128)S(1)} %get-tuple-element.23), channel_id=1, source_target_pairs={{0,6},{1,7},{4,3},{5,2},{8,1},{9,0},{12,4},{13,5},{14,8},{15,9},{1... | collective-permute-start | bytes 3080 | tf_op jit(solution)/shard_map/ppermute | solution.py:245
  20.6 3.9 %collective-permute-start.10 = (f32[1,256]{1,0:T(1,128)S(1)}, f32[1,256]{1,0:T(1,128)S(1)}, u32[]{:S(2)}, u32[]{:S(2)}) collective-permute-start(f32[1,256]{1,0:T(1,128)S(1)} %get-tuple-element.24), channel_id=1, source_target_pairs={{0,8},{1,9},{4,13},{5,12},{8,15},{9,14},{12,11},{13,10},{14,7},{15... | collective-permute-start | bytes 3080 | tf_op jit(solution)/shard_map/ppermute | solution.py:245

commit v9 on v8

--- a/solution.py
+++ b/solution.py
@@ -24,9 +24,9 @@
 LABEL_ROWS = 16
 VMEM_BYTES = 32 * 2**20
 NEAR_COST = 1
-FIRST_COST = 5
+FIRST_COST = 200
 BACK_COST = 2
-SECOND_COST = 200
+LAST_COST = 5
 
 
 def put_unit(unit, chunk, at, size):
@@ -156,32 +156,28 @@
     found[...] = best_of(queries, queries, *near)
 
 
-def far_back_kernel(own, succ_a, succ_b, back_a, ahead_a, back_b, found, back, ahead):
+def far_back_kernel(own, others, succ_a, succ_b, back_a, ahead_a, back_b, found, back, ahead):
     rows = found.shape[1]
     half = rows // 2
-    rest, first = second_half(back_a, back_b, rows), first_half(ahead_a, rows)
-    back[:, :half] = found[:, :half]
-    back[:, half:] = best_of(rest, packed(own, rows), whole(succ_a, succ_b, rows), first)
-    ahead[...] = jnp.maximum(found[:, half:], best_of(first, rest))
-
-
-def far_second_kernel(own, prev_a, prev_b, back_a, ahead_a, back_b, ahead_b, *refs):
+    prev_other, succ_other = packed(others.at[0], rows), packed(others.at[1], rows)
+    first, rest = first_half(back_a, rows), second_half(back_a, back_b, rows)
+    first_ahead = first_half(ahead_a, rows)
+    keys = packed(own, rows), whole(succ_a, succ_b, rows), first_ahead
+    both = best_of(joined(first, rest), succ_other)
+    back[:, :half] = jnp.maximum(found[:, :half], both[:, :half])
+    back[:, half:] = jnp.maximum(best_of(rest, *keys), both[:, half:])
+    ahead[...] = jnp.maximum(found[:, half:], best_of(first_ahead, rest, prev_other))
+
+
+def far_last_kernel(own, others, prev_a, prev_b, back_a, ahead_a, back_b, ahead_b, *refs):
     back_found, ahead_found, to_back, to_ahead = refs
     rows = to_back.shape[1]
     half = rows // 2
     back, rest = whole(back_a, back_b, rows), second_half(ahead_a, ahead_b, rows)
+    keys = packed(own, rows), whole(prev_a, prev_b, rows), packed(others.at[0], rows), back
     to_back[...] = jnp.maximum(back_found[...], best_of(back, rest))
     to_ahead[:, :half] = ahead_found[...]
-    to_ahead[:, half:] = best_of(rest, packed(own, rows), whole(prev_a, prev_b, rows), back)
-
-
-def far_other_kernel(others, back_a, ahead_a, back_b, ahead_b, *refs):
-    back_found, ahead_found, to_back, to_ahead = refs
-    rows = to_back.shape[1]
-    back, ahead = whole(back_a, back_b, rows), whole(ahead_a, ahead_b, rows)
-    prev, succ = packed(others.at[0], rows), packed(others.at[1], rows)
-    to_back[...] = jnp.maximum(back_found[...], best_of(back, succ))
-    to_ahead[...] = jnp.maximum(ahead_found[...], best_of(ahead, prev))
+    to_ahead[:, half:] = best_of(rest, *keys)
 
 
 def own_kernel(own, others, back_a, ahead_a, back_b, ahead_b, near, mine):
@@ -284,10 +280,14 @@
         far_first_kernel, [own, *prev, *succ, back_a, ahead_a], [line], FIRST_COST
     )
     found = kernel_call(
-        far_back_kernel, [own, *succ, back_a, ahead_a, back_b, found], [line, half_line], BACK_COST
-    )
-    found = kernel_call(far_second_kernel, [own, *prev, *far, *found], [line] * 2, SECOND_COST)
-    to_back, to_ahead = kernel_call(far_other_kernel, [others, *far, *found], [line] * 2, 2)
+        far_back_kernel,
+        [own, others, *succ, back_a, ahead_a, back_b, found],
+        [line, half_line],
+        BACK_COST,
+    )
+    to_back, to_ahead = kernel_call(
+        far_last_kernel, [own, others, *prev, *far, *found], [line] * 2, LAST_COST
+    )
     (mine,) = kernel_call(own_kernel, [own, others, *far, mine], [line], 5)
     best = jnp.maximum(
         mine, jnp.maximum(send(to_back, "home_back"), send(to_ahead, "home_ahead"))

time: 25.2 us -> 24.9 us (0.988)
    pallas_call x7 -> x6, Pallas kernels: 2.82 us -> 2.68 us  [kernel_call(): pl.pallas_call(kernel, out_shape=outputs, in_specs=[vmem] * len(inputs),...]
  transfers between devices with their start and end apart: 11 -> 11, of which waited for: 8 -> 8; matrix products, arithmetic and copies ran while one was open for 0% -> 0% of each run, Pallas kernels for 10% -> 9%
where the time goes in v9:
time: 24.9 us; the launch traced here: 24.8 us
  starting transfers between devices  12.9 us (52%)
  waiting for transfers between devices  7.49 us (30%)
  Pallas kernels  3.79 us (15%)
  other arithmetic  0.57 us (2%)
    ppermute x11, starting transfers between devices, send(): return lax.ppermute(value, GROUP, perms[name])  12.9 us
    ppermute x11, waiting for transfers between devices, send(): return lax.ppermute(value, GROUP, perms[name])  7.49 us
    pallas_call x6, Pallas kernels, kernel_call(): pl.pallas_call(kernel, out_shape=outputs, in_specs=[vmem] * len(inputs),...  2.68 us
    pallas_call x1, Pallas kernels, on_ring(): pl.pallas_call(pack_first_kernel, out_shape=chunk(half, True), in_specs=[...  1.1 us
    max x1, other arithmetic, on_ring(): jnp.maximum(mine, jnp.maximum(send(to_back, 'home_back'), send(to_ahead,...  0.57 us
  transfers between devices with their start and end apart: 11, of which 8 were waited for; matrix products, arithmetic and copies ran while one was open for 0% of the time, Pallas kernels for 9%

profile of v9, /device:TPU:0, one launch (start us, length us, event | category | flops | bytes accessed | tf_op | source)
XLA Modules:
  0.0 24.8 jit_solution(12235640351779098927)
XLA Ops:
  0.0 0.0 copy-start
  0.0 1.1 %pack_first.1.first = bf16[528,128]{1,0:T(8,128)(2,1)S(1)} custom-call(bf16[256,512]{1,0:T(8,128)(2,1)} %embeds.3, s32[1,256]{1,0:T(1,128)} %bitcast.2), custom_call_target="tpu_custom_call" | custom-call | tf_op jit(solution)/shard_map/pack_first/pallas_call | solution.py:252
  1.1 2.5 %collective-permute-start = (bf16[528,128]{1,0:T(8,128)(2,1)S(1)}, bf16[528,128]{1,0:T(8,128)(2,1)S(1)}, u32[]{:S(2)}, u32[]{:S(2)}) collective-permute-start(bf16[528,128]{1,0:T(8,128)(2,1)S(1)} %pack_first.1.first), channel_id=1, source_target_pairs={{0,5},{1,4},{4,8},{5,9},{8,12},{9,13},{12,14},{13,15},{14,10},{15,... | collective-permute-start | bytes 405512 | tf_op jit(solution)/shard_map/ppermute | solution.py:241
  3.6 0.0 collective-permute-start.2
  3.6 0.0 copy-done
  3.6 0.1 pack_second_kernel.1
  3.8 2.1 %collective-permute-start.1 = (bf16[512,128]{1,0:T(8,128)(2,1)S(1)}, bf16[512,128]{1,0:T(8,128)(2,1)S(1)}, u32[]{:S(2)}, u32[]{:S(2)}) collective-permute-start(bf16[512,128]{1,0:T(8,128)(2,1)S(1)} %get-tuple-element.14), channel_id=1, source_target_pairs={{0,5},{1,4},{4,8},{5,9},{8,12},{9,13},{12,14},{13,15},{14,10},{15,... | collective-permute-start | bytes 393224 | tf_op jit(solution)/shard_map/ppermute | solution.py:241
  5.9 0.3 %collective-permute-start.3 = (bf16[512,128]{1,0:T(8,128)(2,1)S(1)}, bf16[512,128]{1,0:T(8,128)(2,1)S(1)}, u32[]{:S(2)}, u32[]{:S(2)}) collective-permute-start(bf16[512,128]{1,0:T(8,128)(2,1)S(1)} %get-tuple-element.14), channel_id=1, source_target_pairs={{0,3},{1,2},{4,0},{5,1},{8,4},{9,5},{12,9},{13,8},{14,13},{15,12},... | collective-permute-start | bytes 393224 | tf_op jit(solution)/shard_map/ppermute | solution.py:241
  6.1 1.5 %collective-permute-done.prev_a = bf16[528,128]{1,0:T(8,128)(2,1)S(1)} collective-permute-done((bf16[528,128]{1,0:T(8,128)(2,1)S(1)}, bf16[528,128]{1,0:T(8,128)(2,1)S(1)}, u32[]{:S(2)}, u32[]{:S(2)}) %collective-permute-start) | collective-permute-done | bytes 135200 | tf_op jit(solution)/shard_map/ppermute | solution.py:241
  7.6 2.5 %collective-permute-start.5 = (bf16[528,128]{1,0:T(8,128)(2,1)S(1)}, bf16[528,128]{1,0:T(8,128)(2,1)S(1)}, u32[]{:S(2)}, u32[]{:S(2)}) collective-permute-start(bf16[528,128]{1,0:T(8,128)(2,1)S(1)} %collective-permute-done.prev_a), channel_id=1, source_target_pairs={{0,4},{1,5},{4,8},{5,9},{8,12},{9,13},{12,14},{13,15},{14,10},{15,... | collective-permute-start | bytes 405512 | tf_op jit(solution)/shard_map/ppermute | solution.py:241
  10.1 0.0 collective-permute-done.2.succ_a
  10.1 0.0 collective-permute-start.6
  10.1 0.3 %collective-permute-done.1.prev_b = bf16[512,128]{1,0:T(8,128)(2,1)S(1)} collective-permute-done((bf16[512,128]{1,0:T(8,128)(2,1)S(1)}, bf16[512,128]{1,0:T(8,128)(2,1)S(1)}, u32[]{:S(2)}, u32[]{:S(2)}) %collective-permute-start.1) | collective-permute-done | bytes 131104 | tf_op jit(solution)/shard_map/ppermute | solution.py:241
  10.4 2.5 %collective-permute-start.7 = (bf16[512,128]{1,0:T(8,128)(2,1)S(1)}, bf16[512,128]{1,0:T(8,128)(2,1)S(1)}, u32[]{:S(2)}, u32[]{:S(2)}) collective-permute-start(bf16[512,128]{1,0:T(8,128)(2,1)S(1)} %collective-permute-done.1.prev_b), channel_id=1, source_target_pairs={{0,4},{1,5},{4,8},{5,9},{8,12},{9,13},{12,14},{13,15},{14,10},{15,... | collective-permute-start | bytes 393224 | tf_op jit(solution)/shard_map/ppermute | solution.py:241
  12.9 0.0 collective-permute-done.3.succ_b
  12.9 0.0 collective-permute-start.8
  12.9 0.5 %near_kernel.1 = (f32[1,256]{1,0:T(1,128)S(1)}, bf16[3,1040,128]{2,1,0:T(8,128)(2,1)S(1)}) custom-call(bf16[1040,128]{1,0:T(8,128)(2,1)S(1)} %get-tuple-element.13.own, bf16[528,128]{1,0:T(8,128)(2,1)S(1)} %collective-permute-done.prev_a, bf16[512,128]{1,0:T(8,128)(2,1)S(1)} %collective-permute-done.1.prev_b, ...), custom_call_target="tpu_custom_call" | custom-call | flops 67108864 | bytes 1048576 | tf_op jit(solution)/shard_map/near_kernel/pallas_call | solution.py:222
  13.4 0.1 collective-permute-start.4
  13.4 0.5 %collective-permute-done.5.back_a = bf16[528,128]{1,0:T(8,128)(2,1)S(1)} collective-permute-done((bf16[528,128]{1,0:T(8,128)(2,1)S(1)}, bf16[528,128]{1,0:T(8,128)(2,1)S(1)}, u32[]{:S(2)}, u32[]{:S(2)}) %collective-permute-start.5) | collective-permute-done | bytes 135200 | tf_op jit(solution)/shard_map/ppermute | solution.py:241
  14.0 1.6 %collective-permute-done.6.ahead_a = bf16[528,128]{1,0:T(8,128)(2,1)S(1)} collective-permute-done((bf16[528,128]{1,0:T(8,128)(2,1)S(1)}, bf16[528,128]{1,0:T(8,128)(2,1)S(1)}, u32[]{:S(2)}, u32[]{:S(2)}) %collective-permute-start.6) | collective-permute-done | bytes 135200 | tf_op jit(solution)/shard_map/ppermute | solution.py:241
  15.6 0.5 %far_first_kernel.1.found = f32[1,256]{1,0:T(1,128)S(1)} custom-call(bf16[1040,128]{1,0:T(8,128)(2,1)S(1)} %get-tuple-element.13.own, bf16[528,128]{1,0:T(8,128)(2,1)S(1)} %collective-permute-done.prev_a, bf16[512,128]{1,0:T(8,128)(2,1)S(1)} %collective-permute-done.1.prev_b, bf16[528,128]{1,0:T(8,128)(2,1)S(1)} %collective-permute-done.2.succ_a, ...), custom_call_target="tpu_custom_call" | custom-call | flops 13421772800 | bytes 1048576 | tf_op jit(solution)/shard_map/far_first_kernel/pallas_call | solution.py:222
  16.1 0.3 %collective-permute-done.7.back_b = bf16[512,128]{1,0:T(8,128)(2,1)S(1)} collective-permute-done((bf16[512,128]{1,0:T(8,128)(2,1)S(1)}, bf16[512,128]{1,0:T(8,128)(2,1)S(1)}, u32[]{:S(2)}, u32[]{:S(2)}) %collective-permute-start.7) | collective-permute-done | bytes 131104 | tf_op jit(solution)/shard_map/ppermute | solution.py:241
  16.4 0.0 collective-permute-done.4.others
  16.4 0.5 %far_back_kernel.1 = (f32[1,256]{1,0:T(1,128)S(1)}, f32[1,128]{1,0:T(1,128)S(1)}) custom-call(bf16[1040,128]{1,0:T(8,128)(2,1)S(1)} %get-tuple-element.13.own, bf16[3,1040,128]{2,1,0:T(8,128)(2,1)S(1)} %collective-permute-done.4.others, bf16[528,128]{1,0:T(8,128)(2,1)S(1)} %collective-permute-done.2.succ_a, ...), custom_call_target="tpu_custom_call" | custom-call | flops 134217728 | bytes 1048576 | tf_op jit(solution)/shard_map/far_back_kernel/pallas_call | solution.py:222
  17.0 1.3 %collective-permute-done.8.ahead_b = bf16[512,128]{1,0:T(8,128)(2,1)S(1)} collective-permute-done((bf16[512,128]{1,0:T(8,128)(2,1)S(1)}, bf16[512,128]{1,0:T(8,128)(2,1)S(1)}, u32[]{:S(2)}, u32[]{:S(2)}) %collective-permute-start.8) | collective-permute-done | bytes 131104 | tf_op jit(solution)/shard_map/ppermute | solution.py:241
  18.3 0.5 %far_last_kernel.1 = (f32[1,256]{1,0:T(1,128)S(1)}, f32[1,256]{1,0:T(1,128)S(1)}) custom-call(bf16[1040,128]{1,0:T(8,128)(2,1)S(1)} %get-tuple-element.13.own, bf16[3,1040,128]{2,1,0:T(8,128)(2,1)S(1)} %collective-permute-done.4.others, bf16[528,128]{1,0:T(8,128)(2,1)S(1)} %collective-permute-done.prev_a, ...), custom_call_target="tpu_custom_call" | custom-call | flops 335544320 | bytes 1048576 | tf_op jit(solution)/shard_map/far_last_kernel/pallas_call | solution.py:222
  18.8 1.5 %collective-permute-start.9 = (f32[1,256]{1,0:T(1,128)S(1)}, f32[1,256]{1,0:T(1,128)S(1)}, u32[]{:S(2)}, u32[]{:S(2)}) collective-permute-start(f32[1,256]{1,0:T(1,128)S(1)} %get-tuple-element.19), channel_id=1, source_target_pairs={{0,6},{1,7},{4,3},{5,2},{8,1},{9,0},{12,4},{13,5},{14,8},{15,9},{1... | collective-permute-start | bytes 3080 | tf_op jit(solution)/shard_map/ppermute | solution.py:241
  20.3 1.5 %collective-permute-start.10 = (f32[1,256]{1,0:T(1,128)S(1)}, f32[1,256]{1,0:T(1,128)S(1)}, u32[]{:S(2)}, u32[]{:S(2)}) collective-permute-start(f32[1,256]{1,0:T(1,128)S(1)} %get-tuple-element.20), channel_id=1, source_target_pairs={{0,8},{1,9},{4,13},{5,12},{8,15},{9,14},{12,11},{13,10},{14,7},{15... | collective-permute-start | bytes 3080 | tf_op jit(solution)/shard_map/ppermute | solution.py:241
  21.8 0.6 %own_kernel.1 = f32[1,256]{1,0:T(1,128)S(1)} custom-call(bf16[1040,128]{1,0:T(8,128)(2,1)S(1)} %get-tuple-element.13.own, bf16[3,1040,128]{2,1,0:T(8,128)(2,1)S(1)} %collective-permute-done.4.others, bf16[528,128]{1,0:T(8,128)(2,1)S(1)} %collective-permute-done.5.back_a, bf16[528,128]{1,0:T(8,128)(2,1)S(1)} %collective-permute-done.6.ahead_a, ...), custom_call_target="tpu_custom_call" | custom-call | flops 335544320 | bytes 1048576 | tf_op jit(solution)/shard_map/own_kernel/pallas_call | solution.py:222
  22.4 0.4 %collective-permute-done.9 = f32[1,256]{1,0:T(1,128)S(1)} collective-permute-done((f32[1,256]{1,0:T(1,128)S(1)}, f32[1,256]{1,0:T(1,128)S(1)}, u32[]{:S(2)}, u32[]{:S(2)}) %collective-permute-start.9) | collective-permute-done | bytes 1056 | tf_op jit(solution)/shard_map/ppermute | solution.py:241
  22.8 1.4 %collective-permute-done.10 = f32[1,256]{1,0:T(1,128)S(1)} collective-permute-done((f32[1,256]{1,0:T(1,128)S(1)}, f32[1,256]{1,0:T(1,128)S(1)}, u32[]{:S(2)}, u32[]{:S(2)}) %collective-permute-start.10) | collective-permute-done | bytes 1056 | tf_op jit(solution)/shard_map/ppermute | solution.py:241
  24.2 0.6 %maximum_maximum_fusion = f32[1,256]{1,0:T(1,128)} fusion(f32[1,256]{1,0:T(1,128)S(1)} %own_kernel.1, f32[1,256]{1,0:T(1,128)S(1)} %collective-permute-done.9, f32[1,256]{1,0:T(1,128)S(1)} %collective-permute-done.10), kind=kLoop, calls=%fused_computation | loop fusion | flops 512 | bytes 4096 | tf_op jit(solution)/shard_map/max | solution.py:292
Async XLA Ops:
  0.0 3.6 %copy-start = (bf16[256,512]{1,0:T(8,128)(2,1)S(1)}, bf16[256,512]{1,0:T(8,128)(2,1)}, u32[]{:S(2)}) copy-start(bf16[256,512]{1,0:T(8,128)(2,1)} %embeds.3) | copy-start | bytes 786436
  1.1 6.5 %collective-permute-start = (bf16[528,128]{1,0:T(8,128)(2,1)S(1)}, bf16[528,128]{1,0:T(8,128)(2,1)S(1)}, u32[]{:S(2)}, u32[]{:S(2)}) collective-permute-start(bf16[528,128]{1,0:T(8,128)(2,1)S(1)} %pack_first.1.first), channel_id=1, source_target_pairs={{0,5},{1,4},{4,8},{5,9},{8,12},{9,13},{12,14},{13,15},{14,10},{15,... | collective-permute-start | bytes 405512 | tf_op jit(solution)/shard_map/ppermute | solution.py:241
  3.6 6.5 %collective-permute-start.2 = (bf16[528,128]{1,0:T(8,128)(2,1)S(1)}, bf16[528,128]{1,0:T(8,128)(2,1)S(1)}, u32[]{:S(2)}, u32[]{:S(2)}) collective-permute-start(bf16[528,128]{1,0:T(8,128)(2,1)S(1)} %pack_first.1.first), channel_id=1, source_target_pairs={{0,3},{1,2},{4,0},{5,1},{8,4},{9,5},{12,9},{13,8},{14,13},{15,12},... | collective-permute-start | bytes 405512 | tf_op jit(solution)/shard_map/ppermute | solution.py:241
  3.8 6.6 %collective-permute-start.1 = (bf16[512,128]{1,0:T(8,128)(2,1)S(1)}, bf16[512,128]{1,0:T(8,128)(2,1)S(1)}, u32[]{:S(2)}, u32[]{:S(2)}) collective-permute-start(bf16[512,128]{1,0:T(8,128)(2,1)S(1)} %get-tuple-element.14), channel_id=1, source_target_pairs={{0,5},{1,4},{4,8},{5,9},{8,12},{9,13},{12,14},{13,15},{14,10},{15,... | collective-permute-start | bytes 393224 | tf_op jit(solution)/shard_map/ppermute | solution.py:241
  5.9 7.0 %collective-permute-start.3 = (bf16[512,128]{1,0:T(8,128)(2,1)S(1)}, bf16[512,128]{1,0:T(8,128)(2,1)S(1)}, u32[]{:S(2)}, u32[]{:S(2)}) collective-permute-start(bf16[512,128]{1,0:T(8,128)(2,1)S(1)} %get-tuple-element.14), channel_id=1, source_target_pairs={{0,3},{1,2},{4,0},{5,1},{8,4},{9,5},{12,9},{13,8},{14,13},{15,12},... | collective-permute-start | bytes 393224 | tf_op jit(solution)/shard_map/ppermute | solution.py:241
  7.6 6.4 %collective-permute-start.5 = (bf16[528,128]{1,0:T(8,128)(2,1)S(1)}, bf16[528,128]{1,0:T(8,128)(2,1)S(1)}, u32[]{:S(2)}, u32[]{:S(2)}) collective-permute-start(bf16[528,128]{1,0:T(8,128)(2,1)S(1)} %collective-permute-done.prev_a), channel_id=1, source_target_pairs={{0,4},{1,5},{4,8},{5,9},{8,12},{9,13},{12,14},{13,15},{14,10},{15,... | collective-permute-start | bytes 405512 | tf_op jit(solution)/shard_map/ppermute | solution.py:241
  10.1 5.5 %collective-permute-start.6 = (bf16[528,128]{1,0:T(8,128)(2,1)S(1)}, bf16[528,128]{1,0:T(8,128)(2,1)S(1)}, u32[]{:S(2)}, u32[]{:S(2)}) collective-permute-start(bf16[528,128]{1,0:T(8,128)(2,1)S(1)} %collective-permute-done.2.succ_a), channel_id=1, source_target_pairs={{0,2},{1,3},{4,0},{5,1},{8,4},{9,5},{12,8},{13,9},{14,12},{15,13},... | collective-permute-start | bytes 405512 | tf_op jit(solution)/shard_map/ppermute | solution.py:241
  10.4 6.0 %collective-permute-start.7 = (bf16[512,128]{1,0:T(8,128)(2,1)S(1)}, bf16[512,128]{1,0:T(8,128)(2,1)S(1)}, u32[]{:S(2)}, u32[]{:S(2)}) collective-permute-start(bf16[512,128]{1,0:T(8,128)(2,1)S(1)} %collective-permute-done.1.prev_b), channel_id=1, source_target_pairs={{0,4},{1,5},{4,8},{5,9},{8,12},{9,13},{12,14},{13,15},{14,10},{15,... | collective-permute-start | bytes 393224 | tf_op jit(solution)/shard_map/ppermute | solution.py:241
  12.9 5.4 %collective-permute-start.8 = (bf16[512,128]{1,0:T(8,128)(2,1)S(1)}, bf16[512,128]{1,0:T(8,128)(2,1)S(1)}, u32[]{:S(2)}, u32[]{:S(2)}) collective-permute-start(bf16[512,128]{1,0:T(8,128)(2,1)S(1)} %collective-permute-done.3.succ_b), channel_id=1, source_target_pairs={{0,2},{1,3},{4,0},{5,1},{8,4},{9,5},{12,8},{13,9},{14,12},{15,13},... | collective-permute-start | bytes 393224 | tf_op jit(solution)/shard_map/ppermute | solution.py:241
  13.4 3.1 %collective-permute-start.4 = (bf16[3,1040,128]{2,1,0:T(8,128)(2,1)S(1)}, bf16[3,1040,128]{2,1,0:T(8,128)(2,1)S(1)}, u32[]{:S(2)}, u32[]{:S(2)}) collective-permute-start(bf16[3,1040,128]{2,1,0:T(8,128)(2,1)S(1)} %get-tuple-element.15), channel_id=1, source_target_pairs={{0,1},{1,0},{4,5},{5,4},{8,9},{9,8},{12,13},{13,12},{14,15},{15,14... | collective-permute-start | bytes 2396168 | tf_op jit(solution)/shard_map/ppermute | solution.py:241
  18.8 4.0 %collective-permute-start.9 = (f32[1,256]{1,0:T(1,128)S(1)}, f32[1,256]{1,0:T(1,128)S(1)}, u32[]{:S(2)}, u32[]{:S(2)}) collective-permute-start(f32[1,256]{1,0:T(1,128)S(1)} %get-tuple-element.19), channel_id=1, source_target_pairs={{0,6},{1,7},{4,3},{5,2},{8,1},{9,0},{12,4},{13,5},{14,8},{15,9},{1... | collective-permute-start | bytes 3080 | tf_op jit(solution)/shard_map/ppermute | solution.py:241
  20.3 3.9 %collective-permute-start.10 = (f32[1,256]{1,0:T(1,128)S(1)}, f32[1,256]{1,0:T(1,128)S(1)}, u32[]{:S(2)}, u32[]{:S(2)}) collective-permute-start(f32[1,256]{1,0:T(1,128)S(1)} %get-tuple-element.20), channel_id=1, source_target_pairs={{0,8},{1,9},{4,13},{5,12},{8,15},{9,14},{12,11},{13,10},{14,7},{15... | collective-permute-start | bytes 3080 | tf_op jit(solution)/shard_map/ppermute | solution.py:241

commit v10 on v9

--- a/solution.py
+++ b/solution.py
@@ -22,6 +22,7 @@
 
 LANES = 128
 LABEL_ROWS = 16
+PARTS = 4
 VMEM_BYTES = 32 * 2**20
 NEAR_COST = 1
 FIRST_COST = 200
@@ -38,10 +39,11 @@
 def pack_first_kernel(embeds, label, first, raw, line, sems):
     rows, width = embeds.shape
     half = rows // 2
-    copies = [
-        pltpu.make_async_copy(label, line, sems.at[0]),
-        pltpu.make_async_copy(embeds.at[pl.ds(0, half)], raw, sems.at[1]),
-    ]
+    step = half // PARTS
+    copies = [pltpu.make_async_copy(label, line, sems.at[PARTS])]
+    for i in range(PARTS):
+        part = pl.ds(i * step, step)
+        copies.append(pltpu.make_async_copy(embeds.at[part], raw.at[part], sems.at[i]))
     for copy in copies:
         copy.start()
     copies[0].wait()
@@ -51,8 +53,9 @@
         piece = line[:, i * LANES : (i + 1) * LANES].astype(jnp.float32)
         lines = jnp.where(row == i, piece, lines)
     first[half * width // LANES :, :] = lines.astype(jnp.bfloat16)
-    copies[1].wait()
-    put_unit(normalised(raw[...]), first, 0, half)
+    for i in range(PARTS):
+        copies[1 + i].wait()
+        put_unit(normalised(raw[i * step : (i + 1) * step, :]), first, i * step, half)
 
 
 def pack_second_kernel(embeds, first, second, both):
@@ -121,23 +124,33 @@
 
 
 def best_of(queries, *all_keys):
-    best = None
+    best = jnp.full((queries.rows, LANES), -1.0, jnp.float32)
+    column = queries.column()
     for keys in all_keys:
         sims = lax.dot_general(
-            keys.unit, queries.unit, (((1,), (1,)), ((), ())), preferred_element_type=jnp.float32
+            queries.unit, keys.unit, (((1,), (1,)), ((), ())), preferred_element_type=jnp.float32
         )
-        pieces = []
-        for start in range(0, queries.rows, LANES):
-            keep = keys.column() == queries.label[:, start : start + LANES]
+        for start in range(0, keys.rows, LANES):
+            keep = column == keys.label[:, start : start + LANES]
             if keys is queries:
                 row = lax.broadcasted_iota(jnp.int32, keep.shape, 0)
-                column = lax.broadcasted_iota(jnp.int32, keep.shape, 1) + start
-                keep = keep & (row != column)
+                lane = lax.broadcasted_iota(jnp.int32, keep.shape, 1) + start
+                keep = keep & (row != lane)
             found = jnp.where(keep, sims[:, start : start + LANES], -1.0)
-            pieces.append(jnp.max(found, axis=0, keepdims=True))
-        found = jnp.concatenate(pieces, axis=1)
-        best = found if best is None else jnp.maximum(best, found)
-    return best
+            best = jnp.maximum(best, found)
+    return jnp.max(jnp.transpose(best), axis=0, keepdims=True)
+
+
+def best_of_each(queries, keys):
+    sims = lax.dot_general(
+        keys.unit, queries.unit, (((1,), (1,)), ((), ())), preferred_element_type=jnp.float32
+    )
+    pieces = []
+    for start in range(0, queries.rows, LANES):
+        keep = keys.column() == queries.label[:, start : start + LANES]
+        found = jnp.where(keep, sims[:, start : start + LANES], -1.0)
+        pieces.append(jnp.max(found, axis=0, keepdims=True))
+    return jnp.concatenate(pieces, axis=1)
 
 
 def near_kernel(own, prev_a, prev_b, succ_a, succ_b, mine, bundle):
@@ -175,7 +188,7 @@
     half = rows // 2
     back, rest = whole(back_a, back_b, rows), second_half(ahead_a, ahead_b, rows)
     keys = packed(own, rows), whole(prev_a, prev_b, rows), packed(others.at[0], rows), back
-    to_back[...] = jnp.maximum(back_found[...], best_of(back, rest))
+    to_back[...] = jnp.maximum(back_found[...], best_of_each(back, rest))
     to_ahead[:, :half] = ahead_found[...]
     to_ahead[:, half:] = best_of(rest, *keys)
 
@@ -257,7 +270,7 @@
         scratch_shapes=[
             pltpu.VMEM((half, width), jnp.bfloat16),
             pltpu.VMEM((1, rows), jnp.int32),
-            pltpu.SemaphoreType.DMA((2,)),
+            pltpu.SemaphoreType.DMA((PARTS + 1,)),
         ],
         compiler_params=pltpu.CompilerParams(vmem_limit_bytes=VMEM_BYTES),
         name="pack_first",

time: 24.9 us -> 25.1 us (level)
  Pallas kernels: 3.79 us -> 4.27 us
  waiting for transfers between devices: 7.49 us -> 7.18 us
    pallas_call x6, Pallas kernels: 2.68 us -> 3.02 us  [kernel_call(): pl.pallas_call(kernel, out_shape=outputs, in_specs=[vmem] * len(inputs),...]
    ppermute x11, waiting for transfers between devices: 7.49 us -> 7.18 us  [send(): return lax.ppermute(value, GROUP, perms[name])]
  transfers between devices with their start and end apart: 11 -> 11, of which waited for: 8 -> 8; matrix products, arithmetic and copies ran while one was open for 0% -> 0% of each run, Pallas kernels for 9% -> 10%
where the time goes in v10:
time: 25.1 us; the launch traced here: 24.9 us
  starting transfers between devices  12.9 us (51%)
  waiting for transfers between devices  7.18 us (29%)
  Pallas kernels  4.27 us (17%)
  other arithmetic  0.57 us (2%)
    ppermute x11, starting transfers between devices, send(): return lax.ppermute(value, GROUP, perms[name])  12.9 us
    ppermute x11, waiting for transfers between devices, send(): return lax.ppermute(value, GROUP, perms[name])  7.18 us
    pallas_call x6, Pallas kernels, kernel_call(): pl.pallas_call(kernel, out_shape=outputs, in_specs=[vmem] * len(inputs),...  3.02 us
    pallas_call x1, Pallas kernels, on_ring(): pl.pallas_call(pack_first_kernel, out_shape=chunk(half, True), in_specs=[...  1.25 us
    max x1, other arithmetic, on_ring(): jnp.maximum(mine, jnp.maximum(send(to_back, 'home_back'), send(to_ahead,...  0.57 us
  transfers between devices with their start and end apart: 11, of which 8 were waited for; matrix products, arithmetic and copies ran while one was open for 0% of the time, Pallas kernels for 10%

profile of v10, /device:TPU:0, one launch (start us, length us, event | category | flops | bytes accessed | tf_op | source)
XLA Modules:
  0.0 24.9 jit_solution(9116281429364037814)
XLA Ops:
  0.0 0.0 copy-start
  0.0 1.3 %pack_first.1.first = bf16[528,128]{1,0:T(8,128)(2,1)S(1)} custom-call(bf16[256,512]{1,0:T(8,128)(2,1)} %embeds.3, s32[1,256]{1,0:T(1,128)} %bitcast.2), custom_call_target="tpu_custom_call" | custom-call | tf_op jit(solution)/shard_map/pack_first/pallas_call | solution.py:265
  1.3 2.5 %collective-permute-start = (bf16[528,128]{1,0:T(8,128)(2,1)S(1)}, bf16[528,128]{1,0:T(8,128)(2,1)S(1)}, u32[]{:S(2)}, u32[]{:S(2)}) collective-permute-start(bf16[528,128]{1,0:T(8,128)(2,1)S(1)} %pack_first.1.first), channel_id=1, source_target_pairs={{0,5},{1,4},{4,8},{5,9},{8,12},{9,13},{12,14},{13,15},{14,10},{15,... | collective-permute-start | bytes 405512 | tf_op jit(solution)/shard_map/ppermute | solution.py:254
  3.8 0.0 collective-permute-start.2
  3.8 0.0 copy-done
  3.8 0.1 pack_second_kernel.1
  3.9 2.1 %collective-permute-start.1 = (bf16[512,128]{1,0:T(8,128)(2,1)S(1)}, bf16[512,128]{1,0:T(8,128)(2,1)S(1)}, u32[]{:S(2)}, u32[]{:S(2)}) collective-permute-start(bf16[512,128]{1,0:T(8,128)(2,1)S(1)} %get-tuple-element.14), channel_id=1, source_target_pairs={{0,5},{1,4},{4,8},{5,9},{8,12},{9,13},{12,14},{13,15},{14,10},{15,... | collective-permute-start | bytes 393224 | tf_op jit(solution)/shard_map/ppermute | solution.py:254
  6.0 0.3 %collective-permute-start.3 = (bf16[512,128]{1,0:T(8,128)(2,1)S(1)}, bf16[512,128]{1,0:T(8,128)(2,1)S(1)}, u32[]{:S(2)}, u32[]{:S(2)}) collective-permute-start(bf16[512,128]{1,0:T(8,128)(2,1)S(1)} %get-tuple-element.14), channel_id=1, source_target_pairs={{0,3},{1,2},{4,0},{5,1},{8,4},{9,5},{12,9},{13,8},{14,13},{15,12},... | collective-permute-start | bytes 393224 | tf_op jit(solution)/shard_map/ppermute | solution.py:254
  6.3 1.5 %collective-permute-done.prev_a = bf16[528,128]{1,0:T(8,128)(2,1)S(1)} collective-permute-done((bf16[528,128]{1,0:T(8,128)(2,1)S(1)}, bf16[528,128]{1,0:T(8,128)(2,1)S(1)}, u32[]{:S(2)}, u32[]{:S(2)}) %collective-permute-start) | collective-permute-done | bytes 135200 | tf_op jit(solution)/shard_map/ppermute | solution.py:254
  7.8 2.5 %collective-permute-start.5 = (bf16[528,128]{1,0:T(8,128)(2,1)S(1)}, bf16[528,128]{1,0:T(8,128)(2,1)S(1)}, u32[]{:S(2)}, u32[]{:S(2)}) collective-permute-start(bf16[528,128]{1,0:T(8,128)(2,1)S(1)} %collective-permute-done.prev_a), channel_id=1, source_target_pairs={{0,4},{1,5},{4,8},{5,9},{8,12},{9,13},{12,14},{13,15},{14,10},{15,... | collective-permute-start | bytes 405512 | tf_op jit(solution)/shard_map/ppermute | solution.py:254
  10.2 0.0 collective-permute-done.2.succ_a
  10.3 0.0 collective-permute-start.6
  10.3 0.3 %collective-permute-done.1.prev_b = bf16[512,128]{1,0:T(8,128)(2,1)S(1)} collective-permute-done((bf16[512,128]{1,0:T(8,128)(2,1)S(1)}, bf16[512,128]{1,0:T(8,128)(2,1)S(1)}, u32[]{:S(2)}, u32[]{:S(2)}) %collective-permute-start.1) | collective-permute-done | bytes 131104 | tf_op jit(solution)/shard_map/ppermute | solution.py:254
  10.6 2.5 %collective-permute-start.7 = (bf16[512,128]{1,0:T(8,128)(2,1)S(1)}, bf16[512,128]{1,0:T(8,128)(2,1)S(1)}, u32[]{:S(2)}, u32[]{:S(2)}) collective-permute-start(bf16[512,128]{1,0:T(8,128)(2,1)S(1)} %collective-permute-done.1.prev_b), channel_id=1, source_target_pairs={{0,4},{1,5},{4,8},{5,9},{8,12},{9,13},{12,14},{13,15},{14,10},{15,... | collective-permute-start | bytes 393224 | tf_op jit(solution)/shard_map/ppermute | solution.py:254
  13.0 0.0 collective-permute-done.3.succ_b
  13.0 0.0 collective-permute-start.8
  13.0 0.6 %near_kernel.1 = (f32[1,256]{1,0:T(1,128)S(1)}, bf16[3,1040,128]{2,1,0:T(8,128)(2,1)S(1)}) custom-call(bf16[1040,128]{1,0:T(8,128)(2,1)S(1)} %get-tuple-element.13.own, bf16[528,128]{1,0:T(8,128)(2,1)S(1)} %collective-permute-done.prev_a, bf16[512,128]{1,0:T(8,128)(2,1)S(1)} %collective-permute-done.1.prev_b, ...), custom_call_target="tpu_custom_call" | custom-call | flops 67108864 | bytes 1048576 | tf_op jit(solution)/shard_map/near_kernel/pallas_call | solution.py:235
  13.6 0.1 collective-permute-start.4
  13.7 0.5 %collective-permute-done.5.back_a = bf16[528,128]{1,0:T(8,128)(2,1)S(1)} collective-permute-done((bf16[528,128]{1,0:T(8,128)(2,1)S(1)}, bf16[528,128]{1,0:T(8,128)(2,1)S(1)}, u32[]{:S(2)}, u32[]{:S(2)}) %collective-permute-start.5) | collective-permute-done | bytes 135200 | tf_op jit(solution)/shard_map/ppermute | solution.py:254
  14.1 1.6 %collective-permute-done.6.ahead_a = bf16[528,128]{1,0:T(8,128)(2,1)S(1)} collective-permute-done((bf16[528,128]{1,0:T(8,128)(2,1)S(1)}, bf16[528,128]{1,0:T(8,128)(2,1)S(1)}, u32[]{:S(2)}, u32[]{:S(2)}) %collective-permute-start.6) | collective-permute-done | bytes 135200 | tf_op jit(solution)/shard_map/ppermute | solution.py:254
  15.8 0.5 %far_first_kernel.1.found = f32[1,256]{1,0:T(1,128)S(1)} custom-call(bf16[1040,128]{1,0:T(8,128)(2,1)S(1)} %get-tuple-element.13.own, bf16[528,128]{1,0:T(8,128)(2,1)S(1)} %collective-permute-done.prev_a, bf16[512,128]{1,0:T(8,128)(2,1)S(1)} %collective-permute-done.1.prev_b, bf16[528,128]{1,0:T(8,128)(2,1)S(1)} %collective-permute-done.2.succ_a, ...), custom_call_target="tpu_custom_call" | custom-call | flops 13421772800 | bytes 1048576 | tf_op jit(solution)/shard_map/far_first_kernel/pallas_call | solution.py:235
  16.3 0.3 %collective-permute-done.7.back_b = bf16[512,128]{1,0:T(8,128)(2,1)S(1)} collective-permute-done((bf16[512,128]{1,0:T(8,128)(2,1)S(1)}, bf16[512,128]{1,0:T(8,128)(2,1)S(1)}, u32[]{:S(2)}, u32[]{:S(2)}) %collective-permute-start.7) | collective-permute-done | bytes 131104 | tf_op jit(solution)/shard_map/ppermute | solution.py:254
  16.6 0.0 collective-permute-done.4.others
  16.6 0.6 %far_back_kernel.1 = (f32[1,256]{1,0:T(1,128)S(1)}, f32[1,128]{1,0:T(1,128)S(1)}) custom-call(bf16[1040,128]{1,0:T(8,128)(2,1)S(1)} %get-tuple-element.13.own, bf16[3,1040,128]{2,1,0:T(8,128)(2,1)S(1)} %collective-permute-done.4.others, bf16[528,128]{1,0:T(8,128)(2,1)S(1)} %collective-permute-done.2.succ_a, ...), custom_call_target="tpu_custom_call" | custom-call | flops 134217728 | bytes 1048576 | tf_op jit(solution)/shard_map/far_back_kernel/pallas_call | solution.py:235
  17.2 1.3 %collective-permute-done.8.ahead_b = bf16[512,128]{1,0:T(8,128)(2,1)S(1)} collective-permute-done((bf16[512,128]{1,0:T(8,128)(2,1)S(1)}, bf16[512,128]{1,0:T(8,128)(2,1)S(1)}, u32[]{:S(2)}, u32[]{:S(2)}) %collective-permute-start.8) | collective-permute-done | bytes 131104 | tf_op jit(solution)/shard_map/ppermute | solution.py:254
  18.5 0.6 %far_last_kernel.1 = (f32[1,256]{1,0:T(1,128)S(1)}, f32[1,256]{1,0:T(1,128)S(1)}) custom-call(bf16[1040,128]{1,0:T(8,128)(2,1)S(1)} %get-tuple-element.13.own, bf16[3,1040,128]{2,1,0:T(8,128)(2,1)S(1)} %collective-permute-done.4.others, bf16[528,128]{1,0:T(8,128)(2,1)S(1)} %collective-permute-done.prev_a, ...), custom_call_target="tpu_custom_call" | custom-call | flops 335544320 | bytes 1048576 | tf_op jit(solution)/shard_map/far_last_kernel/pallas_call | solution.py:235
  19.0 1.5 %collective-permute-start.9 = (f32[1,256]{1,0:T(1,128)S(1)}, f32[1,256]{1,0:T(1,128)S(1)}, u32[]{:S(2)}, u32[]{:S(2)}) collective-permute-start(f32[1,256]{1,0:T(1,128)S(1)} %get-tuple-element.19), channel_id=1, source_target_pairs={{0,6},{1,7},{4,3},{5,2},{8,1},{9,0},{12,4},{13,5},{14,8},{15,9},{1... | collective-permute-start | bytes 3080 | tf_op jit(solution)/shard_map/ppermute | solution.py:254
  20.5 1.5 %collective-permute-start.10 = (f32[1,256]{1,0:T(1,128)S(1)}, f32[1,256]{1,0:T(1,128)S(1)}, u32[]{:S(2)}, u32[]{:S(2)}) collective-permute-start(f32[1,256]{1,0:T(1,128)S(1)} %get-tuple-element.20), channel_id=1, source_target_pairs={{0,8},{1,9},{4,13},{5,12},{8,15},{9,14},{12,11},{13,10},{14,7},{15... | collective-permute-start | bytes 3080 | tf_op jit(solution)/shard_map/ppermute | solution.py:254
  22.0 0.6 %own_kernel.1 = f32[1,256]{1,0:T(1,128)S(1)} custom-call(bf16[1040,128]{1,0:T(8,128)(2,1)S(1)} %get-tuple-element.13.own, bf16[3,1040,128]{2,1,0:T(8,128)(2,1)S(1)} %collective-permute-done.4.others, bf16[528,128]{1,0:T(8,128)(2,1)S(1)} %collective-permute-done.5.back_a, bf16[528,128]{1,0:T(8,128)(2,1)S(1)} %collective-permute-done.6.ahead_a, ...), custom_call_target="tpu_custom_call" | custom-call | flops 335544320 | bytes 1048576 | tf_op jit(solution)/shard_map/own_kernel/pallas_call | solution.py:235
  22.7 0.3 %collective-permute-done.9 = f32[1,256]{1,0:T(1,128)S(1)} collective-permute-done((f32[1,256]{1,0:T(1,128)S(1)}, f32[1,256]{1,0:T(1,128)S(1)}, u32[]{:S(2)}, u32[]{:S(2)}) %collective-permute-start.9) | collective-permute-done | bytes 1056 | tf_op jit(solution)/shard_map/ppermute | solution.py:254
  23.0 1.4 %collective-permute-done.10 = f32[1,256]{1,0:T(1,128)S(1)} collective-permute-done((f32[1,256]{1,0:T(1,128)S(1)}, f32[1,256]{1,0:T(1,128)S(1)}, u32[]{:S(2)}, u32[]{:S(2)}) %collective-permute-start.10) | collective-permute-done | bytes 1056 | tf_op jit(solution)/shard_map/ppermute | solution.py:254
  24.4 0.6 %maximum_maximum_fusion = f32[1,256]{1,0:T(1,128)} fusion(f32[1,256]{1,0:T(1,128)S(1)} %own_kernel.1, f32[1,256]{1,0:T(1,128)S(1)} %collective-permute-done.9, f32[1,256]{1,0:T(1,128)S(1)} %collective-permute-done.10), kind=kLoop, calls=%fused_computation | loop fusion | flops 512 | bytes 4096 | tf_op jit(solution)/shard_map/max | solution.py:305
Async XLA Ops:
  0.0 3.8 %copy-start = (bf16[256,512]{1,0:T(8,128)(2,1)S(1)}, bf16[256,512]{1,0:T(8,128)(2,1)}, u32[]{:S(2)}) copy-start(bf16[256,512]{1,0:T(8,128)(2,1)} %embeds.3) | copy-start | bytes 786436
  1.3 6.5 %collective-permute-start = (bf16[528,128]{1,0:T(8,128)(2,1)S(1)}, bf16[528,128]{1,0:T(8,128)(2,1)S(1)}, u32[]{:S(2)}, u32[]{:S(2)}) collective-permute-start(bf16[528,128]{1,0:T(8,128)(2,1)S(1)} %pack_first.1.first), channel_id=1, source_target_pairs={{0,5},{1,4},{4,8},{5,9},{8,12},{9,13},{12,14},{13,15},{14,10},{15,... | collective-permute-start | bytes 405512 | tf_op jit(solution)/shard_map/ppermute | solution.py:254
  3.8 6.5 %collective-permute-start.2 = (bf16[528,128]{1,0:T(8,128)(2,1)S(1)}, bf16[528,128]{1,0:T(8,128)(2,1)S(1)}, u32[]{:S(2)}, u32[]{:S(2)}) collective-permute-start(bf16[528,128]{1,0:T(8,128)(2,1)S(1)} %pack_first.1.first), channel_id=1, source_target_pairs={{0,3},{1,2},{4,0},{5,1},{8,4},{9,5},{12,9},{13,8},{14,13},{15,12},... | collective-permute-start | bytes 405512 | tf_op jit(solution)/shard_map/ppermute | solution.py:254
  3.9 6.6 %collective-permute-start.1 = (bf16[512,128]{1,0:T(8,128)(2,1)S(1)}, bf16[512,128]{1,0:T(8,128)(2,1)S(1)}, u32[]{:S(2)}, u32[]{:S(2)}) collective-permute-start(bf16[512,128]{1,0:T(8,128)(2,1)S(1)} %get-tuple-element.14), channel_id=1, source_target_pairs={{0,5},{1,4},{4,8},{5,9},{8,12},{9,13},{12,14},{13,15},{14,10},{15,... | collective-permute-start | bytes 393224 | tf_op jit(solution)/shard_map/ppermute | solution.py:254
  6.0 7.0 %collective-permute-start.3 = (bf16[512,128]{1,0:T(8,128)(2,1)S(1)}, bf16[512,128]{1,0:T(8,128)(2,1)S(1)}, u32[]{:S(2)}, u32[]{:S(2)}) collective-permute-start(bf16[512,128]{1,0:T(8,128)(2,1)S(1)} %get-tuple-element.14), channel_id=1, source_target_pairs={{0,3},{1,2},{4,0},{5,1},{8,4},{9,5},{12,9},{13,8},{14,13},{15,12},... | collective-permute-start | bytes 393224 | tf_op jit(solution)/shard_map/ppermute | solution.py:254
  7.8 6.4 %collective-permute-start.5 = (bf16[528,128]{1,0:T(8,128)(2,1)S(1)}, bf16[528,128]{1,0:T(8,128)(2,1)S(1)}, u32[]{:S(2)}, u32[]{:S(2)}) collective-permute-start(bf16[528,128]{1,0:T(8,128)(2,1)S(1)} %collective-permute-done.prev_a), channel_id=1, source_target_pairs={{0,4},{1,5},{4,8},{5,9},{8,12},{9,13},{12,14},{13,15},{14,10},{15,... | collective-permute-start | bytes 405512 | tf_op jit(solution)/shard_map/ppermute | solution.py:254
  10.3 5.5 %collective-permute-start.6 = (bf16[528,128]{1,0:T(8,128)(2,1)S(1)}, bf16[528,128]{1,0:T(8,128)(2,1)S(1)}, u32[]{:S(2)}, u32[]{:S(2)}) collective-permute-start(bf16[528,128]{1,0:T(8,128)(2,1)S(1)} %collective-permute-done.2.succ_a), channel_id=1, source_target_pairs={{0,2},{1,3},{4,0},{5,1},{8,4},{9,5},{12,8},{13,9},{14,12},{15,13},... | collective-permute-start | bytes 405512 | tf_op jit(solution)/shard_map/ppermute | solution.py:254
  10.6 6.0 %collective-permute-start.7 = (bf16[512,128]{1,0:T(8,128)(2,1)S(1)}, bf16[512,128]{1,0:T(8,128)(2,1)S(1)}, u32[]{:S(2)}, u32[]{:S(2)}) collective-permute-start(bf16[512,128]{1,0:T(8,128)(2,1)S(1)} %collective-permute-done.1.prev_b), channel_id=1, source_target_pairs={{0,4},{1,5},{4,8},{5,9},{8,12},{9,13},{12,14},{13,15},{14,10},{15,... | collective-permute-start | bytes 393224 | tf_op jit(solution)/shard_map/ppermute | solution.py:254
  13.0 5.4 %collective-permute-start.8 = (bf16[512,128]{1,0:T(8,128)(2,1)S(1)}, bf16[512,128]{1,0:T(8,128)(2,1)S(1)}, u32[]{:S(2)}, u32[]{:S(2)}) collective-permute-start(bf16[512,128]{1,0:T(8,128)(2,1)S(1)} %collective-permute-done.3.succ_b), channel_id=1, source_target_pairs={{0,2},{1,3},{4,0},{5,1},{8,4},{9,5},{12,8},{13,9},{14,12},{15,13},... | collective-permute-start | bytes 393224 | tf_op jit(solution)/shard_map/ppermute | solution.py:254
  13.6 3.0 %collective-permute-start.4 = (bf16[3,1040,128]{2,1,0:T(8,128)(2,1)S(1)}, bf16[3,1040,128]{2,1,0:T(8,128)(2,1)S(1)}, u32[]{:S(2)}, u32[]{:S(2)}) collective-permute-start(bf16[3,1040,128]{2,1,0:T(8,128)(2,1)S(1)} %get-tuple-element.15), channel_id=1, source_target_pairs={{0,1},{1,0},{4,5},{5,4},{8,9},{9,8},{12,13},{13,12},{14,15},{15,14... | collective-permute-start | bytes 2396168 | tf_op jit(solution)/shard_map/ppermute | solution.py:254
  19.0 4.0 %collective-permute-start.9 = (f32[1,256]{1,0:T(1,128)S(1)}, f32[1,256]{1,0:T(1,128)S(1)}, u32[]{:S(2)}, u32[]{:S(2)}) collective-permute-start(f32[1,256]{1,0:T(1,128)S(1)} %get-tuple-element.19), channel_id=1, source_target_pairs={{0,6},{1,7},{4,3},{5,2},{8,1},{9,0},{12,4},{13,5},{14,8},{15,9},{1... | collective-permute-start | bytes 3080 | tf_op jit(solution)/shard_map/ppermute | solution.py:254
  20.5 3.9 %collective-permute-start.10 = (f32[1,256]{1,0:T(1,128)S(1)}, f32[1,256]{1,0:T(1,128)S(1)}, u32[]{:S(2)}, u32[]{:S(2)}) collective-permute-start(f32[1,256]{1,0:T(1,128)S(1)} %get-tuple-element.20), channel_id=1, source_target_pairs={{0,8},{1,9},{4,13},{5,12},{8,15},{9,14},{12,11},{13,10},{14,7},{15... | collective-permute-start | bytes 3080 | tf_op jit(solution)/shard_map/ppermute | solution.py:254

commit v11 on v9

--- a/solution.py
+++ b/solution.py
@@ -201,10 +201,10 @@
         ]
 
     def from_prev(place, core):
-        return core ^ (place % chips in (0, 1))
+        return core ^ (place % chips in (0, chips - 1))
 
     def from_next(place, core):
-        return core ^ (place % chips not in (0, 1))
+        return core ^ (place % chips not in (0, chips - 1))
 
     return {
         "sibling": perm(lambda p, k: (p, 1 - k)),

time: 24.9 us -> 25.2 us (1.012)
  waiting for transfers between devices: 7.49 us -> 8.48 us
  starting transfers between devices: 12.9 us -> 12.1 us
    ppermute x11, waiting for transfers between devices: 7.49 us -> 8.48 us  [send(): return lax.ppermute(value, GROUP, perms[name])]
    ppermute x11, starting transfers between devices: 12.9 us -> 12.1 us  [send(): return lax.ppermute(value, GROUP, perms[name])]
where the time goes in v11:
time: 25.2 us; the launch traced here: 25 us
  starting transfers between devices  12.1 us (48%)
  waiting for transfers between devices  8.48 us (34%)
  Pallas kernels  3.79 us (15%)
  other arithmetic  0.57 us (2%)
    ppermute x11, starting transfers between devices, send(): return lax.ppermute(value, GROUP, perms[name])  12.1 us
    ppermute x11, waiting for transfers between devices, send(): return lax.ppermute(value, GROUP, perms[name])  8.48 us
    pallas_call x6, Pallas kernels, kernel_call(): pl.pallas_call(kernel, out_shape=outputs, in_specs=[vmem] * len(inputs),...  2.69 us
    pallas_call x1, Pallas kernels, on_ring(): pl.pallas_call(pack_first_kernel, out_shape=chunk(half, True), in_specs=[...  1.1 us
    max x1, other arithmetic, on_ring(): jnp.maximum(mine, jnp.maximum(send(to_back, 'home_back'), send(to_ahead,...  0.57 us
  transfers between devices with their start and end apart: 11, of which 8 were waited for; matrix products, arithmetic and copies ran while one was open for 0% of the time, Pallas kernels for 9%

profile of v11, /device:TPU:0, one launch (start us, length us, event | category | flops | bytes accessed | tf_op | source)
XLA Modules:
  0.0 25.0 jit_solution(10181058906995828795)
XLA Ops:
  0.0 0.0 copy-start
  0.0 1.1 %pack_first.1.first = bf16[528,128]{1,0:T(8,128)(2,1)S(1)} custom-call(bf16[256,512]{1,0:T(8,128)(2,1)} %embeds.3, s32[1,256]{1,0:T(1,128)} %bitcast.2), custom_call_target="tpu_custom_call" | custom-call | tf_op jit(solution)/shard_map/pack_first/pallas_call | solution.py:252
  1.1 3.1 %collective-permute-start = (bf16[528,128]{1,0:T(8,128)(2,1)S(1)}, bf16[528,128]{1,0:T(8,128)(2,1)S(1)}, u32[]{:S(2)}, u32[]{:S(2)}) collective-permute-start(bf16[528,128]{1,0:T(8,128)(2,1)S(1)} %pack_first.1.first), channel_id=1, source_target_pairs={{0,4},{1,5},{4,8},{5,9},{8,12},{9,13},{12,14},{13,15},{14,10},{15,... | collective-permute-start | bytes 405512 | tf_op jit(solution)/shard_map/ppermute | solution.py:241
  4.2 0.0 collective-permute-start.2
  4.2 0.0 copy-done
  4.2 0.1 pack_second_kernel.1
  4.3 2.1 %collective-permute-start.1 = (bf16[512,128]{1,0:T(8,128)(2,1)S(1)}, bf16[512,128]{1,0:T(8,128)(2,1)S(1)}, u32[]{:S(2)}, u32[]{:S(2)}) collective-permute-start(bf16[512,128]{1,0:T(8,128)(2,1)S(1)} %get-tuple-element.14), channel_id=1, source_target_pairs={{0,4},{1,5},{4,8},{5,9},{8,12},{9,13},{12,14},{13,15},{14,10},{15,... | collective-permute-start | bytes 393224 | tf_op jit(solution)/shard_map/ppermute | solution.py:241
  6.4 0.0 collective-permute-start.3
  6.4 1.8 %collective-permute-done.prev_a = bf16[528,128]{1,0:T(8,128)(2,1)S(1)} collective-permute-done((bf16[528,128]{1,0:T(8,128)(2,1)S(1)}, bf16[528,128]{1,0:T(8,128)(2,1)S(1)}, u32[]{:S(2)}, u32[]{:S(2)}) %collective-permute-start) | collective-permute-done | bytes 135200 | tf_op jit(solution)/shard_map/ppermute | solution.py:241
  8.2 2.5 %collective-permute-start.5 = (bf16[528,128]{1,0:T(8,128)(2,1)S(1)}, bf16[528,128]{1,0:T(8,128)(2,1)S(1)}, u32[]{:S(2)}, u32[]{:S(2)}) collective-permute-start(bf16[528,128]{1,0:T(8,128)(2,1)S(1)} %collective-permute-done.prev_a), channel_id=1, source_target_pairs={{0,4},{1,5},{4,8},{5,9},{8,12},{9,13},{12,14},{13,15},{14,10},{15,... | collective-permute-start | bytes 405512 | tf_op jit(solution)/shard_map/ppermute | solution.py:241
  10.7 0.0 collective-permute-done.2.succ_a
  10.7 0.0 collective-permute-start.6
  10.7 0.3 %collective-permute-done.1.prev_b = bf16[512,128]{1,0:T(8,128)(2,1)S(1)} collective-permute-done((bf16[512,128]{1,0:T(8,128)(2,1)S(1)}, bf16[512,128]{1,0:T(8,128)(2,1)S(1)}, u32[]{:S(2)}, u32[]{:S(2)}) %collective-permute-start.1) | collective-permute-done | bytes 131104 | tf_op jit(solution)/shard_map/ppermute | solution.py:241
  11.0 2.5 %collective-permute-start.7 = (bf16[512,128]{1,0:T(8,128)(2,1)S(1)}, bf16[512,128]{1,0:T(8,128)(2,1)S(1)}, u32[]{:S(2)}, u32[]{:S(2)}) collective-permute-start(bf16[512,128]{1,0:T(8,128)(2,1)S(1)} %collective-permute-done.1.prev_b), channel_id=1, source_target_pairs={{0,4},{1,5},{4,8},{5,9},{8,12},{9,13},{12,14},{13,15},{14,10},{15,... | collective-permute-start | bytes 393224 | tf_op jit(solution)/shard_map/ppermute | solution.py:241
  13.5 0.0 collective-permute-done.3.succ_b
  13.5 0.0 collective-permute-start.8
  13.5 0.5 %near_kernel.1 = (f32[1,256]{1,0:T(1,128)S(1)}, bf16[3,1040,128]{2,1,0:T(8,128)(2,1)S(1)}) custom-call(bf16[1040,128]{1,0:T(8,128)(2,1)S(1)} %get-tuple-element.13.own, bf16[528,128]{1,0:T(8,128)(2,1)S(1)} %collective-permute-done.prev_a, bf16[512,128]{1,0:T(8,128)(2,1)S(1)} %collective-permute-done.1.prev_b, ...), custom_call_target="tpu_custom_call" | custom-call | flops 67108864 | bytes 1048576 | tf_op jit(solution)/shard_map/near_kernel/pallas_call | solution.py:222
  14.0 0.1 collective-permute-start.4
  14.0 0.3 %collective-permute-done.5.back_a = bf16[528,128]{1,0:T(8,128)(2,1)S(1)} collective-permute-done((bf16[528,128]{1,0:T(8,128)(2,1)S(1)}, bf16[528,128]{1,0:T(8,128)(2,1)S(1)}, u32[]{:S(2)}, u32[]{:S(2)}) %collective-permute-start.5) | collective-permute-done | bytes 135200 | tf_op jit(solution)/shard_map/ppermute | solution.py:241
  14.4 1.5 %collective-permute-done.6.ahead_a = bf16[528,128]{1,0:T(8,128)(2,1)S(1)} collective-permute-done((bf16[528,128]{1,0:T(8,128)(2,1)S(1)}, bf16[528,128]{1,0:T(8,128)(2,1)S(1)}, u32[]{:S(2)}, u32[]{:S(2)}) %collective-permute-start.6) | collective-permute-done | bytes 135200 | tf_op jit(solution)/shard_map/ppermute | solution.py:241
  15.9 0.5 %far_first_kernel.1.found = f32[1,256]{1,0:T(1,128)S(1)} custom-call(bf16[1040,128]{1,0:T(8,128)(2,1)S(1)} %get-tuple-element.13.own, bf16[528,128]{1,0:T(8,128)(2,1)S(1)} %collective-permute-done.prev_a, bf16[512,128]{1,0:T(8,128)(2,1)S(1)} %collective-permute-done.1.prev_b, bf16[528,128]{1,0:T(8,128)(2,1)S(1)} %collective-permute-done.2.succ_a, ...), custom_call_target="tpu_custom_call" | custom-call | flops 13421772800 | bytes 1048576 | tf_op jit(solution)/shard_map/far_first_kernel/pallas_call | solution.py:222
  16.4 0.4 %collective-permute-done.7.back_b = bf16[512,128]{1,0:T(8,128)(2,1)S(1)} collective-permute-done((bf16[512,128]{1,0:T(8,128)(2,1)S(1)}, bf16[512,128]{1,0:T(8,128)(2,1)S(1)}, u32[]{:S(2)}, u32[]{:S(2)}) %collective-permute-start.7) | collective-permute-done | bytes 131104 | tf_op jit(solution)/shard_map/ppermute | solution.py:241
  16.8 0.0 collective-permute-done.4.others
  16.8 0.5 %far_back_kernel.1 = (f32[1,256]{1,0:T(1,128)S(1)}, f32[1,128]{1,0:T(1,128)S(1)}) custom-call(bf16[1040,128]{1,0:T(8,128)(2,1)S(1)} %get-tuple-element.13.own, bf16[3,1040,128]{2,1,0:T(8,128)(2,1)S(1)} %collective-permute-done.4.others, bf16[528,128]{1,0:T(8,128)(2,1)S(1)} %collective-permute-done.2.succ_a, ...), custom_call_target="tpu_custom_call" | custom-call | flops 134217728 | bytes 1048576 | tf_op jit(solution)/shard_map/far_back_kernel/pallas_call | solution.py:222
  17.3 1.2 %collective-permute-done.8.ahead_b = bf16[512,128]{1,0:T(8,128)(2,1)S(1)} collective-permute-done((bf16[512,128]{1,0:T(8,128)(2,1)S(1)}, bf16[512,128]{1,0:T(8,128)(2,1)S(1)}, u32[]{:S(2)}, u32[]{:S(2)}) %collective-permute-start.8) | collective-permute-done | bytes 131104 | tf_op jit(solution)/shard_map/ppermute | solution.py:241
  18.5 0.5 %far_last_kernel.1 = (f32[1,256]{1,0:T(1,128)S(1)}, f32[1,256]{1,0:T(1,128)S(1)}) custom-call(bf16[1040,128]{1,0:T(8,128)(2,1)S(1)} %get-tuple-element.13.own, bf16[3,1040,128]{2,1,0:T(8,128)(2,1)S(1)} %collective-permute-done.4.others, bf16[528,128]{1,0:T(8,128)(2,1)S(1)} %collective-permute-done.prev_a, ...), custom_call_target="tpu_custom_call" | custom-call | flops 335544320 | bytes 1048576 | tf_op jit(solution)/shard_map/far_last_kernel/pallas_call | solution.py:222
  19.0 1.0 %collective-permute-start.9 = (f32[1,256]{1,0:T(1,128)S(1)}, f32[1,256]{1,0:T(1,128)S(1)}, u32[]{:S(2)}, u32[]{:S(2)}) collective-permute-start(f32[1,256]{1,0:T(1,128)S(1)} %get-tuple-element.19), channel_id=1, source_target_pairs={{0,7},{1,6},{4,3},{5,2},{8,0},{9,1},{12,4},{13,5},{14,8},{15,9},{1... | collective-permute-start | bytes 3080 | tf_op jit(solution)/shard_map/ppermute | solution.py:241
  20.0 1.0 %collective-permute-start.10 = (f32[1,256]{1,0:T(1,128)S(1)}, f32[1,256]{1,0:T(1,128)S(1)}, u32[]{:S(2)}, u32[]{:S(2)}) collective-permute-start(f32[1,256]{1,0:T(1,128)S(1)} %get-tuple-element.20), channel_id=1, source_target_pairs={{0,9},{1,8},{4,13},{5,12},{8,15},{9,14},{12,11},{13,10},{14,7},{15... | collective-permute-start | bytes 3080 | tf_op jit(solution)/shard_map/ppermute | solution.py:241
  21.0 0.6 %own_kernel.1 = f32[1,256]{1,0:T(1,128)S(1)} custom-call(bf16[1040,128]{1,0:T(8,128)(2,1)S(1)} %get-tuple-element.13.own, bf16[3,1040,128]{2,1,0:T(8,128)(2,1)S(1)} %collective-permute-done.4.others, bf16[528,128]{1,0:T(8,128)(2,1)S(1)} %collective-permute-done.5.back_a, bf16[528,128]{1,0:T(8,128)(2,1)S(1)} %collective-permute-done.6.ahead_a, ...), custom_call_target="tpu_custom_call" | custom-call | flops 335544320 | bytes 1048576 | tf_op jit(solution)/shard_map/own_kernel/pallas_call | solution.py:222
  21.5 2.0 %collective-permute-done.9 = f32[1,256]{1,0:T(1,128)S(1)} collective-permute-done((f32[1,256]{1,0:T(1,128)S(1)}, f32[1,256]{1,0:T(1,128)S(1)}, u32[]{:S(2)}, u32[]{:S(2)}) %collective-permute-start.9) | collective-permute-done | bytes 1056 | tf_op jit(solution)/shard_map/ppermute | solution.py:241
  23.6 0.9 %collective-permute-done.10 = f32[1,256]{1,0:T(1,128)S(1)} collective-permute-done((f32[1,256]{1,0:T(1,128)S(1)}, f32[1,256]{1,0:T(1,128)S(1)}, u32[]{:S(2)}, u32[]{:S(2)}) %collective-permute-start.10) | collective-permute-done | bytes 1056 | tf_op jit(solution)/shard_map/ppermute | solution.py:241
  24.5 0.6 %maximum_maximum_fusion = f32[1,256]{1,0:T(1,128)} fusion(f32[1,256]{1,0:T(1,128)S(1)} %own_kernel.1, f32[1,256]{1,0:T(1,128)S(1)} %collective-permute-done.9, f32[1,256]{1,0:T(1,128)S(1)} %collective-permute-done.10), kind=kLoop, calls=%fused_computation | loop fusion | flops 512 | bytes 4096 | tf_op jit(solution)/shard_map/max | solution.py:292
Async XLA Ops:
  0.0 4.2 %copy-start = (bf16[256,512]{1,0:T(8,128)(2,1)S(1)}, bf16[256,512]{1,0:T(8,128)(2,1)}, u32[]{:S(2)}) copy-start(bf16[256,512]{1,0:T(8,128)(2,1)} %embeds.3) | copy-start | bytes 786436
  1.1 7.1 %collective-permute-start = (bf16[528,128]{1,0:T(8,128)(2,1)S(1)}, bf16[528,128]{1,0:T(8,128)(2,1)S(1)}, u32[]{:S(2)}, u32[]{:S(2)}) collective-permute-start(bf16[528,128]{1,0:T(8,128)(2,1)S(1)} %pack_first.1.first), channel_id=1, source_target_pairs={{0,4},{1,5},{4,8},{5,9},{8,12},{9,13},{12,14},{13,15},{14,10},{15,... | collective-permute-start | bytes 405512 | tf_op jit(solution)/shard_map/ppermute | solution.py:241
  4.2 6.5 %collective-permute-start.2 = (bf16[528,128]{1,0:T(8,128)(2,1)S(1)}, bf16[528,128]{1,0:T(8,128)(2,1)S(1)}, u32[]{:S(2)}, u32[]{:S(2)}) collective-permute-start(bf16[528,128]{1,0:T(8,128)(2,1)S(1)} %pack_first.1.first), channel_id=1, source_target_pairs={{0,2},{1,3},{4,0},{5,1},{8,5},{9,4},{12,9},{13,8},{14,13},{15,12},... | collective-permute-start | bytes 405512 | tf_op jit(solution)/shard_map/ppermute | solution.py:241
  4.3 6.7 %collective-permute-start.1 = (bf16[512,128]{1,0:T(8,128)(2,1)S(1)}, bf16[512,128]{1,0:T(8,128)(2,1)S(1)}, u32[]{:S(2)}, u32[]{:S(2)}) collective-permute-start(bf16[512,128]{1,0:T(8,128)(2,1)S(1)} %get-tuple-element.14), channel_id=1, source_target_pairs={{0,4},{1,5},{4,8},{5,9},{8,12},{9,13},{12,14},{13,15},{14,10},{15,... | collective-permute-start | bytes 393224 | tf_op jit(solution)/shard_map/ppermute | solution.py:241
  6.4 7.1 %collective-permute-start.3 = (bf16[512,128]{1,0:T(8,128)(2,1)S(1)}, bf16[512,128]{1,0:T(8,128)(2,1)S(1)}, u32[]{:S(2)}, u32[]{:S(2)}) collective-permute-start(bf16[512,128]{1,0:T(8,128)(2,1)S(1)} %get-tuple-element.14), channel_id=1, source_target_pairs={{0,2},{1,3},{4,0},{5,1},{8,5},{9,4},{12,9},{13,8},{14,13},{15,12},... | collective-permute-start | bytes 393224 | tf_op jit(solution)/shard_map/ppermute | solution.py:241
  8.2 6.2 %collective-permute-start.5 = (bf16[528,128]{1,0:T(8,128)(2,1)S(1)}, bf16[528,128]{1,0:T(8,128)(2,1)S(1)}, u32[]{:S(2)}, u32[]{:S(2)}) collective-permute-start(bf16[528,128]{1,0:T(8,128)(2,1)S(1)} %collective-permute-done.prev_a), channel_id=1, source_target_pairs={{0,4},{1,5},{4,8},{5,9},{8,12},{9,13},{12,14},{13,15},{14,10},{15,... | collective-permute-start | bytes 405512 | tf_op jit(solution)/shard_map/ppermute | solution.py:241
  10.7 5.2 %collective-permute-start.6 = (bf16[528,128]{1,0:T(8,128)(2,1)S(1)}, bf16[528,128]{1,0:T(8,128)(2,1)S(1)}, u32[]{:S(2)}, u32[]{:S(2)}) collective-permute-start(bf16[528,128]{1,0:T(8,128)(2,1)S(1)} %collective-permute-done.2.succ_a), channel_id=1, source_target_pairs={{0,2},{1,3},{4,0},{5,1},{8,4},{9,5},{12,8},{13,9},{14,12},{15,13},... | collective-permute-start | bytes 405512 | tf_op jit(solution)/shard_map/ppermute | solution.py:241
  11.0 5.8 %collective-permute-start.7 = (bf16[512,128]{1,0:T(8,128)(2,1)S(1)}, bf16[512,128]{1,0:T(8,128)(2,1)S(1)}, u32[]{:S(2)}, u32[]{:S(2)}) collective-permute-start(bf16[512,128]{1,0:T(8,128)(2,1)S(1)} %collective-permute-done.1.prev_b), channel_id=1, source_target_pairs={{0,4},{1,5},{4,8},{5,9},{8,12},{9,13},{12,14},{13,15},{14,10},{15,... | collective-permute-start | bytes 393224 | tf_op jit(solution)/shard_map/ppermute | solution.py:241
  13.5 5.0 %collective-permute-start.8 = (bf16[512,128]{1,0:T(8,128)(2,1)S(1)}, bf16[512,128]{1,0:T(8,128)(2,1)S(1)}, u32[]{:S(2)}, u32[]{:S(2)}) collective-permute-start(bf16[512,128]{1,0:T(8,128)(2,1)S(1)} %collective-permute-done.3.succ_b), channel_id=1, source_target_pairs={{0,2},{1,3},{4,0},{5,1},{8,4},{9,5},{12,8},{13,9},{14,12},{15,13},... | collective-permute-start | bytes 393224 | tf_op jit(solution)/shard_map/ppermute | solution.py:241
  14.0 2.8 %collective-permute-start.4 = (bf16[3,1040,128]{2,1,0:T(8,128)(2,1)S(1)}, bf16[3,1040,128]{2,1,0:T(8,128)(2,1)S(1)}, u32[]{:S(2)}, u32[]{:S(2)}) collective-permute-start(bf16[3,1040,128]{2,1,0:T(8,128)(2,1)S(1)} %get-tuple-element.15), channel_id=1, source_target_pairs={{0,1},{1,0},{4,5},{5,4},{8,9},{9,8},{12,13},{13,12},{14,15},{15,14... | collective-permute-start | bytes 2396168 | tf_op jit(solution)/shard_map/ppermute | solution.py:241
  19.0 4.5 %collective-permute-start.9 = (f32[1,256]{1,0:T(1,128)S(1)}, f32[1,256]{1,0:T(1,128)S(1)}, u32[]{:S(2)}, u32[]{:S(2)}) collective-permute-start(f32[1,256]{1,0:T(1,128)S(1)} %get-tuple-element.19), channel_id=1, source_target_pairs={{0,7},{1,6},{4,3},{5,2},{8,0},{9,1},{12,4},{13,5},{14,8},{15,9},{1... | collective-permute-start | bytes 3080 | tf_op jit(solution)/shard_map/ppermute | solution.py:241
  20.0 4.5 %collective-permute-start.10 = (f32[1,256]{1,0:T(1,128)S(1)}, f32[1,256]{1,0:T(1,128)S(1)}, u32[]{:S(2)}, u32[]{:S(2)}) collective-permute-start(f32[1,256]{1,0:T(1,128)S(1)} %get-tuple-element.20), channel_id=1, source_target_pairs={{0,9},{1,8},{4,13},{5,12},{8,15},{9,14},{12,11},{13,10},{14,7},{15... | collective-permute-start | bytes 3080 | tf_op jit(solution)/shard_map/ppermute | solution.py:241

commit v12 on v7

--- a/solution.py
+++ b/solution.py
@@ -24,9 +24,8 @@
 LANES = 128
 VMEM_BYTES = 32 * 2**20
 NEAR_COST = 2
-OWN_COST = 100
-FIRST_COST = 5
-SECOND_COST = 5
+OWN_COST = 200
+ROWS_COST = 6
 
 
 def pack_kernel(embeds, label, packed, raw, line, sems):
@@ -100,7 +99,7 @@
     best[...] = best_of(Block(rows, size), *(Block(key, size) for key in keys))
 
 
-def last_kernel(rows, *refs):
+def after_kernel(rows, *refs):
     *keys, _, best = refs
     rows_kernel(rows, *keys, best)
 
@@ -111,6 +110,10 @@
     best[...] = jnp.maximum(best[...], found[...])
 
 
+KEYS_FAR = (3, 6, 5, 0, 7, 2, 1, 4)
+KEYS_TWO = (2, 7, 4, 1, 6, 3, 0, 5)
+
+
 def ring_perms(size_x, size_y, size_z):
     chips = size_x * size_y
 
@@ -119,18 +122,19 @@
         x, y = (place, 0) if place < size_x else (chips - 1 - place, 1)
         return (x * size_y + y) * size_z + core
 
-    def perm(to):
+    def perm(source, swap=0):
         return [
-            (device(p, k), device(*to(p, k))) for p in range(chips) for k in range(size_z)
+            (device(source(p), k), device(p, k ^ swap))
+            for p in range(chips)
+            for k in range(size_z)
         ]
 
-    step = (1, -1)
     return {
-        "sibling": perm(lambda p, k: (p, 1 - k)),
-        "lane": perm(lambda p, k: (p + step[k], k)),
-        "other_lane": perm(lambda p, k: (p + step[1 - k], 1 - k)),
-        "home": perm(lambda p, k: (p - 2 * step[k], k)),
-        "home_other": perm(lambda p, k: (p - 2 * step[k], 1 - k)),
+        "sibling": perm(lambda p: p, swap=1),
+        "next": perm(lambda p: p - 1),
+        "prev": perm(lambda p: p + 1),
+        "far": perm(lambda p: KEYS_FAR[p]),
+        "two": perm(lambda p: KEYS_TWO[p]),
     }
 
 
@@ -175,22 +179,19 @@
     )
     other = send(own, "sibling")
     near = kernel_call(near_kernel, rows, [own, other], NEAR_COST, "near")
+    far, two = send(own, "far"), send(own, "two")
     own_again, near = lax.optimization_barrier((own, near))
-    one_first, one_second = send(own, "lane"), send(own_again, "other_lane")
-    two_first, two_second = send(one_first, "lane"), send(one_second, "lane")
-    beyond = [send(block, "sibling") for block in (one_first, one_second, two_first)]
-    keys = [own, other, *beyond]
-    mine = kernel_call(
-        more_kernel, rows, [own, one_first, one_second, *beyond[:2], near], OWN_COST, "own"
-    )
-    found_first = kernel_call(
-        last_kernel, rows, [two_first, *keys, mine], FIRST_COST, "first"
-    )
-    found_second = kernel_call(
-        last_kernel, rows, [two_second, *keys, found_first], SECOND_COST, "second"
-    )
+    behind, ahead = send(own_again, "next"), send(own_again, "prev")
+    far_other, two_other = send(far, "sibling"), send(two, "sibling")
+    mine = kernel_call(more_kernel, rows, [own, far, two, near], OWN_COST, "own")
+    keys = [own, other, far, two, far_other, two_other]
+    found_behind = kernel_call(after_kernel, rows, [behind, *keys, mine], ROWS_COST, "behind")
+    found_ahead = kernel_call(
+        after_kernel, rows, [ahead, *keys, found_behind], ROWS_COST, "ahead"
+    )
+    mine = kernel_call(more_kernel, rows, [own, far_other, two_other, mine], 2, "rest")
     best = jnp.maximum(
-        mine, jnp.maximum(send(found_first, "home"), send(found_second, "home_other"))
+        mine, jnp.maximum(send(found_behind, "prev"), send(found_ahead, "next"))
     )
     return best.reshape(rows)
 

time: 27.3 us -> 31.9 us (1.17)
  waiting for transfers between devices: 9.62 us -> 17.8 us
  starting transfers between devices: 13.8 us -> 9.89 us
  Pallas kernels: 3.13 us -> 3.49 us
    ppermute x10 -> x9, waiting for transfers between devices: 9.62 us -> 17.8 us  [send(): return lax.ppermute(value, GROUP, perms[name])]
    ppermute x10 -> x9, starting transfers between devices: 13.8 us -> 9.89 us  [send(): return lax.ppermute(value, GROUP, perms[name])]
    pallas_call x4 -> x5, Pallas kernels: 1.96 us -> 2.32 us  [kernel_call(): pl.pallas_call(kernel, out_shape=jax.ShapeDtypeStruct((1, rows), jnp.floa...]
  transfers between devices with their start and end apart: 10 -> 9, of which waited for: 5 -> 4; matrix products, arithmetic and copies ran while one was open for 0% -> 0% of each run, Pallas kernels for 5% -> 7%
where the time goes in v12:
time: 31.9 us; the launch traced here: 31.8 us
  waiting for transfers between devices  17.8 us (56%)
  starting transfers between devices  9.89 us (31%)
  Pallas kernels  3.49 us (11%)
  other arithmetic  0.57 us (2%)
    ppermute x9, waiting for transfers between devices, send(): return lax.ppermute(value, GROUP, perms[name])  17.8 us
    ppermute x9, starting transfers between devices, send(): return lax.ppermute(value, GROUP, perms[name])  9.89 us
    pallas_call x5, Pallas kernels, kernel_call(): pl.pallas_call(kernel, out_shape=jax.ShapeDtypeStruct((1, rows), jnp.floa...  2.32 us
    pallas_call x1, Pallas kernels, on_ring(): pl.pallas_call(pack_kernel, out_shape=jax.ShapeDtypeStruct((rows * width...  1.17 us
  transfers between devices with their start and end apart: 9, of which 4 were waited for; matrix products, arithmetic and copies ran while one was open for 0% of the time, Pallas kernels for 7%

profile of v12, /device:TPU:0, one launch (start us, length us, event | category | flops | bytes accessed | tf_op | source)
XLA Modules:
  0.0 31.8 jit_solution(18303068895927337003)
XLA Ops:
  0.0 1.2 %pack.1.rows.refs_0_ = bf16[1040,128]{1,0:T(8,128)(2,1)S(1)} custom-call(bf16[256,512]{1,0:T(8,128)(2,1)} %embeds.1, s32[1,256]{1,0:T(1,128)} %bitcast.2), custom_call_target="tpu_custom_call" | custom-call | tf_op jit(solution)/shard_map/pack/pallas_call | solution.py:164
  1.2 0.5 %collective-permute-start.4 = (bf16[1040,128]{1,0:T(8,128)(2,1)S(1)}, bf16[1040,128]{1,0:T(8,128)(2,1)S(1)}, u32[]{:S(2)}, u32[]{:S(2)}) collective-permute-start(bf16[1040,128]{1,0:T(8,128)(2,1)S(1)} %pack.1.rows.refs_0_), channel_id=1, source_target_pairs={{0,1},{1,0},{4,5},{5,4},{8,9},{9,8},{12,13},{13,12},{14,15},{15,14... | collective-permute-start | bytes 798728 | tf_op jit(solution)/shard_map/ppermute | solution.py:161
  1.7 4.7 %collective-permute-start = (bf16[1040,128]{1,0:T(8,128)(2,1)S(1)}, bf16[1040,128]{1,0:T(8,128)(2,1)S(1)}, u32[]{:S(2)}, u32[]{:S(2)}) collective-permute-start(bf16[1040,128]{1,0:T(8,128)(2,1)S(1)} %pack.1.rows.refs_0_), channel_id=1, source_target_pairs={{12,0},{13,1},{6,4},{7,5},{10,8},{11,9},{0,12},{1,13},{2,14},{3,15... | collective-permute-start | bytes 798728 | tf_op jit(solution)/shard_map/ppermute | solution.py:161
  6.4 0.0 collective-permute-start.2
  6.4 0.0 collective-permute-done.4.other.refs_1_
  6.4 0.4 %near.1.refs_2_ = f32[1,256]{1,0:T(1,128)S(1)} custom-call(bf16[1040,128]{1,0:T(8,128)(2,1)S(1)} %pack.1.rows.refs_0_, bf16[1040,128]{1,0:T(8,128)(2,1)S(1)} %collective-permute-done.4.other.refs_1_), custom_call_target="tpu_custom_call" | custom-call | flops 134217728 | bytes 1048576 | tf_op jit(solution)/shard_map/near/pallas_call | solution.py:143
  6.7 0.7 %collective-permute-start.5 = (bf16[1040,128]{1,0:T(8,128)(2,1)S(1)}, bf16[1040,128]{1,0:T(8,128)(2,1)S(1)}, u32[]{:S(2)}, u32[]{:S(2)}) collective-permute-start(bf16[1040,128]{1,0:T(8,128)(2,1)S(1)} %pack.1.rows.refs_0_), channel_id=1, source_target_pairs={{2,0},{3,1},{0,4},{1,5},{4,8},{5,9},{8,12},{9,13},{12,14},{13,15},... | collective-permute-start | bytes 798728 | tf_op jit(solution)/shard_map/ppermute | solution.py:161
  7.4 1.4 %collective-permute-start.7 = (bf16[1040,128]{1,0:T(8,128)(2,1)S(1)}, bf16[1040,128]{1,0:T(8,128)(2,1)S(1)}, u32[]{:S(2)}, u32[]{:S(2)}) collective-permute-start(bf16[1040,128]{1,0:T(8,128)(2,1)S(1)} %pack.1.rows.refs_0_), channel_id=1, source_target_pairs={{4,0},{5,1},{8,4},{9,5},{12,8},{13,9},{14,12},{15,13},{10,14},{11,... | collective-permute-start | bytes 798728 | tf_op jit(solution)/shard_map/ppermute | solution.py:161
  8.8 4.9 %collective-permute-done.refs_0_.refs_2_ = bf16[1040,128]{1,0:T(8,128)(2,1)S(1)} collective-permute-done((bf16[1040,128]{1,0:T(8,128)(2,1)S(1)}, bf16[1040,128]{1,0:T(8,128)(2,1)S(1)}, u32[]{:S(2)}, u32[]{:S(2)}) %collective-permute-start) | collective-permute-done | bytes 266272 | tf_op jit(solution)/shard_map/ppermute | solution.py:161
  13.7 0.0 collective-permute-start.1
  13.7 5.5 %collective-permute-done.2.refs_1_.refs_3_ = bf16[1040,128]{1,0:T(8,128)(2,1)S(1)} collective-permute-done((bf16[1040,128]{1,0:T(8,128)(2,1)S(1)}, bf16[1040,128]{1,0:T(8,128)(2,1)S(1)}, u32[]{:S(2)}, u32[]{:S(2)}) %collective-permute-start.2) | collective-permute-done | bytes 266272 | tf_op jit(solution)/shard_map/ppermute | solution.py:161
  19.2 0.0 collective-permute-start.3
  19.2 0.4 %own.1.refs_2_.refs_6_ = f32[1,256]{1,0:T(1,128)S(1)} custom-call(bf16[1040,128]{1,0:T(8,128)(2,1)S(1)} %pack.1.rows.refs_0_, bf16[1040,128]{1,0:T(8,128)(2,1)S(1)} %collective-permute-done.refs_0_.refs_2_, bf16[1040,128]{1,0:T(8,128)(2,1)S(1)} %collective-permute-done.2.refs_1_.refs_3_, f32[1,256]{1,0:T(1,128)S(1)} %near.1.refs_2_), custom_call_target="tpu_custom_call" | custom-call | flops 13421772800 | bytes 1048576 | tf_op jit(solution)/shard_map/own/pallas_call | solution.py:143
  19.5 4.6 %collective-permute-done.5.rows = bf16[1040,128]{1,0:T(8,128)(2,1)S(1)} collective-permute-done((bf16[1040,128]{1,0:T(8,128)(2,1)S(1)}, bf16[1040,128]{1,0:T(8,128)(2,1)S(1)}, u32[]{:S(2)}, u32[]{:S(2)}) %collective-permute-start.5) | collective-permute-done | bytes 266272 | tf_op jit(solution)/shard_map/ppermute | solution.py:161
  24.1 0.0 collective-permute-done.1.refs_0_.refs_4_
  24.1 0.0 collective-permute-done.3.refs_1_.refs_5_
  24.1 0.6 %behind.1.refs_6_ = f32[1,256]{1,0:T(1,128)S(1)} custom-call(bf16[1040,128]{1,0:T(8,128)(2,1)S(1)} %collective-permute-done.5.rows, bf16[1040,128]{1,0:T(8,128)(2,1)S(1)} %pack.1.rows.refs_0_, bf16[1040,128]{1,0:T(8,128)(2,1)S(1)} %collective-permute-done.4.other.refs_1_, bf16[1040,128]{1,0:T(8,128)(2,1)S(1)} %collective-permute-done.refs_0_.refs_2_, ...), custom_call_target="tpu_custom_call" | custom-call | flops 402653184 | bytes 1048576 | tf_op jit(solution)/shard_map/behind/pallas_call | solution.py:143
  24.8 2.2 %collective-permute-start.6 = (f32[1,256]{1,0:T(1,128)S(1)}, f32[1,256]{1,0:T(1,128)S(1)}, u32[]{:S(2)}, u32[]{:S(2)}) collective-permute-start(f32[1,256]{1,0:T(1,128)S(1)} %behind.1.refs_6_), channel_id=1, source_target_pairs={{4,0},{5,1},{8,4},{9,5},{12,8},{13,9},{14,12},{15,13},{10,14},{11,... | collective-permute-start | bytes 3080 | tf_op jit(solution)/shard_map/ppermute | solution.py:161
  27.0 0.0 collective-permute-done.7.rows
  27.0 0.6 %ahead.1 = f32[1,256]{1,0:T(1,128)S(1)} custom-call(bf16[1040,128]{1,0:T(8,128)(2,1)S(1)} %collective-permute-done.7.rows, bf16[1040,128]{1,0:T(8,128)(2,1)S(1)} %pack.1.rows.refs_0_, bf16[1040,128]{1,0:T(8,128)(2,1)S(1)} %collective-permute-done.4.other.refs_1_, bf16[1040,128]{1,0:T(8,128)(2,1)S(1)} %collective-permute-done.refs_0_.refs_2_, ...), custom_call_target="tpu_custom_call" | custom-call | flops 402653184 | bytes 1048576 | tf_op jit(solution)/shard_map/ahead/pallas_call | solution.py:143
  27.6 0.4 %collective-permute-start.8 = (f32[1,256]{1,0:T(1,128)S(1)}, f32[1,256]{1,0:T(1,128)S(1)}, u32[]{:S(2)}, u32[]{:S(2)}) collective-permute-start(f32[1,256]{1,0:T(1,128)S(1)} %ahead.1), channel_id=1, source_target_pairs={{2,0},{3,1},{0,4},{1,5},{4,8},{5,9},{8,12},{9,13},{12,14},{13,15},... | collective-permute-start | bytes 3080 | tf_op jit(solution)/shard_map/ppermute | solution.py:161
  28.0 0.4 %rest.1 = f32[1,256]{1,0:T(1,128)S(1)} custom-call(bf16[1040,128]{1,0:T(8,128)(2,1)S(1)} %pack.1.rows.refs_0_, bf16[1040,128]{1,0:T(8,128)(2,1)S(1)} %collective-permute-done.1.refs_0_.refs_4_, bf16[1040,128]{1,0:T(8,128)(2,1)S(1)} %collective-permute-done.3.refs_1_.refs_5_, f32[1,256]{1,0:T(1,128)S(1)} %own.1.refs_2_.refs_6_), custom_call_target="tpu_custom_call" | custom-call | flops 134217728 | bytes 1048576 | tf_op jit(solution)/shard_map/rest/pallas_call | solution.py:143
  28.4 2.8 %collective-permute-done.8 = f32[1,256]{1,0:T(1,128)S(1)} collective-permute-done((f32[1,256]{1,0:T(1,128)S(1)}, f32[1,256]{1,0:T(1,128)S(1)}, u32[]{:S(2)}, u32[]{:S(2)}) %collective-permute-start.8) | collective-permute-done | bytes 1056 | tf_op jit(solution)/shard_map/ppermute | solution.py:161
  31.2 0.0 collective-permute-done.6
  31.2 0.6 %maximum_maximum_fusion = f32[1,256]{1,0:T(1,128)} fusion(f32[1,256]{1,0:T(1,128)S(1)} %rest.1, f32[1,256]{1,0:T(1,128)S(1)} %collective-permute-done.6, f32[1,256]{1,0:T(1,128)S(1)} %collective-permute-done.8), kind=kLoop, calls=%fused_computation | loop fusion | flops 512 | bytes 4096 | tf_op jit(solution)/shard_map/max | solution.py:193
Async XLA Ops:
  1.2 5.2 %collective-permute-start.4 = (bf16[1040,128]{1,0:T(8,128)(2,1)S(1)}, bf16[1040,128]{1,0:T(8,128)(2,1)S(1)}, u32[]{:S(2)}, u32[]{:S(2)}) collective-permute-start(bf16[1040,128]{1,0:T(8,128)(2,1)S(1)} %pack.1.rows.refs_0_), channel_id=1, source_target_pairs={{0,1},{1,0},{4,5},{5,4},{8,9},{9,8},{12,13},{13,12},{14,15},{15,14... | collective-permute-start | bytes 798728 | tf_op jit(solution)/shard_map/ppermute | solution.py:161
  1.7 12.0 %collective-permute-start = (bf16[1040,128]{1,0:T(8,128)(2,1)S(1)}, bf16[1040,128]{1,0:T(8,128)(2,1)S(1)}, u32[]{:S(2)}, u32[]{:S(2)}) collective-permute-start(bf16[1040,128]{1,0:T(8,128)(2,1)S(1)} %pack.1.rows.refs_0_), channel_id=1, source_target_pairs={{12,0},{13,1},{6,4},{7,5},{10,8},{11,9},{0,12},{1,13},{2,14},{3,15... | collective-permute-start | bytes 798728 | tf_op jit(solution)/shard_map/ppermute | solution.py:161
  6.4 12.8 %collective-permute-start.2 = (bf16[1040,128]{1,0:T(8,128)(2,1)S(1)}, bf16[1040,128]{1,0:T(8,128)(2,1)S(1)}, u32[]{:S(2)}, u32[]{:S(2)}) collective-permute-start(bf16[1040,128]{1,0:T(8,128)(2,1)S(1)} %pack.1.rows.refs_0_), channel_id=1, source_target_pairs={{8,0},{9,1},{2,4},{3,5},{14,8},{15,9},{4,12},{5,13},{6,14},{7,15},... | collective-permute-start | bytes 798728 | tf_op jit(solution)/shard_map/ppermute | solution.py:161
  6.7 17.4 %collective-permute-start.5 = (bf16[1040,128]{1,0:T(8,128)(2,1)S(1)}, bf16[1040,128]{1,0:T(8,128)(2,1)S(1)}, u32[]{:S(2)}, u32[]{:S(2)}) collective-permute-start(bf16[1040,128]{1,0:T(8,128)(2,1)S(1)} %pack.1.rows.refs_0_), channel_id=1, source_target_pairs={{2,0},{3,1},{0,4},{1,5},{4,8},{5,9},{8,12},{9,13},{12,14},{13,15},... | collective-permute-start | bytes 798728 | tf_op jit(solution)/shard_map/ppermute | solution.py:161
  7.4 19.5 %collective-permute-start.7 = (bf16[1040,128]{1,0:T(8,128)(2,1)S(1)}, bf16[1040,128]{1,0:T(8,128)(2,1)S(1)}, u32[]{:S(2)}, u32[]{:S(2)}) collective-permute-start(bf16[1040,128]{1,0:T(8,128)(2,1)S(1)} %pack.1.rows.refs_0_), channel_id=1, source_target_pairs={{4,0},{5,1},{8,4},{9,5},{12,8},{13,9},{14,12},{15,13},{10,14},{11,... | collective-permute-start | bytes 798728 | tf_op jit(solution)/shard_map/ppermute | solution.py:161
  13.7 10.4 %collective-permute-start.1 = (bf16[1040,128]{1,0:T(8,128)(2,1)S(1)}, bf16[1040,128]{1,0:T(8,128)(2,1)S(1)}, u32[]{:S(2)}, u32[]{:S(2)}) collective-permute-start(bf16[1040,128]{1,0:T(8,128)(2,1)S(1)} %collective-permute-done.refs_0_.refs_2_), channel_id=1, source_target_pairs={{0,1},{1,0},{4,5},{5,4},{8,9},{9,8},{12,13},{13,12},{14,15},{15,14... | collective-permute-start | bytes 798728 | tf_op jit(solution)/shard_map/ppermute | solution.py:161
  19.2 5.0 %collective-permute-start.3 = (bf16[1040,128]{1,0:T(8,128)(2,1)S(1)}, bf16[1040,128]{1,0:T(8,128)(2,1)S(1)}, u32[]{:S(2)}, u32[]{:S(2)}) collective-permute-start(bf16[1040,128]{1,0:T(8,128)(2,1)S(1)} %collective-permute-done.2.refs_1_.refs_3_), channel_id=1, source_target_pairs={{0,1},{1,0},{4,5},{5,4},{8,9},{9,8},{12,13},{13,12},{14,15},{15,14... | collective-permute-start | bytes 798728 | tf_op jit(solution)/shard_map/ppermute | solution.py:161
  24.8 6.4 %collective-permute-start.6 = (f32[1,256]{1,0:T(1,128)S(1)}, f32[1,256]{1,0:T(1,128)S(1)}, u32[]{:S(2)}, u32[]{:S(2)}) collective-permute-start(f32[1,256]{1,0:T(1,128)S(1)} %behind.1.refs_6_), channel_id=1, source_target_pairs={{4,0},{5,1},{8,4},{9,5},{12,8},{13,9},{14,12},{15,13},{10,14},{11,... | collective-permute-start | bytes 3080 | tf_op jit(solution)/shard_map/ppermute | solution.py:161
  27.6 3.6 %collective-permute-start.8 = (f32[1,256]{1,0:T(1,128)S(1)}, f32[1,256]{1,0:T(1,128)S(1)}, u32[]{:S(2)}, u32[]{:S(2)}) collective-permute-start(f32[1,256]{1,0:T(1,128)S(1)} %ahead.1), channel_id=1, source_target_pairs={{2,0},{3,1},{0,4},{1,5},{4,8},{5,9},{8,12},{9,13},{12,14},{13,15},... | collective-permute-start | bytes 3080 | tf_op jit(solution)/shard_map/ppermute | solution.py:161

commit v13 on v11

--- a/solution.py
+++ b/solution.py
@@ -38,20 +38,18 @@
 def pack_first_kernel(embeds, label, first, raw, line, sems):
     rows, width = embeds.shape
     half = rows // 2
-    copies = [
-        pltpu.make_async_copy(label, line, sems.at[0]),
-        pltpu.make_async_copy(embeds.at[pl.ds(0, half)], raw, sems.at[1]),
-    ]
-    for copy in copies:
-        copy.start()
-    copies[0].wait()
+    rows_copy = pltpu.make_async_copy(embeds.at[pl.ds(0, half)], raw, sems.at[0])
+    line_copy = pltpu.make_async_copy(label, line, sems.at[1])
+    rows_copy.start()
+    line_copy.start()
+    line_copy.wait()
     row = lax.broadcasted_iota(jnp.int32, (LABEL_ROWS, LANES), 0)
     lines = jnp.zeros((LABEL_ROWS, LANES), jnp.float32)
     for i in range(rows // LANES):
         piece = line[:, i * LANES : (i + 1) * LANES].astype(jnp.float32)
         lines = jnp.where(row == i, piece, lines)
     first[half * width // LANES :, :] = lines.astype(jnp.bfloat16)
-    copies[1].wait()
+    rows_copy.wait()
     put_unit(normalised(raw[...]), first, 0, half)
 
 
@@ -201,10 +199,10 @@
         ]
 
     def from_prev(place, core):
-        return core ^ (place % chips in (0, chips - 1))
+        return core ^ (place % chips in (chips // 2 - 1, chips // 2))
 
     def from_next(place, core):
-        return core ^ (place % chips not in (0, chips - 1))
+        return core ^ (place % chips not in (chips // 2 - 1, chips // 2))
 
     return {
         "sibling": perm(lambda p, k: (p, 1 - k)),

time: 25.2 us -> 24.9 us (0.988)
  starting transfers between devices: 12.1 us -> 11 us
  waiting for transfers between devices: 8.48 us -> 9.32 us
    ppermute x11, starting transfers between devices: 12.1 us -> 11 us  [send(): return lax.ppermute(value, GROUP, perms[name])]
    ppermute x11, waiting for transfers between devices: 8.48 us -> 9.32 us  [send(): return lax.ppermute(value, GROUP, perms[name])]
  transfers between devices with their start and end apart: 11 -> 11, of which waited for: 8 -> 9; matrix products, arithmetic and copies ran while one was open for 0% -> 0% of each run, Pallas kernels for 9% -> 9%
where the time goes in v13:
time: 24.9 us; the launch traced here: 24.7 us
  starting transfers between devices  11 us (44%)
  waiting for transfers between devices  9.32 us (37%)
  Pallas kernels  3.8 us (15%)
  other arithmetic  0.57 us (2%)
    ppermute x11, starting transfers between devices, send(): return lax.ppermute(value, GROUP, perms[name])  11 us
    ppermute x11, waiting for transfers between devices, send(): return lax.ppermute(value, GROUP, perms[name])  9.32 us
    pallas_call x6, Pallas kernels, kernel_call(): pl.pallas_call(kernel, out_shape=outputs, in_specs=[vmem] * len(inputs),...  2.69 us
    pallas_call x1, Pallas kernels, on_ring(): pl.pallas_call(pack_first_kernel, out_shape=chunk(half, True), in_specs=[...  1.1 us
    max x1, other arithmetic, on_ring(): jnp.maximum(mine, jnp.maximum(send(to_back, 'home_back'), send(to_ahead,...  0.57 us
  transfers between devices with their start and end apart: 11, of which 9 were waited for; matrix products, arithmetic and copies ran while one was open for 0% of the time, Pallas kernels for 9%

profile of v13, /device:TPU:0, one launch (start us, length us, event | category | flops | bytes accessed | tf_op | source)
XLA Modules:
  0.0 24.7 jit_solution(3792672926891806121)
XLA Ops:
  0.0 0.0 copy-start
  0.0 1.1 %pack_first.1.first = bf16[528,128]{1,0:T(8,128)(2,1)S(1)} custom-call(bf16[256,512]{1,0:T(8,128)(2,1)} %embeds.3, s32[1,256]{1,0:T(1,128)} %bitcast.2), custom_call_target="tpu_custom_call" | custom-call | tf_op jit(solution)/shard_map/pack_first/pallas_call | solution.py:250
  1.1 3.1 %collective-permute-start = (bf16[528,128]{1,0:T(8,128)(2,1)S(1)}, bf16[528,128]{1,0:T(8,128)(2,1)S(1)}, u32[]{:S(2)}, u32[]{:S(2)}) collective-permute-start(bf16[528,128]{1,0:T(8,128)(2,1)S(1)} %pack_first.1.first), channel_id=1, source_target_pairs={{0,4},{1,5},{4,8},{5,9},{8,13},{9,12},{12,15},{13,14},{14,10},{15,... | collective-permute-start | bytes 405512 | tf_op jit(solution)/shard_map/ppermute | solution.py:239
  4.2 0.0 collective-permute-start.2
  4.2 0.0 copy-done
  4.2 0.1 pack_second_kernel.1
  4.3 1.6 %collective-permute-start.1 = (bf16[512,128]{1,0:T(8,128)(2,1)S(1)}, bf16[512,128]{1,0:T(8,128)(2,1)S(1)}, u32[]{:S(2)}, u32[]{:S(2)}) collective-permute-start(bf16[512,128]{1,0:T(8,128)(2,1)S(1)} %get-tuple-element.14), channel_id=1, source_target_pairs={{0,4},{1,5},{4,8},{5,9},{8,13},{9,12},{12,15},{13,14},{14,10},{15,... | collective-permute-start | bytes 393224 | tf_op jit(solution)/shard_map/ppermute | solution.py:239
  6.0 0.1 collective-permute-start.3
  6.1 1.9 %collective-permute-done.prev_a = bf16[528,128]{1,0:T(8,128)(2,1)S(1)} collective-permute-done((bf16[528,128]{1,0:T(8,128)(2,1)S(1)}, bf16[528,128]{1,0:T(8,128)(2,1)S(1)}, u32[]{:S(2)}, u32[]{:S(2)}) %collective-permute-start) | collective-permute-done | bytes 135200 | tf_op jit(solution)/shard_map/ppermute | solution.py:239
  8.0 1.8 %collective-permute-start.5 = (bf16[528,128]{1,0:T(8,128)(2,1)S(1)}, bf16[528,128]{1,0:T(8,128)(2,1)S(1)}, u32[]{:S(2)}, u32[]{:S(2)}) collective-permute-start(bf16[528,128]{1,0:T(8,128)(2,1)S(1)} %collective-permute-done.prev_a), channel_id=1, source_target_pairs={{0,4},{1,5},{4,8},{5,9},{8,12},{9,13},{12,14},{13,15},{14,10},{15,... | collective-permute-start | bytes 405512 | tf_op jit(solution)/shard_map/ppermute | solution.py:239
  9.9 0.1 collective-permute-done.2.succ_a
  9.9 0.1 collective-permute-start.6
  10.1 0.8 %collective-permute-done.1.prev_b = bf16[512,128]{1,0:T(8,128)(2,1)S(1)} collective-permute-done((bf16[512,128]{1,0:T(8,128)(2,1)S(1)}, bf16[512,128]{1,0:T(8,128)(2,1)S(1)}, u32[]{:S(2)}, u32[]{:S(2)}) %collective-permute-start.1) | collective-permute-done | bytes 131104 | tf_op jit(solution)/shard_map/ppermute | solution.py:239
  10.8 1.8 %collective-permute-start.7 = (bf16[512,128]{1,0:T(8,128)(2,1)S(1)}, bf16[512,128]{1,0:T(8,128)(2,1)S(1)}, u32[]{:S(2)}, u32[]{:S(2)}) collective-permute-start(bf16[512,128]{1,0:T(8,128)(2,1)S(1)} %collective-permute-done.1.prev_b), channel_id=1, source_target_pairs={{0,4},{1,5},{4,8},{5,9},{8,12},{9,13},{12,14},{13,15},{14,10},{15,... | collective-permute-start | bytes 393224 | tf_op jit(solution)/shard_map/ppermute | solution.py:239
  12.7 0.1 collective-permute-done.3.succ_b
  12.7 0.1 collective-permute-start.8
  12.9 0.5 %near_kernel.1 = (f32[1,256]{1,0:T(1,128)S(1)}, bf16[3,1040,128]{2,1,0:T(8,128)(2,1)S(1)}) custom-call(bf16[1040,128]{1,0:T(8,128)(2,1)S(1)} %get-tuple-element.13.own, bf16[528,128]{1,0:T(8,128)(2,1)S(1)} %collective-permute-done.prev_a, bf16[512,128]{1,0:T(8,128)(2,1)S(1)} %collective-permute-done.1.prev_b, ...), custom_call_target="tpu_custom_call" | custom-call | flops 67108864 | bytes 1048576 | tf_op jit(solution)/shard_map/near_kernel/pallas_call | solution.py:220
  13.3 0.2 collective-permute-start.4
  13.5 0.2 collective-permute-done.5.back_a
  13.7 2.3 %collective-permute-done.6.ahead_a = bf16[528,128]{1,0:T(8,128)(2,1)S(1)} collective-permute-done((bf16[528,128]{1,0:T(8,128)(2,1)S(1)}, bf16[528,128]{1,0:T(8,128)(2,1)S(1)}, u32[]{:S(2)}, u32[]{:S(2)}) %collective-permute-start.6) | collective-permute-done | bytes 135200 | tf_op jit(solution)/shard_map/ppermute | solution.py:239
  16.0 0.5 %far_first_kernel.1.found = f32[1,256]{1,0:T(1,128)S(1)} custom-call(bf16[1040,128]{1,0:T(8,128)(2,1)S(1)} %get-tuple-element.13.own, bf16[528,128]{1,0:T(8,128)(2,1)S(1)} %collective-permute-done.prev_a, bf16[512,128]{1,0:T(8,128)(2,1)S(1)} %collective-permute-done.1.prev_b, bf16[528,128]{1,0:T(8,128)(2,1)S(1)} %collective-permute-done.2.succ_a, ...), custom_call_target="tpu_custom_call" | custom-call | flops 13421772800 | bytes 1048576 | tf_op jit(solution)/shard_map/far_first_kernel/pallas_call | solution.py:220
  16.5 0.0 collective-permute-done.7.back_b
  16.5 0.0 collective-permute-done.4.others
  16.5 0.5 %far_back_kernel.1 = (f32[1,256]{1,0:T(1,128)S(1)}, f32[1,128]{1,0:T(1,128)S(1)}) custom-call(bf16[1040,128]{1,0:T(8,128)(2,1)S(1)} %get-tuple-element.13.own, bf16[3,1040,128]{2,1,0:T(8,128)(2,1)S(1)} %collective-permute-done.4.others, bf16[528,128]{1,0:T(8,128)(2,1)S(1)} %collective-permute-done.2.succ_a, ...), custom_call_target="tpu_custom_call" | custom-call | flops 134217728 | bytes 1048576 | tf_op jit(solution)/shard_map/far_back_kernel/pallas_call | solution.py:220
  17.0 1.6 %collective-permute-done.8.ahead_b = bf16[512,128]{1,0:T(8,128)(2,1)S(1)} collective-permute-done((bf16[512,128]{1,0:T(8,128)(2,1)S(1)}, bf16[512,128]{1,0:T(8,128)(2,1)S(1)}, u32[]{:S(2)}, u32[]{:S(2)}) %collective-permute-start.8) | collective-permute-done | bytes 131104 | tf_op jit(solution)/shard_map/ppermute | solution.py:239
  18.6 0.5 %far_last_kernel.1 = (f32[1,256]{1,0:T(1,128)S(1)}, f32[1,256]{1,0:T(1,128)S(1)}) custom-call(bf16[1040,128]{1,0:T(8,128)(2,1)S(1)} %get-tuple-element.13.own, bf16[3,1040,128]{2,1,0:T(8,128)(2,1)S(1)} %collective-permute-done.4.others, bf16[528,128]{1,0:T(8,128)(2,1)S(1)} %collective-permute-done.prev_a, ...), custom_call_target="tpu_custom_call" | custom-call | flops 335544320 | bytes 1048576 | tf_op jit(solution)/shard_map/far_last_kernel/pallas_call | solution.py:220
  19.2 1.1 %collective-permute-start.9 = (f32[1,256]{1,0:T(1,128)S(1)}, f32[1,256]{1,0:T(1,128)S(1)}, u32[]{:S(2)}, u32[]{:S(2)}) collective-permute-start(f32[1,256]{1,0:T(1,128)S(1)} %get-tuple-element.19), channel_id=1, source_target_pairs={{0,6},{1,7},{4,2},{5,3},{8,0},{9,1},{12,4},{13,5},{14,9},{15,8},{1... | collective-permute-start | bytes 3080 | tf_op jit(solution)/shard_map/ppermute | solution.py:239
  20.3 0.9 %collective-permute-start.10 = (f32[1,256]{1,0:T(1,128)S(1)}, f32[1,256]{1,0:T(1,128)S(1)}, u32[]{:S(2)}, u32[]{:S(2)}) collective-permute-start(f32[1,256]{1,0:T(1,128)S(1)} %get-tuple-element.20), channel_id=1, source_target_pairs={{0,9},{1,8},{4,13},{5,12},{8,14},{9,15},{12,10},{13,11},{14,7},{15... | collective-permute-start | bytes 3080 | tf_op jit(solution)/shard_map/ppermute | solution.py:239
  21.2 0.6 %own_kernel.1 = f32[1,256]{1,0:T(1,128)S(1)} custom-call(bf16[1040,128]{1,0:T(8,128)(2,1)S(1)} %get-tuple-element.13.own, bf16[3,1040,128]{2,1,0:T(8,128)(2,1)S(1)} %collective-permute-done.4.others, bf16[528,128]{1,0:T(8,128)(2,1)S(1)} %collective-permute-done.5.back_a, bf16[528,128]{1,0:T(8,128)(2,1)S(1)} %collective-permute-done.6.ahead_a, ...), custom_call_target="tpu_custom_call" | custom-call | flops 335544320 | bytes 1048576 | tf_op jit(solution)/shard_map/own_kernel/pallas_call | solution.py:220
  21.7 1.9 %collective-permute-done.9 = f32[1,256]{1,0:T(1,128)S(1)} collective-permute-done((f32[1,256]{1,0:T(1,128)S(1)}, f32[1,256]{1,0:T(1,128)S(1)}, u32[]{:S(2)}, u32[]{:S(2)}) %collective-permute-start.9) | collective-permute-done | bytes 1056 | tf_op jit(solution)/shard_map/ppermute | solution.py:239
  23.7 0.5 %collective-permute-done.10 = f32[1,256]{1,0:T(1,128)S(1)} collective-permute-done((f32[1,256]{1,0:T(1,128)S(1)}, f32[1,256]{1,0:T(1,128)S(1)}, u32[]{:S(2)}, u32[]{:S(2)}) %collective-permute-start.10) | collective-permute-done | bytes 1056 | tf_op jit(solution)/shard_map/ppermute | solution.py:239
  24.2 0.6 %maximum_maximum_fusion = f32[1,256]{1,0:T(1,128)} fusion(f32[1,256]{1,0:T(1,128)S(1)} %own_kernel.1, f32[1,256]{1,0:T(1,128)S(1)} %collective-permute-done.9, f32[1,256]{1,0:T(1,128)S(1)} %collective-permute-done.10), kind=kLoop, calls=%fused_computation | loop fusion | flops 512 | bytes 4096 | tf_op jit(solution)/shard_map/max | solution.py:290
Async XLA Ops:
  0.0 4.2 %copy-start = (bf16[256,512]{1,0:T(8,128)(2,1)S(1)}, bf16[256,512]{1,0:T(8,128)(2,1)}, u32[]{:S(2)}) copy-start(bf16[256,512]{1,0:T(8,128)(2,1)} %embeds.3) | copy-start | bytes 786436
  1.1 6.9 %collective-permute-start = (bf16[528,128]{1,0:T(8,128)(2,1)S(1)}, bf16[528,128]{1,0:T(8,128)(2,1)S(1)}, u32[]{:S(2)}, u32[]{:S(2)}) collective-permute-start(bf16[528,128]{1,0:T(8,128)(2,1)S(1)} %pack_first.1.first), channel_id=1, source_target_pairs={{0,4},{1,5},{4,8},{5,9},{8,13},{9,12},{12,15},{13,14},{14,10},{15,... | collective-permute-start | bytes 405512 | tf_op jit(solution)/shard_map/ppermute | solution.py:239
  4.2 5.7 %collective-permute-start.2 = (bf16[528,128]{1,0:T(8,128)(2,1)S(1)}, bf16[528,128]{1,0:T(8,128)(2,1)S(1)}, u32[]{:S(2)}, u32[]{:S(2)}) collective-permute-start(bf16[528,128]{1,0:T(8,128)(2,1)S(1)} %pack_first.1.first), channel_id=1, source_target_pairs={{0,3},{1,2},{4,1},{5,0},{8,5},{9,4},{12,9},{13,8},{14,12},{15,13},... | collective-permute-start | bytes 405512 | tf_op jit(solution)/shard_map/ppermute | solution.py:239
  4.3 6.5 %collective-permute-start.1 = (bf16[512,128]{1,0:T(8,128)(2,1)S(1)}, bf16[512,128]{1,0:T(8,128)(2,1)S(1)}, u32[]{:S(2)}, u32[]{:S(2)}) collective-permute-start(bf16[512,128]{1,0:T(8,128)(2,1)S(1)} %get-tuple-element.14), channel_id=1, source_target_pairs={{0,4},{1,5},{4,8},{5,9},{8,13},{9,12},{12,15},{13,14},{14,10},{15,... | collective-permute-start | bytes 393224 | tf_op jit(solution)/shard_map/ppermute | solution.py:239
  6.0 6.8 %collective-permute-start.3 = (bf16[512,128]{1,0:T(8,128)(2,1)S(1)}, bf16[512,128]{1,0:T(8,128)(2,1)S(1)}, u32[]{:S(2)}, u32[]{:S(2)}) collective-permute-start(bf16[512,128]{1,0:T(8,128)(2,1)S(1)} %get-tuple-element.14), channel_id=1, source_target_pairs={{0,3},{1,2},{4,1},{5,0},{8,5},{9,4},{12,9},{13,8},{14,12},{15,13},... | collective-permute-start | bytes 393224 | tf_op jit(solution)/shard_map/ppermute | solution.py:239
  8.0 5.7 %collective-permute-start.5 = (bf16[528,128]{1,0:T(8,128)(2,1)S(1)}, bf16[528,128]{1,0:T(8,128)(2,1)S(1)}, u32[]{:S(2)}, u32[]{:S(2)}) collective-permute-start(bf16[528,128]{1,0:T(8,128)(2,1)S(1)} %collective-permute-done.prev_a), channel_id=1, source_target_pairs={{0,4},{1,5},{4,8},{5,9},{8,12},{9,13},{12,14},{13,15},{14,10},{15,... | collective-permute-start | bytes 405512 | tf_op jit(solution)/shard_map/ppermute | solution.py:239
  9.9 6.0 %collective-permute-start.6 = (bf16[528,128]{1,0:T(8,128)(2,1)S(1)}, bf16[528,128]{1,0:T(8,128)(2,1)S(1)}, u32[]{:S(2)}, u32[]{:S(2)}) collective-permute-start(bf16[528,128]{1,0:T(8,128)(2,1)S(1)} %collective-permute-done.2.succ_a), channel_id=1, source_target_pairs={{0,2},{1,3},{4,0},{5,1},{8,4},{9,5},{12,8},{13,9},{14,12},{15,13},... | collective-permute-start | bytes 405512 | tf_op jit(solution)/shard_map/ppermute | solution.py:239
  10.8 5.6 %collective-permute-start.7 = (bf16[512,128]{1,0:T(8,128)(2,1)S(1)}, bf16[512,128]{1,0:T(8,128)(2,1)S(1)}, u32[]{:S(2)}, u32[]{:S(2)}) collective-permute-start(bf16[512,128]{1,0:T(8,128)(2,1)S(1)} %collective-permute-done.1.prev_b), channel_id=1, source_target_pairs={{0,4},{1,5},{4,8},{5,9},{8,12},{9,13},{12,14},{13,15},{14,10},{15,... | collective-permute-start | bytes 393224 | tf_op jit(solution)/shard_map/ppermute | solution.py:239
  12.7 5.9 %collective-permute-start.8 = (bf16[512,128]{1,0:T(8,128)(2,1)S(1)}, bf16[512,128]{1,0:T(8,128)(2,1)S(1)}, u32[]{:S(2)}, u32[]{:S(2)}) collective-permute-start(bf16[512,128]{1,0:T(8,128)(2,1)S(1)} %collective-permute-done.3.succ_b), channel_id=1, source_target_pairs={{0,2},{1,3},{4,0},{5,1},{8,4},{9,5},{12,8},{13,9},{14,12},{15,13},... | collective-permute-start | bytes 393224 | tf_op jit(solution)/shard_map/ppermute | solution.py:239
  13.3 3.1 %collective-permute-start.4 = (bf16[3,1040,128]{2,1,0:T(8,128)(2,1)S(1)}, bf16[3,1040,128]{2,1,0:T(8,128)(2,1)S(1)}, u32[]{:S(2)}, u32[]{:S(2)}) collective-permute-start(bf16[3,1040,128]{2,1,0:T(8,128)(2,1)S(1)} %get-tuple-element.15), channel_id=1, source_target_pairs={{0,1},{1,0},{4,5},{5,4},{8,9},{9,8},{12,13},{13,12},{14,15},{15,14... | collective-permute-start | bytes 2396168 | tf_op jit(solution)/shard_map/ppermute | solution.py:239
  19.2 4.5 %collective-permute-start.9 = (f32[1,256]{1,0:T(1,128)S(1)}, f32[1,256]{1,0:T(1,128)S(1)}, u32[]{:S(2)}, u32[]{:S(2)}) collective-permute-start(f32[1,256]{1,0:T(1,128)S(1)} %get-tuple-element.19), channel_id=1, source_target_pairs={{0,6},{1,7},{4,2},{5,3},{8,0},{9,1},{12,4},{13,5},{14,9},{15,8},{1... | collective-permute-start | bytes 3080 | tf_op jit(solution)/shard_map/ppermute | solution.py:239
  20.3 3.9 %collective-permute-start.10 = (f32[1,256]{1,0:T(1,128)S(1)}, f32[1,256]{1,0:T(1,128)S(1)}, u32[]{:S(2)}, u32[]{:S(2)}) collective-permute-start(f32[1,256]{1,0:T(1,128)S(1)} %get-tuple-element.20), channel_id=1, source_target_pairs={{0,9},{1,8},{4,13},{5,12},{8,14},{9,15},{12,10},{13,11},{14,7},{15... | collective-permute-start | bytes 3080 | tf_op jit(solution)/shard_map/ppermute | solution.py:239

commit v14 on v9

--- a/solution.py
+++ b/solution.py
@@ -169,15 +169,37 @@
     ahead[...] = jnp.maximum(found[:, half:], best_of(first_ahead, rest, prev_other))
 
 
+def place_and_core():
+    x, y = lax.axis_index("gx"), lax.axis_index("gy")
+    chips = lax.axis_size("gx") * lax.axis_size("gy")
+    return jnp.where(y == 0, x, chips - 1 - x), lax.axis_index("gz")
+
+
+def line_of(place, core):
+    return place % (lax.axis_size("gx") * lax.axis_size("gy")) * lax.axis_size("gz") + core
+
+
 def far_last_kernel(own, others, prev_a, prev_b, back_a, ahead_a, back_b, ahead_b, *refs):
-    back_found, ahead_found, to_back, to_ahead = refs
-    rows = to_back.shape[1]
+    back_found, ahead_found, table = refs
+    rows = table.shape[1]
     half = rows // 2
     back, rest = whole(back_a, back_b, rows), second_half(ahead_a, ahead_b, rows)
     keys = packed(own, rows), whole(prev_a, prev_b, rows), packed(others.at[0], rows), back
-    to_back[...] = jnp.maximum(back_found[...], best_of(back, rest))
-    to_ahead[:, :half] = ahead_found[...]
-    to_ahead[:, half:] = best_of(rest, *keys)
+    place, core = place_and_core()
+    chips = lax.axis_size("gx") * lax.axis_size("gy")
+    to_back = line_of(place + chips - 2, core ^ changes((place + chips - 1) % chips))
+    to_ahead = line_of(place + 2, core ^ 1 ^ changes((place + 1) % chips))
+    back_best = jnp.maximum(back_found[...], best_of(back, rest))
+    ahead_best = jnp.concatenate([ahead_found[...], best_of(rest, *keys)], axis=1)
+    line = lax.broadcasted_iota(jnp.int32, table.shape, 0)
+    others_best = jnp.where(line == to_ahead, ahead_best, -1.0)
+    table[...] = jnp.where(line == to_back, back_best, others_best)
+
+
+def last_kernel(table, mine, best):
+    line = lax.broadcasted_iota(jnp.int32, table.shape, 0)
+    found = jnp.where(line == line_of(*place_and_core()), table[...], -1.0)
+    best[...] = jnp.maximum(mine[...], jnp.max(found, axis=0, keepdims=True))
 
 
 def own_kernel(own, others, back_a, ahead_a, back_b, ahead_b, near, mine):
@@ -185,6 +207,10 @@
     keys = [packed(others.at[at], rows) for at in range(3)]
     keys += [whole(back_a, back_b, rows), whole(ahead_a, ahead_b, rows)]
     mine[...] = jnp.maximum(near[...], best_of(packed(own, rows), *keys))
+
+
+def changes(place):
+    return jnp.int32(place < 2)
 
 
 def ring_perms(size_x, size_y, size_z):
@@ -285,13 +311,15 @@
         [line, half_line],
         BACK_COST,
     )
-    to_back, to_ahead = kernel_call(
-        far_last_kernel, [own, others, *prev, *far, *found], [line] * 2, LAST_COST
+    devices = lax.axis_size(GROUP)
+    (table,) = kernel_call(
+        far_last_kernel,
+        [own, others, *prev, *far, *found],
+        [jax.ShapeDtypeStruct((devices, rows), jnp.float32)],
+        LAST_COST,
     )
     (mine,) = kernel_call(own_kernel, [own, others, *far, mine], [line], 5)
-    best = jnp.maximum(
-        mine, jnp.maximum(send(to_back, "home_back"), send(to_ahead, "home_ahead"))
-    )
+    (best,) = kernel_call(last_kernel, [lax.pmax(table, GROUP), mine], [line], 1)
     return best.reshape(rows)
 
 

time: 24.9 us -> 80.1 us (3.22)
  blocking collectives: 0 us -> 60 us
  starting transfers between devices: 12.9 us -> 9.86 us
  waiting for transfers between devices: 7.49 us -> 5.71 us
    pmax x0 -> x1, blocking collectives: none -> 60 us  [on_ring(): best, = kernel_call(last_kernel, [lax.pmax(table, GROUP), mine], [line], 1)]
    ppermute x11 -> x9, starting transfers between devices: 12.9 us -> 9.86 us  [send(): return lax.ppermute(value, GROUP, perms[name])]
    ppermute x11 -> x9, waiting for transfers between devices: 7.49 us -> 5.71 us  [send(): return lax.ppermute(value, GROUP, perms[name])]
    pallas_call x6 -> x7, Pallas kernels: 2.68 us -> 3.27 us  [kernel_call(): pl.pallas_call(kernel, out_shape=outputs, in_specs=[vmem] * len(inputs),...]
  transfers between devices with their start and end apart: 11 -> 9, of which waited for: 8 -> 6; matrix products, arithmetic and copies ran while one was open for 0% -> 0% of each run, Pallas kernels for 9% -> 2%
where the time goes in v14:
time: 80.1 us; the launch traced here: 80 us
  blocking collectives  60 us (75%)
  starting transfers between devices  9.86 us (12%)
  waiting for transfers between devices  5.71 us (7%)
  Pallas kernels  4.37 us (5%)
    pmax x1, blocking collectives, on_ring(): best, = kernel_call(last_kernel, [lax.pmax(table, GROUP), mine], [line], 1)  60 us
    ppermute x9, starting transfers between devices, send(): return lax.ppermute(value, GROUP, perms[name])  9.86 us
    ppermute x9, waiting for transfers between devices, send(): return lax.ppermute(value, GROUP, perms[name])  5.71 us
    pallas_call x7, Pallas kernels, kernel_call(): pl.pallas_call(kernel, out_shape=outputs, in_specs=[vmem] * len(inputs),...  3.27 us
  transfers between devices with their start and end apart: 9, of which 6 were waited for; matrix products, arithmetic and copies ran while one was open for 0% of the time, Pallas kernels for 2%

profile of v14, /device:TPU:0, one launch (start us, length us, event | category | flops | bytes accessed | tf_op | source)
XLA Modules:
  0.0 80.0 jit_solution(8975343951475054619)
XLA Ops:
  0.0 0.0 copy-start
  0.0 1.1 %pack_first.1.first = bf16[528,128]{1,0:T(8,128)(2,1)S(1)} custom-call(bf16[256,512]{1,0:T(8,128)(2,1)} %embeds.3, s32[1,256]{1,0:T(1,128)} %bitcast.2), custom_call_target="tpu_custom_call" | custom-call | tf_op jit(solution)/shard_map/pack_first/pallas_call | solution.py:278
  1.1 2.5 %collective-permute-start = (bf16[528,128]{1,0:T(8,128)(2,1)S(1)}, bf16[528,128]{1,0:T(8,128)(2,1)S(1)}, u32[]{:S(2)}, u32[]{:S(2)}) collective-permute-start(bf16[528,128]{1,0:T(8,128)(2,1)S(1)} %pack_first.1.first), channel_id=1, source_target_pairs={{0,5},{1,4},{4,8},{5,9},{8,12},{9,13},{12,14},{13,15},{14,10},{15,... | collective-permute-start | bytes 405512 | tf_op jit(solution)/shard_map/ppermute | solution.py:267
  3.6 0.0 collective-permute-start.2
  3.6 0.0 copy-done
  3.6 0.1 pack_second_kernel.1
  3.8 2.1 %collective-permute-start.1 = (bf16[512,128]{1,0:T(8,128)(2,1)S(1)}, bf16[512,128]{1,0:T(8,128)(2,1)S(1)}, u32[]{:S(2)}, u32[]{:S(2)}) collective-permute-start(bf16[512,128]{1,0:T(8,128)(2,1)S(1)} %get-tuple-element.12), channel_id=1, source_target_pairs={{0,5},{1,4},{4,8},{5,9},{8,12},{9,13},{12,14},{13,15},{14,10},{15,... | collective-permute-start | bytes 393224 | tf_op jit(solution)/shard_map/ppermute | solution.py:267
  5.9 0.3 collective-permute-start.3
  6.1 1.5 %collective-permute-done.prev_a = bf16[528,128]{1,0:T(8,128)(2,1)S(1)} collective-permute-done((bf16[528,128]{1,0:T(8,128)(2,1)S(1)}, bf16[528,128]{1,0:T(8,128)(2,1)S(1)}, u32[]{:S(2)}, u32[]{:S(2)}) %collective-permute-start) | collective-permute-done | bytes 135200 | tf_op jit(solution)/shard_map/ppermute | solution.py:267
  7.6 2.5 %collective-permute-start.5 = (bf16[528,128]{1,0:T(8,128)(2,1)S(1)}, bf16[528,128]{1,0:T(8,128)(2,1)S(1)}, u32[]{:S(2)}, u32[]{:S(2)}) collective-permute-start(bf16[528,128]{1,0:T(8,128)(2,1)S(1)} %collective-permute-done.prev_a), channel_id=1, source_target_pairs={{0,4},{1,5},{4,8},{5,9},{8,12},{9,13},{12,14},{13,15},{14,10},{15,... | collective-permute-start | bytes 405512 | tf_op jit(solution)/shard_map/ppermute | solution.py:267
  10.1 0.0 collective-permute-done.2.succ_a
  10.1 0.0 collective-permute-start.6
  10.1 0.3 collective-permute-done.1.prev_b
  10.4 2.5 %collective-permute-start.7 = (bf16[512,128]{1,0:T(8,128)(2,1)S(1)}, bf16[512,128]{1,0:T(8,128)(2,1)S(1)}, u32[]{:S(2)}, u32[]{:S(2)}) collective-permute-start(bf16[512,128]{1,0:T(8,128)(2,1)S(1)} %collective-permute-done.1.prev_b), channel_id=1, source_target_pairs={{0,4},{1,5},{4,8},{5,9},{8,12},{9,13},{12,14},{13,15},{14,10},{15,... | collective-permute-start | bytes 393224 | tf_op jit(solution)/shard_map/ppermute | solution.py:267
  12.9 0.0 collective-permute-done.3.succ_b
  12.9 0.0 collective-permute-start.8
  12.9 0.5 near_kernel.1
  13.3 0.1 collective-permute-start.4
  13.4 0.6 collective-permute-done.5.back_a
  14.0 1.6 %collective-permute-done.6.ahead_a = bf16[528,128]{1,0:T(8,128)(2,1)S(1)} collective-permute-done((bf16[528,128]{1,0:T(8,128)(2,1)S(1)}, bf16[528,128]{1,0:T(8,128)(2,1)S(1)}, u32[]{:S(2)}, u32[]{:S(2)}) %collective-permute-start.6) | collective-permute-done | bytes 135200 | tf_op jit(solution)/shard_map/ppermute | solution.py:267
  15.6 0.5 far_first_kernel.1.found
  16.1 0.3 collective-permute-done.7.back_b
  16.4 0.0 collective-permute-done.4.others
  16.4 0.5 far_back_kernel.1
  17.0 1.3 %collective-permute-done.8.ahead_b = bf16[512,128]{1,0:T(8,128)(2,1)S(1)} collective-permute-done((bf16[512,128]{1,0:T(8,128)(2,1)S(1)}, bf16[512,128]{1,0:T(8,128)(2,1)S(1)}, u32[]{:S(2)}, u32[]{:S(2)}) %collective-permute-start.8) | collective-permute-done | bytes 131104 | tf_op jit(solution)/shard_map/ppermute | solution.py:267
  18.3 0.5 far_last_kernel.1
  18.9 60.0 %pmax.7.table = f32[16,256]{1,0:T(8,128)S(1)} all-reduce(f32[16,256]{1,0:T(8,128)S(1)} %far_last_kernel.1), channel_id=1, replica_groups=mesh['parts'=2,'gx'=4,'gy'=2,'gz'=2] {'gx','gy','gz'}, use_global_device_ids=true, to_apply=%region_0.0 | all-reduce | flops 4096 | bytes 32768 | tf_op jit(solution)/shard_map/pmax | solution.py:322
  78.8 0.5 own_kernel.1.mine
  79.4 0.6 last_kernel.1
Async XLA Ops:
  0.0 3.6 %copy-start = (bf16[256,512]{1,0:T(8,128)(2,1)S(1)}, bf16[256,512]{1,0:T(8,128)(2,1)}, u32[]{:S(2)}) copy-start(bf16[256,512]{1,0:T(8,128)(2,1)} %embeds.3) | copy-start | bytes 786436
  1.1 6.5 %collective-permute-start = (bf16[528,128]{1,0:T(8,128)(2,1)S(1)}, bf16[528,128]{1,0:T(8,128)(2,1)S(1)}, u32[]{:S(2)}, u32[]{:S(2)}) collective-permute-start(bf16[528,128]{1,0:T(8,128)(2,1)S(1)} %pack_first.1.first), channel_id=1, source_target_pairs={{0,5},{1,4},{4,8},{5,9},{8,12},{9,13},{12,14},{13,15},{14,10},{15,... | collective-permute-start | bytes 405512 | tf_op jit(solution)/shard_map/ppermute | solution.py:267
  3.6 6.5 %collective-permute-start.2 = (bf16[528,128]{1,0:T(8,128)(2,1)S(1)}, bf16[528,128]{1,0:T(8,128)(2,1)S(1)}, u32[]{:S(2)}, u32[]{:S(2)}) collective-permute-start(bf16[528,128]{1,0:T(8,128)(2,1)S(1)} %pack_first.1.first), channel_id=1, source_target_pairs={{0,3},{1,2},{4,0},{5,1},{8,4},{9,5},{12,9},{13,8},{14,13},{15,12},... | collective-permute-start | bytes 405512 | tf_op jit(solution)/shard_map/ppermute | solution.py:267
  3.8 6.6 %collective-permute-start.1 = (bf16[512,128]{1,0:T(8,128)(2,1)S(1)}, bf16[512,128]{1,0:T(8,128)(2,1)S(1)}, u32[]{:S(2)}, u32[]{:S(2)}) collective-permute-start(bf16[512,128]{1,0:T(8,128)(2,1)S(1)} %get-tuple-element.12), channel_id=1, source_target_pairs={{0,5},{1,4},{4,8},{5,9},{8,12},{9,13},{12,14},{13,15},{14,10},{15,... | collective-permute-start | bytes 393224 | tf_op jit(solution)/shard_map/ppermute | solution.py:267
  5.9 7.0 %collective-permute-start.3 = (bf16[512,128]{1,0:T(8,128)(2,1)S(1)}, bf16[512,128]{1,0:T(8,128)(2,1)S(1)}, u32[]{:S(2)}, u32[]{:S(2)}) collective-permute-start(bf16[512,128]{1,0:T(8,128)(2,1)S(1)} %get-tuple-element.12), channel_id=1, source_target_pairs={{0,3},{1,2},{4,0},{5,1},{8,4},{9,5},{12,9},{13,8},{14,13},{15,12},... | collective-permute-start | bytes 393224 | tf_op jit(solution)/shard_map/ppermute | solution.py:267
  7.6 6.4 %collective-permute-start.5 = (bf16[528,128]{1,0:T(8,128)(2,1)S(1)}, bf16[528,128]{1,0:T(8,128)(2,1)S(1)}, u32[]{:S(2)}, u32[]{:S(2)}) collective-permute-start(bf16[528,128]{1,0:T(8,128)(2,1)S(1)} %collective-permute-done.prev_a), channel_id=1, source_target_pairs={{0,4},{1,5},{4,8},{5,9},{8,12},{9,13},{12,14},{13,15},{14,10},{15,... | collective-permute-start | bytes 405512 | tf_op jit(solution)/shard_map/ppermute | solution.py:267
  10.1 5.5 %collective-permute-start.6 = (bf16[528,128]{1,0:T(8,128)(2,1)S(1)}, bf16[528,128]{1,0:T(8,128)(2,1)S(1)}, u32[]{:S(2)}, u32[]{:S(2)}) collective-permute-start(bf16[528,128]{1,0:T(8,128)(2,1)S(1)} %collective-permute-done.2.succ_a), channel_id=1, source_target_pairs={{0,2},{1,3},{4,0},{5,1},{8,4},{9,5},{12,8},{13,9},{14,12},{15,13},... | collective-permute-start | bytes 405512 | tf_op jit(solution)/shard_map/ppermute | solution.py:267
  10.4 6.0 %collective-permute-start.7 = (bf16[512,128]{1,0:T(8,128)(2,1)S(1)}, bf16[512,128]{1,0:T(8,128)(2,1)S(1)}, u32[]{:S(2)}, u32[]{:S(2)}) collective-permute-start(bf16[512,128]{1,0:T(8,128)(2,1)S(1)} %collective-permute-done.1.prev_b), channel_id=1, source_target_pairs={{0,4},{1,5},{4,8},{5,9},{8,12},{9,13},{12,14},{13,15},{14,10},{15,... | collective-permute-start | bytes 393224 | tf_op jit(solution)/shard_map/ppermute | solution.py:267
  12.9 5.4 %collective-permute-start.8 = (bf16[512,128]{1,0:T(8,128)(2,1)S(1)}, bf16[512,128]{1,0:T(8,128)(2,1)S(1)}, u32[]{:S(2)}, u32[]{:S(2)}) collective-permute-start(bf16[512,128]{1,0:T(8,128)(2,1)S(1)} %collective-permute-done.3.succ_b), channel_id=1, source_target_pairs={{0,2},{1,3},{4,0},{5,1},{8,4},{9,5},{12,8},{13,9},{14,12},{15,13},... | collective-permute-start | bytes 393224 | tf_op jit(solution)/shard_map/ppermute | solution.py:267
  13.3 3.1 %collective-permute-start.4 = (bf16[3,1040,128]{2,1,0:T(8,128)(2,1)S(1)}, bf16[3,1040,128]{2,1,0:T(8,128)(2,1)S(1)}, u32[]{:S(2)}, u32[]{:S(2)}) collective-permute-start(bf16[3,1040,128]{2,1,0:T(8,128)(2,1)S(1)} %get-tuple-element.13), channel_id=1, source_target_pairs={{0,1},{1,0},{4,5},{5,4},{8,9},{9,8},{12,13},{13,12},{14,15},{15,14... | collective-permute-start | bytes 2396168 | tf_op jit(solution)/shard_map/ppermute | solution.py:267

commit v15 on v9

--- a/solution.py
+++ b/solution.py
@@ -192,7 +192,7 @@
 
     def device(place, core):
         place = place % chips
-        x, y = (place, 0) if place < size_x else (chips - 1 - place, 1)
+        x, y = (place, 1) if place < size_x else (chips - 1 - place, 0)
         return (x * size_y + y) * size_z + core
 
     def perm(to):

time: 24.9 us -> 25 us (level)
  starting transfers between devices: 12.9 us -> 11.5 us
  waiting for transfers between devices: 7.49 us -> 8.87 us
    ppermute x11, waiting for transfers between devices: 7.49 us -> 8.87 us  [send(): return lax.ppermute(value, GROUP, perms[name])]
    ppermute x11, starting transfers between devices: 12.9 us -> 11.5 us  [send(): return lax.ppermute(value, GROUP, perms[name])]
  transfers between devices with their start and end apart: 11 -> 11, of which waited for: 8 -> 7; matrix products, arithmetic and copies ran while one was open for 0% -> 0% of each run, Pallas kernels for 9% -> 9%
where the time goes in v15:
time: 25 us; the launch traced here: 24.8 us
  starting transfers between devices  11.5 us (46%)
  waiting for transfers between devices  8.87 us (35%)
  Pallas kernels  3.78 us (15%)
  other arithmetic  0.57 us (2%)
    ppermute x11, starting transfers between devices, send(): return lax.ppermute(value, GROUP, perms[name])  11.5 us
    ppermute x11, waiting for transfers between devices, send(): return lax.ppermute(value, GROUP, perms[name])  8.87 us
    pallas_call x6, Pallas kernels, kernel_call(): pl.pallas_call(kernel, out_shape=outputs, in_specs=[vmem] * len(inputs),...  2.68 us
    pallas_call x1, Pallas kernels, on_ring(): pl.pallas_call(pack_first_kernel, out_shape=chunk(half, True), in_specs=[...  1.1 us
    max x1, other arithmetic, on_ring(): jnp.maximum(mine, jnp.maximum(send(to_back, 'home_back'), send(to_ahead,...  0.57 us
  transfers between devices with their start and end apart: 11, of which 7 were waited for; matrix products, arithmetic and copies ran while one was open for 0% of the time, Pallas kernels for 9%

profile of v15, /device:TPU:0, one launch (start us, length us, event | category | flops | bytes accessed | tf_op | source)
XLA Modules:
  0.0 24.8 jit_solution(13745679099069583337)
XLA Ops:
  0.0 0.0 copy-start
  0.0 1.1 %pack_first.1.first = bf16[528,128]{1,0:T(8,128)(2,1)S(1)} custom-call(bf16[256,512]{1,0:T(8,128)(2,1)} %embeds.3, s32[1,256]{1,0:T(1,128)} %bitcast.2), custom_call_target="tpu_custom_call" | custom-call | tf_op jit(solution)/shard_map/pack_first/pallas_call | solution.py:252
  1.1 2.4 %collective-permute-start = (bf16[528,128]{1,0:T(8,128)(2,1)S(1)}, bf16[528,128]{1,0:T(8,128)(2,1)S(1)}, u32[]{:S(2)}, u32[]{:S(2)}) collective-permute-start(bf16[528,128]{1,0:T(8,128)(2,1)S(1)} %pack_first.1.first), channel_id=1, source_target_pairs={{2,7},{3,6},{6,10},{7,11},{10,14},{11,15},{14,12},{15,13},{12,8},{... | collective-permute-start | bytes 405512 | tf_op jit(solution)/shard_map/ppermute | solution.py:241
  3.6 0.2 collective-permute-start.2
  3.7 0.0 copy-done
  3.7 0.1 pack_second_kernel.1
  3.8 1.8 %collective-permute-start.1 = (bf16[512,128]{1,0:T(8,128)(2,1)S(1)}, bf16[512,128]{1,0:T(8,128)(2,1)S(1)}, u32[]{:S(2)}, u32[]{:S(2)}) collective-permute-start(bf16[512,128]{1,0:T(8,128)(2,1)S(1)} %get-tuple-element.14), channel_id=1, source_target_pairs={{2,7},{3,6},{6,10},{7,11},{10,14},{11,15},{14,12},{15,13},{12,8},{... | collective-permute-start | bytes 393224 | tf_op jit(solution)/shard_map/ppermute | solution.py:241
  5.6 0.6 %collective-permute-start.3 = (bf16[512,128]{1,0:T(8,128)(2,1)S(1)}, bf16[512,128]{1,0:T(8,128)(2,1)S(1)}, u32[]{:S(2)}, u32[]{:S(2)}) collective-permute-start(bf16[512,128]{1,0:T(8,128)(2,1)S(1)} %get-tuple-element.14), channel_id=1, source_target_pairs={{2,1},{3,0},{6,2},{7,3},{10,6},{11,7},{14,11},{15,10},{12,15},{13,... | collective-permute-start | bytes 393224 | tf_op jit(solution)/shard_map/ppermute | solution.py:241
  6.2 1.9 %collective-permute-done.prev_a = bf16[528,128]{1,0:T(8,128)(2,1)S(1)} collective-permute-done((bf16[528,128]{1,0:T(8,128)(2,1)S(1)}, bf16[528,128]{1,0:T(8,128)(2,1)S(1)}, u32[]{:S(2)}, u32[]{:S(2)}) %collective-permute-start) | collective-permute-done | bytes 135200 | tf_op jit(solution)/shard_map/ppermute | solution.py:241
  8.1 1.9 %collective-permute-start.5 = (bf16[528,128]{1,0:T(8,128)(2,1)S(1)}, bf16[528,128]{1,0:T(8,128)(2,1)S(1)}, u32[]{:S(2)}, u32[]{:S(2)}) collective-permute-start(bf16[528,128]{1,0:T(8,128)(2,1)S(1)} %collective-permute-done.prev_a), channel_id=1, source_target_pairs={{2,6},{3,7},{6,10},{7,11},{10,14},{11,15},{14,12},{15,13},{12,8},{... | collective-permute-start | bytes 405512 | tf_op jit(solution)/shard_map/ppermute | solution.py:241
  10.0 0.0 collective-permute-done.2.succ_a
  10.0 0.2 collective-permute-start.6
  10.1 0.8 %collective-permute-done.1.prev_b = bf16[512,128]{1,0:T(8,128)(2,1)S(1)} collective-permute-done((bf16[512,128]{1,0:T(8,128)(2,1)S(1)}, bf16[512,128]{1,0:T(8,128)(2,1)S(1)}, u32[]{:S(2)}, u32[]{:S(2)}) %collective-permute-start.1) | collective-permute-done | bytes 131104 | tf_op jit(solution)/shard_map/ppermute | solution.py:241
  10.9 1.9 %collective-permute-start.7 = (bf16[512,128]{1,0:T(8,128)(2,1)S(1)}, bf16[512,128]{1,0:T(8,128)(2,1)S(1)}, u32[]{:S(2)}, u32[]{:S(2)}) collective-permute-start(bf16[512,128]{1,0:T(8,128)(2,1)S(1)} %collective-permute-done.1.prev_b), channel_id=1, source_target_pairs={{2,6},{3,7},{6,10},{7,11},{10,14},{11,15},{14,12},{15,13},{12,8},{... | collective-permute-start | bytes 393224 | tf_op jit(solution)/shard_map/ppermute | solution.py:241
  12.8 0.0 collective-permute-done.3.succ_b
  12.8 0.2 collective-permute-start.8
  13.0 0.5 %near_kernel.1 = (f32[1,256]{1,0:T(1,128)S(1)}, bf16[3,1040,128]{2,1,0:T(8,128)(2,1)S(1)}) custom-call(bf16[1040,128]{1,0:T(8,128)(2,1)S(1)} %get-tuple-element.13.own, bf16[528,128]{1,0:T(8,128)(2,1)S(1)} %collective-permute-done.prev_a, bf16[512,128]{1,0:T(8,128)(2,1)S(1)} %collective-permute-done.1.prev_b, ...), custom_call_target="tpu_custom_call" | custom-call | flops 67108864 | bytes 1048576 | tf_op jit(solution)/shard_map/near_kernel/pallas_call | solution.py:222
  13.4 0.1 collective-permute-start.4
  13.5 0.4 %collective-permute-done.5.back_a = bf16[528,128]{1,0:T(8,128)(2,1)S(1)} collective-permute-done((bf16[528,128]{1,0:T(8,128)(2,1)S(1)}, bf16[528,128]{1,0:T(8,128)(2,1)S(1)}, u32[]{:S(2)}, u32[]{:S(2)}) %collective-permute-start.5) | collective-permute-done | bytes 135200 | tf_op jit(solution)/shard_map/ppermute | solution.py:241
  13.9 2.5 %collective-permute-done.6.ahead_a = bf16[528,128]{1,0:T(8,128)(2,1)S(1)} collective-permute-done((bf16[528,128]{1,0:T(8,128)(2,1)S(1)}, bf16[528,128]{1,0:T(8,128)(2,1)S(1)}, u32[]{:S(2)}, u32[]{:S(2)}) %collective-permute-start.6) | collective-permute-done | bytes 135200 | tf_op jit(solution)/shard_map/ppermute | solution.py:241
  16.4 0.5 %far_first_kernel.1.found = f32[1,256]{1,0:T(1,128)S(1)} custom-call(bf16[1040,128]{1,0:T(8,128)(2,1)S(1)} %get-tuple-element.13.own, bf16[528,128]{1,0:T(8,128)(2,1)S(1)} %collective-permute-done.prev_a, bf16[512,128]{1,0:T(8,128)(2,1)S(1)} %collective-permute-done.1.prev_b, bf16[528,128]{1,0:T(8,128)(2,1)S(1)} %collective-permute-done.2.succ_a, ...), custom_call_target="tpu_custom_call" | custom-call | flops 13421772800 | bytes 1048576 | tf_op jit(solution)/shard_map/far_first_kernel/pallas_call | solution.py:222
  16.9 0.0 collective-permute-done.7.back_b
  16.9 0.0 collective-permute-done.4.others
  16.9 0.5 %far_back_kernel.1 = (f32[1,256]{1,0:T(1,128)S(1)}, f32[1,128]{1,0:T(1,128)S(1)}) custom-call(bf16[1040,128]{1,0:T(8,128)(2,1)S(1)} %get-tuple-element.13.own, bf16[3,1040,128]{2,1,0:T(8,128)(2,1)S(1)} %collective-permute-done.4.others, bf16[528,128]{1,0:T(8,128)(2,1)S(1)} %collective-permute-done.2.succ_a, ...), custom_call_target="tpu_custom_call" | custom-call | flops 134217728 | bytes 1048576 | tf_op jit(solution)/shard_map/far_back_kernel/pallas_call | solution.py:222
  17.5 1.2 %collective-permute-done.8.ahead_b = bf16[512,128]{1,0:T(8,128)(2,1)S(1)} collective-permute-done((bf16[512,128]{1,0:T(8,128)(2,1)S(1)}, bf16[512,128]{1,0:T(8,128)(2,1)S(1)}, u32[]{:S(2)}, u32[]{:S(2)}) %collective-permute-start.8) | collective-permute-done | bytes 131104 | tf_op jit(solution)/shard_map/ppermute | solution.py:241
  18.7 0.5 %far_last_kernel.1 = (f32[1,256]{1,0:T(1,128)S(1)}, f32[1,256]{1,0:T(1,128)S(1)}) custom-call(bf16[1040,128]{1,0:T(8,128)(2,1)S(1)} %get-tuple-element.13.own, bf16[3,1040,128]{2,1,0:T(8,128)(2,1)S(1)} %collective-permute-done.4.others, bf16[528,128]{1,0:T(8,128)(2,1)S(1)} %collective-permute-done.prev_a, ...), custom_call_target="tpu_custom_call" | custom-call | flops 335544320 | bytes 1048576 | tf_op jit(solution)/shard_map/far_last_kernel/pallas_call | solution.py:222
  19.2 1.2 %collective-permute-start.9 = (f32[1,256]{1,0:T(1,128)S(1)}, f32[1,256]{1,0:T(1,128)S(1)}, u32[]{:S(2)}, u32[]{:S(2)}) collective-permute-start(f32[1,256]{1,0:T(1,128)S(1)} %get-tuple-element.19), channel_id=1, source_target_pairs={{2,4},{3,5},{6,1},{7,0},{10,3},{11,2},{14,6},{15,7},{12,10},{13,11... | collective-permute-start | bytes 3080 | tf_op jit(solution)/shard_map/ppermute | solution.py:241
  20.4 1.3 %collective-permute-start.10 = (f32[1,256]{1,0:T(1,128)S(1)}, f32[1,256]{1,0:T(1,128)S(1)}, u32[]{:S(2)}, u32[]{:S(2)}) collective-permute-start(f32[1,256]{1,0:T(1,128)S(1)} %get-tuple-element.20), channel_id=1, source_target_pairs={{2,10},{3,11},{6,15},{7,14},{10,13},{11,12},{14,9},{15,8},{12,5},{... | collective-permute-start | bytes 3080 | tf_op jit(solution)/shard_map/ppermute | solution.py:241
  21.7 0.6 %own_kernel.1 = f32[1,256]{1,0:T(1,128)S(1)} custom-call(bf16[1040,128]{1,0:T(8,128)(2,1)S(1)} %get-tuple-element.13.own, bf16[3,1040,128]{2,1,0:T(8,128)(2,1)S(1)} %collective-permute-done.4.others, bf16[528,128]{1,0:T(8,128)(2,1)S(1)} %collective-permute-done.5.back_a, bf16[528,128]{1,0:T(8,128)(2,1)S(1)} %collective-permute-done.6.ahead_a, ...), custom_call_target="tpu_custom_call" | custom-call | flops 335544320 | bytes 1048576 | tf_op jit(solution)/shard_map/own_kernel/pallas_call | solution.py:222
  22.2 0.9 %collective-permute-done.9 = f32[1,256]{1,0:T(1,128)S(1)} collective-permute-done((f32[1,256]{1,0:T(1,128)S(1)}, f32[1,256]{1,0:T(1,128)S(1)}, u32[]{:S(2)}, u32[]{:S(2)}) %collective-permute-start.9) | collective-permute-done | bytes 1056 | tf_op jit(solution)/shard_map/ppermute | solution.py:241
  23.1 1.1 %collective-permute-done.10 = f32[1,256]{1,0:T(1,128)S(1)} collective-permute-done((f32[1,256]{1,0:T(1,128)S(1)}, f32[1,256]{1,0:T(1,128)S(1)}, u32[]{:S(2)}, u32[]{:S(2)}) %collective-permute-start.10) | collective-permute-done | bytes 1056 | tf_op jit(solution)/shard_map/ppermute | solution.py:241
  24.3 0.6 %maximum_maximum_fusion = f32[1,256]{1,0:T(1,128)} fusion(f32[1,256]{1,0:T(1,128)S(1)} %own_kernel.1, f32[1,256]{1,0:T(1,128)S(1)} %collective-permute-done.9, f32[1,256]{1,0:T(1,128)S(1)} %collective-permute-done.10), kind=kLoop, calls=%fused_computation | loop fusion | flops 512 | bytes 4096 | tf_op jit(solution)/shard_map/max | solution.py:292
Async XLA Ops:
  0.0 3.7 %copy-start = (bf16[256,512]{1,0:T(8,128)(2,1)S(1)}, bf16[256,512]{1,0:T(8,128)(2,1)}, u32[]{:S(2)}) copy-start(bf16[256,512]{1,0:T(8,128)(2,1)} %embeds.3) | copy-start | bytes 786436
  1.1 7.0 %collective-permute-start = (bf16[528,128]{1,0:T(8,128)(2,1)S(1)}, bf16[528,128]{1,0:T(8,128)(2,1)S(1)}, u32[]{:S(2)}, u32[]{:S(2)}) collective-permute-start(bf16[528,128]{1,0:T(8,128)(2,1)S(1)} %pack_first.1.first), channel_id=1, source_target_pairs={{2,7},{3,6},{6,10},{7,11},{10,14},{11,15},{14,12},{15,13},{12,8},{... | collective-permute-start | bytes 405512 | tf_op jit(solution)/shard_map/ppermute | solution.py:241
  3.6 6.4 %collective-permute-start.2 = (bf16[528,128]{1,0:T(8,128)(2,1)S(1)}, bf16[528,128]{1,0:T(8,128)(2,1)S(1)}, u32[]{:S(2)}, u32[]{:S(2)}) collective-permute-start(bf16[528,128]{1,0:T(8,128)(2,1)S(1)} %pack_first.1.first), channel_id=1, source_target_pairs={{2,1},{3,0},{6,2},{7,3},{10,6},{11,7},{14,11},{15,10},{12,15},{13,... | collective-permute-start | bytes 405512 | tf_op jit(solution)/shard_map/ppermute | solution.py:241
  3.8 7.1 %collective-permute-start.1 = (bf16[512,128]{1,0:T(8,128)(2,1)S(1)}, bf16[512,128]{1,0:T(8,128)(2,1)S(1)}, u32[]{:S(2)}, u32[]{:S(2)}) collective-permute-start(bf16[512,128]{1,0:T(8,128)(2,1)S(1)} %get-tuple-element.14), channel_id=1, source_target_pairs={{2,7},{3,6},{6,10},{7,11},{10,14},{11,15},{14,12},{15,13},{12,8},{... | collective-permute-start | bytes 393224 | tf_op jit(solution)/shard_map/ppermute | solution.py:241
  5.6 7.2 %collective-permute-start.3 = (bf16[512,128]{1,0:T(8,128)(2,1)S(1)}, bf16[512,128]{1,0:T(8,128)(2,1)S(1)}, u32[]{:S(2)}, u32[]{:S(2)}) collective-permute-start(bf16[512,128]{1,0:T(8,128)(2,1)S(1)} %get-tuple-element.14), channel_id=1, source_target_pairs={{2,1},{3,0},{6,2},{7,3},{10,6},{11,7},{14,11},{15,10},{12,15},{13,... | collective-permute-start | bytes 393224 | tf_op jit(solution)/shard_map/ppermute | solution.py:241
  8.1 5.8 %collective-permute-start.5 = (bf16[528,128]{1,0:T(8,128)(2,1)S(1)}, bf16[528,128]{1,0:T(8,128)(2,1)S(1)}, u32[]{:S(2)}, u32[]{:S(2)}) collective-permute-start(bf16[528,128]{1,0:T(8,128)(2,1)S(1)} %collective-permute-done.prev_a), channel_id=1, source_target_pairs={{2,6},{3,7},{6,10},{7,11},{10,14},{11,15},{14,12},{15,13},{12,8},{... | collective-permute-start | bytes 405512 | tf_op jit(solution)/shard_map/ppermute | solution.py:241
  10.0 6.4 %collective-permute-start.6 = (bf16[528,128]{1,0:T(8,128)(2,1)S(1)}, bf16[528,128]{1,0:T(8,128)(2,1)S(1)}, u32[]{:S(2)}, u32[]{:S(2)}) collective-permute-start(bf16[528,128]{1,0:T(8,128)(2,1)S(1)} %collective-permute-done.2.succ_a), channel_id=1, source_target_pairs={{2,0},{3,1},{6,2},{7,3},{10,6},{11,7},{14,10},{15,11},{12,14},{13,... | collective-permute-start | bytes 405512 | tf_op jit(solution)/shard_map/ppermute | solution.py:241
  10.9 6.0 %collective-permute-start.7 = (bf16[512,128]{1,0:T(8,128)(2,1)S(1)}, bf16[512,128]{1,0:T(8,128)(2,1)S(1)}, u32[]{:S(2)}, u32[]{:S(2)}) collective-permute-start(bf16[512,128]{1,0:T(8,128)(2,1)S(1)} %collective-permute-done.1.prev_b), channel_id=1, source_target_pairs={{2,6},{3,7},{6,10},{7,11},{10,14},{11,15},{14,12},{15,13},{12,8},{... | collective-permute-start | bytes 393224 | tf_op jit(solution)/shard_map/ppermute | solution.py:241
  12.8 5.9 %collective-permute-start.8 = (bf16[512,128]{1,0:T(8,128)(2,1)S(1)}, bf16[512,128]{1,0:T(8,128)(2,1)S(1)}, u32[]{:S(2)}, u32[]{:S(2)}) collective-permute-start(bf16[512,128]{1,0:T(8,128)(2,1)S(1)} %collective-permute-done.3.succ_b), channel_id=1, source_target_pairs={{2,0},{3,1},{6,2},{7,3},{10,6},{11,7},{14,10},{15,11},{12,14},{13,... | collective-permute-start | bytes 393224 | tf_op jit(solution)/shard_map/ppermute | solution.py:241
  13.4 3.5 %collective-permute-start.4 = (bf16[3,1040,128]{2,1,0:T(8,128)(2,1)S(1)}, bf16[3,1040,128]{2,1,0:T(8,128)(2,1)S(1)}, u32[]{:S(2)}, u32[]{:S(2)}) collective-permute-start(bf16[3,1040,128]{2,1,0:T(8,128)(2,1)S(1)} %get-tuple-element.15), channel_id=1, source_target_pairs={{2,3},{3,2},{6,7},{7,6},{10,11},{11,10},{14,15},{15,14},{12,13},{1... | collective-permute-start | bytes 2396168 | tf_op jit(solution)/shard_map/ppermute | solution.py:241
  19.2 4.0 %collective-permute-start.9 = (f32[1,256]{1,0:T(1,128)S(1)}, f32[1,256]{1,0:T(1,128)S(1)}, u32[]{:S(2)}, u32[]{:S(2)}) collective-permute-start(f32[1,256]{1,0:T(1,128)S(1)} %get-tuple-element.19), channel_id=1, source_target_pairs={{2,4},{3,5},{6,1},{7,0},{10,3},{11,2},{14,6},{15,7},{12,10},{13,11... | collective-permute-start | bytes 3080 | tf_op jit(solution)/shard_map/ppermute | solution.py:241
  20.4 3.9 %collective-permute-start.10 = (f32[1,256]{1,0:T(1,128)S(1)}, f32[1,256]{1,0:T(1,128)S(1)}, u32[]{:S(2)}, u32[]{:S(2)}) collective-permute-start(f32[1,256]{1,0:T(1,128)S(1)} %get-tuple-element.20), channel_id=1, source_target_pairs={{2,10},{3,11},{6,15},{7,14},{10,13},{11,12},{14,9},{15,8},{12,5},{... | collective-permute-start | bytes 3080 | tf_op jit(solution)/shard_map/ppermute | solution.py:241

commit v16 on v9

--- a/solution.py
+++ b/solution.py
@@ -29,47 +29,43 @@
 LAST_COST = 5
 
 
-def put_unit(unit, chunk, at, size):
+def put_unit(unit, chunk):
     count, width = unit.shape
     for j in range(width // LANES):
-        chunk[j * size + at : j * size + at + count, :] = unit[:, j * LANES : (j + 1) * LANES]
-
-
-def pack_first_kernel(embeds, label, first, raw, line, sems):
+        chunk[j * count : (j + 1) * count, :] = unit[:, j * LANES : (j + 1) * LANES]
+
+
+def pack_first_kernel(embeds, label, first, line, sems):
     rows, width = embeds.shape
     half = rows // 2
-    copies = [
-        pltpu.make_async_copy(label, line, sems.at[0]),
-        pltpu.make_async_copy(embeds.at[pl.ds(0, half)], raw, sems.at[1]),
-    ]
+    copies = []
+    for j in range(width // LANES):
+        part = embeds.at[pl.ds(0, half), pl.ds(j * LANES, LANES)]
+        copies.append(pltpu.make_async_copy(part, first.at[pl.ds(j * half, half)], sems.at[j]))
+    copies.append(pltpu.make_async_copy(label, line, sems.at[width // LANES]))
     for copy in copies:
         copy.start()
-    copies[0].wait()
+    copies[-1].wait()
     row = lax.broadcasted_iota(jnp.int32, (LABEL_ROWS, LANES), 0)
     lines = jnp.zeros((LABEL_ROWS, LANES), jnp.float32)
     for i in range(rows // LANES):
         piece = line[:, i * LANES : (i + 1) * LANES].astype(jnp.float32)
         lines = jnp.where(row == i, piece, lines)
     first[half * width // LANES :, :] = lines.astype(jnp.bfloat16)
-    copies[1].wait()
-    put_unit(normalised(raw[...]), first, 0, half)
+    for copy in copies[:-1]:
+        copy.wait()
 
 
 def pack_second_kernel(embeds, first, second, both):
     rows, width = embeds.shape
-    half = rows // 2
-    unit = normalised(embeds[half:, :])
-    put_unit(unit, second, 0, half)
-    put_chunks(first, second, both, rows)
-
-
-def put_chunks(first, second, both, rows):
-    size = second.shape[0]
-    half = rows // 2
-    for at in range(0, size, half):
-        both[2 * at : 2 * at + half, :] = first[at : at + half, :]
-        both[2 * at + half : 2 * (at + half), :] = second[at : at + half, :]
-    both[2 * size :, :] = first[size:, :]
+    unit = normalised(embeds[...])
+    put_unit(unit[rows // 2 :, :], second)
+    put_unit(unit, both)
+    put_labels(first, both)
+
+
+def put_labels(source, both):
+    both[both.shape[0] - LABEL_ROWS :, :] = source[source.shape[0] - LABEL_ROWS :, :]
 
 
 class Block:
@@ -100,7 +96,7 @@
 
 def first_half(first, rows):
     half = rows // 2
-    unit = unit_in(first, half, first.shape[0] - LABEL_ROWS)
+    unit = normalised(unit_in(first, half, first.shape[0] - LABEL_ROWS))
     return Block(unit, labels_in(first, rows)[:, :half])
 
 
@@ -140,50 +136,55 @@
     return best
 
 
-def near_kernel(own, prev_a, prev_b, succ_a, succ_b, mine, bundle):
+def near_kernel(own, succ_a, succ_b, prev_a, prev_b, mine, bundle):
     rows = mine.shape[1]
-    put_chunks(prev_a, prev_b, bundle.at[0], rows)
-    put_chunks(succ_a, succ_b, bundle.at[1], rows)
+    prev, succ = whole(prev_a, prev_b, rows), whole(succ_a, succ_b, rows)
+    for at, block, first in ((0, prev, prev_a), (1, succ, succ_a)):
+        put_unit(block.unit, bundle.at[at])
+        put_labels(first, bundle.at[at])
     bundle[2] = own[...]
     own = packed(own, rows)
-    mine[...] = best_of(own, own, whole(prev_a, prev_b, rows), whole(succ_a, succ_b, rows))
-
-
-def far_first_kernel(own, prev_a, prev_b, succ_a, succ_b, back_a, ahead_a, found):
+    mine[...] = best_of(own, own, prev, succ)
+
+
+def far_first_kernel(bundle, back_a, ahead_a, found):
     rows = found.shape[1]
-    near = packed(own, rows), whole(prev_a, prev_b, rows), whole(succ_a, succ_b, rows)
     queries = joined(first_half(back_a, rows), first_half(ahead_a, rows))
-    found[...] = best_of(queries, queries, *near)
-
-
-def far_back_kernel(own, others, succ_a, succ_b, back_a, ahead_a, back_b, found, back, ahead):
+    found[...] = best_of(queries, queries, *(packed(bundle.at[at], rows) for at in range(3)))
+
+
+def far_back_kernel(bundle, others, back_a, ahead_a, back_b, found, *refs):
+    back_found, ahead_found, back_packed = refs
     rows = found.shape[1]
     half = rows // 2
+    succ, own = packed(bundle.at[1], rows), packed(bundle.at[2], rows)
     prev_other, succ_other = packed(others.at[0], rows), packed(others.at[1], rows)
     first, rest = first_half(back_a, rows), second_half(back_a, back_b, rows)
     first_ahead = first_half(ahead_a, rows)
-    keys = packed(own, rows), whole(succ_a, succ_b, rows), first_ahead
-    both = best_of(joined(first, rest), succ_other)
-    back[:, :half] = jnp.maximum(found[:, :half], both[:, :half])
-    back[:, half:] = jnp.maximum(best_of(rest, *keys), both[:, half:])
-    ahead[...] = jnp.maximum(found[:, half:], best_of(first_ahead, rest, prev_other))
-
-
-def far_last_kernel(own, others, prev_a, prev_b, back_a, ahead_a, back_b, ahead_b, *refs):
+    back = joined(first, rest)
+    put_unit(back.unit, back_packed)
+    put_labels(back_a, back_packed)
+    both = best_of(back, succ_other)
+    back_found[:, :half] = jnp.maximum(found[:, :half], both[:, :half])
+    back_found[:, half:] = jnp.maximum(best_of(rest, own, succ, first_ahead), both[:, half:])
+    ahead_found[...] = jnp.maximum(found[:, half:], best_of(first_ahead, rest, prev_other))
+
+
+def far_last_kernel(bundle, others, back, ahead_a, ahead_b, *refs):
     back_found, ahead_found, to_back, to_ahead = refs
     rows = to_back.shape[1]
     half = rows // 2
-    back, rest = whole(back_a, back_b, rows), second_half(ahead_a, ahead_b, rows)
-    keys = packed(own, rows), whole(prev_a, prev_b, rows), packed(others.at[0], rows), back
+    back, rest = packed(back, rows), second_half(ahead_a, ahead_b, rows)
+    keys = (packed(ref, rows) for ref in (bundle.at[2], bundle.at[0], others.at[0]))
     to_back[...] = jnp.maximum(back_found[...], best_of(back, rest))
     to_ahead[:, :half] = ahead_found[...]
-    to_ahead[:, half:] = best_of(rest, *keys)
-
-
-def own_kernel(own, others, back_a, ahead_a, back_b, ahead_b, near, mine):
+    to_ahead[:, half:] = best_of(rest, *keys, back)
+
+
+def own_kernel(own, others, back, ahead_a, ahead_b, near, mine):
     rows = mine.shape[1]
     keys = [packed(others.at[at], rows) for at in range(3)]
-    keys += [whole(back_a, back_b, rows), whole(ahead_a, ahead_b, rows)]
+    keys += [packed(back, rows), whole(ahead_a, ahead_b, rows)]
     mine[...] = jnp.maximum(near[...], best_of(packed(own, rows), *keys))
 
 
@@ -255,9 +256,8 @@
         in_specs=[anywhere] * 2,
         out_specs=vmem,
         scratch_shapes=[
-            pltpu.VMEM((half, width), jnp.bfloat16),
             pltpu.VMEM((1, rows), jnp.int32),
-            pltpu.SemaphoreType.DMA((2,)),
+            pltpu.SemaphoreType.DMA((width // LANES + 1,)),
         ],
         compiler_params=pltpu.CompilerParams(vmem_limit_bytes=VMEM_BYTES),
         name="pack_first",
@@ -272,21 +272,22 @@
     prev_b, succ_b = send(own_b, "next"), send(own_b, "prev")
     back_a, ahead_a = send(prev_a, "on_next"), send(succ_a, "on_prev")
     back_b, ahead_b = send(prev_b, "on_next"), send(succ_b, "on_prev")
-    prev, succ, far = [prev_a, prev_b], [succ_a, succ_b], [back_a, ahead_a, back_b, ahead_b]
-    bundle_shape = jax.ShapeDtypeStruct((3, *chunk(rows, True).shape), jnp.bfloat16)
-    mine, bundle = kernel_call(near_kernel, [own, *prev, *succ], [line, bundle_shape], NEAR_COST)
+    block = chunk(rows, True)
+    bundle_shape = jax.ShapeDtypeStruct((3, *block.shape), jnp.bfloat16)
+    mine, bundle = kernel_call(
+        near_kernel, [own, succ_a, succ_b, prev_a, prev_b], [line, bundle_shape], NEAR_COST
+    )
     others = send(bundle, "sibling")
-    (found,) = kernel_call(
-        far_first_kernel, [own, *prev, *succ, back_a, ahead_a], [line], FIRST_COST
-    )
-    found = kernel_call(
+    (found,) = kernel_call(far_first_kernel, [bundle, back_a, ahead_a], [line], FIRST_COST)
+    *found, back = kernel_call(
         far_back_kernel,
-        [own, others, *succ, back_a, ahead_a, back_b, found],
-        [line, half_line],
+        [bundle, others, back_a, ahead_a, back_b, found],
+        [line, half_line, block],
         BACK_COST,
     )
+    far = [back, ahead_a, ahead_b]
     to_back, to_ahead = kernel_call(
-        far_last_kernel, [own, others, *prev, *far, *found], [line] * 2, LAST_COST
+        far_last_kernel, [bundle, others, *far, *found], [line] * 2, LAST_COST
     )
     (mine,) = kernel_call(own_kernel, [own, others, *far, mine], [line], 5)
     best = jnp.maximum(

time: 24.9 us -> 24.7 us (level)
  transfers between devices with their start and end apart: 11 -> 11, of which waited for: 8 -> 8; matrix products, arithmetic and copies ran while one was open for 0% -> 0% of each run, Pallas kernels for 9% -> 10%
where the time goes in v16:
time: 24.7 us; the launch traced here: 24.5 us
  starting transfers between devices  12.8 us (52%)
  waiting for transfers between devices  7.29 us (30%)
  Pallas kernels  3.79 us (15%)
  other arithmetic  0.57 us (2%)
    ppermute x11, starting transfers between devices, send(): return lax.ppermute(value, GROUP, perms[name])  12.8 us
    ppermute x11, waiting for transfers between devices, send(): return lax.ppermute(value, GROUP, perms[name])  7.29 us
    pallas_call x6, Pallas kernels, kernel_call(): pl.pallas_call(kernel, out_shape=outputs, in_specs=[vmem] * len(inputs),...  2.89 us
    pallas_call x1, Pallas kernels, on_ring(): pl.pallas_call(pack_first_kernel, out_shape=chunk(half, True), in_specs=[...  0.89 us
    max x1, other arithmetic, on_ring(): jnp.maximum(mine, jnp.maximum(send(to_back, 'home_back'), send(to_ahead,...  0.57 us
  transfers between devices with their start and end apart: 11, of which 8 were waited for; matrix products, arithmetic and copies ran while one was open for 0% of the time, Pallas kernels for 10%

profile of v16, /device:TPU:0, one launch (start us, length us, event | category | flops | bytes accessed | tf_op | source)
XLA Modules:
  0.0 24.5 jit_solution(11480587310112946457)
XLA Ops:
  0.0 0.0 copy-start
  0.0 0.9 %pack_first.1.first = bf16[528,128]{1,0:T(8,128)(2,1)S(1)} custom-call(bf16[256,512]{1,0:T(8,128)(2,1)} %embeds.3, s32[1,256]{1,0:T(1,128)} %bitcast.2), custom_call_target="tpu_custom_call" | custom-call | tf_op jit(solution)/shard_map/pack_first/pallas_call | solution.py:253
  0.9 2.5 %collective-permute-start.2 = (bf16[528,128]{1,0:T(8,128)(2,1)S(1)}, bf16[528,128]{1,0:T(8,128)(2,1)S(1)}, u32[]{:S(2)}, u32[]{:S(2)}) collective-permute-start(bf16[528,128]{1,0:T(8,128)(2,1)S(1)} %pack_first.1.first), channel_id=1, source_target_pairs={{0,5},{1,4},{4,8},{5,9},{8,12},{9,13},{12,14},{13,15},{14,10},{15,... | collective-permute-start | bytes 405512 | tf_op jit(solution)/shard_map/ppermute | solution.py:242
  3.4 0.0 collective-permute-start
  3.4 0.0 copy-done
  3.4 0.1 pack_second_kernel.1
  3.6 2.1 %collective-permute-start.3 = (bf16[512,128]{1,0:T(8,128)(2,1)S(1)}, bf16[512,128]{1,0:T(8,128)(2,1)S(1)}, u32[]{:S(2)}, u32[]{:S(2)}) collective-permute-start(bf16[512,128]{1,0:T(8,128)(2,1)S(1)} %get-tuple-element.15), channel_id=1, source_target_pairs={{0,5},{1,4},{4,8},{5,9},{8,12},{9,13},{12,14},{13,15},{14,10},{15,... | collective-permute-start | bytes 393224 | tf_op jit(solution)/shard_map/ppermute | solution.py:242
  5.7 0.3 %collective-permute-start.1 = (bf16[512,128]{1,0:T(8,128)(2,1)S(1)}, bf16[512,128]{1,0:T(8,128)(2,1)S(1)}, u32[]{:S(2)}, u32[]{:S(2)}) collective-permute-start(bf16[512,128]{1,0:T(8,128)(2,1)S(1)} %get-tuple-element.15), channel_id=1, source_target_pairs={{0,3},{1,2},{4,0},{5,1},{8,4},{9,5},{12,9},{13,8},{14,13},{15,12},... | collective-permute-start | bytes 393224 | tf_op jit(solution)/shard_map/ppermute | solution.py:242
  5.9 1.5 %collective-permute-done.2.prev_a = bf16[528,128]{1,0:T(8,128)(2,1)S(1)} collective-permute-done((bf16[528,128]{1,0:T(8,128)(2,1)S(1)}, bf16[528,128]{1,0:T(8,128)(2,1)S(1)}, u32[]{:S(2)}, u32[]{:S(2)}) %collective-permute-start.2) | collective-permute-done | bytes 135200 | tf_op jit(solution)/shard_map/ppermute | solution.py:242
  7.4 2.5 %collective-permute-start.5 = (bf16[528,128]{1,0:T(8,128)(2,1)S(1)}, bf16[528,128]{1,0:T(8,128)(2,1)S(1)}, u32[]{:S(2)}, u32[]{:S(2)}) collective-permute-start(bf16[528,128]{1,0:T(8,128)(2,1)S(1)} %collective-permute-done.2.prev_a), channel_id=1, source_target_pairs={{0,4},{1,5},{4,8},{5,9},{8,12},{9,13},{12,14},{13,15},{14,10},{15,... | collective-permute-start | bytes 405512 | tf_op jit(solution)/shard_map/ppermute | solution.py:242
  9.9 0.0 collective-permute-done.succ_a
  9.9 0.0 collective-permute-start.6
  9.9 0.3 %collective-permute-done.3.prev_b = bf16[512,128]{1,0:T(8,128)(2,1)S(1)} collective-permute-done((bf16[512,128]{1,0:T(8,128)(2,1)S(1)}, bf16[512,128]{1,0:T(8,128)(2,1)S(1)}, u32[]{:S(2)}, u32[]{:S(2)}) %collective-permute-start.3) | collective-permute-done | bytes 131104 | tf_op jit(solution)/shard_map/ppermute | solution.py:242
  10.2 2.5 %collective-permute-start.7 = (bf16[512,128]{1,0:T(8,128)(2,1)S(1)}, bf16[512,128]{1,0:T(8,128)(2,1)S(1)}, u32[]{:S(2)}, u32[]{:S(2)}) collective-permute-start(bf16[512,128]{1,0:T(8,128)(2,1)S(1)} %collective-permute-done.3.prev_b), channel_id=1, source_target_pairs={{0,4},{1,5},{4,8},{5,9},{8,12},{9,13},{12,14},{13,15},{14,10},{15,... | collective-permute-start | bytes 393224 | tf_op jit(solution)/shard_map/ppermute | solution.py:242
  12.7 0.0 collective-permute-done.1.succ_b
  12.7 0.0 collective-permute-start.8
  12.7 0.5 %near_kernel.1 = (f32[1,256]{1,0:T(1,128)S(1)}, bf16[3,1040,128]{2,1,0:T(8,128)(2,1)S(1)}) custom-call(bf16[1040,128]{1,0:T(8,128)(2,1)S(1)} %get-tuple-element.14.own, bf16[528,128]{1,0:T(8,128)(2,1)S(1)} %collective-permute-done.succ_a, bf16[512,128]{1,0:T(8,128)(2,1)S(1)} %collective-permute-done.1.succ_b, ...), custom_call_target="tpu_custom_call" | custom-call | flops 67108864 | bytes 1048576 | tf_op jit(solution)/shard_map/near_kernel/pallas_call | solution.py:223
  13.2 0.1 collective-permute-start.4
  13.2 0.5 %collective-permute-done.5.back_a = bf16[528,128]{1,0:T(8,128)(2,1)S(1)} collective-permute-done((bf16[528,128]{1,0:T(8,128)(2,1)S(1)}, bf16[528,128]{1,0:T(8,128)(2,1)S(1)}, u32[]{:S(2)}, u32[]{:S(2)}) %collective-permute-start.5) | collective-permute-done | bytes 135200 | tf_op jit(solution)/shard_map/ppermute | solution.py:242
  13.8 1.7 %collective-permute-done.6.ahead_a = bf16[528,128]{1,0:T(8,128)(2,1)S(1)} collective-permute-done((bf16[528,128]{1,0:T(8,128)(2,1)S(1)}, bf16[528,128]{1,0:T(8,128)(2,1)S(1)}, u32[]{:S(2)}, u32[]{:S(2)}) %collective-permute-start.6) | collective-permute-done | bytes 135200 | tf_op jit(solution)/shard_map/ppermute | solution.py:242
  15.4 0.6 %far_first_kernel.1.found = f32[1,256]{1,0:T(1,128)S(1)} custom-call(bf16[3,1040,128]{2,1,0:T(8,128)(2,1)S(1)} %get-tuple-element.16.bundle, bf16[528,128]{1,0:T(8,128)(2,1)S(1)} %collective-permute-done.5.back_a, bf16[528,128]{1,0:T(8,128)(2,1)S(1)} %collective-permute-done.6.ahead_a), custom_call_target="tpu_custom_call" | custom-call | flops 13421772800 | bytes 1048576 | tf_op jit(solution)/shard_map/far_first_kernel/pallas_call | solution.py:223
  16.0 0.2 collective-permute-done.7.back_b
  16.2 0.0 collective-permute-done.4.others
  16.2 0.6 %far_back_kernel.1 = (f32[1,256]{1,0:T(1,128)S(1)}, f32[1,128]{1,0:T(1,128)S(1)}, bf16[1040,128]{1,0:T(8,128)(2,1)S(1)}) custom-call(bf16[3,1040,128]{2,1,0:T(8,128)(2,1)S(1)} %get-tuple-element.16.bundle, bf16[3,1040,128]{2,1,0:T(8,128)(2,1)S(1)} %collective-permute-done.4.others, bf16[528,128]{1,0:T(8,128)(2,1)S(1)} %collective-permute-done.5.back_a, ...), custom_call_target="tpu_custom_call" | custom-call | flops 134217728 | bytes 1048576 | tf_op jit(solution)/shard_map/far_back_kernel/pallas_call | solution.py:223
  16.9 1.3 %collective-permute-done.8.ahead_b = bf16[512,128]{1,0:T(8,128)(2,1)S(1)} collective-permute-done((bf16[512,128]{1,0:T(8,128)(2,1)S(1)}, bf16[512,128]{1,0:T(8,128)(2,1)S(1)}, u32[]{:S(2)}, u32[]{:S(2)}) %collective-permute-start.8) | collective-permute-done | bytes 131104 | tf_op jit(solution)/shard_map/ppermute | solution.py:242
  18.1 0.5 %far_last_kernel.1 = (f32[1,256]{1,0:T(1,128)S(1)}, f32[1,256]{1,0:T(1,128)S(1)}) custom-call(bf16[3,1040,128]{2,1,0:T(8,128)(2,1)S(1)} %get-tuple-element.16.bundle, bf16[3,1040,128]{2,1,0:T(8,128)(2,1)S(1)} %collective-permute-done.4.others, bf16[1040,128]{1,0:T(8,128)(2,1)S(1)} %get-tuple-element.17.back, ...), custom_call_target="tpu_custom_call" | custom-call | flops 335544320 | bytes 1048576 | tf_op jit(solution)/shard_map/far_last_kernel/pallas_call | solution.py:223
  18.6 1.5 %collective-permute-start.9 = (f32[1,256]{1,0:T(1,128)S(1)}, f32[1,256]{1,0:T(1,128)S(1)}, u32[]{:S(2)}, u32[]{:S(2)}) collective-permute-start(f32[1,256]{1,0:T(1,128)S(1)} %get-tuple-element.21), channel_id=1, source_target_pairs={{0,6},{1,7},{4,3},{5,2},{8,1},{9,0},{12,4},{13,5},{14,8},{15,9},{1... | collective-permute-start | bytes 3080 | tf_op jit(solution)/shard_map/ppermute | solution.py:242
  20.1 1.5 %collective-permute-start.10 = (f32[1,256]{1,0:T(1,128)S(1)}, f32[1,256]{1,0:T(1,128)S(1)}, u32[]{:S(2)}, u32[]{:S(2)}) collective-permute-start(f32[1,256]{1,0:T(1,128)S(1)} %get-tuple-element.22), channel_id=1, source_target_pairs={{0,8},{1,9},{4,13},{5,12},{8,15},{9,14},{12,11},{13,10},{14,7},{15... | collective-permute-start | bytes 3080 | tf_op jit(solution)/shard_map/ppermute | solution.py:242
  21.6 0.6 %own_kernel.1 = f32[1,256]{1,0:T(1,128)S(1)} custom-call(bf16[1040,128]{1,0:T(8,128)(2,1)S(1)} %get-tuple-element.14.own, bf16[3,1040,128]{2,1,0:T(8,128)(2,1)S(1)} %collective-permute-done.4.others, bf16[1040,128]{1,0:T(8,128)(2,1)S(1)} %get-tuple-element.17.back, bf16[528,128]{1,0:T(8,128)(2,1)S(1)} %collective-permute-done.6.ahead_a, ...), custom_call_target="tpu_custom_call" | custom-call | flops 335544320 | bytes 1048576 | tf_op jit(solution)/shard_map/own_kernel/pallas_call | solution.py:223
  22.2 0.4 %collective-permute-done.9 = f32[1,256]{1,0:T(1,128)S(1)} collective-permute-done((f32[1,256]{1,0:T(1,128)S(1)}, f32[1,256]{1,0:T(1,128)S(1)}, u32[]{:S(2)}, u32[]{:S(2)}) %collective-permute-start.9) | collective-permute-done | bytes 1056 | tf_op jit(solution)/shard_map/ppermute | solution.py:242
  22.6 1.4 %collective-permute-done.10 = f32[1,256]{1,0:T(1,128)S(1)} collective-permute-done((f32[1,256]{1,0:T(1,128)S(1)}, f32[1,256]{1,0:T(1,128)S(1)}, u32[]{:S(2)}, u32[]{:S(2)}) %collective-permute-start.10) | collective-permute-done | bytes 1056 | tf_op jit(solution)/shard_map/ppermute | solution.py:242
  24.0 0.6 %maximum_maximum_fusion = f32[1,256]{1,0:T(1,128)} fusion(f32[1,256]{1,0:T(1,128)S(1)} %own_kernel.1, f32[1,256]{1,0:T(1,128)S(1)} %collective-permute-done.9, f32[1,256]{1,0:T(1,128)S(1)} %collective-permute-done.10), kind=kLoop, calls=%fused_computation | loop fusion | flops 512 | bytes 4096 | tf_op jit(solution)/shard_map/max | solution.py:293
Async XLA Ops:
  0.0 3.4 %copy-start = (bf16[256,512]{1,0:T(8,128)(2,1)S(1)}, bf16[256,512]{1,0:T(8,128)(2,1)}, u32[]{:S(2)}) copy-start(bf16[256,512]{1,0:T(8,128)(2,1)} %embeds.3) | copy-start | bytes 786436
  0.9 6.5 %collective-permute-start.2 = (bf16[528,128]{1,0:T(8,128)(2,1)S(1)}, bf16[528,128]{1,0:T(8,128)(2,1)S(1)}, u32[]{:S(2)}, u32[]{:S(2)}) collective-permute-start(bf16[528,128]{1,0:T(8,128)(2,1)S(1)} %pack_first.1.first), channel_id=1, source_target_pairs={{0,5},{1,4},{4,8},{5,9},{8,12},{9,13},{12,14},{13,15},{14,10},{15,... | collective-permute-start | bytes 405512 | tf_op jit(solution)/shard_map/ppermute | solution.py:242
  3.4 6.5 %collective-permute-start = (bf16[528,128]{1,0:T(8,128)(2,1)S(1)}, bf16[528,128]{1,0:T(8,128)(2,1)S(1)}, u32[]{:S(2)}, u32[]{:S(2)}) collective-permute-start(bf16[528,128]{1,0:T(8,128)(2,1)S(1)} %pack_first.1.first), channel_id=1, source_target_pairs={{0,3},{1,2},{4,0},{5,1},{8,4},{9,5},{12,9},{13,8},{14,13},{15,12},... | collective-permute-start | bytes 405512 | tf_op jit(solution)/shard_map/ppermute | solution.py:242
  3.6 6.6 %collective-permute-start.3 = (bf16[512,128]{1,0:T(8,128)(2,1)S(1)}, bf16[512,128]{1,0:T(8,128)(2,1)S(1)}, u32[]{:S(2)}, u32[]{:S(2)}) collective-permute-start(bf16[512,128]{1,0:T(8,128)(2,1)S(1)} %get-tuple-element.15), channel_id=1, source_target_pairs={{0,5},{1,4},{4,8},{5,9},{8,12},{9,13},{12,14},{13,15},{14,10},{15,... | collective-permute-start | bytes 393224 | tf_op jit(solution)/shard_map/ppermute | solution.py:242
  5.7 7.0 %collective-permute-start.1 = (bf16[512,128]{1,0:T(8,128)(2,1)S(1)}, bf16[512,128]{1,0:T(8,128)(2,1)S(1)}, u32[]{:S(2)}, u32[]{:S(2)}) collective-permute-start(bf16[512,128]{1,0:T(8,128)(2,1)S(1)} %get-tuple-element.15), channel_id=1, source_target_pairs={{0,3},{1,2},{4,0},{5,1},{8,4},{9,5},{12,9},{13,8},{14,13},{15,12},... | collective-permute-start | bytes 393224 | tf_op jit(solution)/shard_map/ppermute | solution.py:242
  7.4 6.3 %collective-permute-start.5 = (bf16[528,128]{1,0:T(8,128)(2,1)S(1)}, bf16[528,128]{1,0:T(8,128)(2,1)S(1)}, u32[]{:S(2)}, u32[]{:S(2)}) collective-permute-start(bf16[528,128]{1,0:T(8,128)(2,1)S(1)} %collective-permute-done.2.prev_a), channel_id=1, source_target_pairs={{0,4},{1,5},{4,8},{5,9},{8,12},{9,13},{12,14},{13,15},{14,10},{15,... | collective-permute-start | bytes 405512 | tf_op jit(solution)/shard_map/ppermute | solution.py:242
  9.9 5.5 %collective-permute-start.6 = (bf16[528,128]{1,0:T(8,128)(2,1)S(1)}, bf16[528,128]{1,0:T(8,128)(2,1)S(1)}, u32[]{:S(2)}, u32[]{:S(2)}) collective-permute-start(bf16[528,128]{1,0:T(8,128)(2,1)S(1)} %collective-permute-done.succ_a), channel_id=1, source_target_pairs={{0,2},{1,3},{4,0},{5,1},{8,4},{9,5},{12,8},{13,9},{14,12},{15,13},... | collective-permute-start | bytes 405512 | tf_op jit(solution)/shard_map/ppermute | solution.py:242
  10.2 6.0 %collective-permute-start.7 = (bf16[512,128]{1,0:T(8,128)(2,1)S(1)}, bf16[512,128]{1,0:T(8,128)(2,1)S(1)}, u32[]{:S(2)}, u32[]{:S(2)}) collective-permute-start(bf16[512,128]{1,0:T(8,128)(2,1)S(1)} %collective-permute-done.3.prev_b), channel_id=1, source_target_pairs={{0,4},{1,5},{4,8},{5,9},{8,12},{9,13},{12,14},{13,15},{14,10},{15,... | collective-permute-start | bytes 393224 | tf_op jit(solution)/shard_map/ppermute | solution.py:242
  12.7 5.4 %collective-permute-start.8 = (bf16[512,128]{1,0:T(8,128)(2,1)S(1)}, bf16[512,128]{1,0:T(8,128)(2,1)S(1)}, u32[]{:S(2)}, u32[]{:S(2)}) collective-permute-start(bf16[512,128]{1,0:T(8,128)(2,1)S(1)} %collective-permute-done.1.succ_b), channel_id=1, source_target_pairs={{0,2},{1,3},{4,0},{5,1},{8,4},{9,5},{12,8},{13,9},{14,12},{15,13},... | collective-permute-start | bytes 393224 | tf_op jit(solution)/shard_map/ppermute | solution.py:242
  13.2 3.1 %collective-permute-start.4 = (bf16[3,1040,128]{2,1,0:T(8,128)(2,1)S(1)}, bf16[3,1040,128]{2,1,0:T(8,128)(2,1)S(1)}, u32[]{:S(2)}, u32[]{:S(2)}) collective-permute-start(bf16[3,1040,128]{2,1,0:T(8,128)(2,1)S(1)} %get-tuple-element.16.bundle), channel_id=1, source_target_pairs={{0,1},{1,0},{4,5},{5,4},{8,9},{9,8},{12,13},{13,12},{14,15},{15,14... | collective-permute-start | bytes 2396168 | tf_op jit(solution)/shard_map/ppermute | solution.py:242
  18.6 4.0 %collective-permute-start.9 = (f32[1,256]{1,0:T(1,128)S(1)}, f32[1,256]{1,0:T(1,128)S(1)}, u32[]{:S(2)}, u32[]{:S(2)}) collective-permute-start(f32[1,256]{1,0:T(1,128)S(1)} %get-tuple-element.21), channel_id=1, source_target_pairs={{0,6},{1,7},{4,3},{5,2},{8,1},{9,0},{12,4},{13,5},{14,8},{15,9},{1... | collective-permute-start | bytes 3080 | tf_op jit(solution)/shard_map/ppermute | solution.py:242
  20.1 3.9 %collective-permute-start.10 = (f32[1,256]{1,0:T(1,128)S(1)}, f32[1,256]{1,0:T(1,128)S(1)}, u32[]{:S(2)}, u32[]{:S(2)}) collective-permute-start(f32[1,256]{1,0:T(1,128)S(1)} %get-tuple-element.22), channel_id=1, source_target_pairs={{0,8},{1,9},{4,13},{5,12},{8,15},{9,14},{12,11},{13,10},{14,7},{15... | collective-permute-start | bytes 3080 | tf_op jit(solution)/shard_map/ppermute | solution.py:242

commit v17 on v16

--- a/solution.py
+++ b/solution.py
@@ -117,23 +117,25 @@
 
 
 def best_of(queries, *all_keys):
-    best = None
-    for keys in all_keys:
-        sims = lax.dot_general(
-            keys.unit, queries.unit, (((1,), (1,)), ((), ())), preferred_element_type=jnp.float32
-        )
-        pieces = []
-        for start in range(0, queries.rows, LANES):
+    keys_unit = jnp.concatenate([keys.unit for keys in all_keys], axis=0)
+    sims = lax.dot_general(
+        keys_unit, queries.unit, (((1,), (1,)), ((), ())), preferred_element_type=jnp.float32
+    )
+    pieces = []
+    for start in range(0, queries.rows, LANES):
+        best, at = None, 0
+        for keys in all_keys:
             keep = keys.column() == queries.label[:, start : start + LANES]
             if keys is queries:
                 row = lax.broadcasted_iota(jnp.int32, keep.shape, 0)
                 column = lax.broadcasted_iota(jnp.int32, keep.shape, 1) + start
                 keep = keep & (row != column)
-            found = jnp.where(keep, sims[:, start : start + LANES], -1.0)
-            pieces.append(jnp.max(found, axis=0, keepdims=True))
-        found = jnp.concatenate(pieces, axis=1)
-        best = found if best is None else jnp.maximum(best, found)
-    return best
+            found = jnp.where(keep, sims[at : at + keys.rows, start : start + LANES], -1.0)
+            found = jnp.max(found, axis=0, keepdims=True)
+            best = found if best is None else jnp.maximum(best, found)
+            at += keys.rows
+        pieces.append(best)
+    return jnp.concatenate(pieces, axis=1)
 
 
 def near_kernel(own, succ_a, succ_b, prev_a, prev_b, mine, bundle):

time: 24.7 us -> 24.7 us (level)
  no operation moved by 1% of the time
where the time goes in v17:
time: 24.7 us; the launch traced here: 24.5 us
  starting transfers between devices  12.9 us (52%)
  waiting for transfers between devices  7.29 us (30%)
  Pallas kernels  3.75 us (15%)
  other arithmetic  0.57 us (2%)
    ppermute x11, starting transfers between devices, send(): return lax.ppermute(value, GROUP, perms[name])  12.9 us
    ppermute x11, waiting for transfers between devices, send(): return lax.ppermute(value, GROUP, perms[name])  7.29 us
    pallas_call x6, Pallas kernels, kernel_call(): pl.pallas_call(kernel, out_shape=outputs, in_specs=[vmem] * len(inputs),...  2.86 us
    pallas_call x1, Pallas kernels, on_ring(): pl.pallas_call(pack_first_kernel, out_shape=chunk(half, True), in_specs=[...  0.89 us
    max x1, other arithmetic, on_ring(): jnp.maximum(mine, jnp.maximum(send(to_back, 'home_back'), send(to_ahead,...  0.57 us
  transfers between devices with their start and end apart: 11, of which 8 were waited for; matrix products, arithmetic and copies ran while one was open for 0% of the time, Pallas kernels for 10%

profile of v17, /device:TPU:0, one launch (start us, length us, event | category | flops | bytes accessed | tf_op | source)
XLA Modules:
  0.0 24.5 jit_solution(1355655604735499427)
XLA Ops:
  0.0 0.0 copy-start
  0.0 0.9 %pack_first.1.first = bf16[528,128]{1,0:T(8,128)(2,1)S(1)} custom-call(bf16[256,512]{1,0:T(8,128)(2,1)} %embeds.3, s32[1,256]{1,0:T(1,128)} %bitcast.2), custom_call_target="tpu_custom_call" | custom-call | tf_op jit(solution)/shard_map/pack_first/pallas_call | solution.py:255
  0.9 2.5 %collective-permute-start.2 = (bf16[528,128]{1,0:T(8,128)(2,1)S(1)}, bf16[528,128]{1,0:T(8,128)(2,1)S(1)}, u32[]{:S(2)}, u32[]{:S(2)}) collective-permute-start(bf16[528,128]{1,0:T(8,128)(2,1)S(1)} %pack_first.1.first), channel_id=1, source_target_pairs={{0,5},{1,4},{4,8},{5,9},{8,12},{9,13},{12,14},{13,15},{14,10},{15,... | collective-permute-start | bytes 405512 | tf_op jit(solution)/shard_map/ppermute | solution.py:244
  3.4 0.0 collective-permute-start
  3.4 0.0 copy-done
  3.4 0.1 pack_second_kernel.1
  3.6 2.1 %collective-permute-start.3 = (bf16[512,128]{1,0:T(8,128)(2,1)S(1)}, bf16[512,128]{1,0:T(8,128)(2,1)S(1)}, u32[]{:S(2)}, u32[]{:S(2)}) collective-permute-start(bf16[512,128]{1,0:T(8,128)(2,1)S(1)} %get-tuple-element.15), channel_id=1, source_target_pairs={{0,5},{1,4},{4,8},{5,9},{8,12},{9,13},{12,14},{13,15},{14,10},{15,... | collective-permute-start | bytes 393224 | tf_op jit(solution)/shard_map/ppermute | solution.py:244
  5.7 0.3 %collective-permute-start.1 = (bf16[512,128]{1,0:T(8,128)(2,1)S(1)}, bf16[512,128]{1,0:T(8,128)(2,1)S(1)}, u32[]{:S(2)}, u32[]{:S(2)}) collective-permute-start(bf16[512,128]{1,0:T(8,128)(2,1)S(1)} %get-tuple-element.15), channel_id=1, source_target_pairs={{0,3},{1,2},{4,0},{5,1},{8,4},{9,5},{12,9},{13,8},{14,13},{15,12},... | collective-permute-start | bytes 393224 | tf_op jit(solution)/shard_map/ppermute | solution.py:244
  5.9 1.5 %collective-permute-done.2.prev_a = bf16[528,128]{1,0:T(8,128)(2,1)S(1)} collective-permute-done((bf16[528,128]{1,0:T(8,128)(2,1)S(1)}, bf16[528,128]{1,0:T(8,128)(2,1)S(1)}, u32[]{:S(2)}, u32[]{:S(2)}) %collective-permute-start.2) | collective-permute-done | bytes 135200 | tf_op jit(solution)/shard_map/ppermute | solution.py:244
  7.4 2.5 %collective-permute-start.5 = (bf16[528,128]{1,0:T(8,128)(2,1)S(1)}, bf16[528,128]{1,0:T(8,128)(2,1)S(1)}, u32[]{:S(2)}, u32[]{:S(2)}) collective-permute-start(bf16[528,128]{1,0:T(8,128)(2,1)S(1)} %collective-permute-done.2.prev_a), channel_id=1, source_target_pairs={{0,4},{1,5},{4,8},{5,9},{8,12},{9,13},{12,14},{13,15},{14,10},{15,... | collective-permute-start | bytes 405512 | tf_op jit(solution)/shard_map/ppermute | solution.py:244
  9.9 0.0 collective-permute-done.succ_a
  9.9 0.0 collective-permute-start.6
  9.9 0.3 %collective-permute-done.3.prev_b = bf16[512,128]{1,0:T(8,128)(2,1)S(1)} collective-permute-done((bf16[512,128]{1,0:T(8,128)(2,1)S(1)}, bf16[512,128]{1,0:T(8,128)(2,1)S(1)}, u32[]{:S(2)}, u32[]{:S(2)}) %collective-permute-start.3) | collective-permute-done | bytes 131104 | tf_op jit(solution)/shard_map/ppermute | solution.py:244
  10.2 2.5 %collective-permute-start.7 = (bf16[512,128]{1,0:T(8,128)(2,1)S(1)}, bf16[512,128]{1,0:T(8,128)(2,1)S(1)}, u32[]{:S(2)}, u32[]{:S(2)}) collective-permute-start(bf16[512,128]{1,0:T(8,128)(2,1)S(1)} %collective-permute-done.3.prev_b), channel_id=1, source_target_pairs={{0,4},{1,5},{4,8},{5,9},{8,12},{9,13},{12,14},{13,15},{14,10},{15,... | collective-permute-start | bytes 393224 | tf_op jit(solution)/shard_map/ppermute | solution.py:244
  12.7 0.0 collective-permute-done.1.succ_b
  12.7 0.0 collective-permute-start.8
  12.7 0.5 %near_kernel.1 = (f32[1,256]{1,0:T(1,128)S(1)}, bf16[3,1040,128]{2,1,0:T(8,128)(2,1)S(1)}) custom-call(bf16[1040,128]{1,0:T(8,128)(2,1)S(1)} %get-tuple-element.14.own, bf16[528,128]{1,0:T(8,128)(2,1)S(1)} %collective-permute-done.succ_a, bf16[512,128]{1,0:T(8,128)(2,1)S(1)} %collective-permute-done.1.succ_b, ...), custom_call_target="tpu_custom_call" | custom-call | flops 67108864 | bytes 1048576 | tf_op jit(solution)/shard_map/near_kernel/pallas_call | solution.py:225
  13.1 0.1 collective-permute-start.4
  13.2 0.5 %collective-permute-done.5.back_a = bf16[528,128]{1,0:T(8,128)(2,1)S(1)} collective-permute-done((bf16[528,128]{1,0:T(8,128)(2,1)S(1)}, bf16[528,128]{1,0:T(8,128)(2,1)S(1)}, u32[]{:S(2)}, u32[]{:S(2)}) %collective-permute-start.5) | collective-permute-done | bytes 135200 | tf_op jit(solution)/shard_map/ppermute | solution.py:244
  13.8 1.7 %collective-permute-done.6.ahead_a = bf16[528,128]{1,0:T(8,128)(2,1)S(1)} collective-permute-done((bf16[528,128]{1,0:T(8,128)(2,1)S(1)}, bf16[528,128]{1,0:T(8,128)(2,1)S(1)}, u32[]{:S(2)}, u32[]{:S(2)}) %collective-permute-start.6) | collective-permute-done | bytes 135200 | tf_op jit(solution)/shard_map/ppermute | solution.py:244
  15.4 0.6 %far_first_kernel.1.found = f32[1,256]{1,0:T(1,128)S(1)} custom-call(bf16[3,1040,128]{2,1,0:T(8,128)(2,1)S(1)} %get-tuple-element.16.bundle, bf16[528,128]{1,0:T(8,128)(2,1)S(1)} %collective-permute-done.5.back_a, bf16[528,128]{1,0:T(8,128)(2,1)S(1)} %collective-permute-done.6.ahead_a), custom_call_target="tpu_custom_call" | custom-call | flops 13421772800 | bytes 1048576 | tf_op jit(solution)/shard_map/far_first_kernel/pallas_call | solution.py:225
  16.0 0.2 collective-permute-done.7.back_b
  16.2 0.0 collective-permute-done.4.others
  16.2 0.6 %far_back_kernel.1 = (f32[1,256]{1,0:T(1,128)S(1)}, f32[1,128]{1,0:T(1,128)S(1)}, bf16[1040,128]{1,0:T(8,128)(2,1)S(1)}) custom-call(bf16[3,1040,128]{2,1,0:T(8,128)(2,1)S(1)} %get-tuple-element.16.bundle, bf16[3,1040,128]{2,1,0:T(8,128)(2,1)S(1)} %collective-permute-done.4.others, bf16[528,128]{1,0:T(8,128)(2,1)S(1)} %collective-permute-done.5.back_a, ...), custom_call_target="tpu_custom_call" | custom-call | flops 134217728 | bytes 1048576 | tf_op jit(solution)/shard_map/far_back_kernel/pallas_call | solution.py:225
  16.8 1.3 %collective-permute-done.8.ahead_b = bf16[512,128]{1,0:T(8,128)(2,1)S(1)} collective-permute-done((bf16[512,128]{1,0:T(8,128)(2,1)S(1)}, bf16[512,128]{1,0:T(8,128)(2,1)S(1)}, u32[]{:S(2)}, u32[]{:S(2)}) %collective-permute-start.8) | collective-permute-done | bytes 131104 | tf_op jit(solution)/shard_map/ppermute | solution.py:244
  18.1 0.5 %far_last_kernel.1 = (f32[1,256]{1,0:T(1,128)S(1)}, f32[1,256]{1,0:T(1,128)S(1)}) custom-call(bf16[3,1040,128]{2,1,0:T(8,128)(2,1)S(1)} %get-tuple-element.16.bundle, bf16[3,1040,128]{2,1,0:T(8,128)(2,1)S(1)} %collective-permute-done.4.others, bf16[1040,128]{1,0:T(8,128)(2,1)S(1)} %get-tuple-element.17.back, ...), custom_call_target="tpu_custom_call" | custom-call | flops 335544320 | bytes 1048576 | tf_op jit(solution)/shard_map/far_last_kernel/pallas_call | solution.py:225
  18.6 1.5 %collective-permute-start.9 = (f32[1,256]{1,0:T(1,128)S(1)}, f32[1,256]{1,0:T(1,128)S(1)}, u32[]{:S(2)}, u32[]{:S(2)}) collective-permute-start(f32[1,256]{1,0:T(1,128)S(1)} %get-tuple-element.21), channel_id=1, source_target_pairs={{0,6},{1,7},{4,3},{5,2},{8,1},{9,0},{12,4},{13,5},{14,8},{15,9},{1... | collective-permute-start | bytes 3080 | tf_op jit(solution)/shard_map/ppermute | solution.py:244
  20.1 1.5 %collective-permute-start.10 = (f32[1,256]{1,0:T(1,128)S(1)}, f32[1,256]{1,0:T(1,128)S(1)}, u32[]{:S(2)}, u32[]{:S(2)}) collective-permute-start(f32[1,256]{1,0:T(1,128)S(1)} %get-tuple-element.22), channel_id=1, source_target_pairs={{0,8},{1,9},{4,13},{5,12},{8,15},{9,14},{12,11},{13,10},{14,7},{15... | collective-permute-start | bytes 3080 | tf_op jit(solution)/shard_map/ppermute | solution.py:244
  21.6 0.6 %own_kernel.1 = f32[1,256]{1,0:T(1,128)S(1)} custom-call(bf16[1040,128]{1,0:T(8,128)(2,1)S(1)} %get-tuple-element.14.own, bf16[3,1040,128]{2,1,0:T(8,128)(2,1)S(1)} %collective-permute-done.4.others, bf16[1040,128]{1,0:T(8,128)(2,1)S(1)} %get-tuple-element.17.back, bf16[528,128]{1,0:T(8,128)(2,1)S(1)} %collective-permute-done.6.ahead_a, ...), custom_call_target="tpu_custom_call" | custom-call | flops 335544320 | bytes 1048576 | tf_op jit(solution)/shard_map/own_kernel/pallas_call | solution.py:225
  22.2 0.4 %collective-permute-done.9 = f32[1,256]{1,0:T(1,128)S(1)} collective-permute-done((f32[1,256]{1,0:T(1,128)S(1)}, f32[1,256]{1,0:T(1,128)S(1)}, u32[]{:S(2)}, u32[]{:S(2)}) %collective-permute-start.9) | collective-permute-done | bytes 1056 | tf_op jit(solution)/shard_map/ppermute | solution.py:244
  22.6 1.4 %collective-permute-done.10 = f32[1,256]{1,0:T(1,128)S(1)} collective-permute-done((f32[1,256]{1,0:T(1,128)S(1)}, f32[1,256]{1,0:T(1,128)S(1)}, u32[]{:S(2)}, u32[]{:S(2)}) %collective-permute-start.10) | collective-permute-done | bytes 1056 | tf_op jit(solution)/shard_map/ppermute | solution.py:244
  24.0 0.6 %maximum_maximum_fusion = f32[1,256]{1,0:T(1,128)} fusion(f32[1,256]{1,0:T(1,128)S(1)} %own_kernel.1, f32[1,256]{1,0:T(1,128)S(1)} %collective-permute-done.9, f32[1,256]{1,0:T(1,128)S(1)} %collective-permute-done.10), kind=kLoop, calls=%fused_computation | loop fusion | flops 512 | bytes 4096 | tf_op jit(solution)/shard_map/max | solution.py:295
Async XLA Ops:
  0.0 3.4 %copy-start = (bf16[256,512]{1,0:T(8,128)(2,1)S(1)}, bf16[256,512]{1,0:T(8,128)(2,1)}, u32[]{:S(2)}) copy-start(bf16[256,512]{1,0:T(8,128)(2,1)} %embeds.3) | copy-start | bytes 786436
  0.9 6.5 %collective-permute-start.2 = (bf16[528,128]{1,0:T(8,128)(2,1)S(1)}, bf16[528,128]{1,0:T(8,128)(2,1)S(1)}, u32[]{:S(2)}, u32[]{:S(2)}) collective-permute-start(bf16[528,128]{1,0:T(8,128)(2,1)S(1)} %pack_first.1.first), channel_id=1, source_target_pairs={{0,5},{1,4},{4,8},{5,9},{8,12},{9,13},{12,14},{13,15},{14,10},{15,... | collective-permute-start | bytes 405512 | tf_op jit(solution)/shard_map/ppermute | solution.py:244
  3.4 6.5 %collective-permute-start = (bf16[528,128]{1,0:T(8,128)(2,1)S(1)}, bf16[528,128]{1,0:T(8,128)(2,1)S(1)}, u32[]{:S(2)}, u32[]{:S(2)}) collective-permute-start(bf16[528,128]{1,0:T(8,128)(2,1)S(1)} %pack_first.1.first), channel_id=1, source_target_pairs={{0,3},{1,2},{4,0},{5,1},{8,4},{9,5},{12,9},{13,8},{14,13},{15,12},... | collective-permute-start | bytes 405512 | tf_op jit(solution)/shard_map/ppermute | solution.py:244
  3.6 6.6 %collective-permute-start.3 = (bf16[512,128]{1,0:T(8,128)(2,1)S(1)}, bf16[512,128]{1,0:T(8,128)(2,1)S(1)}, u32[]{:S(2)}, u32[]{:S(2)}) collective-permute-start(bf16[512,128]{1,0:T(8,128)(2,1)S(1)} %get-tuple-element.15), channel_id=1, source_target_pairs={{0,5},{1,4},{4,8},{5,9},{8,12},{9,13},{12,14},{13,15},{14,10},{15,... | collective-permute-start | bytes 393224 | tf_op jit(solution)/shard_map/ppermute | solution.py:244
  5.7 7.0 %collective-permute-start.1 = (bf16[512,128]{1,0:T(8,128)(2,1)S(1)}, bf16[512,128]{1,0:T(8,128)(2,1)S(1)}, u32[]{:S(2)}, u32[]{:S(2)}) collective-permute-start(bf16[512,128]{1,0:T(8,128)(2,1)S(1)} %get-tuple-element.15), channel_id=1, source_target_pairs={{0,3},{1,2},{4,0},{5,1},{8,4},{9,5},{12,9},{13,8},{14,13},{15,12},... | collective-permute-start | bytes 393224 | tf_op jit(solution)/shard_map/ppermute | solution.py:244
  7.4 6.3 %collective-permute-start.5 = (bf16[528,128]{1,0:T(8,128)(2,1)S(1)}, bf16[528,128]{1,0:T(8,128)(2,1)S(1)}, u32[]{:S(2)}, u32[]{:S(2)}) collective-permute-start(bf16[528,128]{1,0:T(8,128)(2,1)S(1)} %collective-permute-done.2.prev_a), channel_id=1, source_target_pairs={{0,4},{1,5},{4,8},{5,9},{8,12},{9,13},{12,14},{13,15},{14,10},{15,... | collective-permute-start | bytes 405512 | tf_op jit(solution)/shard_map/ppermute | solution.py:244
  9.9 5.5 %collective-permute-start.6 = (bf16[528,128]{1,0:T(8,128)(2,1)S(1)}, bf16[528,128]{1,0:T(8,128)(2,1)S(1)}, u32[]{:S(2)}, u32[]{:S(2)}) collective-permute-start(bf16[528,128]{1,0:T(8,128)(2,1)S(1)} %collective-permute-done.succ_a), channel_id=1, source_target_pairs={{0,2},{1,3},{4,0},{5,1},{8,4},{9,5},{12,8},{13,9},{14,12},{15,13},... | collective-permute-start | bytes 405512 | tf_op jit(solution)/shard_map/ppermute | solution.py:244
  10.2 6.0 %collective-permute-start.7 = (bf16[512,128]{1,0:T(8,128)(2,1)S(1)}, bf16[512,128]{1,0:T(8,128)(2,1)S(1)}, u32[]{:S(2)}, u32[]{:S(2)}) collective-permute-start(bf16[512,128]{1,0:T(8,128)(2,1)S(1)} %collective-permute-done.3.prev_b), channel_id=1, source_target_pairs={{0,4},{1,5},{4,8},{5,9},{8,12},{9,13},{12,14},{13,15},{14,10},{15,... | collective-permute-start | bytes 393224 | tf_op jit(solution)/shard_map/ppermute | solution.py:244
  12.7 5.4 %collective-permute-start.8 = (bf16[512,128]{1,0:T(8,128)(2,1)S(1)}, bf16[512,128]{1,0:T(8,128)(2,1)S(1)}, u32[]{:S(2)}, u32[]{:S(2)}) collective-permute-start(bf16[512,128]{1,0:T(8,128)(2,1)S(1)} %collective-permute-done.1.succ_b), channel_id=1, source_target_pairs={{0,2},{1,3},{4,0},{5,1},{8,4},{9,5},{12,8},{13,9},{14,12},{15,13},... | collective-permute-start | bytes 393224 | tf_op jit(solution)/shard_map/ppermute | solution.py:244
  13.1 3.1 %collective-permute-start.4 = (bf16[3,1040,128]{2,1,0:T(8,128)(2,1)S(1)}, bf16[3,1040,128]{2,1,0:T(8,128)(2,1)S(1)}, u32[]{:S(2)}, u32[]{:S(2)}) collective-permute-start(bf16[3,1040,128]{2,1,0:T(8,128)(2,1)S(1)} %get-tuple-element.16.bundle), channel_id=1, source_target_pairs={{0,1},{1,0},{4,5},{5,4},{8,9},{9,8},{12,13},{13,12},{14,15},{15,14... | collective-permute-start | bytes 2396168 | tf_op jit(solution)/shard_map/ppermute | solution.py:244
  18.6 4.0 %collective-permute-start.9 = (f32[1,256]{1,0:T(1,128)S(1)}, f32[1,256]{1,0:T(1,128)S(1)}, u32[]{:S(2)}, u32[]{:S(2)}) collective-permute-start(f32[1,256]{1,0:T(1,128)S(1)} %get-tuple-element.21), channel_id=1, source_target_pairs={{0,6},{1,7},{4,3},{5,2},{8,1},{9,0},{12,4},{13,5},{14,8},{15,9},{1... | collective-permute-start | bytes 3080 | tf_op jit(solution)/shard_map/ppermute | solution.py:244
  20.1 3.9 %collective-permute-start.10 = (f32[1,256]{1,0:T(1,128)S(1)}, f32[1,256]{1,0:T(1,128)S(1)}, u32[]{:S(2)}, u32[]{:S(2)}) collective-permute-start(f32[1,256]{1,0:T(1,128)S(1)} %get-tuple-element.22), channel_id=1, source_target_pairs={{0,8},{1,9},{4,13},{5,12},{8,15},{9,14},{12,11},{13,10},{14,7},{15... | collective-permute-start | bytes 3080 | tf_op jit(solution)/shard_map/ppermute | solution.py:244

commit v18 on v17

--- a/solution.py
+++ b/solution.py
@@ -69,11 +69,11 @@
 
 
 class Block:
-    def __init__(self, unit, label):
+    def __init__(self, unit, label, column=None):
         self.unit = unit
         self.label = label
         self.rows = unit.shape[0]
-        self.along_rows = None
+        self.along_rows = column
 
     def column(self):
         if self.along_rows is None:
@@ -90,8 +90,9 @@
     return jnp.concatenate([lines[i : i + 1] for i in range(rows // LANES)], axis=1)
 
 
-def packed(both, rows):
-    return Block(unit_in(both, rows, both.shape[0] - LABEL_ROWS), labels_in(both, rows))
+def packed(both, rows, column=None):
+    unit = unit_in(both, rows, both.shape[0] - LABEL_ROWS)
+    return Block(unit, labels_in(both, rows), None if column is None else column[...])
 
 
 def first_half(first, rows):
@@ -138,7 +139,7 @@
     return jnp.concatenate(pieces, axis=1)
 
 
-def near_kernel(own, succ_a, succ_b, prev_a, prev_b, mine, bundle):
+def near_kernel(own, succ_a, succ_b, prev_a, prev_b, mine, bundle, columns):
     rows = mine.shape[1]
     prev, succ = whole(prev_a, prev_b, rows), whole(succ_a, succ_b, rows)
     for at, block, first in ((0, prev, prev_a), (1, succ, succ_a)):
@@ -147,37 +148,43 @@
     bundle[2] = own[...]
     own = packed(own, rows)
     mine[...] = best_of(own, own, prev, succ)
-
-
-def far_first_kernel(bundle, back_a, ahead_a, found):
+    for at, block in enumerate((prev, succ, own)):
+        columns[at] = block.column()
+
+
+def far_first_kernel(bundle, columns, back_a, ahead_a, found):
     rows = found.shape[1]
     queries = joined(first_half(back_a, rows), first_half(ahead_a, rows))
-    found[...] = best_of(queries, queries, *(packed(bundle.at[at], rows) for at in range(3)))
-
-
-def far_back_kernel(bundle, others, back_a, ahead_a, back_b, found, *refs):
-    back_found, ahead_found, back_packed = refs
+    keys = [packed(bundle.at[at], rows, columns.at[at]) for at in range(3)]
+    found[...] = best_of(queries, queries, *keys)
+
+
+def far_back_kernel(bundle, columns, others, back_a, ahead_a, back_b, found, *refs):
+    back_found, ahead_found, back_packed, back_column, other_column = refs
     rows = found.shape[1]
     half = rows // 2
-    succ, own = packed(bundle.at[1], rows), packed(bundle.at[2], rows)
+    succ, own = (packed(bundle.at[at], rows, columns.at[at]) for at in (1, 2))
     prev_other, succ_other = packed(others.at[0], rows), packed(others.at[1], rows)
     first, rest = first_half(back_a, rows), second_half(back_a, back_b, rows)
     first_ahead = first_half(ahead_a, rows)
     back = joined(first, rest)
     put_unit(back.unit, back_packed)
     put_labels(back_a, back_packed)
+    back_column[:half, :], back_column[half:, :] = first.column(), rest.column()
+    other_column[...] = prev_other.column()
     both = best_of(back, succ_other)
     back_found[:, :half] = jnp.maximum(found[:, :half], both[:, :half])
     back_found[:, half:] = jnp.maximum(best_of(rest, own, succ, first_ahead), both[:, half:])
     ahead_found[...] = jnp.maximum(found[:, half:], best_of(first_ahead, rest, prev_other))
 
 
-def far_last_kernel(bundle, others, back, ahead_a, ahead_b, *refs):
-    back_found, ahead_found, to_back, to_ahead = refs
+def far_last_kernel(bundle, columns, others, back, ahead_a, ahead_b, *refs):
+    back_found, ahead_found, back_column, other_column, to_back, to_ahead = refs
     rows = to_back.shape[1]
     half = rows // 2
-    back, rest = packed(back, rows), second_half(ahead_a, ahead_b, rows)
-    keys = (packed(ref, rows) for ref in (bundle.at[2], bundle.at[0], others.at[0]))
+    back, rest = packed(back, rows, back_column), second_half(ahead_a, ahead_b, rows)
+    keys = [packed(bundle.at[at], rows, columns.at[at]) for at in (0, 2)]
+    keys.append(packed(others.at[0], rows, other_column))
     to_back[...] = jnp.maximum(back_found[...], best_of(back, rest))
     to_ahead[:, :half] = ahead_found[...]
     to_ahead[:, half:] = best_of(rest, *keys, back)
@@ -276,20 +283,27 @@
     back_b, ahead_b = send(prev_b, "on_next"), send(succ_b, "on_prev")
     block = chunk(rows, True)
     bundle_shape = jax.ShapeDtypeStruct((3, *block.shape), jnp.bfloat16)
-    mine, bundle = kernel_call(
-        near_kernel, [own, succ_a, succ_b, prev_a, prev_b], [line, bundle_shape], NEAR_COST
+    column = jax.ShapeDtypeStruct((rows, LANES), jnp.float32)
+    mine, bundle, columns = kernel_call(
+        near_kernel,
+        [own, succ_a, succ_b, prev_a, prev_b],
+        [line, bundle_shape, jax.ShapeDtypeStruct((3, *column.shape), jnp.float32)],
+        NEAR_COST,
     )
     others = send(bundle, "sibling")
-    (found,) = kernel_call(far_first_kernel, [bundle, back_a, ahead_a], [line], FIRST_COST)
-    *found, back = kernel_call(
+    (found,) = kernel_call(far_first_kernel, [bundle, columns, back_a, ahead_a], [line], FIRST_COST)
+    back_found, ahead_found, back, *turned = kernel_call(
         far_back_kernel,
-        [bundle, others, back_a, ahead_a, back_b, found],
-        [line, half_line, block],
+        [bundle, columns, others, back_a, ahead_a, back_b, found],
+        [line, half_line, block, column, column],
         BACK_COST,
     )
     far = [back, ahead_a, ahead_b]
     to_back, to_ahead = kernel_call(
-        far_last_kernel, [bundle, others, *far, *found], [line] * 2, LAST_COST
+        far_last_kernel,
+        [bundle, columns, others, *far, back_found, ahead_found, *turned],
+        [line] * 2,
+        LAST_COST,
     )
     (mine,) = kernel_call(own_kernel, [own, others, *far, mine], [line], 5)
     best = jnp.maximum(

time: 24.7 us -> 24.7 us (level)
  no operation moved by 1% of the time
where the time goes in v18:
time: 24.7 us; the launch traced here: 24.5 us
  starting transfers between devices  12.9 us (52%)
  waiting for transfers between devices  7.3 us (30%)
  Pallas kernels  3.75 us (15%)
  other arithmetic  0.57 us (2%)
    ppermute x11, starting transfers between devices, send(): return lax.ppermute(value, GROUP, perms[name])  12.9 us
    ppermute x11, waiting for transfers between devices, send(): return lax.ppermute(value, GROUP, perms[name])  7.3 us
    pallas_call x6, Pallas kernels, kernel_call(): pl.pallas_call(kernel, out_shape=outputs, in_specs=[vmem] * len(inputs),...  2.86 us
    pallas_call x1, Pallas kernels, on_ring(): pl.pallas_call(pack_first_kernel, out_shape=chunk(half, True), in_specs=[...  0.89 us
    max x1, other arithmetic, on_ring(): jnp.maximum(mine, jnp.maximum(send(to_back, 'home_back'), send(to_ahead,...  0.57 us
  transfers between devices with their start and end apart: 11, of which 8 were waited for; matrix products, arithmetic and copies ran while one was open for 0% of the time, Pallas kernels for 10%

profile of v18, /device:TPU:0, one launch (start us, length us, event | category | flops | bytes accessed | tf_op | source)
XLA Modules:
  0.0 24.5 jit_solution(3055145506489783302)
XLA Ops:
  0.0 0.0 copy-start
  0.0 0.9 %pack_first.1.first = bf16[528,128]{1,0:T(8,128)(2,1)S(1)} custom-call(bf16[256,512]{1,0:T(8,128)(2,1)} %embeds.3, s32[1,256]{1,0:T(1,128)} %bitcast.2), custom_call_target="tpu_custom_call" | custom-call | tf_op jit(solution)/shard_map/pack_first/pallas_call | solution.py:262
  0.9 2.5 %collective-permute-start.2 = (bf16[528,128]{1,0:T(8,128)(2,1)S(1)}, bf16[528,128]{1,0:T(8,128)(2,1)S(1)}, u32[]{:S(2)}, u32[]{:S(2)}) collective-permute-start(bf16[528,128]{1,0:T(8,128)(2,1)S(1)} %pack_first.1.first), channel_id=1, source_target_pairs={{0,5},{1,4},{4,8},{5,9},{8,12},{9,13},{12,14},{13,15},{14,10},{15,... | collective-permute-start | bytes 405512 | tf_op jit(solution)/shard_map/ppermute | solution.py:251
  3.4 0.0 collective-permute-start
  3.4 0.0 copy-done
  3.4 0.1 pack_second_kernel.1
  3.6 2.1 %collective-permute-start.3 = (bf16[512,128]{1,0:T(8,128)(2,1)S(1)}, bf16[512,128]{1,0:T(8,128)(2,1)S(1)}, u32[]{:S(2)}, u32[]{:S(2)}) collective-permute-start(bf16[512,128]{1,0:T(8,128)(2,1)S(1)} %get-tuple-element.18), channel_id=1, source_target_pairs={{0,5},{1,4},{4,8},{5,9},{8,12},{9,13},{12,14},{13,15},{14,10},{15,... | collective-permute-start | bytes 393224 | tf_op jit(solution)/shard_map/ppermute | solution.py:251
  5.7 0.3 %collective-permute-start.1 = (bf16[512,128]{1,0:T(8,128)(2,1)S(1)}, bf16[512,128]{1,0:T(8,128)(2,1)S(1)}, u32[]{:S(2)}, u32[]{:S(2)}) collective-permute-start(bf16[512,128]{1,0:T(8,128)(2,1)S(1)} %get-tuple-element.18), channel_id=1, source_target_pairs={{0,3},{1,2},{4,0},{5,1},{8,4},{9,5},{12,9},{13,8},{14,13},{15,12},... | collective-permute-start | bytes 393224 | tf_op jit(solution)/shard_map/ppermute | solution.py:251
  5.9 1.5 %collective-permute-done.2.prev_a = bf16[528,128]{1,0:T(8,128)(2,1)S(1)} collective-permute-done((bf16[528,128]{1,0:T(8,128)(2,1)S(1)}, bf16[528,128]{1,0:T(8,128)(2,1)S(1)}, u32[]{:S(2)}, u32[]{:S(2)}) %collective-permute-start.2) | collective-permute-done | bytes 135200 | tf_op jit(solution)/shard_map/ppermute | solution.py:251
  7.4 2.5 %collective-permute-start.5 = (bf16[528,128]{1,0:T(8,128)(2,1)S(1)}, bf16[528,128]{1,0:T(8,128)(2,1)S(1)}, u32[]{:S(2)}, u32[]{:S(2)}) collective-permute-start(bf16[528,128]{1,0:T(8,128)(2,1)S(1)} %collective-permute-done.2.prev_a), channel_id=1, source_target_pairs={{0,4},{1,5},{4,8},{5,9},{8,12},{9,13},{12,14},{13,15},{14,10},{15,... | collective-permute-start | bytes 405512 | tf_op jit(solution)/shard_map/ppermute | solution.py:251
  9.9 0.0 collective-permute-done.succ_a
  9.9 0.0 collective-permute-start.6
  9.9 0.3 %collective-permute-done.3.prev_b = bf16[512,128]{1,0:T(8,128)(2,1)S(1)} collective-permute-done((bf16[512,128]{1,0:T(8,128)(2,1)S(1)}, bf16[512,128]{1,0:T(8,128)(2,1)S(1)}, u32[]{:S(2)}, u32[]{:S(2)}) %collective-permute-start.3) | collective-permute-done | bytes 131104 | tf_op jit(solution)/shard_map/ppermute | solution.py:251
  10.2 2.5 %collective-permute-start.7 = (bf16[512,128]{1,0:T(8,128)(2,1)S(1)}, bf16[512,128]{1,0:T(8,128)(2,1)S(1)}, u32[]{:S(2)}, u32[]{:S(2)}) collective-permute-start(bf16[512,128]{1,0:T(8,128)(2,1)S(1)} %collective-permute-done.3.prev_b), channel_id=1, source_target_pairs={{0,4},{1,5},{4,8},{5,9},{8,12},{9,13},{12,14},{13,15},{14,10},{15,... | collective-permute-start | bytes 393224 | tf_op jit(solution)/shard_map/ppermute | solution.py:251
  12.7 0.0 collective-permute-done.1.succ_b
  12.7 0.0 collective-permute-start.8
  12.7 0.5 %near_kernel.1 = (f32[1,256]{1,0:T(1,128)S(1)}, bf16[3,1040,128]{2,1,0:T(8,128)(2,1)S(1)}, f32[3,256,128]{2,1,0:T(8,128)S(1)}) custom-call(bf16[1040,128]{1,0:T(8,128)(2,1)S(1)} %get-tuple-element.17.own, bf16[528,128]{1,0:T(8,128)(2,1)S(1)} %collective-permute-done.succ_a, bf16[512,128]{1,0:T(8,128)(2,1)S(1)} %collective-permute-done.1.succ_b, ...), custom_call_target="tpu_custom_call" | custom-call | flops 67108864 | bytes 1048576 | tf_op jit(solution)/shard_map/near_kernel/pallas_call | solution.py:232
  13.1 0.1 collective-permute-start.4
  13.2 0.5 %collective-permute-done.5.back_a = bf16[528,128]{1,0:T(8,128)(2,1)S(1)} collective-permute-done((bf16[528,128]{1,0:T(8,128)(2,1)S(1)}, bf16[528,128]{1,0:T(8,128)(2,1)S(1)}, u32[]{:S(2)}, u32[]{:S(2)}) %collective-permute-start.5) | collective-permute-done | bytes 135200 | tf_op jit(solution)/shard_map/ppermute | solution.py:251
  13.8 1.7 %collective-permute-done.6.ahead_a = bf16[528,128]{1,0:T(8,128)(2,1)S(1)} collective-permute-done((bf16[528,128]{1,0:T(8,128)(2,1)S(1)}, bf16[528,128]{1,0:T(8,128)(2,1)S(1)}, u32[]{:S(2)}, u32[]{:S(2)}) %collective-permute-start.6) | collective-permute-done | bytes 135200 | tf_op jit(solution)/shard_map/ppermute | solution.py:251
  15.4 0.6 %far_first_kernel.1.found = f32[1,256]{1,0:T(1,128)S(1)} custom-call(bf16[3,1040,128]{2,1,0:T(8,128)(2,1)S(1)} %get-tuple-element.19.bundle, f32[3,256,128]{2,1,0:T(8,128)S(1)} %get-tuple-element.20.columns, bf16[528,128]{1,0:T(8,128)(2,1)S(1)} %collective-permute-done.5.back_a, bf16[528,128]{1,0:T(8,128)(2,1)S(1)} %collective-permute-done.6.ahead_a), custom_call_target="tpu_custom_call" | custom-call | flops 13421772800 | bytes 1048576 | tf_op jit(solution)/shard_map/far_first_kernel/pallas_call | solution.py:232
  16.0 0.2 collective-permute-done.7.back_b
  16.2 0.0 collective-permute-done.4.others
  16.2 0.6 %far_back_kernel.1 = (f32[1,256]{1,0:T(1,128)S(1)}, f32[1,128]{1,0:T(1,128)S(1)}, bf16[1040,128]{1,0:T(8,128)(2,1)S(1)}, f32[256,128]{1,0:T(8,128)S(1)}, f32[256,128]{1,0:T(8,128)S(1)}) custom-call(bf16[3,1040,128]{2,1,0:T(8,128)(2,1)S(1)} %get-tuple-element.19.bundle, f32[3,256,128]{2,1,0:T(8,128)S(1)} %get-tuple-element.20.columns, ...), custom_call_target="tpu_custom_call" | custom-call | flops 134217728 | bytes 1048576 | tf_op jit(solution)/shard_map/far_back_kernel/pallas_call | solution.py:232
  16.8 1.3 %collective-permute-done.8.ahead_b = bf16[512,128]{1,0:T(8,128)(2,1)S(1)} collective-permute-done((bf16[512,128]{1,0:T(8,128)(2,1)S(1)}, bf16[512,128]{1,0:T(8,128)(2,1)S(1)}, u32[]{:S(2)}, u32[]{:S(2)}) %collective-permute-start.8) | collective-permute-done | bytes 131104 | tf_op jit(solution)/shard_map/ppermute | solution.py:251
  18.1 0.5 %far_last_kernel.1 = (f32[1,256]{1,0:T(1,128)S(1)}, f32[1,256]{1,0:T(1,128)S(1)}) custom-call(bf16[3,1040,128]{2,1,0:T(8,128)(2,1)S(1)} %get-tuple-element.19.bundle, f32[3,256,128]{2,1,0:T(8,128)S(1)} %get-tuple-element.20.columns, bf16[3,1040,128]{2,1,0:T(8,128)(2,1)S(1)} %collective-permute-done.4.others, bf16[1040,128]{1,0:T(8,128)(2,1)S(1)} %get-tuple-element.21.back, ...), custom_call_target="tpu_custom_call" | custom-call | flops 335544320 | bytes 1048576 | tf_op jit(solution)/shard_map/far_last_kernel/pallas_call | solution.py:232
  18.6 1.5 %collective-permute-start.9 = (f32[1,256]{1,0:T(1,128)S(1)}, f32[1,256]{1,0:T(1,128)S(1)}, u32[]{:S(2)}, u32[]{:S(2)}) collective-permute-start(f32[1,256]{1,0:T(1,128)S(1)} %get-tuple-element.27), channel_id=1, source_target_pairs={{0,6},{1,7},{4,3},{5,2},{8,1},{9,0},{12,4},{13,5},{14,8},{15,9},{1... | collective-permute-start | bytes 3080 | tf_op jit(solution)/shard_map/ppermute | solution.py:251
  20.1 1.5 %collective-permute-start.10 = (f32[1,256]{1,0:T(1,128)S(1)}, f32[1,256]{1,0:T(1,128)S(1)}, u32[]{:S(2)}, u32[]{:S(2)}) collective-permute-start(f32[1,256]{1,0:T(1,128)S(1)} %get-tuple-element.28), channel_id=1, source_target_pairs={{0,8},{1,9},{4,13},{5,12},{8,15},{9,14},{12,11},{13,10},{14,7},{15... | collective-permute-start | bytes 3080 | tf_op jit(solution)/shard_map/ppermute | solution.py:251
  21.6 0.6 %own_kernel.1 = f32[1,256]{1,0:T(1,128)S(1)} custom-call(bf16[1040,128]{1,0:T(8,128)(2,1)S(1)} %get-tuple-element.17.own, bf16[3,1040,128]{2,1,0:T(8,128)(2,1)S(1)} %collective-permute-done.4.others, bf16[1040,128]{1,0:T(8,128)(2,1)S(1)} %get-tuple-element.21.back, bf16[528,128]{1,0:T(8,128)(2,1)S(1)} %collective-permute-done.6.ahead_a, ...), custom_call_target="tpu_custom_call" | custom-call | flops 335544320 | bytes 1048576 | tf_op jit(solution)/shard_map/own_kernel/pallas_call | solution.py:232
  22.2 0.4 %collective-permute-done.9 = f32[1,256]{1,0:T(1,128)S(1)} collective-permute-done((f32[1,256]{1,0:T(1,128)S(1)}, f32[1,256]{1,0:T(1,128)S(1)}, u32[]{:S(2)}, u32[]{:S(2)}) %collective-permute-start.9) | collective-permute-done | bytes 1056 | tf_op jit(solution)/shard_map/ppermute | solution.py:251
  22.6 1.4 %collective-permute-done.10 = f32[1,256]{1,0:T(1,128)S(1)} collective-permute-done((f32[1,256]{1,0:T(1,128)S(1)}, f32[1,256]{1,0:T(1,128)S(1)}, u32[]{:S(2)}, u32[]{:S(2)}) %collective-permute-start.10) | collective-permute-done | bytes 1056 | tf_op jit(solution)/shard_map/ppermute | solution.py:251
  24.0 0.6 %maximum_maximum_fusion = f32[1,256]{1,0:T(1,128)} fusion(f32[1,256]{1,0:T(1,128)S(1)} %own_kernel.1, f32[1,256]{1,0:T(1,128)S(1)} %collective-permute-done.9, f32[1,256]{1,0:T(1,128)S(1)} %collective-permute-done.10), kind=kLoop, calls=%fused_computation | loop fusion | flops 512 | bytes 4096 | tf_op jit(solution)/shard_map/max | solution.py:309
Async XLA Ops:
  0.0 3.4 %copy-start = (bf16[256,512]{1,0:T(8,128)(2,1)S(1)}, bf16[256,512]{1,0:T(8,128)(2,1)}, u32[]{:S(2)}) copy-start(bf16[256,512]{1,0:T(8,128)(2,1)} %embeds.3) | copy-start | bytes 786436
  0.9 6.5 %collective-permute-start.2 = (bf16[528,128]{1,0:T(8,128)(2,1)S(1)}, bf16[528,128]{1,0:T(8,128)(2,1)S(1)}, u32[]{:S(2)}, u32[]{:S(2)}) collective-permute-start(bf16[528,128]{1,0:T(8,128)(2,1)S(1)} %pack_first.1.first), channel_id=1, source_target_pairs={{0,5},{1,4},{4,8},{5,9},{8,12},{9,13},{12,14},{13,15},{14,10},{15,... | collective-permute-start | bytes 405512 | tf_op jit(solution)/shard_map/ppermute | solution.py:251
  3.4 6.5 %collective-permute-start = (bf16[528,128]{1,0:T(8,128)(2,1)S(1)}, bf16[528,128]{1,0:T(8,128)(2,1)S(1)}, u32[]{:S(2)}, u32[]{:S(2)}) collective-permute-start(bf16[528,128]{1,0:T(8,128)(2,1)S(1)} %pack_first.1.first), channel_id=1, source_target_pairs={{0,3},{1,2},{4,0},{5,1},{8,4},{9,5},{12,9},{13,8},{14,13},{15,12},... | collective-permute-start | bytes 405512 | tf_op jit(solution)/shard_map/ppermute | solution.py:251
  3.6 6.6 %collective-permute-start.3 = (bf16[512,128]{1,0:T(8,128)(2,1)S(1)}, bf16[512,128]{1,0:T(8,128)(2,1)S(1)}, u32[]{:S(2)}, u32[]{:S(2)}) collective-permute-start(bf16[512,128]{1,0:T(8,128)(2,1)S(1)} %get-tuple-element.18), channel_id=1, source_target_pairs={{0,5},{1,4},{4,8},{5,9},{8,12},{9,13},{12,14},{13,15},{14,10},{15,... | collective-permute-start | bytes 393224 | tf_op jit(solution)/shard_map/ppermute | solution.py:251
  5.7 7.0 %collective-permute-start.1 = (bf16[512,128]{1,0:T(8,128)(2,1)S(1)}, bf16[512,128]{1,0:T(8,128)(2,1)S(1)}, u32[]{:S(2)}, u32[]{:S(2)}) collective-permute-start(bf16[512,128]{1,0:T(8,128)(2,1)S(1)} %get-tuple-element.18), channel_id=1, source_target_pairs={{0,3},{1,2},{4,0},{5,1},{8,4},{9,5},{12,9},{13,8},{14,13},{15,12},... | collective-permute-start | bytes 393224 | tf_op jit(solution)/shard_map/ppermute | solution.py:251
  7.4 6.3 %collective-permute-start.5 = (bf16[528,128]{1,0:T(8,128)(2,1)S(1)}, bf16[528,128]{1,0:T(8,128)(2,1)S(1)}, u32[]{:S(2)}, u32[]{:S(2)}) collective-permute-start(bf16[528,128]{1,0:T(8,128)(2,1)S(1)} %collective-permute-done.2.prev_a), channel_id=1, source_target_pairs={{0,4},{1,5},{4,8},{5,9},{8,12},{9,13},{12,14},{13,15},{14,10},{15,... | collective-permute-start | bytes 405512 | tf_op jit(solution)/shard_map/ppermute | solution.py:251
  9.9 5.5 %collective-permute-start.6 = (bf16[528,128]{1,0:T(8,128)(2,1)S(1)}, bf16[528,128]{1,0:T(8,128)(2,1)S(1)}, u32[]{:S(2)}, u32[]{:S(2)}) collective-permute-start(bf16[528,128]{1,0:T(8,128)(2,1)S(1)} %collective-permute-done.succ_a), channel_id=1, source_target_pairs={{0,2},{1,3},{4,0},{5,1},{8,4},{9,5},{12,8},{13,9},{14,12},{15,13},... | collective-permute-start | bytes 405512 | tf_op jit(solution)/shard_map/ppermute | solution.py:251
  10.2 6.0 %collective-permute-start.7 = (bf16[512,128]{1,0:T(8,128)(2,1)S(1)}, bf16[512,128]{1,0:T(8,128)(2,1)S(1)}, u32[]{:S(2)}, u32[]{:S(2)}) collective-permute-start(bf16[512,128]{1,0:T(8,128)(2,1)S(1)} %collective-permute-done.3.prev_b), channel_id=1, source_target_pairs={{0,4},{1,5},{4,8},{5,9},{8,12},{9,13},{12,14},{13,15},{14,10},{15,... | collective-permute-start | bytes 393224 | tf_op jit(solution)/shard_map/ppermute | solution.py:251
  12.7 5.4 %collective-permute-start.8 = (bf16[512,128]{1,0:T(8,128)(2,1)S(1)}, bf16[512,128]{1,0:T(8,128)(2,1)S(1)}, u32[]{:S(2)}, u32[]{:S(2)}) collective-permute-start(bf16[512,128]{1,0:T(8,128)(2,1)S(1)} %collective-permute-done.1.succ_b), channel_id=1, source_target_pairs={{0,2},{1,3},{4,0},{5,1},{8,4},{9,5},{12,8},{13,9},{14,12},{15,13},... | collective-permute-start | bytes 393224 | tf_op jit(solution)/shard_map/ppermute | solution.py:251
  13.1 3.1 %collective-permute-start.4 = (bf16[3,1040,128]{2,1,0:T(8,128)(2,1)S(1)}, bf16[3,1040,128]{2,1,0:T(8,128)(2,1)S(1)}, u32[]{:S(2)}, u32[]{:S(2)}) collective-permute-start(bf16[3,1040,128]{2,1,0:T(8,128)(2,1)S(1)} %get-tuple-element.19.bundle), channel_id=1, source_target_pairs={{0,1},{1,0},{4,5},{5,4},{8,9},{9,8},{12,13},{13,12},{14,15},{15,14... | collective-permute-start | bytes 2396168 | tf_op jit(solution)/shard_map/ppermute | solution.py:251
  18.6 4.0 %collective-permute-start.9 = (f32[1,256]{1,0:T(1,128)S(1)}, f32[1,256]{1,0:T(1,128)S(1)}, u32[]{:S(2)}, u32[]{:S(2)}) collective-permute-start(f32[1,256]{1,0:T(1,128)S(1)} %get-tuple-element.27), channel_id=1, source_target_pairs={{0,6},{1,7},{4,3},{5,2},{8,1},{9,0},{12,4},{13,5},{14,8},{15,9},{1... | collective-permute-start | bytes 3080 | tf_op jit(solution)/shard_map/ppermute | solution.py:251
  20.1 3.9 %collective-permute-start.10 = (f32[1,256]{1,0:T(1,128)S(1)}, f32[1,256]{1,0:T(1,128)S(1)}, u32[]{:S(2)}, u32[]{:S(2)}) collective-permute-start(f32[1,256]{1,0:T(1,128)S(1)} %get-tuple-element.28), channel_id=1, source_target_pairs={{0,8},{1,9},{4,13},{5,12},{8,15},{9,14},{12,11},{13,10},{14,7},{15... | collective-permute-start | bytes 3080 | tf_op jit(solution)/shard_map/ppermute | solution.py:251

commit v19 on v17

--- a/solution.py
+++ b/solution.py
@@ -1,3 +1,5 @@
+import functools
+
 import jax
 import jax.numpy as jnp
 from jax import lax
@@ -138,6 +140,23 @@
     return jnp.concatenate(pieces, axis=1)
 
 
+def masked(queries, first, *others):
+    all_keys = (first, *others)
+    sims = lax.dot_general(
+        jnp.concatenate([keys.unit for keys in all_keys], axis=0),
+        queries.unit,
+        (((1,), (1,)), ((), ())),
+        preferred_element_type=jnp.float32,
+    )
+    found, at = [], 0
+    for keys in all_keys:
+        keep = keys.column() == queries.label
+        found.append(jnp.where(keep, sims[at : at + keys.rows, :], -1.0))
+        at += keys.rows
+    best = [jnp.max(block, axis=0, keepdims=True) for block in found]
+    return found[0], functools.reduce(jnp.maximum, best)
+
+
 def near_kernel(own, succ_a, succ_b, prev_a, prev_b, mine, bundle):
     rows = mine.shape[1]
     prev, succ = whole(prev_a, prev_b, rows), whole(succ_a, succ_b, rows)
@@ -177,10 +196,12 @@
     rows = to_back.shape[1]
     half = rows // 2
     back, rest = packed(back, rows), second_half(ahead_a, ahead_b, rows)
-    keys = (packed(ref, rows) for ref in (bundle.at[2], bundle.at[0], others.at[0]))
-    to_back[...] = jnp.maximum(back_found[...], best_of(back, rest))
+    keys = [packed(ref, rows) for ref in (bundle.at[2], bundle.at[0], others.at[0])]
+    sims, found = masked(rest, back, *keys)
     to_ahead[:, :half] = ahead_found[...]
-    to_ahead[:, half:] = best_of(rest, *keys, back)
+    to_ahead[:, half:] = found
+    best = jnp.max(jnp.transpose(sims), axis=0, keepdims=True)
+    to_back[...] = jnp.maximum(back_found[...], best)
 
 
 def own_kernel(own, others, back, ahead_a, ahead_b, near, mine):

time: 24.7 us -> 24.6 us (level)
  no operation moved by 1% of the time
where the time goes in v19:
time: 24.6 us; the launch traced here: 24.5 us
  starting transfers between devices  12.8 us (52%)
  waiting for transfers between devices  7.31 us (30%)
  Pallas kernels  3.71 us (15%)
  other arithmetic  0.57 us (2%)
    ppermute x11, starting transfers between devices, send(): return lax.ppermute(value, GROUP, perms[name])  12.8 us
    ppermute x11, waiting for transfers between devices, send(): return lax.ppermute(value, GROUP, perms[name])  7.31 us
    pallas_call x6, Pallas kernels, kernel_call(): pl.pallas_call(kernel, out_shape=outputs, in_specs=[vmem] * len(inputs),...  2.82 us
    pallas_call x1, Pallas kernels, on_ring(): pl.pallas_call(pack_first_kernel, out_shape=chunk(half, True), in_specs=[...  0.89 us
    max x1, other arithmetic, on_ring(): jnp.maximum(mine, jnp.maximum(send(to_back, 'home_back'), send(to_ahead,...  0.57 us
  transfers between devices with their start and end apart: 11, of which 8 were waited for; matrix products, arithmetic and copies ran while one was open for 0% of the time, Pallas kernels for 10%

profile of v19, /device:TPU:0, one launch (start us, length us, event | category | flops | bytes accessed | tf_op | source)
XLA Modules:
  0.0 24.5 jit_solution(11081027606677522729)
XLA Ops:
  0.0 0.0 copy-start
  0.0 0.9 %pack_first.1.first = bf16[528,128]{1,0:T(8,128)(2,1)S(1)} custom-call(bf16[256,512]{1,0:T(8,128)(2,1)} %embeds.3, s32[1,256]{1,0:T(1,128)} %bitcast.2), custom_call_target="tpu_custom_call" | custom-call | tf_op jit(solution)/shard_map/pack_first/pallas_call | solution.py:276
  0.9 2.5 %collective-permute-start.2 = (bf16[528,128]{1,0:T(8,128)(2,1)S(1)}, bf16[528,128]{1,0:T(8,128)(2,1)S(1)}, u32[]{:S(2)}, u32[]{:S(2)}) collective-permute-start(bf16[528,128]{1,0:T(8,128)(2,1)S(1)} %pack_first.1.first), channel_id=1, source_target_pairs={{0,5},{1,4},{4,8},{5,9},{8,12},{9,13},{12,14},{13,15},{14,10},{15,... | collective-permute-start | bytes 405512 | tf_op jit(solution)/shard_map/ppermute | solution.py:265
  3.4 0.0 collective-permute-start
  3.4 0.0 copy-done
  3.4 0.1 pack_second_kernel.1
  3.6 2.1 %collective-permute-start.3 = (bf16[512,128]{1,0:T(8,128)(2,1)S(1)}, bf16[512,128]{1,0:T(8,128)(2,1)S(1)}, u32[]{:S(2)}, u32[]{:S(2)}) collective-permute-start(bf16[512,128]{1,0:T(8,128)(2,1)S(1)} %get-tuple-element.15), channel_id=1, source_target_pairs={{0,5},{1,4},{4,8},{5,9},{8,12},{9,13},{12,14},{13,15},{14,10},{15,... | collective-permute-start | bytes 393224 | tf_op jit(solution)/shard_map/ppermute | solution.py:265
  5.7 0.3 %collective-permute-start.1 = (bf16[512,128]{1,0:T(8,128)(2,1)S(1)}, bf16[512,128]{1,0:T(8,128)(2,1)S(1)}, u32[]{:S(2)}, u32[]{:S(2)}) collective-permute-start(bf16[512,128]{1,0:T(8,128)(2,1)S(1)} %get-tuple-element.15), channel_id=1, source_target_pairs={{0,3},{1,2},{4,0},{5,1},{8,4},{9,5},{12,9},{13,8},{14,13},{15,12},... | collective-permute-start | bytes 393224 | tf_op jit(solution)/shard_map/ppermute | solution.py:265
  5.9 1.5 %collective-permute-done.2.prev_a = bf16[528,128]{1,0:T(8,128)(2,1)S(1)} collective-permute-done((bf16[528,128]{1,0:T(8,128)(2,1)S(1)}, bf16[528,128]{1,0:T(8,128)(2,1)S(1)}, u32[]{:S(2)}, u32[]{:S(2)}) %collective-permute-start.2) | collective-permute-done | bytes 135200 | tf_op jit(solution)/shard_map/ppermute | solution.py:265
  7.4 2.5 %collective-permute-start.5 = (bf16[528,128]{1,0:T(8,128)(2,1)S(1)}, bf16[528,128]{1,0:T(8,128)(2,1)S(1)}, u32[]{:S(2)}, u32[]{:S(2)}) collective-permute-start(bf16[528,128]{1,0:T(8,128)(2,1)S(1)} %collective-permute-done.2.prev_a), channel_id=1, source_target_pairs={{0,4},{1,5},{4,8},{5,9},{8,12},{9,13},{12,14},{13,15},{14,10},{15,... | collective-permute-start | bytes 405512 | tf_op jit(solution)/shard_map/ppermute | solution.py:265
  9.9 0.0 collective-permute-done.succ_a
  9.9 0.0 collective-permute-start.6
  9.9 0.3 %collective-permute-done.3.prev_b = bf16[512,128]{1,0:T(8,128)(2,1)S(1)} collective-permute-done((bf16[512,128]{1,0:T(8,128)(2,1)S(1)}, bf16[512,128]{1,0:T(8,128)(2,1)S(1)}, u32[]{:S(2)}, u32[]{:S(2)}) %collective-permute-start.3) | collective-permute-done | bytes 131104 | tf_op jit(solution)/shard_map/ppermute | solution.py:265
  10.2 2.5 %collective-permute-start.7 = (bf16[512,128]{1,0:T(8,128)(2,1)S(1)}, bf16[512,128]{1,0:T(8,128)(2,1)S(1)}, u32[]{:S(2)}, u32[]{:S(2)}) collective-permute-start(bf16[512,128]{1,0:T(8,128)(2,1)S(1)} %collective-permute-done.3.prev_b), channel_id=1, source_target_pairs={{0,4},{1,5},{4,8},{5,9},{8,12},{9,13},{12,14},{13,15},{14,10},{15,... | collective-permute-start | bytes 393224 | tf_op jit(solution)/shard_map/ppermute | solution.py:265
  12.7 0.0 collective-permute-done.1.succ_b
  12.7 0.0 collective-permute-start.8
  12.7 0.5 %near_kernel.1 = (f32[1,256]{1,0:T(1,128)S(1)}, bf16[3,1040,128]{2,1,0:T(8,128)(2,1)S(1)}) custom-call(bf16[1040,128]{1,0:T(8,128)(2,1)S(1)} %get-tuple-element.14.own, bf16[528,128]{1,0:T(8,128)(2,1)S(1)} %collective-permute-done.succ_a, bf16[512,128]{1,0:T(8,128)(2,1)S(1)} %collective-permute-done.1.succ_b, ...), custom_call_target="tpu_custom_call" | custom-call | flops 67108864 | bytes 1048576 | tf_op jit(solution)/shard_map/near_kernel/pallas_call | solution.py:246
  13.1 0.1 collective-permute-start.4
  13.2 0.5 %collective-permute-done.5.back_a = bf16[528,128]{1,0:T(8,128)(2,1)S(1)} collective-permute-done((bf16[528,128]{1,0:T(8,128)(2,1)S(1)}, bf16[528,128]{1,0:T(8,128)(2,1)S(1)}, u32[]{:S(2)}, u32[]{:S(2)}) %collective-permute-start.5) | collective-permute-done | bytes 135200 | tf_op jit(solution)/shard_map/ppermute | solution.py:265
  13.8 1.7 %collective-permute-done.6.ahead_a = bf16[528,128]{1,0:T(8,128)(2,1)S(1)} collective-permute-done((bf16[528,128]{1,0:T(8,128)(2,1)S(1)}, bf16[528,128]{1,0:T(8,128)(2,1)S(1)}, u32[]{:S(2)}, u32[]{:S(2)}) %collective-permute-start.6) | collective-permute-done | bytes 135200 | tf_op jit(solution)/shard_map/ppermute | solution.py:265
  15.4 0.6 %far_first_kernel.1.found = f32[1,256]{1,0:T(1,128)S(1)} custom-call(bf16[3,1040,128]{2,1,0:T(8,128)(2,1)S(1)} %get-tuple-element.16.bundle, bf16[528,128]{1,0:T(8,128)(2,1)S(1)} %collective-permute-done.5.back_a, bf16[528,128]{1,0:T(8,128)(2,1)S(1)} %collective-permute-done.6.ahead_a), custom_call_target="tpu_custom_call" | custom-call | flops 13421772800 | bytes 1048576 | tf_op jit(solution)/shard_map/far_first_kernel/pallas_call | solution.py:246
  16.0 0.2 collective-permute-done.7.back_b
  16.2 0.0 collective-permute-done.4.others
  16.2 0.6 %far_back_kernel.1 = (f32[1,256]{1,0:T(1,128)S(1)}, f32[1,128]{1,0:T(1,128)S(1)}, bf16[1040,128]{1,0:T(8,128)(2,1)S(1)}) custom-call(bf16[3,1040,128]{2,1,0:T(8,128)(2,1)S(1)} %get-tuple-element.16.bundle, bf16[3,1040,128]{2,1,0:T(8,128)(2,1)S(1)} %collective-permute-done.4.others, bf16[528,128]{1,0:T(8,128)(2,1)S(1)} %collective-permute-done.5.back_a, ...), custom_call_target="tpu_custom_call" | custom-call | flops 134217728 | bytes 1048576 | tf_op jit(solution)/shard_map/far_back_kernel/pallas_call | solution.py:246
  16.8 1.3 %collective-permute-done.8.ahead_b = bf16[512,128]{1,0:T(8,128)(2,1)S(1)} collective-permute-done((bf16[512,128]{1,0:T(8,128)(2,1)S(1)}, bf16[512,128]{1,0:T(8,128)(2,1)S(1)}, u32[]{:S(2)}, u32[]{:S(2)}) %collective-permute-start.8) | collective-permute-done | bytes 131104 | tf_op jit(solution)/shard_map/ppermute | solution.py:265
  18.1 0.5 %far_last_kernel.1 = (f32[1,256]{1,0:T(1,128)S(1)}, f32[1,256]{1,0:T(1,128)S(1)}) custom-call(bf16[3,1040,128]{2,1,0:T(8,128)(2,1)S(1)} %get-tuple-element.16.bundle, bf16[3,1040,128]{2,1,0:T(8,128)(2,1)S(1)} %collective-permute-done.4.others, bf16[1040,128]{1,0:T(8,128)(2,1)S(1)} %get-tuple-element.17.back, ...), custom_call_target="tpu_custom_call" | custom-call | flops 335544320 | bytes 1048576 | tf_op jit(solution)/shard_map/far_last_kernel/pallas_call | solution.py:246
  18.6 1.5 %collective-permute-start.9 = (f32[1,256]{1,0:T(1,128)S(1)}, f32[1,256]{1,0:T(1,128)S(1)}, u32[]{:S(2)}, u32[]{:S(2)}) collective-permute-start(f32[1,256]{1,0:T(1,128)S(1)} %get-tuple-element.21), channel_id=1, source_target_pairs={{0,6},{1,7},{4,3},{5,2},{8,1},{9,0},{12,4},{13,5},{14,8},{15,9},{1... | collective-permute-start | bytes 3080 | tf_op jit(solution)/shard_map/ppermute | solution.py:265
  20.0 1.5 %collective-permute-start.10 = (f32[1,256]{1,0:T(1,128)S(1)}, f32[1,256]{1,0:T(1,128)S(1)}, u32[]{:S(2)}, u32[]{:S(2)}) collective-permute-start(f32[1,256]{1,0:T(1,128)S(1)} %get-tuple-element.22), channel_id=1, source_target_pairs={{0,8},{1,9},{4,13},{5,12},{8,15},{9,14},{12,11},{13,10},{14,7},{15... | collective-permute-start | bytes 3080 | tf_op jit(solution)/shard_map/ppermute | solution.py:265
  21.6 0.6 %own_kernel.1 = f32[1,256]{1,0:T(1,128)S(1)} custom-call(bf16[1040,128]{1,0:T(8,128)(2,1)S(1)} %get-tuple-element.14.own, bf16[3,1040,128]{2,1,0:T(8,128)(2,1)S(1)} %collective-permute-done.4.others, bf16[1040,128]{1,0:T(8,128)(2,1)S(1)} %get-tuple-element.17.back, bf16[528,128]{1,0:T(8,128)(2,1)S(1)} %collective-permute-done.6.ahead_a, ...), custom_call_target="tpu_custom_call" | custom-call | flops 335544320 | bytes 1048576 | tf_op jit(solution)/shard_map/own_kernel/pallas_call | solution.py:246
  22.1 0.4 %collective-permute-done.9 = f32[1,256]{1,0:T(1,128)S(1)} collective-permute-done((f32[1,256]{1,0:T(1,128)S(1)}, f32[1,256]{1,0:T(1,128)S(1)}, u32[]{:S(2)}, u32[]{:S(2)}) %collective-permute-start.9) | collective-permute-done | bytes 1056 | tf_op jit(solution)/shard_map/ppermute | solution.py:265
  22.5 1.4 %collective-permute-done.10 = f32[1,256]{1,0:T(1,128)S(1)} collective-permute-done((f32[1,256]{1,0:T(1,128)S(1)}, f32[1,256]{1,0:T(1,128)S(1)}, u32[]{:S(2)}, u32[]{:S(2)}) %collective-permute-start.10) | collective-permute-done | bytes 1056 | tf_op jit(solution)/shard_map/ppermute | solution.py:265
  23.9 0.6 %maximum_maximum_fusion = f32[1,256]{1,0:T(1,128)} fusion(f32[1,256]{1,0:T(1,128)S(1)} %own_kernel.1, f32[1,256]{1,0:T(1,128)S(1)} %collective-permute-done.9, f32[1,256]{1,0:T(1,128)S(1)} %collective-permute-done.10), kind=kLoop, calls=%fused_computation | loop fusion | flops 512 | bytes 4096 | tf_op jit(solution)/shard_map/max | solution.py:316
Async XLA Ops:
  0.0 3.4 %copy-start = (bf16[256,512]{1,0:T(8,128)(2,1)S(1)}, bf16[256,512]{1,0:T(8,128)(2,1)}, u32[]{:S(2)}) copy-start(bf16[256,512]{1,0:T(8,128)(2,1)} %embeds.3) | copy-start | bytes 786436
  0.9 6.5 %collective-permute-start.2 = (bf16[528,128]{1,0:T(8,128)(2,1)S(1)}, bf16[528,128]{1,0:T(8,128)(2,1)S(1)}, u32[]{:S(2)}, u32[]{:S(2)}) collective-permute-start(bf16[528,128]{1,0:T(8,128)(2,1)S(1)} %pack_first.1.first), channel_id=1, source_target_pairs={{0,5},{1,4},{4,8},{5,9},{8,12},{9,13},{12,14},{13,15},{14,10},{15,... | collective-permute-start | bytes 405512 | tf_op jit(solution)/shard_map/ppermute | solution.py:265
  3.4 6.5 %collective-permute-start = (bf16[528,128]{1,0:T(8,128)(2,1)S(1)}, bf16[528,128]{1,0:T(8,128)(2,1)S(1)}, u32[]{:S(2)}, u32[]{:S(2)}) collective-permute-start(bf16[528,128]{1,0:T(8,128)(2,1)S(1)} %pack_first.1.first), channel_id=1, source_target_pairs={{0,3},{1,2},{4,0},{5,1},{8,4},{9,5},{12,9},{13,8},{14,13},{15,12},... | collective-permute-start | bytes 405512 | tf_op jit(solution)/shard_map/ppermute | solution.py:265
  3.6 6.6 %collective-permute-start.3 = (bf16[512,128]{1,0:T(8,128)(2,1)S(1)}, bf16[512,128]{1,0:T(8,128)(2,1)S(1)}, u32[]{:S(2)}, u32[]{:S(2)}) collective-permute-start(bf16[512,128]{1,0:T(8,128)(2,1)S(1)} %get-tuple-element.15), channel_id=1, source_target_pairs={{0,5},{1,4},{4,8},{5,9},{8,12},{9,13},{12,14},{13,15},{14,10},{15,... | collective-permute-start | bytes 393224 | tf_op jit(solution)/shard_map/ppermute | solution.py:265
  5.7 7.0 %collective-permute-start.1 = (bf16[512,128]{1,0:T(8,128)(2,1)S(1)}, bf16[512,128]{1,0:T(8,128)(2,1)S(1)}, u32[]{:S(2)}, u32[]{:S(2)}) collective-permute-start(bf16[512,128]{1,0:T(8,128)(2,1)S(1)} %get-tuple-element.15), channel_id=1, source_target_pairs={{0,3},{1,2},{4,0},{5,1},{8,4},{9,5},{12,9},{13,8},{14,13},{15,12},... | collective-permute-start | bytes 393224 | tf_op jit(solution)/shard_map/ppermute | solution.py:265
  7.4 6.3 %collective-permute-start.5 = (bf16[528,128]{1,0:T(8,128)(2,1)S(1)}, bf16[528,128]{1,0:T(8,128)(2,1)S(1)}, u32[]{:S(2)}, u32[]{:S(2)}) collective-permute-start(bf16[528,128]{1,0:T(8,128)(2,1)S(1)} %collective-permute-done.2.prev_a), channel_id=1, source_target_pairs={{0,4},{1,5},{4,8},{5,9},{8,12},{9,13},{12,14},{13,15},{14,10},{15,... | collective-permute-start | bytes 405512 | tf_op jit(solution)/shard_map/ppermute | solution.py:265
  9.9 5.5 %collective-permute-start.6 = (bf16[528,128]{1,0:T(8,128)(2,1)S(1)}, bf16[528,128]{1,0:T(8,128)(2,1)S(1)}, u32[]{:S(2)}, u32[]{:S(2)}) collective-permute-start(bf16[528,128]{1,0:T(8,128)(2,1)S(1)} %collective-permute-done.succ_a), channel_id=1, source_target_pairs={{0,2},{1,3},{4,0},{5,1},{8,4},{9,5},{12,8},{13,9},{14,12},{15,13},... | collective-permute-start | bytes 405512 | tf_op jit(solution)/shard_map/ppermute | solution.py:265
  10.2 6.0 %collective-permute-start.7 = (bf16[512,128]{1,0:T(8,128)(2,1)S(1)}, bf16[512,128]{1,0:T(8,128)(2,1)S(1)}, u32[]{:S(2)}, u32[]{:S(2)}) collective-permute-start(bf16[512,128]{1,0:T(8,128)(2,1)S(1)} %collective-permute-done.3.prev_b), channel_id=1, source_target_pairs={{0,4},{1,5},{4,8},{5,9},{8,12},{9,13},{12,14},{13,15},{14,10},{15,... | collective-permute-start | bytes 393224 | tf_op jit(solution)/shard_map/ppermute | solution.py:265
  12.7 5.4 %collective-permute-start.8 = (bf16[512,128]{1,0:T(8,128)(2,1)S(1)}, bf16[512,128]{1,0:T(8,128)(2,1)S(1)}, u32[]{:S(2)}, u32[]{:S(2)}) collective-permute-start(bf16[512,128]{1,0:T(8,128)(2,1)S(1)} %collective-permute-done.1.succ_b), channel_id=1, source_target_pairs={{0,2},{1,3},{4,0},{5,1},{8,4},{9,5},{12,8},{13,9},{14,12},{15,13},... | collective-permute-start | bytes 393224 | tf_op jit(solution)/shard_map/ppermute | solution.py:265
  13.1 3.1 %collective-permute-start.4 = (bf16[3,1040,128]{2,1,0:T(8,128)(2,1)S(1)}, bf16[3,1040,128]{2,1,0:T(8,128)(2,1)S(1)}, u32[]{:S(2)}, u32[]{:S(2)}) collective-permute-start(bf16[3,1040,128]{2,1,0:T(8,128)(2,1)S(1)} %get-tuple-element.16.bundle), channel_id=1, source_target_pairs={{0,1},{1,0},{4,5},{5,4},{8,9},{9,8},{12,13},{13,12},{14,15},{15,14... | collective-permute-start | bytes 2396168 | tf_op jit(solution)/shard_map/ppermute | solution.py:265
  18.6 4.0 %collective-permute-start.9 = (f32[1,256]{1,0:T(1,128)S(1)}, f32[1,256]{1,0:T(1,128)S(1)}, u32[]{:S(2)}, u32[]{:S(2)}) collective-permute-start(f32[1,256]{1,0:T(1,128)S(1)} %get-tuple-element.21), channel_id=1, source_target_pairs={{0,6},{1,7},{4,3},{5,2},{8,1},{9,0},{12,4},{13,5},{14,8},{15,9},{1... | collective-permute-start | bytes 3080 | tf_op jit(solution)/shard_map/ppermute | solution.py:265
  20.0 3.9 %collective-permute-start.10 = (f32[1,256]{1,0:T(1,128)S(1)}, f32[1,256]{1,0:T(1,128)S(1)}, u32[]{:S(2)}, u32[]{:S(2)}) collective-permute-start(f32[1,256]{1,0:T(1,128)S(1)} %get-tuple-element.22), channel_id=1, source_target_pairs={{0,8},{1,9},{4,13},{5,12},{8,15},{9,14},{12,11},{13,10},{14,7},{15... | collective-permute-start | bytes 3080 | tf_op jit(solution)/shard_map/ppermute | solution.py:265

commit v20 on v19

--- a/solution.py
+++ b/solution.py
@@ -25,7 +25,7 @@
 LANES = 128
 LABEL_ROWS = 16
 VMEM_BYTES = 32 * 2**20
-NEAR_COST = 1
+BUNDLE_COST = 1
 FIRST_COST = 200
 BACK_COST = 2
 LAST_COST = 5
@@ -157,28 +157,27 @@
     return found[0], functools.reduce(jnp.maximum, best)
 
 
-def near_kernel(own, succ_a, succ_b, prev_a, prev_b, mine, bundle):
-    rows = mine.shape[1]
-    prev, succ = whole(prev_a, prev_b, rows), whole(succ_a, succ_b, rows)
-    for at, block, first in ((0, prev, prev_a), (1, succ, succ_a)):
-        put_unit(block.unit, bundle.at[at])
+def put_bundle(rows, own, succ_a, succ_b, prev_a, prev_b, bundle):
+    for at, first, second in ((0, prev_a, prev_b), (1, succ_a, succ_b)):
+        put_unit(whole(first, second, rows).unit, bundle.at[at])
         put_labels(first, bundle.at[at])
     bundle[2] = own[...]
-    own = packed(own, rows)
-    mine[...] = best_of(own, own, prev, succ)
-
-
-def far_first_kernel(bundle, back_a, ahead_a, found):
+
+
+def far_first_kernel(own, bundle, back_a, ahead_a, found, mine):
     rows = found.shape[1]
     queries = joined(first_half(back_a, rows), first_half(ahead_a, rows))
-    found[...] = best_of(queries, queries, *(packed(bundle.at[at], rows) for at in range(3)))
-
-
-def far_back_kernel(bundle, others, back_a, ahead_a, back_b, found, *refs):
+    own = packed(own, rows)
+    near = [packed(bundle.at[at], rows) for at in range(2)]
+    found[...] = best_of(queries, queries, *near, own)
+    mine[...] = best_of(own, own, *near)
+
+
+def far_back_kernel(own, bundle, others, back_a, ahead_a, back_b, found, *refs):
     back_found, ahead_found, back_packed = refs
     rows = found.shape[1]
     half = rows // 2
-    succ, own = packed(bundle.at[1], rows), packed(bundle.at[2], rows)
+    succ, own = packed(bundle.at[1], rows), packed(own, rows)
     prev_other, succ_other = packed(others.at[0], rows), packed(others.at[1], rows)
     first, rest = first_half(back_a, rows), second_half(back_a, back_b, rows)
     first_ahead = first_half(ahead_a, rows)
@@ -191,12 +190,12 @@
     ahead_found[...] = jnp.maximum(found[:, half:], best_of(first_ahead, rest, prev_other))
 
 
-def far_last_kernel(bundle, others, back, ahead_a, ahead_b, *refs):
+def far_last_kernel(own, bundle, others, back, ahead_a, ahead_b, *refs):
     back_found, ahead_found, to_back, to_ahead = refs
     rows = to_back.shape[1]
     half = rows // 2
     back, rest = packed(back, rows), second_half(ahead_a, ahead_b, rows)
-    keys = [packed(ref, rows) for ref in (bundle.at[2], bundle.at[0], others.at[0])]
+    keys = [packed(ref, rows) for ref in (own, bundle.at[0], others.at[0])]
     sims, found = masked(rest, back, *keys)
     to_ahead[:, :half] = ahead_found[...]
     to_ahead[:, half:] = found
@@ -206,7 +205,7 @@
 
 def own_kernel(own, others, back, ahead_a, ahead_b, near, mine):
     rows = mine.shape[1]
-    keys = [packed(others.at[at], rows) for at in range(3)]
+    keys = [packed(ref, rows) for ref in (others.at[at] for at in range(3))]
     keys += [packed(back, rows), whole(ahead_a, ahead_b, rows)]
     mine[...] = jnp.maximum(near[...], best_of(packed(own, rows), *keys))
 
@@ -297,20 +296,26 @@
     back_b, ahead_b = send(prev_b, "on_next"), send(succ_b, "on_prev")
     block = chunk(rows, True)
     bundle_shape = jax.ShapeDtypeStruct((3, *block.shape), jnp.bfloat16)
-    mine, bundle = kernel_call(
-        near_kernel, [own, succ_a, succ_b, prev_a, prev_b], [line, bundle_shape], NEAR_COST
+
+    def bundle_kernel(*refs):
+        put_bundle(rows, *refs)
+
+    (bundle,) = kernel_call(
+        bundle_kernel, [own, succ_a, succ_b, prev_a, prev_b], [bundle_shape], BUNDLE_COST
     )
     others = send(bundle, "sibling")
-    (found,) = kernel_call(far_first_kernel, [bundle, back_a, ahead_a], [line], FIRST_COST)
+    found, mine = kernel_call(
+        far_first_kernel, [own, bundle, back_a, ahead_a], [line] * 2, FIRST_COST
+    )
     *found, back = kernel_call(
         far_back_kernel,
-        [bundle, others, back_a, ahead_a, back_b, found],
+        [own, bundle, others, back_a, ahead_a, back_b, found],
         [line, half_line, block],
         BACK_COST,
     )
     far = [back, ahead_a, ahead_b]
     to_back, to_ahead = kernel_call(
-        far_last_kernel, [bundle, others, *far, *found], [line] * 2, LAST_COST
+        far_last_kernel, [own, bundle, others, *far, *found], [line] * 2, LAST_COST
     )
     (mine,) = kernel_call(own_kernel, [own, others, *far, mine], [line], 5)
     best = jnp.maximum(

time: 24.6 us -> 24.6 us (level)
  transfers between devices with their start and end apart: 11 -> 11, of which waited for: 8 -> 7; matrix products, arithmetic and copies ran while one was open for 0% -> 0% of each run, Pallas kernels for 10% -> 9%
where the time goes in v20:
time: 24.6 us; the launch traced here: 24.5 us
  starting transfers between devices  12.9 us (52%)
  waiting for transfers between devices  7.39 us (30%)
  Pallas kernels  3.6 us (15%)
  other arithmetic  0.57 us (2%)
    ppermute x11, starting transfers between devices, send(): return lax.ppermute(value, GROUP, perms[name])  12.9 us
    ppermute x11, waiting for transfers between devices, send(): return lax.ppermute(value, GROUP, perms[name])  7.39 us
    pallas_call x6, Pallas kernels, kernel_call(): pl.pallas_call(kernel, out_shape=outputs, in_specs=[vmem] * len(inputs),...  2.71 us
    pallas_call x1, Pallas kernels, on_ring(): pl.pallas_call(pack_first_kernel, out_shape=chunk(half, True), in_specs=[...  0.89 us
    max x1, other arithmetic, on_ring(): jnp.maximum(mine, jnp.maximum(send(to_back, 'home_back'), send(to_ahead,...  0.57 us
  transfers between devices with their start and end apart: 11, of which 7 were waited for; matrix products, arithmetic and copies ran while one was open for 0% of the time, Pallas kernels for 9%

profile of v20, /device:TPU:0, one launch (start us, length us, event | category | flops | bytes accessed | tf_op | source)
XLA Modules:
  0.0 24.5 jit_solution(4329991052680923442)
XLA Ops:
  0.0 0.0 copy-start
  0.0 0.9 %pack_first.1.first = bf16[528,128]{1,0:T(8,128)(2,1)S(1)} custom-call(bf16[256,512]{1,0:T(8,128)(2,1)} %embeds.3, s32[1,256]{1,0:T(1,128)} %bitcast.2), custom_call_target="tpu_custom_call" | custom-call | tf_op jit(solution)/shard_map/pack_first/pallas_call | solution.py:275
  0.9 2.5 %collective-permute-start.2 = (bf16[528,128]{1,0:T(8,128)(2,1)S(1)}, bf16[528,128]{1,0:T(8,128)(2,1)S(1)}, u32[]{:S(2)}, u32[]{:S(2)}) collective-permute-start(bf16[528,128]{1,0:T(8,128)(2,1)S(1)} %pack_first.1.first), channel_id=1, source_target_pairs={{0,5},{1,4},{4,8},{5,9},{8,12},{9,13},{12,14},{13,15},{14,10},{15,... | collective-permute-start | bytes 405512 | tf_op jit(solution)/shard_map/ppermute | solution.py:264
  3.4 0.0 collective-permute-start
  3.4 0.0 copy-done
  3.4 0.1 pack_second_kernel.1
  3.6 2.1 %collective-permute-start.3 = (bf16[512,128]{1,0:T(8,128)(2,1)S(1)}, bf16[512,128]{1,0:T(8,128)(2,1)S(1)}, u32[]{:S(2)}, u32[]{:S(2)}) collective-permute-start(bf16[512,128]{1,0:T(8,128)(2,1)S(1)} %get-tuple-element.15), channel_id=1, source_target_pairs={{0,5},{1,4},{4,8},{5,9},{8,12},{9,13},{12,14},{13,15},{14,10},{15,... | collective-permute-start | bytes 393224 | tf_op jit(solution)/shard_map/ppermute | solution.py:264
  5.7 0.3 %collective-permute-start.1 = (bf16[512,128]{1,0:T(8,128)(2,1)S(1)}, bf16[512,128]{1,0:T(8,128)(2,1)S(1)}, u32[]{:S(2)}, u32[]{:S(2)}) collective-permute-start(bf16[512,128]{1,0:T(8,128)(2,1)S(1)} %get-tuple-element.15), channel_id=1, source_target_pairs={{0,3},{1,2},{4,0},{5,1},{8,4},{9,5},{12,9},{13,8},{14,13},{15,12},... | collective-permute-start | bytes 393224 | tf_op jit(solution)/shard_map/ppermute | solution.py:264
  5.9 1.5 %collective-permute-done.2.refs_3_ = bf16[528,128]{1,0:T(8,128)(2,1)S(1)} collective-permute-done((bf16[528,128]{1,0:T(8,128)(2,1)S(1)}, bf16[528,128]{1,0:T(8,128)(2,1)S(1)}, u32[]{:S(2)}, u32[]{:S(2)}) %collective-permute-start.2) | collective-permute-done | bytes 135200 | tf_op jit(solution)/shard_map/ppermute | solution.py:264
  7.4 2.5 %collective-permute-start.5 = (bf16[528,128]{1,0:T(8,128)(2,1)S(1)}, bf16[528,128]{1,0:T(8,128)(2,1)S(1)}, u32[]{:S(2)}, u32[]{:S(2)}) collective-permute-start(bf16[528,128]{1,0:T(8,128)(2,1)S(1)} %collective-permute-done.2.refs_3_), channel_id=1, source_target_pairs={{0,4},{1,5},{4,8},{5,9},{8,12},{9,13},{12,14},{13,15},{14,10},{15,... | collective-permute-start | bytes 405512 | tf_op jit(solution)/shard_map/ppermute | solution.py:264
  9.9 0.0 collective-permute-done.refs_1_
  9.9 0.0 collective-permute-start.6
  9.9 0.3 %collective-permute-done.3.refs_4_ = bf16[512,128]{1,0:T(8,128)(2,1)S(1)} collective-permute-done((bf16[512,128]{1,0:T(8,128)(2,1)S(1)}, bf16[512,128]{1,0:T(8,128)(2,1)S(1)}, u32[]{:S(2)}, u32[]{:S(2)}) %collective-permute-start.3) | collective-permute-done | bytes 131104 | tf_op jit(solution)/shard_map/ppermute | solution.py:264
  10.2 2.5 %collective-permute-start.7 = (bf16[512,128]{1,0:T(8,128)(2,1)S(1)}, bf16[512,128]{1,0:T(8,128)(2,1)S(1)}, u32[]{:S(2)}, u32[]{:S(2)}) collective-permute-start(bf16[512,128]{1,0:T(8,128)(2,1)S(1)} %collective-permute-done.3.refs_4_), channel_id=1, source_target_pairs={{0,4},{1,5},{4,8},{5,9},{8,12},{9,13},{12,14},{13,15},{14,10},{15,... | collective-permute-start | bytes 393224 | tf_op jit(solution)/shard_map/ppermute | solution.py:264
  12.7 0.0 collective-permute-done.1.refs_2_
  12.7 0.0 collective-permute-start.8
  12.7 0.2 bundle_kernel.1.bundle
  12.8 0.1 collective-permute-start.4
  12.9 0.8 %collective-permute-done.5.back_a = bf16[528,128]{1,0:T(8,128)(2,1)S(1)} collective-permute-done((bf16[528,128]{1,0:T(8,128)(2,1)S(1)}, bf16[528,128]{1,0:T(8,128)(2,1)S(1)}, u32[]{:S(2)}, u32[]{:S(2)}) %collective-permute-start.5) | collective-permute-done | bytes 135200 | tf_op jit(solution)/shard_map/ppermute | solution.py:264
  13.8 1.7 %collective-permute-done.6.ahead_a = bf16[528,128]{1,0:T(8,128)(2,1)S(1)} collective-permute-done((bf16[528,128]{1,0:T(8,128)(2,1)S(1)}, bf16[528,128]{1,0:T(8,128)(2,1)S(1)}, u32[]{:S(2)}, u32[]{:S(2)}) %collective-permute-start.6) | collective-permute-done | bytes 135200 | tf_op jit(solution)/shard_map/ppermute | solution.py:264
  15.4 0.8 %far_first_kernel.1 = (f32[1,256]{1,0:T(1,128)S(1)}, f32[1,256]{1,0:T(1,128)S(1)}) custom-call(bf16[1040,128]{1,0:T(8,128)(2,1)S(1)} %get-tuple-element.14.refs_0_.own, bf16[3,1040,128]{2,1,0:T(8,128)(2,1)S(1)} %bundle_kernel.1.bundle, bf16[528,128]{1,0:T(8,128)(2,1)S(1)} %collective-permute-done.5.back_a, bf16[528,128]{1,0:T(8,128)(2,1)S(1)} %collective-permute-done.6.ahead_a), custom_call_target="tpu_custom_call" | custom-call | flops 13421772800 | bytes 1048576 | tf_op jit(solution)/shard_map/far_first_kernel/pallas_call | solution.py:245
  16.2 0.0 collective-permute-done.7.back_b
  16.2 0.0 collective-permute-done.4.others
  16.2 0.6 %far_back_kernel.1 = (f32[1,256]{1,0:T(1,128)S(1)}, f32[1,128]{1,0:T(1,128)S(1)}, bf16[1040,128]{1,0:T(8,128)(2,1)S(1)}) custom-call(bf16[1040,128]{1,0:T(8,128)(2,1)S(1)} %get-tuple-element.14.refs_0_.own, bf16[3,1040,128]{2,1,0:T(8,128)(2,1)S(1)} %bundle_kernel.1.bundle, bf16[3,1040,128]{2,1,0:T(8,128)(2,1)S(1)} %collective-permute-done.4.others, ...), custom_call_target="tpu_custom_call" | custom-call | flops 134217728 | bytes 1048576 | tf_op jit(solution)/shard_map/far_back_kernel/pallas_call | solution.py:245
  16.8 1.3 %collective-permute-done.8.ahead_b = bf16[512,128]{1,0:T(8,128)(2,1)S(1)} collective-permute-done((bf16[512,128]{1,0:T(8,128)(2,1)S(1)}, bf16[512,128]{1,0:T(8,128)(2,1)S(1)}, u32[]{:S(2)}, u32[]{:S(2)}) %collective-permute-start.8) | collective-permute-done | bytes 131104 | tf_op jit(solution)/shard_map/ppermute | solution.py:264
  18.1 0.5 %far_last_kernel.1 = (f32[1,256]{1,0:T(1,128)S(1)}, f32[1,256]{1,0:T(1,128)S(1)}) custom-call(bf16[1040,128]{1,0:T(8,128)(2,1)S(1)} %get-tuple-element.14.refs_0_.own, bf16[3,1040,128]{2,1,0:T(8,128)(2,1)S(1)} %bundle_kernel.1.bundle, bf16[3,1040,128]{2,1,0:T(8,128)(2,1)S(1)} %collective-permute-done.4.others, bf16[1040,128]{1,0:T(8,128)(2,1)S(1)} %get-tuple-element.17.back, ...), custom_call_target="tpu_custom_call" | custom-call | flops 335544320 | bytes 1048576 | tf_op jit(solution)/shard_map/far_last_kernel/pallas_call | solution.py:245
  18.6 1.5 %collective-permute-start.9 = (f32[1,256]{1,0:T(1,128)S(1)}, f32[1,256]{1,0:T(1,128)S(1)}, u32[]{:S(2)}, u32[]{:S(2)}) collective-permute-start(f32[1,256]{1,0:T(1,128)S(1)} %get-tuple-element.21), channel_id=1, source_target_pairs={{0,6},{1,7},{4,3},{5,2},{8,1},{9,0},{12,4},{13,5},{14,8},{15,9},{1... | collective-permute-start | bytes 3080 | tf_op jit(solution)/shard_map/ppermute | solution.py:264
  20.0 1.5 %collective-permute-start.10 = (f32[1,256]{1,0:T(1,128)S(1)}, f32[1,256]{1,0:T(1,128)S(1)}, u32[]{:S(2)}, u32[]{:S(2)}) collective-permute-start(f32[1,256]{1,0:T(1,128)S(1)} %get-tuple-element.22), channel_id=1, source_target_pairs={{0,8},{1,9},{4,13},{5,12},{8,15},{9,14},{12,11},{13,10},{14,7},{15... | collective-permute-start | bytes 3080 | tf_op jit(solution)/shard_map/ppermute | solution.py:264
  21.6 0.6 %own_kernel.1 = f32[1,256]{1,0:T(1,128)S(1)} custom-call(bf16[1040,128]{1,0:T(8,128)(2,1)S(1)} %get-tuple-element.14.refs_0_.own, bf16[3,1040,128]{2,1,0:T(8,128)(2,1)S(1)} %collective-permute-done.4.others, bf16[1040,128]{1,0:T(8,128)(2,1)S(1)} %get-tuple-element.17.back, bf16[528,128]{1,0:T(8,128)(2,1)S(1)} %collective-permute-done.6.ahead_a, ...), custom_call_target="tpu_custom_call" | custom-call | flops 335544320 | bytes 1048576 | tf_op jit(solution)/shard_map/own_kernel/pallas_call | solution.py:245
  22.1 0.4 %collective-permute-done.9 = f32[1,256]{1,0:T(1,128)S(1)} collective-permute-done((f32[1,256]{1,0:T(1,128)S(1)}, f32[1,256]{1,0:T(1,128)S(1)}, u32[]{:S(2)}, u32[]{:S(2)}) %collective-permute-start.9) | collective-permute-done | bytes 1056 | tf_op jit(solution)/shard_map/ppermute | solution.py:264
  22.5 1.4 %collective-permute-done.10 = f32[1,256]{1,0:T(1,128)S(1)} collective-permute-done((f32[1,256]{1,0:T(1,128)S(1)}, f32[1,256]{1,0:T(1,128)S(1)}, u32[]{:S(2)}, u32[]{:S(2)}) %collective-permute-start.10) | collective-permute-done | bytes 1056 | tf_op jit(solution)/shard_map/ppermute | solution.py:264
  23.9 0.6 %maximum_maximum_fusion = f32[1,256]{1,0:T(1,128)} fusion(f32[1,256]{1,0:T(1,128)S(1)} %own_kernel.1, f32[1,256]{1,0:T(1,128)S(1)} %collective-permute-done.9, f32[1,256]{1,0:T(1,128)S(1)} %collective-permute-done.10), kind=kLoop, calls=%fused_computation | loop fusion | flops 512 | bytes 4096 | tf_op jit(solution)/shard_map/max | solution.py:321
Async XLA Ops:
  0.0 3.4 %copy-start = (bf16[256,512]{1,0:T(8,128)(2,1)S(1)}, bf16[256,512]{1,0:T(8,128)(2,1)}, u32[]{:S(2)}) copy-start(bf16[256,512]{1,0:T(8,128)(2,1)} %embeds.3) | copy-start | bytes 786436
  0.9 6.5 %collective-permute-start.2 = (bf16[528,128]{1,0:T(8,128)(2,1)S(1)}, bf16[528,128]{1,0:T(8,128)(2,1)S(1)}, u32[]{:S(2)}, u32[]{:S(2)}) collective-permute-start(bf16[528,128]{1,0:T(8,128)(2,1)S(1)} %pack_first.1.first), channel_id=1, source_target_pairs={{0,5},{1,4},{4,8},{5,9},{8,12},{9,13},{12,14},{13,15},{14,10},{15,... | collective-permute-start | bytes 405512 | tf_op jit(solution)/shard_map/ppermute | solution.py:264
  3.4 6.5 %collective-permute-start = (bf16[528,128]{1,0:T(8,128)(2,1)S(1)}, bf16[528,128]{1,0:T(8,128)(2,1)S(1)}, u32[]{:S(2)}, u32[]{:S(2)}) collective-permute-start(bf16[528,128]{1,0:T(8,128)(2,1)S(1)} %pack_first.1.first), channel_id=1, source_target_pairs={{0,3},{1,2},{4,0},{5,1},{8,4},{9,5},{12,9},{13,8},{14,13},{15,12},... | collective-permute-start | bytes 405512 | tf_op jit(solution)/shard_map/ppermute | solution.py:264
  3.6 6.6 %collective-permute-start.3 = (bf16[512,128]{1,0:T(8,128)(2,1)S(1)}, bf16[512,128]{1,0:T(8,128)(2,1)S(1)}, u32[]{:S(2)}, u32[]{:S(2)}) collective-permute-start(bf16[512,128]{1,0:T(8,128)(2,1)S(1)} %get-tuple-element.15), channel_id=1, source_target_pairs={{0,5},{1,4},{4,8},{5,9},{8,12},{9,13},{12,14},{13,15},{14,10},{15,... | collective-permute-start | bytes 393224 | tf_op jit(solution)/shard_map/ppermute | solution.py:264
  5.7 7.0 %collective-permute-start.1 = (bf16[512,128]{1,0:T(8,128)(2,1)S(1)}, bf16[512,128]{1,0:T(8,128)(2,1)S(1)}, u32[]{:S(2)}, u32[]{:S(2)}) collective-permute-start(bf16[512,128]{1,0:T(8,128)(2,1)S(1)} %get-tuple-element.15), channel_id=1, source_target_pairs={{0,3},{1,2},{4,0},{5,1},{8,4},{9,5},{12,9},{13,8},{14,13},{15,12},... | collective-permute-start | bytes 393224 | tf_op jit(solution)/shard_map/ppermute | solution.py:264
  7.4 6.3 %collective-permute-start.5 = (bf16[528,128]{1,0:T(8,128)(2,1)S(1)}, bf16[528,128]{1,0:T(8,128)(2,1)S(1)}, u32[]{:S(2)}, u32[]{:S(2)}) collective-permute-start(bf16[528,128]{1,0:T(8,128)(2,1)S(1)} %collective-permute-done.2.refs_3_), channel_id=1, source_target_pairs={{0,4},{1,5},{4,8},{5,9},{8,12},{9,13},{12,14},{13,15},{14,10},{15,... | collective-permute-start | bytes 405512 | tf_op jit(solution)/shard_map/ppermute | solution.py:264
  9.9 5.5 %collective-permute-start.6 = (bf16[528,128]{1,0:T(8,128)(2,1)S(1)}, bf16[528,128]{1,0:T(8,128)(2,1)S(1)}, u32[]{:S(2)}, u32[]{:S(2)}) collective-permute-start(bf16[528,128]{1,0:T(8,128)(2,1)S(1)} %collective-permute-done.refs_1_), channel_id=1, source_target_pairs={{0,2},{1,3},{4,0},{5,1},{8,4},{9,5},{12,8},{13,9},{14,12},{15,13},... | collective-permute-start | bytes 405512 | tf_op jit(solution)/shard_map/ppermute | solution.py:264
  10.2 6.0 %collective-permute-start.7 = (bf16[512,128]{1,0:T(8,128)(2,1)S(1)}, bf16[512,128]{1,0:T(8,128)(2,1)S(1)}, u32[]{:S(2)}, u32[]{:S(2)}) collective-permute-start(bf16[512,128]{1,0:T(8,128)(2,1)S(1)} %collective-permute-done.3.refs_4_), channel_id=1, source_target_pairs={{0,4},{1,5},{4,8},{5,9},{8,12},{9,13},{12,14},{13,15},{14,10},{15,... | collective-permute-start | bytes 393224 | tf_op jit(solution)/shard_map/ppermute | solution.py:264
  12.7 5.4 %collective-permute-start.8 = (bf16[512,128]{1,0:T(8,128)(2,1)S(1)}, bf16[512,128]{1,0:T(8,128)(2,1)S(1)}, u32[]{:S(2)}, u32[]{:S(2)}) collective-permute-start(bf16[512,128]{1,0:T(8,128)(2,1)S(1)} %collective-permute-done.1.refs_2_), channel_id=1, source_target_pairs={{0,2},{1,3},{4,0},{5,1},{8,4},{9,5},{12,8},{13,9},{14,12},{15,13},... | collective-permute-start | bytes 393224 | tf_op jit(solution)/shard_map/ppermute | solution.py:264
  12.8 3.4 %collective-permute-start.4 = (bf16[3,1040,128]{2,1,0:T(8,128)(2,1)S(1)}, bf16[3,1040,128]{2,1,0:T(8,128)(2,1)S(1)}, u32[]{:S(2)}, u32[]{:S(2)}) collective-permute-start(bf16[3,1040,128]{2,1,0:T(8,128)(2,1)S(1)} %bundle_kernel.1.bundle), channel_id=1, source_target_pairs={{0,1},{1,0},{4,5},{5,4},{8,9},{9,8},{12,13},{13,12},{14,15},{15,14... | collective-permute-start | bytes 2396168 | tf_op jit(solution)/shard_map/ppermute | solution.py:264
  18.6 4.0 %collective-permute-start.9 = (f32[1,256]{1,0:T(1,128)S(1)}, f32[1,256]{1,0:T(1,128)S(1)}, u32[]{:S(2)}, u32[]{:S(2)}) collective-permute-start(f32[1,256]{1,0:T(1,128)S(1)} %get-tuple-element.21), channel_id=1, source_target_pairs={{0,6},{1,7},{4,3},{5,2},{8,1},{9,0},{12,4},{13,5},{14,8},{15,9},{1... | collective-permute-start | bytes 3080 | tf_op jit(solution)/shard_map/ppermute | solution.py:264
  20.0 3.9 %collective-permute-start.10 = (f32[1,256]{1,0:T(1,128)S(1)}, f32[1,256]{1,0:T(1,128)S(1)}, u32[]{:S(2)}, u32[]{:S(2)}) collective-permute-start(f32[1,256]{1,0:T(1,128)S(1)} %get-tuple-element.22), channel_id=1, source_target_pairs={{0,8},{1,9},{4,13},{5,12},{8,15},{9,14},{12,11},{13,10},{14,7},{15... | collective-permute-start | bytes 3080 | tf_op jit(solution)/shard_map/ppermute | solution.py:264

commit v21 on v20

--- a/solution.py
+++ b/solution.py
@@ -319,7 +319,7 @@
     )
     (mine,) = kernel_call(own_kernel, [own, others, *far, mine], [line], 5)
     best = jnp.maximum(
-        mine, jnp.maximum(send(to_back, "home_back"), send(to_ahead, "home_ahead"))
+        mine, jnp.maximum(send(to_ahead, "home_ahead"), send(to_back, "home_back"))
     )
     return best.reshape(rows)
 

time: 24.6 us -> 26.1 us (1.061)
  waiting for transfers between devices: 7.39 us -> 8.93 us
    ppermute x11, waiting for transfers between devices: 7.39 us -> 8.93 us  [send(): return lax.ppermute(value, GROUP, perms[name])]
where the time goes in v21:
time: 26.1 us; the launch traced here: 25.9 us
  starting transfers between devices  12.8 us (49%)
  waiting for transfers between devices  8.93 us (34%)
  Pallas kernels  3.6 us (14%)
  other arithmetic  0.57 us (2%)
    ppermute x11, starting transfers between devices, send(): return lax.ppermute(value, GROUP, perms[name])  12.8 us
    ppermute x11, waiting for transfers between devices, send(): return lax.ppermute(value, GROUP, perms[name])  8.93 us
    pallas_call x6, Pallas kernels, kernel_call(): pl.pallas_call(kernel, out_shape=outputs, in_specs=[vmem] * len(inputs),...  2.71 us
    pallas_call x1, Pallas kernels, on_ring(): pl.pallas_call(pack_first_kernel, out_shape=chunk(half, True), in_specs=[...  0.89 us
    max x1, other arithmetic, on_ring(): jnp.maximum(mine, jnp.maximum(send(to_ahead, 'home_ahead'), send(to_back,...  0.57 us
  transfers between devices with their start and end apart: 11, of which 7 were waited for; matrix products, arithmetic and copies ran while one was open for 0% of the time, Pallas kernels for 9%

profile of v21, /device:TPU:0, one launch (start us, length us, event | category | flops | bytes accessed | tf_op | source)
XLA Modules:
  0.0 25.9 jit_solution(15452285629476721119)
XLA Ops:
  0.0 0.0 copy-start
  0.0 0.9 %pack_first.1.first = bf16[528,128]{1,0:T(8,128)(2,1)S(1)} custom-call(bf16[256,512]{1,0:T(8,128)(2,1)} %embeds.3, s32[1,256]{1,0:T(1,128)} %bitcast.2), custom_call_target="tpu_custom_call" | custom-call | tf_op jit(solution)/shard_map/pack_first/pallas_call | solution.py:275
  0.9 2.5 %collective-permute-start.2 = (bf16[528,128]{1,0:T(8,128)(2,1)S(1)}, bf16[528,128]{1,0:T(8,128)(2,1)S(1)}, u32[]{:S(2)}, u32[]{:S(2)}) collective-permute-start(bf16[528,128]{1,0:T(8,128)(2,1)S(1)} %pack_first.1.first), channel_id=1, source_target_pairs={{0,5},{1,4},{4,8},{5,9},{8,12},{9,13},{12,14},{13,15},{14,10},{15,... | collective-permute-start | bytes 405512 | tf_op jit(solution)/shard_map/ppermute | solution.py:264
  3.4 0.0 collective-permute-start
  3.4 0.0 copy-done
  3.4 0.1 pack_second_kernel.1
  3.6 2.1 %collective-permute-start.3 = (bf16[512,128]{1,0:T(8,128)(2,1)S(1)}, bf16[512,128]{1,0:T(8,128)(2,1)S(1)}, u32[]{:S(2)}, u32[]{:S(2)}) collective-permute-start(bf16[512,128]{1,0:T(8,128)(2,1)S(1)} %get-tuple-element.15), channel_id=1, source_target_pairs={{0,5},{1,4},{4,8},{5,9},{8,12},{9,13},{12,14},{13,15},{14,10},{15,... | collective-permute-start | bytes 393224 | tf_op jit(solution)/shard_map/ppermute | solution.py:264
  5.7 0.3 %collective-permute-start.1 = (bf16[512,128]{1,0:T(8,128)(2,1)S(1)}, bf16[512,128]{1,0:T(8,128)(2,1)S(1)}, u32[]{:S(2)}, u32[]{:S(2)}) collective-permute-start(bf16[512,128]{1,0:T(8,128)(2,1)S(1)} %get-tuple-element.15), channel_id=1, source_target_pairs={{0,3},{1,2},{4,0},{5,1},{8,4},{9,5},{12,9},{13,8},{14,13},{15,12},... | collective-permute-start | bytes 393224 | tf_op jit(solution)/shard_map/ppermute | solution.py:264
  5.9 1.5 %collective-permute-done.2.refs_3_ = bf16[528,128]{1,0:T(8,128)(2,1)S(1)} collective-permute-done((bf16[528,128]{1,0:T(8,128)(2,1)S(1)}, bf16[528,128]{1,0:T(8,128)(2,1)S(1)}, u32[]{:S(2)}, u32[]{:S(2)}) %collective-permute-start.2) | collective-permute-done | bytes 135200 | tf_op jit(solution)/shard_map/ppermute | solution.py:264
  7.4 2.5 %collective-permute-start.5 = (bf16[528,128]{1,0:T(8,128)(2,1)S(1)}, bf16[528,128]{1,0:T(8,128)(2,1)S(1)}, u32[]{:S(2)}, u32[]{:S(2)}) collective-permute-start(bf16[528,128]{1,0:T(8,128)(2,1)S(1)} %collective-permute-done.2.refs_3_), channel_id=1, source_target_pairs={{0,4},{1,5},{4,8},{5,9},{8,12},{9,13},{12,14},{13,15},{14,10},{15,... | collective-permute-start | bytes 405512 | tf_op jit(solution)/shard_map/ppermute | solution.py:264
  9.9 0.0 collective-permute-done.refs_1_
  9.9 0.0 collective-permute-start.6
  9.9 0.3 %collective-permute-done.3.refs_4_ = bf16[512,128]{1,0:T(8,128)(2,1)S(1)} collective-permute-done((bf16[512,128]{1,0:T(8,128)(2,1)S(1)}, bf16[512,128]{1,0:T(8,128)(2,1)S(1)}, u32[]{:S(2)}, u32[]{:S(2)}) %collective-permute-start.3) | collective-permute-done | bytes 131104 | tf_op jit(solution)/shard_map/ppermute | solution.py:264
  10.2 2.5 %collective-permute-start.7 = (bf16[512,128]{1,0:T(8,128)(2,1)S(1)}, bf16[512,128]{1,0:T(8,128)(2,1)S(1)}, u32[]{:S(2)}, u32[]{:S(2)}) collective-permute-start(bf16[512,128]{1,0:T(8,128)(2,1)S(1)} %collective-permute-done.3.refs_4_), channel_id=1, source_target_pairs={{0,4},{1,5},{4,8},{5,9},{8,12},{9,13},{12,14},{13,15},{14,10},{15,... | collective-permute-start | bytes 393224 | tf_op jit(solution)/shard_map/ppermute | solution.py:264
  12.7 0.0 collective-permute-done.1.refs_2_
  12.7 0.0 collective-permute-start.8
  12.7 0.2 bundle_kernel.1.bundle
  12.8 0.1 collective-permute-start.4
  12.9 0.8 %collective-permute-done.5.back_a = bf16[528,128]{1,0:T(8,128)(2,1)S(1)} collective-permute-done((bf16[528,128]{1,0:T(8,128)(2,1)S(1)}, bf16[528,128]{1,0:T(8,128)(2,1)S(1)}, u32[]{:S(2)}, u32[]{:S(2)}) %collective-permute-start.5) | collective-permute-done | bytes 135200 | tf_op jit(solution)/shard_map/ppermute | solution.py:264
  13.8 1.7 %collective-permute-done.6.ahead_a = bf16[528,128]{1,0:T(8,128)(2,1)S(1)} collective-permute-done((bf16[528,128]{1,0:T(8,128)(2,1)S(1)}, bf16[528,128]{1,0:T(8,128)(2,1)S(1)}, u32[]{:S(2)}, u32[]{:S(2)}) %collective-permute-start.6) | collective-permute-done | bytes 135200 | tf_op jit(solution)/shard_map/ppermute | solution.py:264
  15.4 0.8 %far_first_kernel.1 = (f32[1,256]{1,0:T(1,128)S(1)}, f32[1,256]{1,0:T(1,128)S(1)}) custom-call(bf16[1040,128]{1,0:T(8,128)(2,1)S(1)} %get-tuple-element.14.refs_0_.own, bf16[3,1040,128]{2,1,0:T(8,128)(2,1)S(1)} %bundle_kernel.1.bundle, bf16[528,128]{1,0:T(8,128)(2,1)S(1)} %collective-permute-done.5.back_a, bf16[528,128]{1,0:T(8,128)(2,1)S(1)} %collective-permute-done.6.ahead_a), custom_call_target="tpu_custom_call" | custom-call | flops 13421772800 | bytes 1048576 | tf_op jit(solution)/shard_map/far_first_kernel/pallas_call | solution.py:245
  16.2 0.0 collective-permute-done.7.back_b
  16.2 0.0 collective-permute-done.4.others
  16.2 0.6 %far_back_kernel.1 = (f32[1,256]{1,0:T(1,128)S(1)}, f32[1,128]{1,0:T(1,128)S(1)}, bf16[1040,128]{1,0:T(8,128)(2,1)S(1)}) custom-call(bf16[1040,128]{1,0:T(8,128)(2,1)S(1)} %get-tuple-element.14.refs_0_.own, bf16[3,1040,128]{2,1,0:T(8,128)(2,1)S(1)} %bundle_kernel.1.bundle, bf16[3,1040,128]{2,1,0:T(8,128)(2,1)S(1)} %collective-permute-done.4.others, ...), custom_call_target="tpu_custom_call" | custom-call | flops 134217728 | bytes 1048576 | tf_op jit(solution)/shard_map/far_back_kernel/pallas_call | solution.py:245
  16.8 1.3 %collective-permute-done.8.ahead_b = bf16[512,128]{1,0:T(8,128)(2,1)S(1)} collective-permute-done((bf16[512,128]{1,0:T(8,128)(2,1)S(1)}, bf16[512,128]{1,0:T(8,128)(2,1)S(1)}, u32[]{:S(2)}, u32[]{:S(2)}) %collective-permute-start.8) | collective-permute-done | bytes 131104 | tf_op jit(solution)/shard_map/ppermute | solution.py:264
  18.1 0.5 %far_last_kernel.1 = (f32[1,256]{1,0:T(1,128)S(1)}, f32[1,256]{1,0:T(1,128)S(1)}) custom-call(bf16[1040,128]{1,0:T(8,128)(2,1)S(1)} %get-tuple-element.14.refs_0_.own, bf16[3,1040,128]{2,1,0:T(8,128)(2,1)S(1)} %bundle_kernel.1.bundle, bf16[3,1040,128]{2,1,0:T(8,128)(2,1)S(1)} %collective-permute-done.4.others, bf16[1040,128]{1,0:T(8,128)(2,1)S(1)} %get-tuple-element.17.back, ...), custom_call_target="tpu_custom_call" | custom-call | flops 335544320 | bytes 1048576 | tf_op jit(solution)/shard_map/far_last_kernel/pallas_call | solution.py:245
  18.6 2.9 %collective-permute-start.9 = (f32[1,256]{1,0:T(1,128)S(1)}, f32[1,256]{1,0:T(1,128)S(1)}, u32[]{:S(2)}, u32[]{:S(2)}) collective-permute-start(f32[1,256]{1,0:T(1,128)S(1)} %get-tuple-element.21), channel_id=1, source_target_pairs={{0,8},{1,9},{4,13},{5,12},{8,15},{9,14},{12,11},{13,10},{14,7},{15... | collective-permute-start | bytes 3080 | tf_op jit(solution)/shard_map/ppermute | solution.py:264
  21.5 0.0 collective-permute-start.10
  21.5 0.6 %own_kernel.1 = f32[1,256]{1,0:T(1,128)S(1)} custom-call(bf16[1040,128]{1,0:T(8,128)(2,1)S(1)} %get-tuple-element.14.refs_0_.own, bf16[3,1040,128]{2,1,0:T(8,128)(2,1)S(1)} %collective-permute-done.4.others, bf16[1040,128]{1,0:T(8,128)(2,1)S(1)} %get-tuple-element.17.back, bf16[528,128]{1,0:T(8,128)(2,1)S(1)} %collective-permute-done.6.ahead_a, ...), custom_call_target="tpu_custom_call" | custom-call | flops 335544320 | bytes 1048576 | tf_op jit(solution)/shard_map/own_kernel/pallas_call | solution.py:245
  22.1 0.7 %collective-permute-done.9 = f32[1,256]{1,0:T(1,128)S(1)} collective-permute-done((f32[1,256]{1,0:T(1,128)S(1)}, f32[1,256]{1,0:T(1,128)S(1)}, u32[]{:S(2)}, u32[]{:S(2)}) %collective-permute-start.9) | collective-permute-done | bytes 1056 | tf_op jit(solution)/shard_map/ppermute | solution.py:264
  22.8 2.6 %collective-permute-done.10 = f32[1,256]{1,0:T(1,128)S(1)} collective-permute-done((f32[1,256]{1,0:T(1,128)S(1)}, f32[1,256]{1,0:T(1,128)S(1)}, u32[]{:S(2)}, u32[]{:S(2)}) %collective-permute-start.10) | collective-permute-done | bytes 1056 | tf_op jit(solution)/shard_map/ppermute | solution.py:264
  25.4 0.6 %maximum_maximum_fusion = f32[1,256]{1,0:T(1,128)} fusion(f32[1,256]{1,0:T(1,128)S(1)} %own_kernel.1, f32[1,256]{1,0:T(1,128)S(1)} %collective-permute-done.9, f32[1,256]{1,0:T(1,128)S(1)} %collective-permute-done.10), kind=kLoop, calls=%fused_computation | loop fusion | flops 512 | bytes 4096 | tf_op jit(solution)/shard_map/max | solution.py:321
Async XLA Ops:
  0.0 3.4 %copy-start = (bf16[256,512]{1,0:T(8,128)(2,1)S(1)}, bf16[256,512]{1,0:T(8,128)(2,1)}, u32[]{:S(2)}) copy-start(bf16[256,512]{1,0:T(8,128)(2,1)} %embeds.3) | copy-start | bytes 786436
  0.9 6.5 %collective-permute-start.2 = (bf16[528,128]{1,0:T(8,128)(2,1)S(1)}, bf16[528,128]{1,0:T(8,128)(2,1)S(1)}, u32[]{:S(2)}, u32[]{:S(2)}) collective-permute-start(bf16[528,128]{1,0:T(8,128)(2,1)S(1)} %pack_first.1.first), channel_id=1, source_target_pairs={{0,5},{1,4},{4,8},{5,9},{8,12},{9,13},{12,14},{13,15},{14,10},{15,... | collective-permute-start | bytes 405512 | tf_op jit(solution)/shard_map/ppermute | solution.py:264
  3.4 6.5 %collective-permute-start = (bf16[528,128]{1,0:T(8,128)(2,1)S(1)}, bf16[528,128]{1,0:T(8,128)(2,1)S(1)}, u32[]{:S(2)}, u32[]{:S(2)}) collective-permute-start(bf16[528,128]{1,0:T(8,128)(2,1)S(1)} %pack_first.1.first), channel_id=1, source_target_pairs={{0,3},{1,2},{4,0},{5,1},{8,4},{9,5},{12,9},{13,8},{14,13},{15,12},... | collective-permute-start | bytes 405512 | tf_op jit(solution)/shard_map/ppermute | solution.py:264
  3.6 6.6 %collective-permute-start.3 = (bf16[512,128]{1,0:T(8,128)(2,1)S(1)}, bf16[512,128]{1,0:T(8,128)(2,1)S(1)}, u32[]{:S(2)}, u32[]{:S(2)}) collective-permute-start(bf16[512,128]{1,0:T(8,128)(2,1)S(1)} %get-tuple-element.15), channel_id=1, source_target_pairs={{0,5},{1,4},{4,8},{5,9},{8,12},{9,13},{12,14},{13,15},{14,10},{15,... | collective-permute-start | bytes 393224 | tf_op jit(solution)/shard_map/ppermute | solution.py:264
  5.7 7.0 %collective-permute-start.1 = (bf16[512,128]{1,0:T(8,128)(2,1)S(1)}, bf16[512,128]{1,0:T(8,128)(2,1)S(1)}, u32[]{:S(2)}, u32[]{:S(2)}) collective-permute-start(bf16[512,128]{1,0:T(8,128)(2,1)S(1)} %get-tuple-element.15), channel_id=1, source_target_pairs={{0,3},{1,2},{4,0},{5,1},{8,4},{9,5},{12,9},{13,8},{14,13},{15,12},... | collective-permute-start | bytes 393224 | tf_op jit(solution)/shard_map/ppermute | solution.py:264
  7.4 6.3 %collective-permute-start.5 = (bf16[528,128]{1,0:T(8,128)(2,1)S(1)}, bf16[528,128]{1,0:T(8,128)(2,1)S(1)}, u32[]{:S(2)}, u32[]{:S(2)}) collective-permute-start(bf16[528,128]{1,0:T(8,128)(2,1)S(1)} %collective-permute-done.2.refs_3_), channel_id=1, source_target_pairs={{0,4},{1,5},{4,8},{5,9},{8,12},{9,13},{12,14},{13,15},{14,10},{15,... | collective-permute-start | bytes 405512 | tf_op jit(solution)/shard_map/ppermute | solution.py:264
  9.9 5.5 %collective-permute-start.6 = (bf16[528,128]{1,0:T(8,128)(2,1)S(1)}, bf16[528,128]{1,0:T(8,128)(2,1)S(1)}, u32[]{:S(2)}, u32[]{:S(2)}) collective-permute-start(bf16[528,128]{1,0:T(8,128)(2,1)S(1)} %collective-permute-done.refs_1_), channel_id=1, source_target_pairs={{0,2},{1,3},{4,0},{5,1},{8,4},{9,5},{12,8},{13,9},{14,12},{15,13},... | collective-permute-start | bytes 405512 | tf_op jit(solution)/shard_map/ppermute | solution.py:264
  10.2 6.0 %collective-permute-start.7 = (bf16[512,128]{1,0:T(8,128)(2,1)S(1)}, bf16[512,128]{1,0:T(8,128)(2,1)S(1)}, u32[]{:S(2)}, u32[]{:S(2)}) collective-permute-start(bf16[512,128]{1,0:T(8,128)(2,1)S(1)} %collective-permute-done.3.refs_4_), channel_id=1, source_target_pairs={{0,4},{1,5},{4,8},{5,9},{8,12},{9,13},{12,14},{13,15},{14,10},{15,... | collective-permute-start | bytes 393224 | tf_op jit(solution)/shard_map/ppermute | solution.py:264
  12.7 5.4 %collective-permute-start.8 = (bf16[512,128]{1,0:T(8,128)(2,1)S(1)}, bf16[512,128]{1,0:T(8,128)(2,1)S(1)}, u32[]{:S(2)}, u32[]{:S(2)}) collective-permute-start(bf16[512,128]{1,0:T(8,128)(2,1)S(1)} %collective-permute-done.1.refs_2_), channel_id=1, source_target_pairs={{0,2},{1,3},{4,0},{5,1},{8,4},{9,5},{12,8},{13,9},{14,12},{15,13},... | collective-permute-start | bytes 393224 | tf_op jit(solution)/shard_map/ppermute | solution.py:264
  12.8 3.4 %collective-permute-start.4 = (bf16[3,1040,128]{2,1,0:T(8,128)(2,1)S(1)}, bf16[3,1040,128]{2,1,0:T(8,128)(2,1)S(1)}, u32[]{:S(2)}, u32[]{:S(2)}) collective-permute-start(bf16[3,1040,128]{2,1,0:T(8,128)(2,1)S(1)} %bundle_kernel.1.bundle), channel_id=1, source_target_pairs={{0,1},{1,0},{4,5},{5,4},{8,9},{9,8},{12,13},{13,12},{14,15},{15,14... | collective-permute-start | bytes 2396168 | tf_op jit(solution)/shard_map/ppermute | solution.py:264
  18.6 4.2 %collective-permute-start.9 = (f32[1,256]{1,0:T(1,128)S(1)}, f32[1,256]{1,0:T(1,128)S(1)}, u32[]{:S(2)}, u32[]{:S(2)}) collective-permute-start(f32[1,256]{1,0:T(1,128)S(1)} %get-tuple-element.21), channel_id=1, source_target_pairs={{0,8},{1,9},{4,13},{5,12},{8,15},{9,14},{12,11},{13,10},{14,7},{15... | collective-permute-start | bytes 3080 | tf_op jit(solution)/shard_map/ppermute | solution.py:264
  21.5 3.9 %collective-permute-start.10 = (f32[1,256]{1,0:T(1,128)S(1)}, f32[1,256]{1,0:T(1,128)S(1)}, u32[]{:S(2)}, u32[]{:S(2)}) collective-permute-start(f32[1,256]{1,0:T(1,128)S(1)} %get-tuple-element.22), channel_id=1, source_target_pairs={{0,6},{1,7},{4,3},{5,2},{8,1},{9,0},{12,4},{13,5},{14,8},{15,9},{1... | collective-permute-start | bytes 3080 | tf_op jit(solution)/shard_map/ppermute | solution.py:264

commit v22 on v21

--- a/solution.py
+++ b/solution.py
@@ -191,16 +191,19 @@
 
 
 def far_last_kernel(own, bundle, others, back, ahead_a, ahead_b, *refs):
-    back_found, ahead_found, to_back, to_ahead = refs
-    rows = to_back.shape[1]
+    back_found, ahead_found, along, across = refs
+    rows = along.shape[1]
     half = rows // 2
     back, rest = packed(back, rows), second_half(ahead_a, ahead_b, rows)
     keys = [packed(ref, rows) for ref in (own, bundle.at[0], others.at[0])]
     sims, found = masked(rest, back, *keys)
-    to_ahead[:, :half] = ahead_found[...]
-    to_ahead[:, half:] = found
+    to_ahead = jnp.concatenate([ahead_found[...], found], axis=1)
     best = jnp.max(jnp.transpose(sims), axis=0, keepdims=True)
-    to_back[...] = jnp.maximum(back_found[...], best)
+    to_back = jnp.maximum(back_found[...], best)
+    low = lax.axis_index("gx") < lax.axis_size("gx") // 2
+    ahead_along = low == (lax.axis_index("gy") == 0)
+    along[...] = jnp.where(ahead_along, to_ahead, to_back)
+    across[...] = jnp.where(ahead_along, to_back, to_ahead)
 
 
 def own_kernel(own, others, back, ahead_a, ahead_b, near, mine):
@@ -218,16 +221,32 @@
         x, y = (place, 0) if place < size_x else (chips - 1 - place, 1)
         return (x * size_y + y) * size_z + core
 
-    def perm(to):
-        return [
-            (device(p, k), device(*to(p, k))) for p in range(chips) for k in range(size_z)
-        ]
+    def perm(to, places=range(chips)):
+        return [(device(p, k), device(*to(p, k))) for p in places for k in range(size_z)]
 
     def from_prev(place, core):
         return core ^ (place % chips in (0, 1))
 
     def from_next(place, core):
         return core ^ (place % chips not in (0, 1))
+
+    def back(place, core):
+        return place - 2, from_prev(place - 1, core)
+
+    def ahead(place, core):
+        return place + 2, from_next(place + 1, core)
+
+    def low(place):
+        return device(place, 0) // (size_y * size_z) < size_x // 2
+
+    def ahead_along(place):
+        return low(place) == (place < size_x)
+
+    def along(place, core):
+        return (ahead if ahead_along(place) else back)(place, core)
+
+    def across(place, core):
+        return (back if ahead_along(place) else ahead)(place, core)
 
     return {
         "sibling": perm(lambda p, k: (p, 1 - k)),
@@ -235,8 +254,9 @@
         "prev": perm(lambda p, k: (p - 1, from_next(p - 1, k))),
         "on_next": perm(lambda p, k: (p + 1, k)),
         "on_prev": perm(lambda p, k: (p - 1, k)),
-        "home_back": perm(lambda p, k: (p - 2, from_prev(p - 1, k))),
-        "home_ahead": perm(lambda p, k: (p + 2, from_next(p + 1, k))),
+        "home_low": perm(along, [p for p in range(chips) if not low(p)]),
+        "home_high": perm(along, [p for p in range(chips) if low(p)]),
+        "home_across": perm(across),
     }
 
 
@@ -314,13 +334,15 @@
         BACK_COST,
     )
     far = [back, ahead_a, ahead_b]
-    to_back, to_ahead = kernel_call(
+    along, across = kernel_call(
         far_last_kernel, [own, bundle, others, *far, *found], [line] * 2, LAST_COST
     )
     (mine,) = kernel_call(own_kernel, [own, others, *far, mine], [line], 5)
-    best = jnp.maximum(
-        mine, jnp.maximum(send(to_ahead, "home_ahead"), send(to_back, "home_back"))
-    )
+    found_low = send(along, "home_low")
+    found_across = send(across, "home_across")
+    along, found_low = lax.optimization_barrier((along, found_low))
+    received = found_low + send(along, "home_high")
+    best = jnp.maximum(mine, jnp.maximum(found_across, received))
     return best.reshape(rows)
 
 

time: 26.1 us -> 28.5 us (1.092)
  starting transfers between devices: 12.8 us -> 14.7 us
  waiting for transfers between devices: 8.93 us -> 9.36 us
    ppermute x11 -> x12, starting transfers between devices: 12.8 us -> 14.7 us  [send(): return lax.ppermute(value, GROUP, perms[name])]
    ppermute x11 -> x12, waiting for transfers between devices: 8.93 us -> 9.36 us  [send(): return lax.ppermute(value, GROUP, perms[name])]
  transfers between devices with their start and end apart: 11 -> 12, of which waited for: 7 -> 7; matrix products, arithmetic and copies ran while one was open for 0% -> 0% of each run, Pallas kernels for 9% -> 8%
where the time goes in v22:
time: 28.5 us; the launch traced here: 28.3 us
  starting transfers between devices  14.7 us (52%)
  waiting for transfers between devices  9.36 us (33%)
  Pallas kernels  3.61 us (13%)
  other arithmetic  0.57 us (2%)
    ppermute x12, starting transfers between devices, send(): return lax.ppermute(value, GROUP, perms[name])  14.7 us
    ppermute x12, waiting for transfers between devices, send(): return lax.ppermute(value, GROUP, perms[name])  9.36 us
    pallas_call x6, Pallas kernels, kernel_call(): pl.pallas_call(kernel, out_shape=outputs, in_specs=[vmem] * len(inputs),...  2.72 us
    pallas_call x1, Pallas kernels, on_ring(): pl.pallas_call(pack_first_kernel, out_shape=chunk(half, True), in_specs=[...  0.89 us
  transfers between devices with their start and end apart: 12, of which 7 were waited for; matrix products, arithmetic and copies ran while one was open for 0% of the time, Pallas kernels for 8%

profile of v22, /device:TPU:0, one launch (start us, length us, event | category | flops | bytes accessed | tf_op | source)
XLA Modules:
  0.0 28.3 jit_solution(723450808474857821)
XLA Ops:
  0.0 0.9 %pack_first.1.first = bf16[528,128]{1,0:T(8,128)(2,1)S(1)} custom-call(bf16[256,512]{1,0:T(8,128)(2,1)} %embeds.3, s32[1,256]{1,0:T(1,128)} %bitcast.2), custom_call_target="tpu_custom_call" | custom-call | tf_op jit(solution)/shard_map/pack_first/pallas_call | solution.py:295
  0.9 2.5 %collective-permute-start.2 = (bf16[528,128]{1,0:T(8,128)(2,1)S(1)}, bf16[528,128]{1,0:T(8,128)(2,1)S(1)}, u32[]{:S(2)}, u32[]{:S(2)}) collective-permute-start(bf16[528,128]{1,0:T(8,128)(2,1)S(1)} %pack_first.1.first), channel_id=1, source_target_pairs={{0,5},{1,4},{4,8},{5,9},{8,12},{9,13},{12,14},{13,15},{14,10},{15,... | collective-permute-start | bytes 405512 | tf_op jit(solution)/shard_map/ppermute | solution.py:284
  3.4 0.0 collective-permute-start
  3.4 0.1 pack_second_kernel.1
  3.6 2.1 %collective-permute-start.3 = (bf16[512,128]{1,0:T(8,128)(2,1)S(1)}, bf16[512,128]{1,0:T(8,128)(2,1)S(1)}, u32[]{:S(2)}, u32[]{:S(2)}) collective-permute-start(bf16[512,128]{1,0:T(8,128)(2,1)S(1)} %get-tuple-element.17), channel_id=1, source_target_pairs={{0,5},{1,4},{4,8},{5,9},{8,12},{9,13},{12,14},{13,15},{14,10},{15,... | collective-permute-start | bytes 393224 | tf_op jit(solution)/shard_map/ppermute | solution.py:284
  5.7 0.3 collective-permute-start.1
  5.9 1.5 %collective-permute-done.2.refs_3_ = bf16[528,128]{1,0:T(8,128)(2,1)S(1)} collective-permute-done((bf16[528,128]{1,0:T(8,128)(2,1)S(1)}, bf16[528,128]{1,0:T(8,128)(2,1)S(1)}, u32[]{:S(2)}, u32[]{:S(2)}) %collective-permute-start.2) | collective-permute-done | bytes 135200 | tf_op jit(solution)/shard_map/ppermute | solution.py:284
  7.4 2.5 %collective-permute-start.5 = (bf16[528,128]{1,0:T(8,128)(2,1)S(1)}, bf16[528,128]{1,0:T(8,128)(2,1)S(1)}, u32[]{:S(2)}, u32[]{:S(2)}) collective-permute-start(bf16[528,128]{1,0:T(8,128)(2,1)S(1)} %collective-permute-done.2.refs_3_), channel_id=1, source_target_pairs={{0,4},{1,5},{4,8},{5,9},{8,12},{9,13},{12,14},{13,15},{14,10},{15,... | collective-permute-start | bytes 405512 | tf_op jit(solution)/shard_map/ppermute | solution.py:284
  9.9 0.0 collective-permute-done.refs_1_
  9.9 0.0 collective-permute-start.6
  9.9 0.3 %collective-permute-done.3.refs_4_ = bf16[512,128]{1,0:T(8,128)(2,1)S(1)} collective-permute-done((bf16[512,128]{1,0:T(8,128)(2,1)S(1)}, bf16[512,128]{1,0:T(8,128)(2,1)S(1)}, u32[]{:S(2)}, u32[]{:S(2)}) %collective-permute-start.3) | collective-permute-done | bytes 131104 | tf_op jit(solution)/shard_map/ppermute | solution.py:284
  10.2 2.5 %collective-permute-start.7 = (bf16[512,128]{1,0:T(8,128)(2,1)S(1)}, bf16[512,128]{1,0:T(8,128)(2,1)S(1)}, u32[]{:S(2)}, u32[]{:S(2)}) collective-permute-start(bf16[512,128]{1,0:T(8,128)(2,1)S(1)} %collective-permute-done.3.refs_4_), channel_id=1, source_target_pairs={{0,4},{1,5},{4,8},{5,9},{8,12},{9,13},{12,14},{13,15},{14,10},{15,... | collective-permute-start | bytes 393224 | tf_op jit(solution)/shard_map/ppermute | solution.py:284
  12.7 0.0 collective-permute-done.1.refs_2_
  12.7 0.0 collective-permute-start.8
  12.7 0.2 bundle_kernel.1.bundle
  12.8 0.1 collective-permute-start.4
  12.9 0.8 %collective-permute-done.5.back_a = bf16[528,128]{1,0:T(8,128)(2,1)S(1)} collective-permute-done((bf16[528,128]{1,0:T(8,128)(2,1)S(1)}, bf16[528,128]{1,0:T(8,128)(2,1)S(1)}, u32[]{:S(2)}, u32[]{:S(2)}) %collective-permute-start.5) | collective-permute-done | bytes 135200 | tf_op jit(solution)/shard_map/ppermute | solution.py:284
  13.8 1.7 %collective-permute-done.6.ahead_a = bf16[528,128]{1,0:T(8,128)(2,1)S(1)} collective-permute-done((bf16[528,128]{1,0:T(8,128)(2,1)S(1)}, bf16[528,128]{1,0:T(8,128)(2,1)S(1)}, u32[]{:S(2)}, u32[]{:S(2)}) %collective-permute-start.6) | collective-permute-done | bytes 135200 | tf_op jit(solution)/shard_map/ppermute | solution.py:284
  15.4 0.8 %far_first_kernel.1 = (f32[1,256]{1,0:T(1,128)S(1)}, f32[1,256]{1,0:T(1,128)S(1)}) custom-call(bf16[1040,128]{1,0:T(8,128)(2,1)S(1)} %get-tuple-element.16.refs_0_.own, bf16[3,1040,128]{2,1,0:T(8,128)(2,1)S(1)} %bundle_kernel.1.bundle, bf16[528,128]{1,0:T(8,128)(2,1)S(1)} %collective-permute-done.5.back_a, bf16[528,128]{1,0:T(8,128)(2,1)S(1)} %collective-permute-done.6.ahead_a), custom_call_target="tpu_custom_call" | custom-call | flops 13421772800 | bytes 1048576 | tf_op jit(solution)/shard_map/far_first_kernel/pallas_call | solution.py:265
  16.2 0.0 collective-permute-done.7.back_b
  16.2 0.0 collective-permute-done.4.others
  16.2 0.6 %far_back_kernel.1 = (f32[1,256]{1,0:T(1,128)S(1)}, f32[1,128]{1,0:T(1,128)S(1)}, bf16[1040,128]{1,0:T(8,128)(2,1)S(1)}) custom-call(bf16[1040,128]{1,0:T(8,128)(2,1)S(1)} %get-tuple-element.16.refs_0_.own, bf16[3,1040,128]{2,1,0:T(8,128)(2,1)S(1)} %bundle_kernel.1.bundle, bf16[3,1040,128]{2,1,0:T(8,128)(2,1)S(1)} %collective-permute-done.4.others, ...), custom_call_target="tpu_custom_call" | custom-call | flops 134217728 | bytes 1048576 | tf_op jit(solution)/shard_map/far_back_kernel/pallas_call | solution.py:265
  16.8 1.3 %collective-permute-done.8.ahead_b = bf16[512,128]{1,0:T(8,128)(2,1)S(1)} collective-permute-done((bf16[512,128]{1,0:T(8,128)(2,1)S(1)}, bf16[512,128]{1,0:T(8,128)(2,1)S(1)}, u32[]{:S(2)}, u32[]{:S(2)}) %collective-permute-start.8) | collective-permute-done | bytes 131104 | tf_op jit(solution)/shard_map/ppermute | solution.py:284
  18.1 0.5 %far_last_kernel.1 = (f32[1,256]{1,0:T(1,128)S(1)}, f32[1,256]{1,0:T(1,128)S(1)}) custom-call(bf16[1040,128]{1,0:T(8,128)(2,1)S(1)} %get-tuple-element.16.refs_0_.own, bf16[3,1040,128]{2,1,0:T(8,128)(2,1)S(1)} %bundle_kernel.1.bundle, bf16[3,1040,128]{2,1,0:T(8,128)(2,1)S(1)} %collective-permute-done.4.others, bf16[1040,128]{1,0:T(8,128)(2,1)S(1)} %get-tuple-element.19.back, ...), custom_call_target="tpu_custom_call" | custom-call | flops 335544320 | bytes 1048576 | tf_op jit(solution)/shard_map/far_last_kernel/pallas_call | solution.py:265
  18.6 1.3 %collective-permute-start.10 = (f32[1,256]{1,0:T(1,128)S(1)}, f32[1,256]{1,0:T(1,128)S(1)}, u32[]{:S(2)}, u32[]{:S(2)}) collective-permute-start(f32[1,256]{1,0:T(1,128)S(1)} %get-tuple-element.26), channel_id=1, source_target_pairs={{8,1},{9,0},{12,4},{13,5},{14,7},{15,6},{10,3},{11,2},{24,17},{25,... | collective-permute-start | bytes 3080 | tf_op jit(solution)/shard_map/ppermute | solution.py:284
  19.9 1.4 %collective-permute-start.9 = (f32[1,256]{1,0:T(1,128)S(1)}, f32[1,256]{1,0:T(1,128)S(1)}, u32[]{:S(2)}, u32[]{:S(2)}) collective-permute-start(f32[1,256]{1,0:T(1,128)S(1)} %get-tuple-element.23), channel_id=1, source_target_pairs={{0,6},{1,7},{4,3},{5,2},{8,15},{9,14},{12,11},{13,10},{14,8},{15,9... | collective-permute-start | bytes 3080 | tf_op jit(solution)/shard_map/ppermute | solution.py:284
  21.3 3.0 %collective-permute-done.10 = f32[1,256]{1,0:T(1,128)S(1)} collective-permute-done((f32[1,256]{1,0:T(1,128)S(1)}, f32[1,256]{1,0:T(1,128)S(1)}, u32[]{:S(2)}, u32[]{:S(2)}) %collective-permute-start.10) | collective-permute-done | bytes 1056 | tf_op jit(solution)/shard_map/ppermute | solution.py:284
  24.4 2.1 %collective-permute-start.11 = (f32[1,256]{1,0:T(1,128)S(1)}, f32[1,256]{1,0:T(1,128)S(1)}, u32[]{:S(2)}, u32[]{:S(2)}) collective-permute-start(f32[1,256]{1,0:T(1,128)S(1)} %get-tuple-element.26), channel_id=1, source_target_pairs={{0,8},{1,9},{4,13},{5,12},{6,14},{7,15},{2,10},{3,11},{16,24},{17,... | collective-permute-start | bytes 3080 | tf_op jit(solution)/shard_map/ppermute | solution.py:284
  26.5 0.6 %own_kernel.1 = f32[1,256]{1,0:T(1,128)S(1)} custom-call(bf16[1040,128]{1,0:T(8,128)(2,1)S(1)} %get-tuple-element.16.refs_0_.own, bf16[3,1040,128]{2,1,0:T(8,128)(2,1)S(1)} %collective-permute-done.4.others, bf16[1040,128]{1,0:T(8,128)(2,1)S(1)} %get-tuple-element.19.back, bf16[528,128]{1,0:T(8,128)(2,1)S(1)} %collective-permute-done.6.ahead_a, ...), custom_call_target="tpu_custom_call" | custom-call | flops 335544320 | bytes 1048576 | tf_op jit(solution)/shard_map/own_kernel/pallas_call | solution.py:265
  27.0 0.0 collective-permute-done.9
  27.1 0.7 %collective-permute-done.11 = f32[1,256]{1,0:T(1,128)S(1)} collective-permute-done((f32[1,256]{1,0:T(1,128)S(1)}, f32[1,256]{1,0:T(1,128)S(1)}, u32[]{:S(2)}, u32[]{:S(2)}) %collective-permute-start.11) | collective-permute-done | bytes 1056 | tf_op jit(solution)/shard_map/ppermute | solution.py:284
  27.8 0.6 %maximum_maximum_fusion = f32[1,256]{1,0:T(1,128)} fusion(f32[1,256]{1,0:T(1,128)S(1)} %own_kernel.1, f32[1,256]{1,0:T(1,128)S(1)} %collective-permute-done.9, f32[1,256]{1,0:T(1,128)S(1)} %collective-permute-done.10, f32[1,256]{1,0:T(1,128)S(1)} %collective-permute-done.11), kind=kLoop, calls=%fused_computation | loop fusion | flops 768 | bytes 5120 | tf_op jit(solution)/shard_map/max | solution.py:345
  (2 shorter events, 0.0 us)
Async XLA Ops:
  0.0 3.4 %copy-start = (bf16[256,512]{1,0:T(8,128)(2,1)S(1)}, bf16[256,512]{1,0:T(8,128)(2,1)}, u32[]{:S(2)}) copy-start(bf16[256,512]{1,0:T(8,128)(2,1)} %embeds.3) | copy-start | bytes 786436
  0.9 6.5 %collective-permute-start.2 = (bf16[528,128]{1,0:T(8,128)(2,1)S(1)}, bf16[528,128]{1,0:T(8,128)(2,1)S(1)}, u32[]{:S(2)}, u32[]{:S(2)}) collective-permute-start(bf16[528,128]{1,0:T(8,128)(2,1)S(1)} %pack_first.1.first), channel_id=1, source_target_pairs={{0,5},{1,4},{4,8},{5,9},{8,12},{9,13},{12,14},{13,15},{14,10},{15,... | collective-permute-start | bytes 405512 | tf_op jit(solution)/shard_map/ppermute | solution.py:284
  3.4 6.5 %collective-permute-start = (bf16[528,128]{1,0:T(8,128)(2,1)S(1)}, bf16[528,128]{1,0:T(8,128)(2,1)S(1)}, u32[]{:S(2)}, u32[]{:S(2)}) collective-permute-start(bf16[528,128]{1,0:T(8,128)(2,1)S(1)} %pack_first.1.first), channel_id=1, source_target_pairs={{0,3},{1,2},{4,0},{5,1},{8,4},{9,5},{12,9},{13,8},{14,13},{15,12},... | collective-permute-start | bytes 405512 | tf_op jit(solution)/shard_map/ppermute | solution.py:284
  3.6 6.6 %collective-permute-start.3 = (bf16[512,128]{1,0:T(8,128)(2,1)S(1)}, bf16[512,128]{1,0:T(8,128)(2,1)S(1)}, u32[]{:S(2)}, u32[]{:S(2)}) collective-permute-start(bf16[512,128]{1,0:T(8,128)(2,1)S(1)} %get-tuple-element.17), channel_id=1, source_target_pairs={{0,5},{1,4},{4,8},{5,9},{8,12},{9,13},{12,14},{13,15},{14,10},{15,... | collective-permute-start | bytes 393224 | tf_op jit(solution)/shard_map/ppermute | solution.py:284
  5.7 7.0 %collective-permute-start.1 = (bf16[512,128]{1,0:T(8,128)(2,1)S(1)}, bf16[512,128]{1,0:T(8,128)(2,1)S(1)}, u32[]{:S(2)}, u32[]{:S(2)}) collective-permute-start(bf16[512,128]{1,0:T(8,128)(2,1)S(1)} %get-tuple-element.17), channel_id=1, source_target_pairs={{0,3},{1,2},{4,0},{5,1},{8,4},{9,5},{12,9},{13,8},{14,13},{15,12},... | collective-permute-start | bytes 393224 | tf_op jit(solution)/shard_map/ppermute | solution.py:284
  7.4 6.3 %collective-permute-start.5 = (bf16[528,128]{1,0:T(8,128)(2,1)S(1)}, bf16[528,128]{1,0:T(8,128)(2,1)S(1)}, u32[]{:S(2)}, u32[]{:S(2)}) collective-permute-start(bf16[528,128]{1,0:T(8,128)(2,1)S(1)} %collective-permute-done.2.refs_3_), channel_id=1, source_target_pairs={{0,4},{1,5},{4,8},{5,9},{8,12},{9,13},{12,14},{13,15},{14,10},{15,... | collective-permute-start | bytes 405512 | tf_op jit(solution)/shard_map/ppermute | solution.py:284
  9.9 5.5 %collective-permute-start.6 = (bf16[528,128]{1,0:T(8,128)(2,1)S(1)}, bf16[528,128]{1,0:T(8,128)(2,1)S(1)}, u32[]{:S(2)}, u32[]{:S(2)}) collective-permute-start(bf16[528,128]{1,0:T(8,128)(2,1)S(1)} %collective-permute-done.refs_1_), channel_id=1, source_target_pairs={{0,2},{1,3},{4,0},{5,1},{8,4},{9,5},{12,8},{13,9},{14,12},{15,13},... | collective-permute-start | bytes 405512 | tf_op jit(solution)/shard_map/ppermute | solution.py:284
  10.2 6.0 %collective-permute-start.7 = (bf16[512,128]{1,0:T(8,128)(2,1)S(1)}, bf16[512,128]{1,0:T(8,128)(2,1)S(1)}, u32[]{:S(2)}, u32[]{:S(2)}) collective-permute-start(bf16[512,128]{1,0:T(8,128)(2,1)S(1)} %collective-permute-done.3.refs_4_), channel_id=1, source_target_pairs={{0,4},{1,5},{4,8},{5,9},{8,12},{9,13},{12,14},{13,15},{14,10},{15,... | collective-permute-start | bytes 393224 | tf_op jit(solution)/shard_map/ppermute | solution.py:284
  12.7 5.4 %collective-permute-start.8 = (bf16[512,128]{1,0:T(8,128)(2,1)S(1)}, bf16[512,128]{1,0:T(8,128)(2,1)S(1)}, u32[]{:S(2)}, u32[]{:S(2)}) collective-permute-start(bf16[512,128]{1,0:T(8,128)(2,1)S(1)} %collective-permute-done.1.refs_2_), channel_id=1, source_target_pairs={{0,2},{1,3},{4,0},{5,1},{8,4},{9,5},{12,8},{13,9},{14,12},{15,13},... | collective-permute-start | bytes 393224 | tf_op jit(solution)/shard_map/ppermute | solution.py:284
  12.8 3.4 %collective-permute-start.4 = (bf16[3,1040,128]{2,1,0:T(8,128)(2,1)S(1)}, bf16[3,1040,128]{2,1,0:T(8,128)(2,1)S(1)}, u32[]{:S(2)}, u32[]{:S(2)}) collective-permute-start(bf16[3,1040,128]{2,1,0:T(8,128)(2,1)S(1)} %bundle_kernel.1.bundle), channel_id=1, source_target_pairs={{0,1},{1,0},{4,5},{5,4},{8,9},{9,8},{12,13},{13,12},{14,15},{15,14... | collective-permute-start | bytes 2396168 | tf_op jit(solution)/shard_map/ppermute | solution.py:284
  18.6 5.8 %collective-permute-start.10 = (f32[1,256]{1,0:T(1,128)S(1)}, f32[1,256]{1,0:T(1,128)S(1)}, u32[]{:S(2)}, u32[]{:S(2)}) collective-permute-start(f32[1,256]{1,0:T(1,128)S(1)} %get-tuple-element.26), channel_id=1, source_target_pairs={{8,1},{9,0},{12,4},{13,5},{14,7},{15,6},{10,3},{11,2},{24,17},{25,... | collective-permute-start | bytes 3080 | tf_op jit(solution)/shard_map/ppermute | solution.py:284
  19.9 7.2 %collective-permute-start.9 = (f32[1,256]{1,0:T(1,128)S(1)}, f32[1,256]{1,0:T(1,128)S(1)}, u32[]{:S(2)}, u32[]{:S(2)}) collective-permute-start(f32[1,256]{1,0:T(1,128)S(1)} %get-tuple-element.23), channel_id=1, source_target_pairs={{0,6},{1,7},{4,3},{5,2},{8,15},{9,14},{12,11},{13,10},{14,8},{15,9... | collective-permute-start | bytes 3080 | tf_op jit(solution)/shard_map/ppermute | solution.py:284
  24.4 3.4 %collective-permute-start.11 = (f32[1,256]{1,0:T(1,128)S(1)}, f32[1,256]{1,0:T(1,128)S(1)}, u32[]{:S(2)}, u32[]{:S(2)}) collective-permute-start(f32[1,256]{1,0:T(1,128)S(1)} %get-tuple-element.26), channel_id=1, source_target_pairs={{0,8},{1,9},{4,13},{5,12},{6,14},{7,15},{2,10},{3,11},{16,24},{17,... | collective-permute-start | bytes 3080 | tf_op jit(solution)/shard_map/ppermute | solution.py:284

commit v23 on v20

--- a/solution.py
+++ b/solution.py
@@ -58,12 +58,14 @@
         copy.wait()
 
 
-def pack_second_kernel(embeds, first, second, both):
+def pack_second_kernel(embeds, first, second, both, mine):
     rows, width = embeds.shape
     unit = normalised(embeds[...])
     put_unit(unit[rows // 2 :, :], second)
     put_unit(unit, both)
     put_labels(first, both)
+    own = Block(unit, labels_in(first, rows))
+    mine[...] = best_of(own, own)
 
 
 def put_labels(source, both):
@@ -164,13 +166,13 @@
     bundle[2] = own[...]
 
 
-def far_first_kernel(own, bundle, back_a, ahead_a, found, mine):
+def far_first_kernel(own, bundle, back_a, ahead_a, self_best, found, mine):
     rows = found.shape[1]
     queries = joined(first_half(back_a, rows), first_half(ahead_a, rows))
     own = packed(own, rows)
     near = [packed(bundle.at[at], rows) for at in range(2)]
     found[...] = best_of(queries, queries, *near, own)
-    mine[...] = best_of(own, own, *near)
+    mine[...] = jnp.maximum(self_best[...], best_of(own, *near))
 
 
 def far_back_kernel(own, bundle, others, back_a, ahead_a, back_b, found, *refs):
@@ -287,8 +289,8 @@
         pltpu.with_memory_space_constraint(embeds, pltpu.HBM),
         pltpu.with_memory_space_constraint(cluster.reshape(1, rows), pltpu.HBM),
     )
-    own_b, own = kernel_call(
-        pack_second_kernel, [embeds, own_a], [chunk(half, False), chunk(rows, True)], 1
+    own_b, own, mine = kernel_call(
+        pack_second_kernel, [embeds, own_a], [chunk(half, False), chunk(rows, True), line], 1
     )
     prev_a, succ_a = send(own_a, "next"), send(own_a, "prev")
     prev_b, succ_b = send(own_b, "next"), send(own_b, "prev")
@@ -305,7 +307,7 @@
     )
     others = send(bundle, "sibling")
     found, mine = kernel_call(
-        far_first_kernel, [own, bundle, back_a, ahead_a], [line] * 2, FIRST_COST
+        far_first_kernel, [own, bundle, back_a, ahead_a, mine], [line] * 2, FIRST_COST
     )
     *found, back = kernel_call(
         far_back_kernel,

time: 24.6 us -> 24.6 us (level)
  transfers between devices with their start and end apart: 11 -> 11, of which waited for: 7 -> 7; matrix products, arithmetic and copies ran while one was open for 0% -> 0% of each run, Pallas kernels for 9% -> 10%
where the time goes in v23:
time: 24.6 us; the launch traced here: 24.5 us
  starting transfers between devices  12.9 us (52%)
  waiting for transfers between devices  7.21 us (29%)
  Pallas kernels  3.77 us (15%)
  other arithmetic  0.57 us (2%)
    ppermute x11, starting transfers between devices, send(): return lax.ppermute(value, GROUP, perms[name])  12.9 us
    ppermute x11, waiting for transfers between devices, send(): return lax.ppermute(value, GROUP, perms[name])  7.21 us
    pallas_call x6, Pallas kernels, kernel_call(): pl.pallas_call(kernel, out_shape=outputs, in_specs=[vmem] * len(inputs),...  2.88 us
    pallas_call x1, Pallas kernels, on_ring(): pl.pallas_call(pack_first_kernel, out_shape=chunk(half, True), in_specs=[...  0.89 us
    max x1, other arithmetic, on_ring(): jnp.maximum(mine, jnp.maximum(send(to_back, 'home_back'), send(to_ahead,...  0.57 us
  transfers between devices with their start and end apart: 11, of which 7 were waited for; matrix products, arithmetic and copies ran while one was open for 0% of the time, Pallas kernels for 10%

profile of v23, /device:TPU:0, one launch (start us, length us, event | category | flops | bytes accessed | tf_op | source)
XLA Modules:
  0.0 24.5 jit_solution(10385650059338922457)
XLA Ops:
  0.0 0.0 copy-start
  0.0 0.9 %pack_first.1.first = bf16[528,128]{1,0:T(8,128)(2,1)S(1)} custom-call(bf16[256,512]{1,0:T(8,128)(2,1)} %embeds.3, s32[1,256]{1,0:T(1,128)} %bitcast.2), custom_call_target="tpu_custom_call" | custom-call | tf_op jit(solution)/shard_map/pack_first/pallas_call | solution.py:277
  0.9 2.5 %collective-permute-start.2 = (bf16[528,128]{1,0:T(8,128)(2,1)S(1)}, bf16[528,128]{1,0:T(8,128)(2,1)S(1)}, u32[]{:S(2)}, u32[]{:S(2)}) collective-permute-start(bf16[528,128]{1,0:T(8,128)(2,1)S(1)} %pack_first.1.first), channel_id=1, source_target_pairs={{0,5},{1,4},{4,8},{5,9},{8,12},{9,13},{12,14},{13,15},{14,10},{15,... | collective-permute-start | bytes 405512 | tf_op jit(solution)/shard_map/ppermute | solution.py:266
  3.4 0.0 collective-permute-start
  3.4 0.0 copy-done
  3.4 0.4 %pack_second_kernel.1 = (bf16[512,128]{1,0:T(8,128)(2,1)S(1)}, bf16[1040,128]{1,0:T(8,128)(2,1)S(1)}, f32[1,256]{1,0:T(1,128)S(1)}) custom-call(bf16[256,512]{1,0:T(8,128)(2,1)S(1)} %copy-done, bf16[528,128]{1,0:T(8,128)(2,1)S(1)} %pack_first.1.first), custom_call_target="tpu_custom_call" | custom-call | flops 67108864 | bytes 1048576 | tf_op jit(solution)/shard_map/pack_second_kernel/pallas_call | solution.py:247
  3.8 2.1 %collective-permute-start.3 = (bf16[512,128]{1,0:T(8,128)(2,1)S(1)}, bf16[512,128]{1,0:T(8,128)(2,1)S(1)}, u32[]{:S(2)}, u32[]{:S(2)}) collective-permute-start(bf16[512,128]{1,0:T(8,128)(2,1)S(1)} %get-tuple-element.16), channel_id=1, source_target_pairs={{0,5},{1,4},{4,8},{5,9},{8,12},{9,13},{12,14},{13,15},{14,10},{15,... | collective-permute-start | bytes 393224 | tf_op jit(solution)/shard_map/ppermute | solution.py:266
  5.9 0.3 %collective-permute-start.1 = (bf16[512,128]{1,0:T(8,128)(2,1)S(1)}, bf16[512,128]{1,0:T(8,128)(2,1)S(1)}, u32[]{:S(2)}, u32[]{:S(2)}) collective-permute-start(bf16[512,128]{1,0:T(8,128)(2,1)S(1)} %get-tuple-element.16), channel_id=1, source_target_pairs={{0,3},{1,2},{4,0},{5,1},{8,4},{9,5},{12,9},{13,8},{14,13},{15,12},... | collective-permute-start | bytes 393224 | tf_op jit(solution)/shard_map/ppermute | solution.py:266
  6.2 1.2 %collective-permute-done.2.refs_3_ = bf16[528,128]{1,0:T(8,128)(2,1)S(1)} collective-permute-done((bf16[528,128]{1,0:T(8,128)(2,1)S(1)}, bf16[528,128]{1,0:T(8,128)(2,1)S(1)}, u32[]{:S(2)}, u32[]{:S(2)}) %collective-permute-start.2) | collective-permute-done | bytes 135200 | tf_op jit(solution)/shard_map/ppermute | solution.py:266
  7.4 2.5 %collective-permute-start.5 = (bf16[528,128]{1,0:T(8,128)(2,1)S(1)}, bf16[528,128]{1,0:T(8,128)(2,1)S(1)}, u32[]{:S(2)}, u32[]{:S(2)}) collective-permute-start(bf16[528,128]{1,0:T(8,128)(2,1)S(1)} %collective-permute-done.2.refs_3_), channel_id=1, source_target_pairs={{0,4},{1,5},{4,8},{5,9},{8,12},{9,13},{12,14},{13,15},{14,10},{15,... | collective-permute-start | bytes 405512 | tf_op jit(solution)/shard_map/ppermute | solution.py:266
  9.9 0.0 collective-permute-done.refs_1_
  9.9 0.0 collective-permute-start.6
  9.9 0.3 %collective-permute-done.3.refs_4_ = bf16[512,128]{1,0:T(8,128)(2,1)S(1)} collective-permute-done((bf16[512,128]{1,0:T(8,128)(2,1)S(1)}, bf16[512,128]{1,0:T(8,128)(2,1)S(1)}, u32[]{:S(2)}, u32[]{:S(2)}) %collective-permute-start.3) | collective-permute-done | bytes 131104 | tf_op jit(solution)/shard_map/ppermute | solution.py:266
  10.2 2.5 %collective-permute-start.7 = (bf16[512,128]{1,0:T(8,128)(2,1)S(1)}, bf16[512,128]{1,0:T(8,128)(2,1)S(1)}, u32[]{:S(2)}, u32[]{:S(2)}) collective-permute-start(bf16[512,128]{1,0:T(8,128)(2,1)S(1)} %collective-permute-done.3.refs_4_), channel_id=1, source_target_pairs={{0,4},{1,5},{4,8},{5,9},{8,12},{9,13},{12,14},{13,15},{14,10},{15,... | collective-permute-start | bytes 393224 | tf_op jit(solution)/shard_map/ppermute | solution.py:266
  12.7 0.0 collective-permute-done.1.refs_2_
  12.7 0.0 collective-permute-start.8
  12.7 0.2 bundle_kernel.1.bundle
  12.8 0.1 collective-permute-start.4
  12.9 0.4 %collective-permute-done.5.back_a = bf16[528,128]{1,0:T(8,128)(2,1)S(1)} collective-permute-done((bf16[528,128]{1,0:T(8,128)(2,1)S(1)}, bf16[528,128]{1,0:T(8,128)(2,1)S(1)}, u32[]{:S(2)}, u32[]{:S(2)}) %collective-permute-start.5) | collective-permute-done | bytes 135200 | tf_op jit(solution)/shard_map/ppermute | solution.py:266
  13.3 2.1 %collective-permute-done.6.ahead_a = bf16[528,128]{1,0:T(8,128)(2,1)S(1)} collective-permute-done((bf16[528,128]{1,0:T(8,128)(2,1)S(1)}, bf16[528,128]{1,0:T(8,128)(2,1)S(1)}, u32[]{:S(2)}, u32[]{:S(2)}) %collective-permute-start.6) | collective-permute-done | bytes 135200 | tf_op jit(solution)/shard_map/ppermute | solution.py:266
  15.4 0.7 %far_first_kernel.1 = (f32[1,256]{1,0:T(1,128)S(1)}, f32[1,256]{1,0:T(1,128)S(1)}) custom-call(bf16[1040,128]{1,0:T(8,128)(2,1)S(1)} %get-tuple-element.15.refs_0_.own, bf16[3,1040,128]{2,1,0:T(8,128)(2,1)S(1)} %bundle_kernel.1.bundle, bf16[528,128]{1,0:T(8,128)(2,1)S(1)} %collective-permute-done.5.back_a, ...), custom_call_target="tpu_custom_call" | custom-call | flops 13421772800 | bytes 1048576 | tf_op jit(solution)/shard_map/far_first_kernel/pallas_call | solution.py:247
  16.1 0.0 collective-permute-done.7.back_b
  16.1 0.0 collective-permute-done.4.others
  16.1 0.6 %far_back_kernel.1 = (f32[1,256]{1,0:T(1,128)S(1)}, f32[1,128]{1,0:T(1,128)S(1)}, bf16[1040,128]{1,0:T(8,128)(2,1)S(1)}) custom-call(bf16[1040,128]{1,0:T(8,128)(2,1)S(1)} %get-tuple-element.15.refs_0_.own, bf16[3,1040,128]{2,1,0:T(8,128)(2,1)S(1)} %bundle_kernel.1.bundle, bf16[3,1040,128]{2,1,0:T(8,128)(2,1)S(1)} %collective-permute-done.4.others, ...), custom_call_target="tpu_custom_call" | custom-call | flops 134217728 | bytes 1048576 | tf_op jit(solution)/shard_map/far_back_kernel/pallas_call | solution.py:247
  16.8 1.3 %collective-permute-done.8.ahead_b = bf16[512,128]{1,0:T(8,128)(2,1)S(1)} collective-permute-done((bf16[512,128]{1,0:T(8,128)(2,1)S(1)}, bf16[512,128]{1,0:T(8,128)(2,1)S(1)}, u32[]{:S(2)}, u32[]{:S(2)}) %collective-permute-start.8) | collective-permute-done | bytes 131104 | tf_op jit(solution)/shard_map/ppermute | solution.py:266
  18.1 0.5 %far_last_kernel.1 = (f32[1,256]{1,0:T(1,128)S(1)}, f32[1,256]{1,0:T(1,128)S(1)}) custom-call(bf16[1040,128]{1,0:T(8,128)(2,1)S(1)} %get-tuple-element.15.refs_0_.own, bf16[3,1040,128]{2,1,0:T(8,128)(2,1)S(1)} %bundle_kernel.1.bundle, bf16[3,1040,128]{2,1,0:T(8,128)(2,1)S(1)} %collective-permute-done.4.others, bf16[1040,128]{1,0:T(8,128)(2,1)S(1)} %get-tuple-element.19.back, ...), custom_call_target="tpu_custom_call" | custom-call | flops 335544320 | bytes 1048576 | tf_op jit(solution)/shard_map/far_last_kernel/pallas_call | solution.py:247
  18.6 1.5 %collective-permute-start.9 = (f32[1,256]{1,0:T(1,128)S(1)}, f32[1,256]{1,0:T(1,128)S(1)}, u32[]{:S(2)}, u32[]{:S(2)}) collective-permute-start(f32[1,256]{1,0:T(1,128)S(1)} %get-tuple-element.23), channel_id=1, source_target_pairs={{0,6},{1,7},{4,3},{5,2},{8,1},{9,0},{12,4},{13,5},{14,8},{15,9},{1... | collective-permute-start | bytes 3080 | tf_op jit(solution)/shard_map/ppermute | solution.py:266
  20.0 1.5 %collective-permute-start.10 = (f32[1,256]{1,0:T(1,128)S(1)}, f32[1,256]{1,0:T(1,128)S(1)}, u32[]{:S(2)}, u32[]{:S(2)}) collective-permute-start(f32[1,256]{1,0:T(1,128)S(1)} %get-tuple-element.24), channel_id=1, source_target_pairs={{0,8},{1,9},{4,13},{5,12},{8,15},{9,14},{12,11},{13,10},{14,7},{15... | collective-permute-start | bytes 3080 | tf_op jit(solution)/shard_map/ppermute | solution.py:266
  21.6 0.6 %own_kernel.1 = f32[1,256]{1,0:T(1,128)S(1)} custom-call(bf16[1040,128]{1,0:T(8,128)(2,1)S(1)} %get-tuple-element.15.refs_0_.own, bf16[3,1040,128]{2,1,0:T(8,128)(2,1)S(1)} %collective-permute-done.4.others, bf16[1040,128]{1,0:T(8,128)(2,1)S(1)} %get-tuple-element.19.back, bf16[528,128]{1,0:T(8,128)(2,1)S(1)} %collective-permute-done.6.ahead_a, ...), custom_call_target="tpu_custom_call" | custom-call | flops 335544320 | bytes 1048576 | tf_op jit(solution)/shard_map/own_kernel/pallas_call | solution.py:247
  22.1 0.4 %collective-permute-done.9 = f32[1,256]{1,0:T(1,128)S(1)} collective-permute-done((f32[1,256]{1,0:T(1,128)S(1)}, f32[1,256]{1,0:T(1,128)S(1)}, u32[]{:S(2)}, u32[]{:S(2)}) %collective-permute-start.9) | collective-permute-done | bytes 1056 | tf_op jit(solution)/shard_map/ppermute | solution.py:266
  22.5 1.4 %collective-permute-done.10 = f32[1,256]{1,0:T(1,128)S(1)} collective-permute-done((f32[1,256]{1,0:T(1,128)S(1)}, f32[1,256]{1,0:T(1,128)S(1)}, u32[]{:S(2)}, u32[]{:S(2)}) %collective-permute-start.10) | collective-permute-done | bytes 1056 | tf_op jit(solution)/shard_map/ppermute | solution.py:266
  23.9 0.6 %maximum_maximum_fusion = f32[1,256]{1,0:T(1,128)} fusion(f32[1,256]{1,0:T(1,128)S(1)} %own_kernel.1, f32[1,256]{1,0:T(1,128)S(1)} %collective-permute-done.9, f32[1,256]{1,0:T(1,128)S(1)} %collective-permute-done.10), kind=kLoop, calls=%fused_computation | loop fusion | flops 512 | bytes 4096 | tf_op jit(solution)/shard_map/max | solution.py:323
Async XLA Ops:
  0.0 3.4 %copy-start = (bf16[256,512]{1,0:T(8,128)(2,1)S(1)}, bf16[256,512]{1,0:T(8,128)(2,1)}, u32[]{:S(2)}) copy-start(bf16[256,512]{1,0:T(8,128)(2,1)} %embeds.3) | copy-start | bytes 786436
  0.9 6.5 %collective-permute-start.2 = (bf16[528,128]{1,0:T(8,128)(2,1)S(1)}, bf16[528,128]{1,0:T(8,128)(2,1)S(1)}, u32[]{:S(2)}, u32[]{:S(2)}) collective-permute-start(bf16[528,128]{1,0:T(8,128)(2,1)S(1)} %pack_first.1.first), channel_id=1, source_target_pairs={{0,5},{1,4},{4,8},{5,9},{8,12},{9,13},{12,14},{13,15},{14,10},{15,... | collective-permute-start | bytes 405512 | tf_op jit(solution)/shard_map/ppermute | solution.py:266
  3.4 6.5 %collective-permute-start = (bf16[528,128]{1,0:T(8,128)(2,1)S(1)}, bf16[528,128]{1,0:T(8,128)(2,1)S(1)}, u32[]{:S(2)}, u32[]{:S(2)}) collective-permute-start(bf16[528,128]{1,0:T(8,128)(2,1)S(1)} %pack_first.1.first), channel_id=1, source_target_pairs={{0,3},{1,2},{4,0},{5,1},{8,4},{9,5},{12,9},{13,8},{14,13},{15,12},... | collective-permute-start | bytes 405512 | tf_op jit(solution)/shard_map/ppermute | solution.py:266
  3.8 6.4 %collective-permute-start.3 = (bf16[512,128]{1,0:T(8,128)(2,1)S(1)}, bf16[512,128]{1,0:T(8,128)(2,1)S(1)}, u32[]{:S(2)}, u32[]{:S(2)}) collective-permute-start(bf16[512,128]{1,0:T(8,128)(2,1)S(1)} %get-tuple-element.16), channel_id=1, source_target_pairs={{0,5},{1,4},{4,8},{5,9},{8,12},{9,13},{12,14},{13,15},{14,10},{15,... | collective-permute-start | bytes 393224 | tf_op jit(solution)/shard_map/ppermute | solution.py:266
  5.9 6.8 %collective-permute-start.1 = (bf16[512,128]{1,0:T(8,128)(2,1)S(1)}, bf16[512,128]{1,0:T(8,128)(2,1)S(1)}, u32[]{:S(2)}, u32[]{:S(2)}) collective-permute-start(bf16[512,128]{1,0:T(8,128)(2,1)S(1)} %get-tuple-element.16), channel_id=1, source_target_pairs={{0,3},{1,2},{4,0},{5,1},{8,4},{9,5},{12,9},{13,8},{14,13},{15,12},... | collective-permute-start | bytes 393224 | tf_op jit(solution)/shard_map/ppermute | solution.py:266
  7.4 5.9 %collective-permute-start.5 = (bf16[528,128]{1,0:T(8,128)(2,1)S(1)}, bf16[528,128]{1,0:T(8,128)(2,1)S(1)}, u32[]{:S(2)}, u32[]{:S(2)}) collective-permute-start(bf16[528,128]{1,0:T(8,128)(2,1)S(1)} %collective-permute-done.2.refs_3_), channel_id=1, source_target_pairs={{0,4},{1,5},{4,8},{5,9},{8,12},{9,13},{12,14},{13,15},{14,10},{15,... | collective-permute-start | bytes 405512 | tf_op jit(solution)/shard_map/ppermute | solution.py:266
  9.9 5.5 %collective-permute-start.6 = (bf16[528,128]{1,0:T(8,128)(2,1)S(1)}, bf16[528,128]{1,0:T(8,128)(2,1)S(1)}, u32[]{:S(2)}, u32[]{:S(2)}) collective-permute-start(bf16[528,128]{1,0:T(8,128)(2,1)S(1)} %collective-permute-done.refs_1_), channel_id=1, source_target_pairs={{0,2},{1,3},{4,0},{5,1},{8,4},{9,5},{12,8},{13,9},{14,12},{15,13},... | collective-permute-start | bytes 405512 | tf_op jit(solution)/shard_map/ppermute | solution.py:266
  10.2 5.9 %collective-permute-start.7 = (bf16[512,128]{1,0:T(8,128)(2,1)S(1)}, bf16[512,128]{1,0:T(8,128)(2,1)S(1)}, u32[]{:S(2)}, u32[]{:S(2)}) collective-permute-start(bf16[512,128]{1,0:T(8,128)(2,1)S(1)} %collective-permute-done.3.refs_4_), channel_id=1, source_target_pairs={{0,4},{1,5},{4,8},{5,9},{8,12},{9,13},{12,14},{13,15},{14,10},{15,... | collective-permute-start | bytes 393224 | tf_op jit(solution)/shard_map/ppermute | solution.py:266
  12.7 5.4 %collective-permute-start.8 = (bf16[512,128]{1,0:T(8,128)(2,1)S(1)}, bf16[512,128]{1,0:T(8,128)(2,1)S(1)}, u32[]{:S(2)}, u32[]{:S(2)}) collective-permute-start(bf16[512,128]{1,0:T(8,128)(2,1)S(1)} %collective-permute-done.1.refs_2_), channel_id=1, source_target_pairs={{0,2},{1,3},{4,0},{5,1},{8,4},{9,5},{12,8},{13,9},{14,12},{15,13},... | collective-permute-start | bytes 393224 | tf_op jit(solution)/shard_map/ppermute | solution.py:266
  12.8 3.3 %collective-permute-start.4 = (bf16[3,1040,128]{2,1,0:T(8,128)(2,1)S(1)}, bf16[3,1040,128]{2,1,0:T(8,128)(2,1)S(1)}, u32[]{:S(2)}, u32[]{:S(2)}) collective-permute-start(bf16[3,1040,128]{2,1,0:T(8,128)(2,1)S(1)} %bundle_kernel.1.bundle), channel_id=1, source_target_pairs={{0,1},{1,0},{4,5},{5,4},{8,9},{9,8},{12,13},{13,12},{14,15},{15,14... | collective-permute-start | bytes 2396168 | tf_op jit(solution)/shard_map/ppermute | solution.py:266
  18.6 4.0 %collective-permute-start.9 = (f32[1,256]{1,0:T(1,128)S(1)}, f32[1,256]{1,0:T(1,128)S(1)}, u32[]{:S(2)}, u32[]{:S(2)}) collective-permute-start(f32[1,256]{1,0:T(1,128)S(1)} %get-tuple-element.23), channel_id=1, source_target_pairs={{0,6},{1,7},{4,3},{5,2},{8,1},{9,0},{12,4},{13,5},{14,8},{15,9},{1... | collective-permute-start | bytes 3080 | tf_op jit(solution)/shard_map/ppermute | solution.py:266
  20.0 3.9 %collective-permute-start.10 = (f32[1,256]{1,0:T(1,128)S(1)}, f32[1,256]{1,0:T(1,128)S(1)}, u32[]{:S(2)}, u32[]{:S(2)}) collective-permute-start(f32[1,256]{1,0:T(1,128)S(1)} %get-tuple-element.24), channel_id=1, source_target_pairs={{0,8},{1,9},{4,13},{5,12},{8,15},{9,14},{12,11},{13,10},{14,7},{15... | collective-permute-start | bytes 3080 | tf_op jit(solution)/shard_map/ppermute | solution.py:266

commit v24 on v23

--- a/solution.py
+++ b/solution.py
@@ -226,10 +226,10 @@
         ]
 
     def from_prev(place, core):
-        return core ^ (place % chips in (0, 1))
+        return core ^ (place % chips in (0, 1, 2, 4))
 
     def from_next(place, core):
-        return core ^ (place % chips not in (0, 1))
+        return core ^ (place % chips not in (0, 1, 2, 4))
 
     return {
         "sibling": perm(lambda p, k: (p, 1 - k)),

time: 24.6 us -> 24.7 us (level)
  starting transfers between devices: 12.9 us -> 12.6 us
where the time goes in v24:
time: 24.7 us; the launch traced here: 24.5 us
  starting transfers between devices  12.6 us (51%)
  waiting for transfers between devices  7.43 us (30%)
  Pallas kernels  3.79 us (15%)
  other arithmetic  0.57 us (2%)
    ppermute x11, starting transfers between devices, send(): return lax.ppermute(value, GROUP, perms[name])  12.6 us
    ppermute x11, waiting for transfers between devices, send(): return lax.ppermute(value, GROUP, perms[name])  7.43 us
    pallas_call x6, Pallas kernels, kernel_call(): pl.pallas_call(kernel, out_shape=outputs, in_specs=[vmem] * len(inputs),...  2.89 us
    pallas_call x1, Pallas kernels, on_ring(): pl.pallas_call(pack_first_kernel, out_shape=chunk(half, True), in_specs=[...  0.89 us
    max x1, other arithmetic, on_ring(): jnp.maximum(mine, jnp.maximum(send(to_back, 'home_back'), send(to_ahead,...  0.57 us
  transfers between devices with their start and end apart: 11, of which 7 were waited for; matrix products, arithmetic and copies ran while one was open for 0% of the time, Pallas kernels for 10%

profile of v24, /device:TPU:0, one launch (start us, length us, event | category | flops | bytes accessed | tf_op | source)
XLA Modules:
  0.0 24.5 jit_solution(6970916610354977688)
XLA Ops:
  0.0 0.0 copy-start
  0.0 0.9 %pack_first.1.first = bf16[528,128]{1,0:T(8,128)(2,1)S(1)} custom-call(bf16[256,512]{1,0:T(8,128)(2,1)} %embeds.3, s32[1,256]{1,0:T(1,128)} %bitcast.2), custom_call_target="tpu_custom_call" | custom-call | tf_op jit(solution)/shard_map/pack_first/pallas_call | solution.py:277
  0.9 2.5 %collective-permute-start.2 = (bf16[528,128]{1,0:T(8,128)(2,1)S(1)}, bf16[528,128]{1,0:T(8,128)(2,1)S(1)}, u32[]{:S(2)}, u32[]{:S(2)}) collective-permute-start(bf16[528,128]{1,0:T(8,128)(2,1)S(1)} %pack_first.1.first), channel_id=1, source_target_pairs={{0,5},{1,4},{4,9},{5,8},{8,12},{9,13},{12,15},{13,14},{14,10},{15,... | collective-permute-start | bytes 405512 | tf_op jit(solution)/shard_map/ppermute | solution.py:266
  3.4 0.0 collective-permute-start
  3.4 0.0 copy-done
  3.4 0.4 %pack_second_kernel.1 = (bf16[512,128]{1,0:T(8,128)(2,1)S(1)}, bf16[1040,128]{1,0:T(8,128)(2,1)S(1)}, f32[1,256]{1,0:T(1,128)S(1)}) custom-call(bf16[256,512]{1,0:T(8,128)(2,1)S(1)} %copy-done, bf16[528,128]{1,0:T(8,128)(2,1)S(1)} %pack_first.1.first), custom_call_target="tpu_custom_call" | custom-call | flops 67108864 | bytes 1048576 | tf_op jit(solution)/shard_map/pack_second_kernel/pallas_call | solution.py:247
  3.8 2.1 %collective-permute-start.3 = (bf16[512,128]{1,0:T(8,128)(2,1)S(1)}, bf16[512,128]{1,0:T(8,128)(2,1)S(1)}, u32[]{:S(2)}, u32[]{:S(2)}) collective-permute-start(bf16[512,128]{1,0:T(8,128)(2,1)S(1)} %get-tuple-element.16), channel_id=1, source_target_pairs={{0,5},{1,4},{4,9},{5,8},{8,12},{9,13},{12,15},{13,14},{14,10},{15,... | collective-permute-start | bytes 393224 | tf_op jit(solution)/shard_map/ppermute | solution.py:266
  5.9 0.2 collective-permute-start.1
  6.1 1.3 %collective-permute-done.2.refs_3_ = bf16[528,128]{1,0:T(8,128)(2,1)S(1)} collective-permute-done((bf16[528,128]{1,0:T(8,128)(2,1)S(1)}, bf16[528,128]{1,0:T(8,128)(2,1)S(1)}, u32[]{:S(2)}, u32[]{:S(2)}) %collective-permute-start.2) | collective-permute-done | bytes 135200 | tf_op jit(solution)/shard_map/ppermute | solution.py:266
  7.4 2.5 %collective-permute-start.5 = (bf16[528,128]{1,0:T(8,128)(2,1)S(1)}, bf16[528,128]{1,0:T(8,128)(2,1)S(1)}, u32[]{:S(2)}, u32[]{:S(2)}) collective-permute-start(bf16[528,128]{1,0:T(8,128)(2,1)S(1)} %collective-permute-done.2.refs_3_), channel_id=1, source_target_pairs={{0,4},{1,5},{4,8},{5,9},{8,12},{9,13},{12,14},{13,15},{14,10},{15,... | collective-permute-start | bytes 405512 | tf_op jit(solution)/shard_map/ppermute | solution.py:266
  9.9 0.0 collective-permute-done.refs_1_
  9.9 0.0 collective-permute-start.6
  9.9 0.3 %collective-permute-done.3.refs_4_ = bf16[512,128]{1,0:T(8,128)(2,1)S(1)} collective-permute-done((bf16[512,128]{1,0:T(8,128)(2,1)S(1)}, bf16[512,128]{1,0:T(8,128)(2,1)S(1)}, u32[]{:S(2)}, u32[]{:S(2)}) %collective-permute-start.3) | collective-permute-done | bytes 131104 | tf_op jit(solution)/shard_map/ppermute | solution.py:266
  10.2 2.5 %collective-permute-start.7 = (bf16[512,128]{1,0:T(8,128)(2,1)S(1)}, bf16[512,128]{1,0:T(8,128)(2,1)S(1)}, u32[]{:S(2)}, u32[]{:S(2)}) collective-permute-start(bf16[512,128]{1,0:T(8,128)(2,1)S(1)} %collective-permute-done.3.refs_4_), channel_id=1, source_target_pairs={{0,4},{1,5},{4,8},{5,9},{8,12},{9,13},{12,14},{13,15},{14,10},{15,... | collective-permute-start | bytes 393224 | tf_op jit(solution)/shard_map/ppermute | solution.py:266
  12.7 0.0 collective-permute-done.1.refs_2_
  12.7 0.0 collective-permute-start.8
  12.7 0.2 bundle_kernel.1.bundle
  12.8 0.1 collective-permute-start.4
  12.9 0.4 %collective-permute-done.5.back_a = bf16[528,128]{1,0:T(8,128)(2,1)S(1)} collective-permute-done((bf16[528,128]{1,0:T(8,128)(2,1)S(1)}, bf16[528,128]{1,0:T(8,128)(2,1)S(1)}, u32[]{:S(2)}, u32[]{:S(2)}) %collective-permute-start.5) | collective-permute-done | bytes 135200 | tf_op jit(solution)/shard_map/ppermute | solution.py:266
  13.3 2.1 %collective-permute-done.6.ahead_a = bf16[528,128]{1,0:T(8,128)(2,1)S(1)} collective-permute-done((bf16[528,128]{1,0:T(8,128)(2,1)S(1)}, bf16[528,128]{1,0:T(8,128)(2,1)S(1)}, u32[]{:S(2)}, u32[]{:S(2)}) %collective-permute-start.6) | collective-permute-done | bytes 135200 | tf_op jit(solution)/shard_map/ppermute | solution.py:266
  15.4 0.7 %far_first_kernel.1 = (f32[1,256]{1,0:T(1,128)S(1)}, f32[1,256]{1,0:T(1,128)S(1)}) custom-call(bf16[1040,128]{1,0:T(8,128)(2,1)S(1)} %get-tuple-element.15.refs_0_.own, bf16[3,1040,128]{2,1,0:T(8,128)(2,1)S(1)} %bundle_kernel.1.bundle, bf16[528,128]{1,0:T(8,128)(2,1)S(1)} %collective-permute-done.5.back_a, ...), custom_call_target="tpu_custom_call" | custom-call | flops 13421772800 | bytes 1048576 | tf_op jit(solution)/shard_map/far_first_kernel/pallas_call | solution.py:247
  16.1 0.0 collective-permute-done.7.back_b
  16.1 0.0 collective-permute-done.4.others
  16.1 0.6 %far_back_kernel.1 = (f32[1,256]{1,0:T(1,128)S(1)}, f32[1,128]{1,0:T(1,128)S(1)}, bf16[1040,128]{1,0:T(8,128)(2,1)S(1)}) custom-call(bf16[1040,128]{1,0:T(8,128)(2,1)S(1)} %get-tuple-element.15.refs_0_.own, bf16[3,1040,128]{2,1,0:T(8,128)(2,1)S(1)} %bundle_kernel.1.bundle, bf16[3,1040,128]{2,1,0:T(8,128)(2,1)S(1)} %collective-permute-done.4.others, ...), custom_call_target="tpu_custom_call" | custom-call | flops 134217728 | bytes 1048576 | tf_op jit(solution)/shard_map/far_back_kernel/pallas_call | solution.py:247
  16.8 1.3 %collective-permute-done.8.ahead_b = bf16[512,128]{1,0:T(8,128)(2,1)S(1)} collective-permute-done((bf16[512,128]{1,0:T(8,128)(2,1)S(1)}, bf16[512,128]{1,0:T(8,128)(2,1)S(1)}, u32[]{:S(2)}, u32[]{:S(2)}) %collective-permute-start.8) | collective-permute-done | bytes 131104 | tf_op jit(solution)/shard_map/ppermute | solution.py:266
  18.1 0.5 %far_last_kernel.1 = (f32[1,256]{1,0:T(1,128)S(1)}, f32[1,256]{1,0:T(1,128)S(1)}) custom-call(bf16[1040,128]{1,0:T(8,128)(2,1)S(1)} %get-tuple-element.15.refs_0_.own, bf16[3,1040,128]{2,1,0:T(8,128)(2,1)S(1)} %bundle_kernel.1.bundle, bf16[3,1040,128]{2,1,0:T(8,128)(2,1)S(1)} %collective-permute-done.4.others, bf16[1040,128]{1,0:T(8,128)(2,1)S(1)} %get-tuple-element.19.back, ...), custom_call_target="tpu_custom_call" | custom-call | flops 335544320 | bytes 1048576 | tf_op jit(solution)/shard_map/far_last_kernel/pallas_call | solution.py:247
  18.6 1.4 %collective-permute-start.9 = (f32[1,256]{1,0:T(1,128)S(1)}, f32[1,256]{1,0:T(1,128)S(1)}, u32[]{:S(2)}, u32[]{:S(2)}) collective-permute-start(f32[1,256]{1,0:T(1,128)S(1)} %get-tuple-element.23), channel_id=1, source_target_pairs={{0,6},{1,7},{4,3},{5,2},{8,1},{9,0},{12,5},{13,4},{14,8},{15,9},{1... | collective-permute-start | bytes 3080 | tf_op jit(solution)/shard_map/ppermute | solution.py:266
  20.0 1.3 %collective-permute-start.10 = (f32[1,256]{1,0:T(1,128)S(1)}, f32[1,256]{1,0:T(1,128)S(1)}, u32[]{:S(2)}, u32[]{:S(2)}) collective-permute-start(f32[1,256]{1,0:T(1,128)S(1)} %get-tuple-element.24), channel_id=1, source_target_pairs={{0,8},{1,9},{4,12},{5,13},{8,15},{9,14},{12,10},{13,11},{14,7},{15... | collective-permute-start | bytes 3080 | tf_op jit(solution)/shard_map/ppermute | solution.py:266
  21.3 0.6 %own_kernel.1 = f32[1,256]{1,0:T(1,128)S(1)} custom-call(bf16[1040,128]{1,0:T(8,128)(2,1)S(1)} %get-tuple-element.15.refs_0_.own, bf16[3,1040,128]{2,1,0:T(8,128)(2,1)S(1)} %collective-permute-done.4.others, bf16[1040,128]{1,0:T(8,128)(2,1)S(1)} %get-tuple-element.19.back, bf16[528,128]{1,0:T(8,128)(2,1)S(1)} %collective-permute-done.6.ahead_a, ...), custom_call_target="tpu_custom_call" | custom-call | flops 335544320 | bytes 1048576 | tf_op jit(solution)/shard_map/own_kernel/pallas_call | solution.py:247
  21.9 0.6 %collective-permute-done.9 = f32[1,256]{1,0:T(1,128)S(1)} collective-permute-done((f32[1,256]{1,0:T(1,128)S(1)}, f32[1,256]{1,0:T(1,128)S(1)}, u32[]{:S(2)}, u32[]{:S(2)}) %collective-permute-start.9) | collective-permute-done | bytes 1056 | tf_op jit(solution)/shard_map/ppermute | solution.py:266
  22.5 1.4 %collective-permute-done.10 = f32[1,256]{1,0:T(1,128)S(1)} collective-permute-done((f32[1,256]{1,0:T(1,128)S(1)}, f32[1,256]{1,0:T(1,128)S(1)}, u32[]{:S(2)}, u32[]{:S(2)}) %collective-permute-start.10) | collective-permute-done | bytes 1056 | tf_op jit(solution)/shard_map/ppermute | solution.py:266
  23.9 0.6 %maximum_maximum_fusion = f32[1,256]{1,0:T(1,128)} fusion(f32[1,256]{1,0:T(1,128)S(1)} %own_kernel.1, f32[1,256]{1,0:T(1,128)S(1)} %collective-permute-done.9, f32[1,256]{1,0:T(1,128)S(1)} %collective-permute-done.10), kind=kLoop, calls=%fused_computation | loop fusion | flops 512 | bytes 4096 | tf_op jit(solution)/shard_map/max | solution.py:323
Async XLA Ops:
  0.0 3.4 %copy-start = (bf16[256,512]{1,0:T(8,128)(2,1)S(1)}, bf16[256,512]{1,0:T(8,128)(2,1)}, u32[]{:S(2)}) copy-start(bf16[256,512]{1,0:T(8,128)(2,1)} %embeds.3) | copy-start | bytes 786436
  0.9 6.5 %collective-permute-start.2 = (bf16[528,128]{1,0:T(8,128)(2,1)S(1)}, bf16[528,128]{1,0:T(8,128)(2,1)S(1)}, u32[]{:S(2)}, u32[]{:S(2)}) collective-permute-start(bf16[528,128]{1,0:T(8,128)(2,1)S(1)} %pack_first.1.first), channel_id=1, source_target_pairs={{0,5},{1,4},{4,9},{5,8},{8,12},{9,13},{12,15},{13,14},{14,10},{15,... | collective-permute-start | bytes 405512 | tf_op jit(solution)/shard_map/ppermute | solution.py:266
  3.4 6.5 %collective-permute-start = (bf16[528,128]{1,0:T(8,128)(2,1)S(1)}, bf16[528,128]{1,0:T(8,128)(2,1)S(1)}, u32[]{:S(2)}, u32[]{:S(2)}) collective-permute-start(bf16[528,128]{1,0:T(8,128)(2,1)S(1)} %pack_first.1.first), channel_id=1, source_target_pairs={{0,3},{1,2},{4,0},{5,1},{8,4},{9,5},{12,8},{13,9},{14,13},{15,12},... | collective-permute-start | bytes 405512 | tf_op jit(solution)/shard_map/ppermute | solution.py:266
  3.8 6.4 %collective-permute-start.3 = (bf16[512,128]{1,0:T(8,128)(2,1)S(1)}, bf16[512,128]{1,0:T(8,128)(2,1)S(1)}, u32[]{:S(2)}, u32[]{:S(2)}) collective-permute-start(bf16[512,128]{1,0:T(8,128)(2,1)S(1)} %get-tuple-element.16), channel_id=1, source_target_pairs={{0,5},{1,4},{4,9},{5,8},{8,12},{9,13},{12,15},{13,14},{14,10},{15,... | collective-permute-start | bytes 393224 | tf_op jit(solution)/shard_map/ppermute | solution.py:266
  5.9 6.8 %collective-permute-start.1 = (bf16[512,128]{1,0:T(8,128)(2,1)S(1)}, bf16[512,128]{1,0:T(8,128)(2,1)S(1)}, u32[]{:S(2)}, u32[]{:S(2)}) collective-permute-start(bf16[512,128]{1,0:T(8,128)(2,1)S(1)} %get-tuple-element.16), channel_id=1, source_target_pairs={{0,3},{1,2},{4,0},{5,1},{8,4},{9,5},{12,8},{13,9},{14,13},{15,12},... | collective-permute-start | bytes 393224 | tf_op jit(solution)/shard_map/ppermute | solution.py:266
  7.4 5.9 %collective-permute-start.5 = (bf16[528,128]{1,0:T(8,128)(2,1)S(1)}, bf16[528,128]{1,0:T(8,128)(2,1)S(1)}, u32[]{:S(2)}, u32[]{:S(2)}) collective-permute-start(bf16[528,128]{1,0:T(8,128)(2,1)S(1)} %collective-permute-done.2.refs_3_), channel_id=1, source_target_pairs={{0,4},{1,5},{4,8},{5,9},{8,12},{9,13},{12,14},{13,15},{14,10},{15,... | collective-permute-start | bytes 405512 | tf_op jit(solution)/shard_map/ppermute | solution.py:266
  9.9 5.5 %collective-permute-start.6 = (bf16[528,128]{1,0:T(8,128)(2,1)S(1)}, bf16[528,128]{1,0:T(8,128)(2,1)S(1)}, u32[]{:S(2)}, u32[]{:S(2)}) collective-permute-start(bf16[528,128]{1,0:T(8,128)(2,1)S(1)} %collective-permute-done.refs_1_), channel_id=1, source_target_pairs={{0,2},{1,3},{4,0},{5,1},{8,4},{9,5},{12,8},{13,9},{14,12},{15,13},... | collective-permute-start | bytes 405512 | tf_op jit(solution)/shard_map/ppermute | solution.py:266
  10.2 5.9 %collective-permute-start.7 = (bf16[512,128]{1,0:T(8,128)(2,1)S(1)}, bf16[512,128]{1,0:T(8,128)(2,1)S(1)}, u32[]{:S(2)}, u32[]{:S(2)}) collective-permute-start(bf16[512,128]{1,0:T(8,128)(2,1)S(1)} %collective-permute-done.3.refs_4_), channel_id=1, source_target_pairs={{0,4},{1,5},{4,8},{5,9},{8,12},{9,13},{12,14},{13,15},{14,10},{15,... | collective-permute-start | bytes 393224 | tf_op jit(solution)/shard_map/ppermute | solution.py:266
  12.7 5.4 %collective-permute-start.8 = (bf16[512,128]{1,0:T(8,128)(2,1)S(1)}, bf16[512,128]{1,0:T(8,128)(2,1)S(1)}, u32[]{:S(2)}, u32[]{:S(2)}) collective-permute-start(bf16[512,128]{1,0:T(8,128)(2,1)S(1)} %collective-permute-done.1.refs_2_), channel_id=1, source_target_pairs={{0,2},{1,3},{4,0},{5,1},{8,4},{9,5},{12,8},{13,9},{14,12},{15,13},... | collective-permute-start | bytes 393224 | tf_op jit(solution)/shard_map/ppermute | solution.py:266
  12.8 3.3 %collective-permute-start.4 = (bf16[3,1040,128]{2,1,0:T(8,128)(2,1)S(1)}, bf16[3,1040,128]{2,1,0:T(8,128)(2,1)S(1)}, u32[]{:S(2)}, u32[]{:S(2)}) collective-permute-start(bf16[3,1040,128]{2,1,0:T(8,128)(2,1)S(1)} %bundle_kernel.1.bundle), channel_id=1, source_target_pairs={{0,1},{1,0},{4,5},{5,4},{8,9},{9,8},{12,13},{13,12},{14,15},{15,14... | collective-permute-start | bytes 2396168 | tf_op jit(solution)/shard_map/ppermute | solution.py:266
  18.6 4.0 %collective-permute-start.9 = (f32[1,256]{1,0:T(1,128)S(1)}, f32[1,256]{1,0:T(1,128)S(1)}, u32[]{:S(2)}, u32[]{:S(2)}) collective-permute-start(f32[1,256]{1,0:T(1,128)S(1)} %get-tuple-element.23), channel_id=1, source_target_pairs={{0,6},{1,7},{4,3},{5,2},{8,1},{9,0},{12,5},{13,4},{14,8},{15,9},{1... | collective-permute-start | bytes 3080 | tf_op jit(solution)/shard_map/ppermute | solution.py:266
  20.0 3.9 %collective-permute-start.10 = (f32[1,256]{1,0:T(1,128)S(1)}, f32[1,256]{1,0:T(1,128)S(1)}, u32[]{:S(2)}, u32[]{:S(2)}) collective-permute-start(f32[1,256]{1,0:T(1,128)S(1)} %get-tuple-element.24), channel_id=1, source_target_pairs={{0,8},{1,9},{4,12},{5,13},{8,15},{9,14},{12,10},{13,11},{14,7},{15... | collective-permute-start | bytes 3080 | tf_op jit(solution)/shard_map/ppermute | solution.py:266

commit v25 on v23

--- a/solution.py
+++ b/solution.py
@@ -73,11 +73,11 @@
 
 
 class Block:
-    def __init__(self, unit, label):
+    def __init__(self, unit, label, column=None):
         self.unit = unit
         self.label = label
         self.rows = unit.shape[0]
-        self.along_rows = None
+        self.along_rows = column
 
     def column(self):
         if self.along_rows is None:
@@ -94,8 +94,9 @@
     return jnp.concatenate([lines[i : i + 1] for i in range(rows // LANES)], axis=1)
 
 
-def packed(both, rows):
-    return Block(unit_in(both, rows, both.shape[0] - LABEL_ROWS), labels_in(both, rows))
+def packed(both, rows, column=None):
+    unit = unit_in(both, rows, both.shape[0] - LABEL_ROWS)
+    return Block(unit, labels_in(both, rows), None if column is None else column[...])
 
 
 def first_half(first, rows):
@@ -166,17 +167,18 @@
     bundle[2] = own[...]
 
 
-def far_first_kernel(own, bundle, back_a, ahead_a, self_best, found, mine):
+def far_first_kernel(own, bundle, back_a, ahead_a, self_best, found, mine, columns):
     rows = found.shape[1]
     queries = joined(first_half(back_a, rows), first_half(ahead_a, rows))
     own = packed(own, rows)
     near = [packed(bundle.at[at], rows) for at in range(2)]
     found[...] = best_of(queries, queries, *near, own)
     mine[...] = jnp.maximum(self_best[...], best_of(own, *near))
+    columns[0], columns[1] = near[0].column(), own.column()
 
 
 def far_back_kernel(own, bundle, others, back_a, ahead_a, back_b, found, *refs):
-    back_found, ahead_found, back_packed = refs
+    back_found, ahead_found, back_packed, columns = refs
     rows = found.shape[1]
     half = rows // 2
     succ, own = packed(bundle.at[1], rows), packed(own, rows)
@@ -186,6 +188,8 @@
     back = joined(first, rest)
     put_unit(back.unit, back_packed)
     put_labels(back_a, back_packed)
+    columns[0, :half, :], columns[0, half:, :] = first.column(), rest.column()
+    columns[1] = prev_other.column()
     both = best_of(back, succ_other)
     back_found[:, :half] = jnp.maximum(found[:, :half], both[:, :half])
     back_found[:, half:] = jnp.maximum(best_of(rest, own, succ, first_ahead), both[:, half:])
@@ -193,11 +197,16 @@
 
 
 def far_last_kernel(own, bundle, others, back, ahead_a, ahead_b, *refs):
-    back_found, ahead_found, to_back, to_ahead = refs
+    back_found, ahead_found, near_columns, far_columns, to_back, to_ahead = refs
     rows = to_back.shape[1]
     half = rows // 2
-    back, rest = packed(back, rows), second_half(ahead_a, ahead_b, rows)
-    keys = [packed(ref, rows) for ref in (own, bundle.at[0], others.at[0])]
+    rest = second_half(ahead_a, ahead_b, rows)
+    back = packed(back, rows, far_columns.at[0])
+    keys = [
+        packed(own, rows, near_columns.at[1]),
+        packed(bundle.at[0], rows, near_columns.at[0]),
+        packed(others.at[0], rows, far_columns.at[1]),
+    ]
     sims, found = masked(rest, back, *keys)
     to_ahead[:, :half] = ahead_found[...]
     to_ahead[:, half:] = found
@@ -306,18 +315,22 @@
         bundle_kernel, [own, succ_a, succ_b, prev_a, prev_b], [bundle_shape], BUNDLE_COST
     )
     others = send(bundle, "sibling")
-    found, mine = kernel_call(
-        far_first_kernel, [own, bundle, back_a, ahead_a, mine], [line] * 2, FIRST_COST
-    )
-    *found, back = kernel_call(
+    columns = jax.ShapeDtypeStruct((2, rows, LANES), jnp.float32)
+    found, mine, near_columns = kernel_call(
+        far_first_kernel, [own, bundle, back_a, ahead_a, mine], [line, line, columns], FIRST_COST
+    )
+    *found, back, far_columns = kernel_call(
         far_back_kernel,
         [own, bundle, others, back_a, ahead_a, back_b, found],
-        [line, half_line, block],
+        [line, half_line, block, columns],
         BACK_COST,
     )
     far = [back, ahead_a, ahead_b]
     to_back, to_ahead = kernel_call(
-        far_last_kernel, [own, bundle, others, *far, *found], [line] * 2, LAST_COST
+        far_last_kernel,
+        [own, bundle, others, *far, *found, near_columns, far_columns],
+        [line] * 2,
+        LAST_COST,
     )
     (mine,) = kernel_call(own_kernel, [own, others, *far, mine], [line], 5)
     best = jnp.maximum(

time: 24.6 us -> 24.6 us (level)
  no operation moved by 1% of the time
where the time goes in v25:
time: 24.6 us; the launch traced here: 24.5 us
  starting transfers between devices  12.8 us (52%)
  waiting for transfers between devices  7.21 us (29%)
  Pallas kernels  3.77 us (15%)
  other arithmetic  0.57 us (2%)
    ppermute x11, starting transfers between devices, send(): return lax.ppermute(value, GROUP, perms[name])  12.8 us
    ppermute x11, waiting for transfers between devices, send(): return lax.ppermute(value, GROUP, perms[name])  7.21 us
    pallas_call x6, Pallas kernels, kernel_call(): pl.pallas_call(kernel, out_shape=outputs, in_specs=[vmem] * len(inputs),...  2.88 us
    pallas_call x1, Pallas kernels, on_ring(): pl.pallas_call(pack_first_kernel, out_shape=chunk(half, True), in_specs=[...  0.89 us
    max x1, other arithmetic, on_ring(): jnp.maximum(mine, jnp.maximum(send(to_back, 'home_back'), send(to_ahead,...  0.57 us
  transfers between devices with their start and end apart: 11, of which 7 were waited for; matrix products, arithmetic and copies ran while one was open for 0% of the time, Pallas kernels for 10%

profile of v25, /device:TPU:0, one launch (start us, length us, event | category | flops | bytes accessed | tf_op | source)
XLA Modules:
  0.0 24.5 jit_solution(6474441195001902333)
XLA Ops:
  0.0 0.0 copy-start
  0.0 0.9 %pack_first.1.first = bf16[528,128]{1,0:T(8,128)(2,1)S(1)} custom-call(bf16[256,512]{1,0:T(8,128)(2,1)} %embeds.3, s32[1,256]{1,0:T(1,128)} %bitcast.2), custom_call_target="tpu_custom_call" | custom-call | tf_op jit(solution)/shard_map/pack_first/pallas_call | solution.py:286
  0.9 2.5 %collective-permute-start.2 = (bf16[528,128]{1,0:T(8,128)(2,1)S(1)}, bf16[528,128]{1,0:T(8,128)(2,1)S(1)}, u32[]{:S(2)}, u32[]{:S(2)}) collective-permute-start(bf16[528,128]{1,0:T(8,128)(2,1)S(1)} %pack_first.1.first), channel_id=1, source_target_pairs={{0,5},{1,4},{4,8},{5,9},{8,12},{9,13},{12,14},{13,15},{14,10},{15,... | collective-permute-start | bytes 405512 | tf_op jit(solution)/shard_map/ppermute | solution.py:275
  3.4 0.0 collective-permute-start
  3.4 0.0 copy-done
  3.4 0.4 %pack_second_kernel.1 = (bf16[512,128]{1,0:T(8,128)(2,1)S(1)}, bf16[1040,128]{1,0:T(8,128)(2,1)S(1)}, f32[1,256]{1,0:T(1,128)S(1)}) custom-call(bf16[256,512]{1,0:T(8,128)(2,1)S(1)} %copy-done, bf16[528,128]{1,0:T(8,128)(2,1)S(1)} %pack_first.1.first), custom_call_target="tpu_custom_call" | custom-call | flops 67108864 | bytes 1048576 | tf_op jit(solution)/shard_map/pack_second_kernel/pallas_call | solution.py:256
  3.8 2.1 %collective-permute-start.3 = (bf16[512,128]{1,0:T(8,128)(2,1)S(1)}, bf16[512,128]{1,0:T(8,128)(2,1)S(1)}, u32[]{:S(2)}, u32[]{:S(2)}) collective-permute-start(bf16[512,128]{1,0:T(8,128)(2,1)S(1)} %get-tuple-element.18), channel_id=1, source_target_pairs={{0,5},{1,4},{4,8},{5,9},{8,12},{9,13},{12,14},{13,15},{14,10},{15,... | collective-permute-start | bytes 393224 | tf_op jit(solution)/shard_map/ppermute | solution.py:275
  5.9 0.3 %collective-permute-start.1 = (bf16[512,128]{1,0:T(8,128)(2,1)S(1)}, bf16[512,128]{1,0:T(8,128)(2,1)S(1)}, u32[]{:S(2)}, u32[]{:S(2)}) collective-permute-start(bf16[512,128]{1,0:T(8,128)(2,1)S(1)} %get-tuple-element.18), channel_id=1, source_target_pairs={{0,3},{1,2},{4,0},{5,1},{8,4},{9,5},{12,9},{13,8},{14,13},{15,12},... | collective-permute-start | bytes 393224 | tf_op jit(solution)/shard_map/ppermute | solution.py:275
  6.2 1.2 %collective-permute-done.2.refs_3_ = bf16[528,128]{1,0:T(8,128)(2,1)S(1)} collective-permute-done((bf16[528,128]{1,0:T(8,128)(2,1)S(1)}, bf16[528,128]{1,0:T(8,128)(2,1)S(1)}, u32[]{:S(2)}, u32[]{:S(2)}) %collective-permute-start.2) | collective-permute-done | bytes 135200 | tf_op jit(solution)/shard_map/ppermute | solution.py:275
  7.4 2.5 %collective-permute-start.5 = (bf16[528,128]{1,0:T(8,128)(2,1)S(1)}, bf16[528,128]{1,0:T(8,128)(2,1)S(1)}, u32[]{:S(2)}, u32[]{:S(2)}) collective-permute-start(bf16[528,128]{1,0:T(8,128)(2,1)S(1)} %collective-permute-done.2.refs_3_), channel_id=1, source_target_pairs={{0,4},{1,5},{4,8},{5,9},{8,12},{9,13},{12,14},{13,15},{14,10},{15,... | collective-permute-start | bytes 405512 | tf_op jit(solution)/shard_map/ppermute | solution.py:275
  9.9 0.0 collective-permute-done.refs_1_
  9.9 0.0 collective-permute-start.6
  9.9 0.3 %collective-permute-done.3.refs_4_ = bf16[512,128]{1,0:T(8,128)(2,1)S(1)} collective-permute-done((bf16[512,128]{1,0:T(8,128)(2,1)S(1)}, bf16[512,128]{1,0:T(8,128)(2,1)S(1)}, u32[]{:S(2)}, u32[]{:S(2)}) %collective-permute-start.3) | collective-permute-done | bytes 131104 | tf_op jit(solution)/shard_map/ppermute | solution.py:275
  10.2 2.5 %collective-permute-start.7 = (bf16[512,128]{1,0:T(8,128)(2,1)S(1)}, bf16[512,128]{1,0:T(8,128)(2,1)S(1)}, u32[]{:S(2)}, u32[]{:S(2)}) collective-permute-start(bf16[512,128]{1,0:T(8,128)(2,1)S(1)} %collective-permute-done.3.refs_4_), channel_id=1, source_target_pairs={{0,4},{1,5},{4,8},{5,9},{8,12},{9,13},{12,14},{13,15},{14,10},{15,... | collective-permute-start | bytes 393224 | tf_op jit(solution)/shard_map/ppermute | solution.py:275
  12.7 0.0 collective-permute-done.1.refs_2_
  12.7 0.0 collective-permute-start.8
  12.7 0.2 bundle_kernel.1.bundle
  12.8 0.1 collective-permute-start.4
  12.9 0.4 %collective-permute-done.5.back_a = bf16[528,128]{1,0:T(8,128)(2,1)S(1)} collective-permute-done((bf16[528,128]{1,0:T(8,128)(2,1)S(1)}, bf16[528,128]{1,0:T(8,128)(2,1)S(1)}, u32[]{:S(2)}, u32[]{:S(2)}) %collective-permute-start.5) | collective-permute-done | bytes 135200 | tf_op jit(solution)/shard_map/ppermute | solution.py:275
  13.3 2.1 %collective-permute-done.6.ahead_a = bf16[528,128]{1,0:T(8,128)(2,1)S(1)} collective-permute-done((bf16[528,128]{1,0:T(8,128)(2,1)S(1)}, bf16[528,128]{1,0:T(8,128)(2,1)S(1)}, u32[]{:S(2)}, u32[]{:S(2)}) %collective-permute-start.6) | collective-permute-done | bytes 135200 | tf_op jit(solution)/shard_map/ppermute | solution.py:275
  15.4 0.7 %far_first_kernel.1 = (f32[1,256]{1,0:T(1,128)S(1)}, f32[1,256]{1,0:T(1,128)S(1)}, f32[2,256,128]{2,1,0:T(8,128)S(1)}) custom-call(bf16[1040,128]{1,0:T(8,128)(2,1)S(1)} %get-tuple-element.17.refs_0_.own, bf16[3,1040,128]{2,1,0:T(8,128)(2,1)S(1)} %bundle_kernel.1.bundle, bf16[528,128]{1,0:T(8,128)(2,1)S(1)} %collective-permute-done.5.back_a, ...), custom_call_target="tpu_custom_call" | custom-call | flops 13421772800 | bytes 1048576 | tf_op jit(solution)/shard_map/far_first_kernel/pallas_call | solution.py:256
  16.1 0.0 collective-permute-done.7.back_b
  16.1 0.0 collective-permute-done.4.others
  16.2 0.6 %far_back_kernel.1 = (f32[1,256]{1,0:T(1,128)S(1)}, f32[1,128]{1,0:T(1,128)S(1)}, bf16[1040,128]{1,0:T(8,128)(2,1)S(1)}, f32[2,256,128]{2,1,0:T(8,128)S(1)}) custom-call(bf16[1040,128]{1,0:T(8,128)(2,1)S(1)} %get-tuple-element.17.refs_0_.own, bf16[3,1040,128]{2,1,0:T(8,128)(2,1)S(1)} %bundle_kernel.1.bundle, ...), custom_call_target="tpu_custom_call" | custom-call | flops 134217728 | bytes 1048576 | tf_op jit(solution)/shard_map/far_back_kernel/pallas_call | solution.py:256
  16.8 1.3 %collective-permute-done.8.ahead_b = bf16[512,128]{1,0:T(8,128)(2,1)S(1)} collective-permute-done((bf16[512,128]{1,0:T(8,128)(2,1)S(1)}, bf16[512,128]{1,0:T(8,128)(2,1)S(1)}, u32[]{:S(2)}, u32[]{:S(2)}) %collective-permute-start.8) | collective-permute-done | bytes 131104 | tf_op jit(solution)/shard_map/ppermute | solution.py:275
  18.1 0.4 %far_last_kernel.1 = (f32[1,256]{1,0:T(1,128)S(1)}, f32[1,256]{1,0:T(1,128)S(1)}) custom-call(bf16[1040,128]{1,0:T(8,128)(2,1)S(1)} %get-tuple-element.17.refs_0_.own, bf16[3,1040,128]{2,1,0:T(8,128)(2,1)S(1)} %bundle_kernel.1.bundle, bf16[3,1040,128]{2,1,0:T(8,128)(2,1)S(1)} %collective-permute-done.4.others, bf16[1040,128]{1,0:T(8,128)(2,1)S(1)} %get-tuple-element.21.back, ...), custom_call_target="tpu_custom_call" | custom-call | flops 335544320 | bytes 1048576 | tf_op jit(solution)/shard_map/far_last_kernel/pallas_call | solution.py:256
  18.6 1.5 %collective-permute-start.9 = (f32[1,256]{1,0:T(1,128)S(1)}, f32[1,256]{1,0:T(1,128)S(1)}, u32[]{:S(2)}, u32[]{:S(2)}) collective-permute-start(f32[1,256]{1,0:T(1,128)S(1)} %get-tuple-element.27), channel_id=1, source_target_pairs={{0,6},{1,7},{4,3},{5,2},{8,1},{9,0},{12,4},{13,5},{14,8},{15,9},{1... | collective-permute-start | bytes 3080 | tf_op jit(solution)/shard_map/ppermute | solution.py:275
  20.0 1.5 %collective-permute-start.10 = (f32[1,256]{1,0:T(1,128)S(1)}, f32[1,256]{1,0:T(1,128)S(1)}, u32[]{:S(2)}, u32[]{:S(2)}) collective-permute-start(f32[1,256]{1,0:T(1,128)S(1)} %get-tuple-element.28), channel_id=1, source_target_pairs={{0,8},{1,9},{4,13},{5,12},{8,15},{9,14},{12,11},{13,10},{14,7},{15... | collective-permute-start | bytes 3080 | tf_op jit(solution)/shard_map/ppermute | solution.py:275
  21.5 0.6 %own_kernel.1 = f32[1,256]{1,0:T(1,128)S(1)} custom-call(bf16[1040,128]{1,0:T(8,128)(2,1)S(1)} %get-tuple-element.17.refs_0_.own, bf16[3,1040,128]{2,1,0:T(8,128)(2,1)S(1)} %collective-permute-done.4.others, bf16[1040,128]{1,0:T(8,128)(2,1)S(1)} %get-tuple-element.21.back, bf16[528,128]{1,0:T(8,128)(2,1)S(1)} %collective-permute-done.6.ahead_a, ...), custom_call_target="tpu_custom_call" | custom-call | flops 335544320 | bytes 1048576 | tf_op jit(solution)/shard_map/own_kernel/pallas_call | solution.py:256
  22.1 0.4 %collective-permute-done.9 = f32[1,256]{1,0:T(1,128)S(1)} collective-permute-done((f32[1,256]{1,0:T(1,128)S(1)}, f32[1,256]{1,0:T(1,128)S(1)}, u32[]{:S(2)}, u32[]{:S(2)}) %collective-permute-start.9) | collective-permute-done | bytes 1056 | tf_op jit(solution)/shard_map/ppermute | solution.py:275
  22.5 1.4 %collective-permute-done.10 = f32[1,256]{1,0:T(1,128)S(1)} collective-permute-done((f32[1,256]{1,0:T(1,128)S(1)}, f32[1,256]{1,0:T(1,128)S(1)}, u32[]{:S(2)}, u32[]{:S(2)}) %collective-permute-start.10) | collective-permute-done | bytes 1056 | tf_op jit(solution)/shard_map/ppermute | solution.py:275
  23.9 0.6 %maximum_maximum_fusion = f32[1,256]{1,0:T(1,128)} fusion(f32[1,256]{1,0:T(1,128)S(1)} %own_kernel.1, f32[1,256]{1,0:T(1,128)S(1)} %collective-permute-done.9, f32[1,256]{1,0:T(1,128)S(1)} %collective-permute-done.10), kind=kLoop, calls=%fused_computation | loop fusion | flops 512 | bytes 4096 | tf_op jit(solution)/shard_map/max | solution.py:336
Async XLA Ops:
  0.0 3.4 %copy-start = (bf16[256,512]{1,0:T(8,128)(2,1)S(1)}, bf16[256,512]{1,0:T(8,128)(2,1)}, u32[]{:S(2)}) copy-start(bf16[256,512]{1,0:T(8,128)(2,1)} %embeds.3) | copy-start | bytes 786436
  0.9 6.5 %collective-permute-start.2 = (bf16[528,128]{1,0:T(8,128)(2,1)S(1)}, bf16[528,128]{1,0:T(8,128)(2,1)S(1)}, u32[]{:S(2)}, u32[]{:S(2)}) collective-permute-start(bf16[528,128]{1,0:T(8,128)(2,1)S(1)} %pack_first.1.first), channel_id=1, source_target_pairs={{0,5},{1,4},{4,8},{5,9},{8,12},{9,13},{12,14},{13,15},{14,10},{15,... | collective-permute-start | bytes 405512 | tf_op jit(solution)/shard_map/ppermute | solution.py:275
  3.4 6.5 %collective-permute-start = (bf16[528,128]{1,0:T(8,128)(2,1)S(1)}, bf16[528,128]{1,0:T(8,128)(2,1)S(1)}, u32[]{:S(2)}, u32[]{:S(2)}) collective-permute-start(bf16[528,128]{1,0:T(8,128)(2,1)S(1)} %pack_first.1.first), channel_id=1, source_target_pairs={{0,3},{1,2},{4,0},{5,1},{8,4},{9,5},{12,9},{13,8},{14,13},{15,12},... | collective-permute-start | bytes 405512 | tf_op jit(solution)/shard_map/ppermute | solution.py:275
  3.8 6.4 %collective-permute-start.3 = (bf16[512,128]{1,0:T(8,128)(2,1)S(1)}, bf16[512,128]{1,0:T(8,128)(2,1)S(1)}, u32[]{:S(2)}, u32[]{:S(2)}) collective-permute-start(bf16[512,128]{1,0:T(8,128)(2,1)S(1)} %get-tuple-element.18), channel_id=1, source_target_pairs={{0,5},{1,4},{4,8},{5,9},{8,12},{9,13},{12,14},{13,15},{14,10},{15,... | collective-permute-start | bytes 393224 | tf_op jit(solution)/shard_map/ppermute | solution.py:275
  5.9 6.8 %collective-permute-start.1 = (bf16[512,128]{1,0:T(8,128)(2,1)S(1)}, bf16[512,128]{1,0:T(8,128)(2,1)S(1)}, u32[]{:S(2)}, u32[]{:S(2)}) collective-permute-start(bf16[512,128]{1,0:T(8,128)(2,1)S(1)} %get-tuple-element.18), channel_id=1, source_target_pairs={{0,3},{1,2},{4,0},{5,1},{8,4},{9,5},{12,9},{13,8},{14,13},{15,12},... | collective-permute-start | bytes 393224 | tf_op jit(solution)/shard_map/ppermute | solution.py:275
  7.4 5.9 %collective-permute-start.5 = (bf16[528,128]{1,0:T(8,128)(2,1)S(1)}, bf16[528,128]{1,0:T(8,128)(2,1)S(1)}, u32[]{:S(2)}, u32[]{:S(2)}) collective-permute-start(bf16[528,128]{1,0:T(8,128)(2,1)S(1)} %collective-permute-done.2.refs_3_), channel_id=1, source_target_pairs={{0,4},{1,5},{4,8},{5,9},{8,12},{9,13},{12,14},{13,15},{14,10},{15,... | collective-permute-start | bytes 405512 | tf_op jit(solution)/shard_map/ppermute | solution.py:275
  9.9 5.5 %collective-permute-start.6 = (bf16[528,128]{1,0:T(8,128)(2,1)S(1)}, bf16[528,128]{1,0:T(8,128)(2,1)S(1)}, u32[]{:S(2)}, u32[]{:S(2)}) collective-permute-start(bf16[528,128]{1,0:T(8,128)(2,1)S(1)} %collective-permute-done.refs_1_), channel_id=1, source_target_pairs={{0,2},{1,3},{4,0},{5,1},{8,4},{9,5},{12,8},{13,9},{14,12},{15,13},... | collective-permute-start | bytes 405512 | tf_op jit(solution)/shard_map/ppermute | solution.py:275
  10.2 5.9 %collective-permute-start.7 = (bf16[512,128]{1,0:T(8,128)(2,1)S(1)}, bf16[512,128]{1,0:T(8,128)(2,1)S(1)}, u32[]{:S(2)}, u32[]{:S(2)}) collective-permute-start(bf16[512,128]{1,0:T(8,128)(2,1)S(1)} %collective-permute-done.3.refs_4_), channel_id=1, source_target_pairs={{0,4},{1,5},{4,8},{5,9},{8,12},{9,13},{12,14},{13,15},{14,10},{15,... | collective-permute-start | bytes 393224 | tf_op jit(solution)/shard_map/ppermute | solution.py:275
  12.7 5.4 %collective-permute-start.8 = (bf16[512,128]{1,0:T(8,128)(2,1)S(1)}, bf16[512,128]{1,0:T(8,128)(2,1)S(1)}, u32[]{:S(2)}, u32[]{:S(2)}) collective-permute-start(bf16[512,128]{1,0:T(8,128)(2,1)S(1)} %collective-permute-done.1.refs_2_), channel_id=1, source_target_pairs={{0,2},{1,3},{4,0},{5,1},{8,4},{9,5},{12,8},{13,9},{14,12},{15,13},... | collective-permute-start | bytes 393224 | tf_op jit(solution)/shard_map/ppermute | solution.py:275
  12.8 3.3 %collective-permute-start.4 = (bf16[3,1040,128]{2,1,0:T(8,128)(2,1)S(1)}, bf16[3,1040,128]{2,1,0:T(8,128)(2,1)S(1)}, u32[]{:S(2)}, u32[]{:S(2)}) collective-permute-start(bf16[3,1040,128]{2,1,0:T(8,128)(2,1)S(1)} %bundle_kernel.1.bundle), channel_id=1, source_target_pairs={{0,1},{1,0},{4,5},{5,4},{8,9},{9,8},{12,13},{13,12},{14,15},{15,14... | collective-permute-start | bytes 2396168 | tf_op jit(solution)/shard_map/ppermute | solution.py:275
  18.6 4.0 %collective-permute-start.9 = (f32[1,256]{1,0:T(1,128)S(1)}, f32[1,256]{1,0:T(1,128)S(1)}, u32[]{:S(2)}, u32[]{:S(2)}) collective-permute-start(f32[1,256]{1,0:T(1,128)S(1)} %get-tuple-element.27), channel_id=1, source_target_pairs={{0,6},{1,7},{4,3},{5,2},{8,1},{9,0},{12,4},{13,5},{14,8},{15,9},{1... | collective-permute-start | bytes 3080 | tf_op jit(solution)/shard_map/ppermute | solution.py:275
  20.0 3.9 %collective-permute-start.10 = (f32[1,256]{1,0:T(1,128)S(1)}, f32[1,256]{1,0:T(1,128)S(1)}, u32[]{:S(2)}, u32[]{:S(2)}) collective-permute-start(f32[1,256]{1,0:T(1,128)S(1)} %get-tuple-element.28), channel_id=1, source_target_pairs={{0,8},{1,9},{4,13},{5,12},{8,15},{9,14},{12,11},{13,10},{14,7},{15... | collective-permute-start | bytes 3080 | tf_op jit(solution)/shard_map/ppermute | solution.py:275

commit v26 on v23

--- a/solution.py
+++ b/solution.py
@@ -217,7 +217,7 @@
 
     def device(place, core):
         place = place % chips
-        x, y = (place, 0) if place < size_x else (chips - 1 - place, 1)
+        x, y = (place, 1) if place < size_x else (chips - 1 - place, 0)
         return (x * size_y + y) * size_z + core
 
     def perm(to):

time: 24.6 us -> 24.7 us (level)
  waiting for transfers between devices: 7.21 us -> 8.24 us
  starting transfers between devices: 12.9 us -> 11.9 us
    ppermute x11, waiting for transfers between devices: 7.21 us -> 8.24 us  [send(): return lax.ppermute(value, GROUP, perms[name])]
    ppermute x11, starting transfers between devices: 12.9 us -> 11.9 us  [send(): return lax.ppermute(value, GROUP, perms[name])]
where the time goes in v26:
time: 24.7 us; the launch traced here: 24.6 us
  starting transfers between devices  11.9 us (48%)
  waiting for transfers between devices  8.24 us (33%)
  Pallas kernels  3.79 us (15%)
  other arithmetic  0.57 us (2%)
    ppermute x11, starting transfers between devices, send(): return lax.ppermute(value, GROUP, perms[name])  11.9 us
    ppermute x11, waiting for transfers between devices, send(): return lax.ppermute(value, GROUP, perms[name])  8.24 us
    pallas_call x6, Pallas kernels, kernel_call(): pl.pallas_call(kernel, out_shape=outputs, in_specs=[vmem] * len(inputs),...  2.89 us
    pallas_call x1, Pallas kernels, on_ring(): pl.pallas_call(pack_first_kernel, out_shape=chunk(half, True), in_specs=[...  0.89 us
    max x1, other arithmetic, on_ring(): jnp.maximum(mine, jnp.maximum(send(to_back, 'home_back'), send(to_ahead,...  0.57 us
  transfers between devices with their start and end apart: 11, of which 7 were waited for; matrix products, arithmetic and copies ran while one was open for 0% of the time, Pallas kernels for 10%

profile of v26, /device:TPU:0, one launch (start us, length us, event | category | flops | bytes accessed | tf_op | source)
XLA Modules:
  0.0 24.6 jit_solution(6545136704411684391)
XLA Ops:
  0.0 0.0 copy-start
  0.0 0.9 %pack_first.1.first = bf16[528,128]{1,0:T(8,128)(2,1)S(1)} custom-call(bf16[256,512]{1,0:T(8,128)(2,1)} %embeds.3, s32[1,256]{1,0:T(1,128)} %bitcast.2), custom_call_target="tpu_custom_call" | custom-call | tf_op jit(solution)/shard_map/pack_first/pallas_call | solution.py:277
  0.9 2.4 %collective-permute-start.2 = (bf16[528,128]{1,0:T(8,128)(2,1)S(1)}, bf16[528,128]{1,0:T(8,128)(2,1)S(1)}, u32[]{:S(2)}, u32[]{:S(2)}) collective-permute-start(bf16[528,128]{1,0:T(8,128)(2,1)S(1)} %pack_first.1.first), channel_id=1, source_target_pairs={{2,7},{3,6},{6,10},{7,11},{10,14},{11,15},{14,12},{15,13},{12,8},{... | collective-permute-start | bytes 405512 | tf_op jit(solution)/shard_map/ppermute | solution.py:266
  3.3 0.2 collective-permute-start
  3.5 0.0 copy-done
  3.5 0.4 %pack_second_kernel.1 = (bf16[512,128]{1,0:T(8,128)(2,1)S(1)}, bf16[1040,128]{1,0:T(8,128)(2,1)S(1)}, f32[1,256]{1,0:T(1,128)S(1)}) custom-call(bf16[256,512]{1,0:T(8,128)(2,1)S(1)} %copy-done, bf16[528,128]{1,0:T(8,128)(2,1)S(1)} %pack_first.1.first), custom_call_target="tpu_custom_call" | custom-call | flops 67108864 | bytes 1048576 | tf_op jit(solution)/shard_map/pack_second_kernel/pallas_call | solution.py:247
  3.9 1.8 %collective-permute-start.3 = (bf16[512,128]{1,0:T(8,128)(2,1)S(1)}, bf16[512,128]{1,0:T(8,128)(2,1)S(1)}, u32[]{:S(2)}, u32[]{:S(2)}) collective-permute-start(bf16[512,128]{1,0:T(8,128)(2,1)S(1)} %get-tuple-element.16), channel_id=1, source_target_pairs={{2,7},{3,6},{6,10},{7,11},{10,14},{11,15},{14,12},{15,13},{12,8},{... | collective-permute-start | bytes 393224 | tf_op jit(solution)/shard_map/ppermute | solution.py:266
  5.6 0.6 %collective-permute-start.1 = (bf16[512,128]{1,0:T(8,128)(2,1)S(1)}, bf16[512,128]{1,0:T(8,128)(2,1)S(1)}, u32[]{:S(2)}, u32[]{:S(2)}) collective-permute-start(bf16[512,128]{1,0:T(8,128)(2,1)S(1)} %get-tuple-element.16), channel_id=1, source_target_pairs={{2,1},{3,0},{6,2},{7,3},{10,6},{11,7},{14,11},{15,10},{12,15},{13,... | collective-permute-start | bytes 393224 | tf_op jit(solution)/shard_map/ppermute | solution.py:266
  6.2 1.4 %collective-permute-done.2.refs_3_ = bf16[528,128]{1,0:T(8,128)(2,1)S(1)} collective-permute-done((bf16[528,128]{1,0:T(8,128)(2,1)S(1)}, bf16[528,128]{1,0:T(8,128)(2,1)S(1)}, u32[]{:S(2)}, u32[]{:S(2)}) %collective-permute-start.2) | collective-permute-done | bytes 135200 | tf_op jit(solution)/shard_map/ppermute | solution.py:266
  7.7 2.1 %collective-permute-start.5 = (bf16[528,128]{1,0:T(8,128)(2,1)S(1)}, bf16[528,128]{1,0:T(8,128)(2,1)S(1)}, u32[]{:S(2)}, u32[]{:S(2)}) collective-permute-start(bf16[528,128]{1,0:T(8,128)(2,1)S(1)} %collective-permute-done.2.refs_3_), channel_id=1, source_target_pairs={{2,6},{3,7},{6,10},{7,11},{10,14},{11,15},{14,12},{15,13},{12,8},{... | collective-permute-start | bytes 405512 | tf_op jit(solution)/shard_map/ppermute | solution.py:266
  9.8 0.0 collective-permute-done.refs_1_
  9.8 0.2 collective-permute-start.6
  9.9 0.5 %collective-permute-done.3.refs_4_ = bf16[512,128]{1,0:T(8,128)(2,1)S(1)} collective-permute-done((bf16[512,128]{1,0:T(8,128)(2,1)S(1)}, bf16[512,128]{1,0:T(8,128)(2,1)S(1)}, u32[]{:S(2)}, u32[]{:S(2)}) %collective-permute-start.3) | collective-permute-done | bytes 131104 | tf_op jit(solution)/shard_map/ppermute | solution.py:266
  10.5 2.1 %collective-permute-start.7 = (bf16[512,128]{1,0:T(8,128)(2,1)S(1)}, bf16[512,128]{1,0:T(8,128)(2,1)S(1)}, u32[]{:S(2)}, u32[]{:S(2)}) collective-permute-start(bf16[512,128]{1,0:T(8,128)(2,1)S(1)} %collective-permute-done.3.refs_4_), channel_id=1, source_target_pairs={{2,6},{3,7},{6,10},{7,11},{10,14},{11,15},{14,12},{15,13},{12,8},{... | collective-permute-start | bytes 393224 | tf_op jit(solution)/shard_map/ppermute | solution.py:266
  12.6 0.0 collective-permute-done.1.refs_2_
  12.6 0.2 collective-permute-start.8
  12.7 0.2 bundle_kernel.1.bundle
  12.9 0.1 collective-permute-start.4
  13.0 0.5 %collective-permute-done.5.back_a = bf16[528,128]{1,0:T(8,128)(2,1)S(1)} collective-permute-done((bf16[528,128]{1,0:T(8,128)(2,1)S(1)}, bf16[528,128]{1,0:T(8,128)(2,1)S(1)}, u32[]{:S(2)}, u32[]{:S(2)}) %collective-permute-start.5) | collective-permute-done | bytes 135200 | tf_op jit(solution)/shard_map/ppermute | solution.py:266
  13.5 2.7 %collective-permute-done.6.ahead_a = bf16[528,128]{1,0:T(8,128)(2,1)S(1)} collective-permute-done((bf16[528,128]{1,0:T(8,128)(2,1)S(1)}, bf16[528,128]{1,0:T(8,128)(2,1)S(1)}, u32[]{:S(2)}, u32[]{:S(2)}) %collective-permute-start.6) | collective-permute-done | bytes 135200 | tf_op jit(solution)/shard_map/ppermute | solution.py:266
  16.2 0.7 %far_first_kernel.1 = (f32[1,256]{1,0:T(1,128)S(1)}, f32[1,256]{1,0:T(1,128)S(1)}) custom-call(bf16[1040,128]{1,0:T(8,128)(2,1)S(1)} %get-tuple-element.15.refs_0_.own, bf16[3,1040,128]{2,1,0:T(8,128)(2,1)S(1)} %bundle_kernel.1.bundle, bf16[528,128]{1,0:T(8,128)(2,1)S(1)} %collective-permute-done.5.back_a, ...), custom_call_target="tpu_custom_call" | custom-call | flops 13421772800 | bytes 1048576 | tf_op jit(solution)/shard_map/far_first_kernel/pallas_call | solution.py:247
  16.9 0.0 collective-permute-done.7.back_b
  16.9 0.0 collective-permute-done.4.others
  16.9 0.6 %far_back_kernel.1 = (f32[1,256]{1,0:T(1,128)S(1)}, f32[1,128]{1,0:T(1,128)S(1)}, bf16[1040,128]{1,0:T(8,128)(2,1)S(1)}) custom-call(bf16[1040,128]{1,0:T(8,128)(2,1)S(1)} %get-tuple-element.15.refs_0_.own, bf16[3,1040,128]{2,1,0:T(8,128)(2,1)S(1)} %bundle_kernel.1.bundle, bf16[3,1040,128]{2,1,0:T(8,128)(2,1)S(1)} %collective-permute-done.4.others, ...), custom_call_target="tpu_custom_call" | custom-call | flops 134217728 | bytes 1048576 | tf_op jit(solution)/shard_map/far_back_kernel/pallas_call | solution.py:247
  17.6 0.9 %collective-permute-done.8.ahead_b = bf16[512,128]{1,0:T(8,128)(2,1)S(1)} collective-permute-done((bf16[512,128]{1,0:T(8,128)(2,1)S(1)}, bf16[512,128]{1,0:T(8,128)(2,1)S(1)}, u32[]{:S(2)}, u32[]{:S(2)}) %collective-permute-start.8) | collective-permute-done | bytes 131104 | tf_op jit(solution)/shard_map/ppermute | solution.py:266
  18.5 0.5 %far_last_kernel.1 = (f32[1,256]{1,0:T(1,128)S(1)}, f32[1,256]{1,0:T(1,128)S(1)}) custom-call(bf16[1040,128]{1,0:T(8,128)(2,1)S(1)} %get-tuple-element.15.refs_0_.own, bf16[3,1040,128]{2,1,0:T(8,128)(2,1)S(1)} %bundle_kernel.1.bundle, bf16[3,1040,128]{2,1,0:T(8,128)(2,1)S(1)} %collective-permute-done.4.others, bf16[1040,128]{1,0:T(8,128)(2,1)S(1)} %get-tuple-element.19.back, ...), custom_call_target="tpu_custom_call" | custom-call | flops 335544320 | bytes 1048576 | tf_op jit(solution)/shard_map/far_last_kernel/pallas_call | solution.py:247
  18.9 1.2 %collective-permute-start.9 = (f32[1,256]{1,0:T(1,128)S(1)}, f32[1,256]{1,0:T(1,128)S(1)}, u32[]{:S(2)}, u32[]{:S(2)}) collective-permute-start(f32[1,256]{1,0:T(1,128)S(1)} %get-tuple-element.23), channel_id=1, source_target_pairs={{2,4},{3,5},{6,1},{7,0},{10,3},{11,2},{14,6},{15,7},{12,10},{13,11... | collective-permute-start | bytes 3080 | tf_op jit(solution)/shard_map/ppermute | solution.py:266
  20.1 1.2 %collective-permute-start.10 = (f32[1,256]{1,0:T(1,128)S(1)}, f32[1,256]{1,0:T(1,128)S(1)}, u32[]{:S(2)}, u32[]{:S(2)}) collective-permute-start(f32[1,256]{1,0:T(1,128)S(1)} %get-tuple-element.24), channel_id=1, source_target_pairs={{2,10},{3,11},{6,15},{7,14},{10,13},{11,12},{14,9},{15,8},{12,5},{... | collective-permute-start | bytes 3080 | tf_op jit(solution)/shard_map/ppermute | solution.py:266
  21.3 0.6 %own_kernel.1 = f32[1,256]{1,0:T(1,128)S(1)} custom-call(bf16[1040,128]{1,0:T(8,128)(2,1)S(1)} %get-tuple-element.15.refs_0_.own, bf16[3,1040,128]{2,1,0:T(8,128)(2,1)S(1)} %collective-permute-done.4.others, bf16[1040,128]{1,0:T(8,128)(2,1)S(1)} %get-tuple-element.19.back, bf16[528,128]{1,0:T(8,128)(2,1)S(1)} %collective-permute-done.6.ahead_a, ...), custom_call_target="tpu_custom_call" | custom-call | flops 335544320 | bytes 1048576 | tf_op jit(solution)/shard_map/own_kernel/pallas_call | solution.py:247
  21.9 1.0 %collective-permute-done.9 = f32[1,256]{1,0:T(1,128)S(1)} collective-permute-done((f32[1,256]{1,0:T(1,128)S(1)}, f32[1,256]{1,0:T(1,128)S(1)}, u32[]{:S(2)}, u32[]{:S(2)}) %collective-permute-start.9) | collective-permute-done | bytes 1056 | tf_op jit(solution)/shard_map/ppermute | solution.py:266
  22.9 1.1 %collective-permute-done.10 = f32[1,256]{1,0:T(1,128)S(1)} collective-permute-done((f32[1,256]{1,0:T(1,128)S(1)}, f32[1,256]{1,0:T(1,128)S(1)}, u32[]{:S(2)}, u32[]{:S(2)}) %collective-permute-start.10) | collective-permute-done | bytes 1056 | tf_op jit(solution)/shard_map/ppermute | solution.py:266
  24.0 0.6 %maximum_maximum_fusion = f32[1,256]{1,0:T(1,128)} fusion(f32[1,256]{1,0:T(1,128)S(1)} %own_kernel.1, f32[1,256]{1,0:T(1,128)S(1)} %collective-permute-done.9, f32[1,256]{1,0:T(1,128)S(1)} %collective-permute-done.10), kind=kLoop, calls=%fused_computation | loop fusion | flops 512 | bytes 4096 | tf_op jit(solution)/shard_map/max | solution.py:323
Async XLA Ops:
  0.0 3.5 %copy-start = (bf16[256,512]{1,0:T(8,128)(2,1)S(1)}, bf16[256,512]{1,0:T(8,128)(2,1)}, u32[]{:S(2)}) copy-start(bf16[256,512]{1,0:T(8,128)(2,1)} %embeds.3) | copy-start | bytes 786436
  0.9 6.8 %collective-permute-start.2 = (bf16[528,128]{1,0:T(8,128)(2,1)S(1)}, bf16[528,128]{1,0:T(8,128)(2,1)S(1)}, u32[]{:S(2)}, u32[]{:S(2)}) collective-permute-start(bf16[528,128]{1,0:T(8,128)(2,1)S(1)} %pack_first.1.first), channel_id=1, source_target_pairs={{2,7},{3,6},{6,10},{7,11},{10,14},{11,15},{14,12},{15,13},{12,8},{... | collective-permute-start | bytes 405512 | tf_op jit(solution)/shard_map/ppermute | solution.py:266
  3.3 6.4 %collective-permute-start = (bf16[528,128]{1,0:T(8,128)(2,1)S(1)}, bf16[528,128]{1,0:T(8,128)(2,1)S(1)}, u32[]{:S(2)}, u32[]{:S(2)}) collective-permute-start(bf16[528,128]{1,0:T(8,128)(2,1)S(1)} %pack_first.1.first), channel_id=1, source_target_pairs={{2,1},{3,0},{6,2},{7,3},{10,6},{11,7},{14,11},{15,10},{12,15},{13,... | collective-permute-start | bytes 405512 | tf_op jit(solution)/shard_map/ppermute | solution.py:266
  3.9 6.6 %collective-permute-start.3 = (bf16[512,128]{1,0:T(8,128)(2,1)S(1)}, bf16[512,128]{1,0:T(8,128)(2,1)S(1)}, u32[]{:S(2)}, u32[]{:S(2)}) collective-permute-start(bf16[512,128]{1,0:T(8,128)(2,1)S(1)} %get-tuple-element.16), channel_id=1, source_target_pairs={{2,7},{3,6},{6,10},{7,11},{10,14},{11,15},{14,12},{15,13},{12,8},{... | collective-permute-start | bytes 393224 | tf_op jit(solution)/shard_map/ppermute | solution.py:266
  5.6 6.9 %collective-permute-start.1 = (bf16[512,128]{1,0:T(8,128)(2,1)S(1)}, bf16[512,128]{1,0:T(8,128)(2,1)S(1)}, u32[]{:S(2)}, u32[]{:S(2)}) collective-permute-start(bf16[512,128]{1,0:T(8,128)(2,1)S(1)} %get-tuple-element.16), channel_id=1, source_target_pairs={{2,1},{3,0},{6,2},{7,3},{10,6},{11,7},{14,11},{15,10},{12,15},{13,... | collective-permute-start | bytes 393224 | tf_op jit(solution)/shard_map/ppermute | solution.py:266
  7.7 5.8 %collective-permute-start.5 = (bf16[528,128]{1,0:T(8,128)(2,1)S(1)}, bf16[528,128]{1,0:T(8,128)(2,1)S(1)}, u32[]{:S(2)}, u32[]{:S(2)}) collective-permute-start(bf16[528,128]{1,0:T(8,128)(2,1)S(1)} %collective-permute-done.2.refs_3_), channel_id=1, source_target_pairs={{2,6},{3,7},{6,10},{7,11},{10,14},{11,15},{14,12},{15,13},{12,8},{... | collective-permute-start | bytes 405512 | tf_op jit(solution)/shard_map/ppermute | solution.py:266
  9.8 6.4 %collective-permute-start.6 = (bf16[528,128]{1,0:T(8,128)(2,1)S(1)}, bf16[528,128]{1,0:T(8,128)(2,1)S(1)}, u32[]{:S(2)}, u32[]{:S(2)}) collective-permute-start(bf16[528,128]{1,0:T(8,128)(2,1)S(1)} %collective-permute-done.refs_1_), channel_id=1, source_target_pairs={{2,0},{3,1},{6,2},{7,3},{10,6},{11,7},{14,10},{15,11},{12,14},{13,... | collective-permute-start | bytes 405512 | tf_op jit(solution)/shard_map/ppermute | solution.py:266
  10.5 6.4 %collective-permute-start.7 = (bf16[512,128]{1,0:T(8,128)(2,1)S(1)}, bf16[512,128]{1,0:T(8,128)(2,1)S(1)}, u32[]{:S(2)}, u32[]{:S(2)}) collective-permute-start(bf16[512,128]{1,0:T(8,128)(2,1)S(1)} %collective-permute-done.3.refs_4_), channel_id=1, source_target_pairs={{2,6},{3,7},{6,10},{7,11},{10,14},{11,15},{14,12},{15,13},{12,8},{... | collective-permute-start | bytes 393224 | tf_op jit(solution)/shard_map/ppermute | solution.py:266
  12.6 5.9 %collective-permute-start.8 = (bf16[512,128]{1,0:T(8,128)(2,1)S(1)}, bf16[512,128]{1,0:T(8,128)(2,1)S(1)}, u32[]{:S(2)}, u32[]{:S(2)}) collective-permute-start(bf16[512,128]{1,0:T(8,128)(2,1)S(1)} %collective-permute-done.1.refs_2_), channel_id=1, source_target_pairs={{2,0},{3,1},{6,2},{7,3},{10,6},{11,7},{14,10},{15,11},{12,14},{13,... | collective-permute-start | bytes 393224 | tf_op jit(solution)/shard_map/ppermute | solution.py:266
  12.9 4.0 %collective-permute-start.4 = (bf16[3,1040,128]{2,1,0:T(8,128)(2,1)S(1)}, bf16[3,1040,128]{2,1,0:T(8,128)(2,1)S(1)}, u32[]{:S(2)}, u32[]{:S(2)}) collective-permute-start(bf16[3,1040,128]{2,1,0:T(8,128)(2,1)S(1)} %bundle_kernel.1.bundle), channel_id=1, source_target_pairs={{2,3},{3,2},{6,7},{7,6},{10,11},{11,10},{14,15},{15,14},{12,13},{1... | collective-permute-start | bytes 2396168 | tf_op jit(solution)/shard_map/ppermute | solution.py:266
  18.9 4.0 %collective-permute-start.9 = (f32[1,256]{1,0:T(1,128)S(1)}, f32[1,256]{1,0:T(1,128)S(1)}, u32[]{:S(2)}, u32[]{:S(2)}) collective-permute-start(f32[1,256]{1,0:T(1,128)S(1)} %get-tuple-element.23), channel_id=1, source_target_pairs={{2,4},{3,5},{6,1},{7,0},{10,3},{11,2},{14,6},{15,7},{12,10},{13,11... | collective-permute-start | bytes 3080 | tf_op jit(solution)/shard_map/ppermute | solution.py:266
  20.1 3.9 %collective-permute-start.10 = (f32[1,256]{1,0:T(1,128)S(1)}, f32[1,256]{1,0:T(1,128)S(1)}, u32[]{:S(2)}, u32[]{:S(2)}) collective-permute-start(f32[1,256]{1,0:T(1,128)S(1)} %get-tuple-element.24), channel_id=1, source_target_pairs={{2,10},{3,11},{6,15},{7,14},{10,13},{11,12},{14,9},{15,8},{12,5},{... | collective-permute-start | bytes 3080 | tf_op jit(solution)/shard_map/ppermute | solution.py:266

commit v27 on v23

--- a/solution.py
+++ b/solution.py
@@ -40,21 +40,20 @@
 def pack_first_kernel(embeds, label, first, line, sems):
     rows, width = embeds.shape
     half = rows // 2
-    copies = []
+    copies = [pltpu.make_async_copy(label, line, sems.at[width // LANES])]
     for j in range(width // LANES):
         part = embeds.at[pl.ds(0, half), pl.ds(j * LANES, LANES)]
         copies.append(pltpu.make_async_copy(part, first.at[pl.ds(j * half, half)], sems.at[j]))
-    copies.append(pltpu.make_async_copy(label, line, sems.at[width // LANES]))
     for copy in copies:
         copy.start()
-    copies[-1].wait()
+    copies[0].wait()
     row = lax.broadcasted_iota(jnp.int32, (LABEL_ROWS, LANES), 0)
     lines = jnp.zeros((LABEL_ROWS, LANES), jnp.float32)
     for i in range(rows // LANES):
         piece = line[:, i * LANES : (i + 1) * LANES].astype(jnp.float32)
         lines = jnp.where(row == i, piece, lines)
     first[half * width // LANES :, :] = lines.astype(jnp.bfloat16)
-    for copy in copies[:-1]:
+    for copy in copies[1:]:
         copy.wait()
 
 

time: 24.6 us -> 24.6 us (level)
  no operation moved by 1% of the time
where the time goes in v27:
time: 24.6 us; the launch traced here: 24.5 us
  starting transfers between devices  12.8 us (52%)
  waiting for transfers between devices  7.21 us (29%)
  Pallas kernels  3.8 us (15%)
  other arithmetic  0.57 us (2%)
    ppermute x11, starting transfers between devices, send(): return lax.ppermute(value, GROUP, perms[name])  12.8 us
    ppermute x11, waiting for transfers between devices, send(): return lax.ppermute(value, GROUP, perms[name])  7.21 us
    pallas_call x6, Pallas kernels, kernel_call(): pl.pallas_call(kernel, out_shape=outputs, in_specs=[vmem] * len(inputs),...  2.89 us
    pallas_call x1, Pallas kernels, on_ring(): pl.pallas_call(pack_first_kernel, out_shape=chunk(half, True), in_specs=[...  0.91 us
    max x1, other arithmetic, on_ring(): jnp.maximum(mine, jnp.maximum(send(to_back, 'home_back'), send(to_ahead,...  0.57 us
  transfers between devices with their start and end apart: 11, of which 7 were waited for; matrix products, arithmetic and copies ran while one was open for 0% of the time, Pallas kernels for 10%

profile of v27, /device:TPU:0, one launch (start us, length us, event | category | flops | bytes accessed | tf_op | source)
XLA Modules:
  0.0 24.5 jit_solution(3529672324130603564)
XLA Ops:
  0.0 0.0 copy-start
  0.0 0.9 %pack_first.1.first = bf16[528,128]{1,0:T(8,128)(2,1)S(1)} custom-call(bf16[256,512]{1,0:T(8,128)(2,1)} %embeds.3, s32[1,256]{1,0:T(1,128)} %bitcast.2), custom_call_target="tpu_custom_call" | custom-call | tf_op jit(solution)/shard_map/pack_first/pallas_call | solution.py:276
  0.9 2.5 %collective-permute-start.2 = (bf16[528,128]{1,0:T(8,128)(2,1)S(1)}, bf16[528,128]{1,0:T(8,128)(2,1)S(1)}, u32[]{:S(2)}, u32[]{:S(2)}) collective-permute-start(bf16[528,128]{1,0:T(8,128)(2,1)S(1)} %pack_first.1.first), channel_id=1, source_target_pairs={{0,5},{1,4},{4,8},{5,9},{8,12},{9,13},{12,14},{13,15},{14,10},{15,... | collective-permute-start | bytes 405512 | tf_op jit(solution)/shard_map/ppermute | solution.py:265
  3.4 0.0 collective-permute-start
  3.4 0.0 copy-done
  3.4 0.4 %pack_second_kernel.1 = (bf16[512,128]{1,0:T(8,128)(2,1)S(1)}, bf16[1040,128]{1,0:T(8,128)(2,1)S(1)}, f32[1,256]{1,0:T(1,128)S(1)}) custom-call(bf16[256,512]{1,0:T(8,128)(2,1)S(1)} %copy-done, bf16[528,128]{1,0:T(8,128)(2,1)S(1)} %pack_first.1.first), custom_call_target="tpu_custom_call" | custom-call | flops 67108864 | bytes 1048576 | tf_op jit(solution)/shard_map/pack_second_kernel/pallas_call | solution.py:246
  3.8 2.1 %collective-permute-start.3 = (bf16[512,128]{1,0:T(8,128)(2,1)S(1)}, bf16[512,128]{1,0:T(8,128)(2,1)S(1)}, u32[]{:S(2)}, u32[]{:S(2)}) collective-permute-start(bf16[512,128]{1,0:T(8,128)(2,1)S(1)} %get-tuple-element.16), channel_id=1, source_target_pairs={{0,5},{1,4},{4,8},{5,9},{8,12},{9,13},{12,14},{13,15},{14,10},{15,... | collective-permute-start | bytes 393224 | tf_op jit(solution)/shard_map/ppermute | solution.py:265
  5.9 0.3 %collective-permute-start.1 = (bf16[512,128]{1,0:T(8,128)(2,1)S(1)}, bf16[512,128]{1,0:T(8,128)(2,1)S(1)}, u32[]{:S(2)}, u32[]{:S(2)}) collective-permute-start(bf16[512,128]{1,0:T(8,128)(2,1)S(1)} %get-tuple-element.16), channel_id=1, source_target_pairs={{0,3},{1,2},{4,0},{5,1},{8,4},{9,5},{12,9},{13,8},{14,13},{15,12},... | collective-permute-start | bytes 393224 | tf_op jit(solution)/shard_map/ppermute | solution.py:265
  6.2 1.2 %collective-permute-done.2.refs_3_ = bf16[528,128]{1,0:T(8,128)(2,1)S(1)} collective-permute-done((bf16[528,128]{1,0:T(8,128)(2,1)S(1)}, bf16[528,128]{1,0:T(8,128)(2,1)S(1)}, u32[]{:S(2)}, u32[]{:S(2)}) %collective-permute-start.2) | collective-permute-done | bytes 135200 | tf_op jit(solution)/shard_map/ppermute | solution.py:265
  7.4 2.5 %collective-permute-start.5 = (bf16[528,128]{1,0:T(8,128)(2,1)S(1)}, bf16[528,128]{1,0:T(8,128)(2,1)S(1)}, u32[]{:S(2)}, u32[]{:S(2)}) collective-permute-start(bf16[528,128]{1,0:T(8,128)(2,1)S(1)} %collective-permute-done.2.refs_3_), channel_id=1, source_target_pairs={{0,4},{1,5},{4,8},{5,9},{8,12},{9,13},{12,14},{13,15},{14,10},{15,... | collective-permute-start | bytes 405512 | tf_op jit(solution)/shard_map/ppermute | solution.py:265
  9.9 0.0 collective-permute-done.refs_1_
  9.9 0.0 collective-permute-start.6
  9.9 0.3 %collective-permute-done.3.refs_4_ = bf16[512,128]{1,0:T(8,128)(2,1)S(1)} collective-permute-done((bf16[512,128]{1,0:T(8,128)(2,1)S(1)}, bf16[512,128]{1,0:T(8,128)(2,1)S(1)}, u32[]{:S(2)}, u32[]{:S(2)}) %collective-permute-start.3) | collective-permute-done | bytes 131104 | tf_op jit(solution)/shard_map/ppermute | solution.py:265
  10.2 2.5 %collective-permute-start.7 = (bf16[512,128]{1,0:T(8,128)(2,1)S(1)}, bf16[512,128]{1,0:T(8,128)(2,1)S(1)}, u32[]{:S(2)}, u32[]{:S(2)}) collective-permute-start(bf16[512,128]{1,0:T(8,128)(2,1)S(1)} %collective-permute-done.3.refs_4_), channel_id=1, source_target_pairs={{0,4},{1,5},{4,8},{5,9},{8,12},{9,13},{12,14},{13,15},{14,10},{15,... | collective-permute-start | bytes 393224 | tf_op jit(solution)/shard_map/ppermute | solution.py:265
  12.7 0.0 collective-permute-done.1.refs_2_
  12.7 0.0 collective-permute-start.8
  12.7 0.2 bundle_kernel.1.bundle
  12.8 0.1 collective-permute-start.4
  12.9 0.4 %collective-permute-done.5.back_a = bf16[528,128]{1,0:T(8,128)(2,1)S(1)} collective-permute-done((bf16[528,128]{1,0:T(8,128)(2,1)S(1)}, bf16[528,128]{1,0:T(8,128)(2,1)S(1)}, u32[]{:S(2)}, u32[]{:S(2)}) %collective-permute-start.5) | collective-permute-done | bytes 135200 | tf_op jit(solution)/shard_map/ppermute | solution.py:265
  13.3 2.1 %collective-permute-done.6.ahead_a = bf16[528,128]{1,0:T(8,128)(2,1)S(1)} collective-permute-done((bf16[528,128]{1,0:T(8,128)(2,1)S(1)}, bf16[528,128]{1,0:T(8,128)(2,1)S(1)}, u32[]{:S(2)}, u32[]{:S(2)}) %collective-permute-start.6) | collective-permute-done | bytes 135200 | tf_op jit(solution)/shard_map/ppermute | solution.py:265
  15.4 0.7 %far_first_kernel.1 = (f32[1,256]{1,0:T(1,128)S(1)}, f32[1,256]{1,0:T(1,128)S(1)}) custom-call(bf16[1040,128]{1,0:T(8,128)(2,1)S(1)} %get-tuple-element.15.refs_0_.own, bf16[3,1040,128]{2,1,0:T(8,128)(2,1)S(1)} %bundle_kernel.1.bundle, bf16[528,128]{1,0:T(8,128)(2,1)S(1)} %collective-permute-done.5.back_a, ...), custom_call_target="tpu_custom_call" | custom-call | flops 13421772800 | bytes 1048576 | tf_op jit(solution)/shard_map/far_first_kernel/pallas_call | solution.py:246
  16.1 0.0 collective-permute-done.7.back_b
  16.2 0.0 collective-permute-done.4.others
  16.2 0.6 %far_back_kernel.1 = (f32[1,256]{1,0:T(1,128)S(1)}, f32[1,128]{1,0:T(1,128)S(1)}, bf16[1040,128]{1,0:T(8,128)(2,1)S(1)}) custom-call(bf16[1040,128]{1,0:T(8,128)(2,1)S(1)} %get-tuple-element.15.refs_0_.own, bf16[3,1040,128]{2,1,0:T(8,128)(2,1)S(1)} %bundle_kernel.1.bundle, bf16[3,1040,128]{2,1,0:T(8,128)(2,1)S(1)} %collective-permute-done.4.others, ...), custom_call_target="tpu_custom_call" | custom-call | flops 134217728 | bytes 1048576 | tf_op jit(solution)/shard_map/far_back_kernel/pallas_call | solution.py:246
  16.8 1.3 %collective-permute-done.8.ahead_b = bf16[512,128]{1,0:T(8,128)(2,1)S(1)} collective-permute-done((bf16[512,128]{1,0:T(8,128)(2,1)S(1)}, bf16[512,128]{1,0:T(8,128)(2,1)S(1)}, u32[]{:S(2)}, u32[]{:S(2)}) %collective-permute-start.8) | collective-permute-done | bytes 131104 | tf_op jit(solution)/shard_map/ppermute | solution.py:265
  18.1 0.5 %far_last_kernel.1 = (f32[1,256]{1,0:T(1,128)S(1)}, f32[1,256]{1,0:T(1,128)S(1)}) custom-call(bf16[1040,128]{1,0:T(8,128)(2,1)S(1)} %get-tuple-element.15.refs_0_.own, bf16[3,1040,128]{2,1,0:T(8,128)(2,1)S(1)} %bundle_kernel.1.bundle, bf16[3,1040,128]{2,1,0:T(8,128)(2,1)S(1)} %collective-permute-done.4.others, bf16[1040,128]{1,0:T(8,128)(2,1)S(1)} %get-tuple-element.19.back, ...), custom_call_target="tpu_custom_call" | custom-call | flops 335544320 | bytes 1048576 | tf_op jit(solution)/shard_map/far_last_kernel/pallas_call | solution.py:246
  18.6 1.5 %collective-permute-start.9 = (f32[1,256]{1,0:T(1,128)S(1)}, f32[1,256]{1,0:T(1,128)S(1)}, u32[]{:S(2)}, u32[]{:S(2)}) collective-permute-start(f32[1,256]{1,0:T(1,128)S(1)} %get-tuple-element.23), channel_id=1, source_target_pairs={{0,6},{1,7},{4,3},{5,2},{8,1},{9,0},{12,4},{13,5},{14,8},{15,9},{1... | collective-permute-start | bytes 3080 | tf_op jit(solution)/shard_map/ppermute | solution.py:265
  20.0 1.5 %collective-permute-start.10 = (f32[1,256]{1,0:T(1,128)S(1)}, f32[1,256]{1,0:T(1,128)S(1)}, u32[]{:S(2)}, u32[]{:S(2)}) collective-permute-start(f32[1,256]{1,0:T(1,128)S(1)} %get-tuple-element.24), channel_id=1, source_target_pairs={{0,8},{1,9},{4,13},{5,12},{8,15},{9,14},{12,11},{13,10},{14,7},{15... | collective-permute-start | bytes 3080 | tf_op jit(solution)/shard_map/ppermute | solution.py:265
  21.6 0.6 %own_kernel.1 = f32[1,256]{1,0:T(1,128)S(1)} custom-call(bf16[1040,128]{1,0:T(8,128)(2,1)S(1)} %get-tuple-element.15.refs_0_.own, bf16[3,1040,128]{2,1,0:T(8,128)(2,1)S(1)} %collective-permute-done.4.others, bf16[1040,128]{1,0:T(8,128)(2,1)S(1)} %get-tuple-element.19.back, bf16[528,128]{1,0:T(8,128)(2,1)S(1)} %collective-permute-done.6.ahead_a, ...), custom_call_target="tpu_custom_call" | custom-call | flops 335544320 | bytes 1048576 | tf_op jit(solution)/shard_map/own_kernel/pallas_call | solution.py:246
  22.1 0.4 %collective-permute-done.9 = f32[1,256]{1,0:T(1,128)S(1)} collective-permute-done((f32[1,256]{1,0:T(1,128)S(1)}, f32[1,256]{1,0:T(1,128)S(1)}, u32[]{:S(2)}, u32[]{:S(2)}) %collective-permute-start.9) | collective-permute-done | bytes 1056 | tf_op jit(solution)/shard_map/ppermute | solution.py:265
  22.5 1.4 %collective-permute-done.10 = f32[1,256]{1,0:T(1,128)S(1)} collective-permute-done((f32[1,256]{1,0:T(1,128)S(1)}, f32[1,256]{1,0:T(1,128)S(1)}, u32[]{:S(2)}, u32[]{:S(2)}) %collective-permute-start.10) | collective-permute-done | bytes 1056 | tf_op jit(solution)/shard_map/ppermute | solution.py:265
  23.9 0.6 %maximum_maximum_fusion = f32[1,256]{1,0:T(1,128)} fusion(f32[1,256]{1,0:T(1,128)S(1)} %own_kernel.1, f32[1,256]{1,0:T(1,128)S(1)} %collective-permute-done.9, f32[1,256]{1,0:T(1,128)S(1)} %collective-permute-done.10), kind=kLoop, calls=%fused_computation | loop fusion | flops 512 | bytes 4096 | tf_op jit(solution)/shard_map/max | solution.py:322
Async XLA Ops:
  0.0 3.4 %copy-start = (bf16[256,512]{1,0:T(8,128)(2,1)S(1)}, bf16[256,512]{1,0:T(8,128)(2,1)}, u32[]{:S(2)}) copy-start(bf16[256,512]{1,0:T(8,128)(2,1)} %embeds.3) | copy-start | bytes 786436
  0.9 6.5 %collective-permute-start.2 = (bf16[528,128]{1,0:T(8,128)(2,1)S(1)}, bf16[528,128]{1,0:T(8,128)(2,1)S(1)}, u32[]{:S(2)}, u32[]{:S(2)}) collective-permute-start(bf16[528,128]{1,0:T(8,128)(2,1)S(1)} %pack_first.1.first), channel_id=1, source_target_pairs={{0,5},{1,4},{4,8},{5,9},{8,12},{9,13},{12,14},{13,15},{14,10},{15,... | collective-permute-start | bytes 405512 | tf_op jit(solution)/shard_map/ppermute | solution.py:265
  3.4 6.5 %collective-permute-start = (bf16[528,128]{1,0:T(8,128)(2,1)S(1)}, bf16[528,128]{1,0:T(8,128)(2,1)S(1)}, u32[]{:S(2)}, u32[]{:S(2)}) collective-permute-start(bf16[528,128]{1,0:T(8,128)(2,1)S(1)} %pack_first.1.first), channel_id=1, source_target_pairs={{0,3},{1,2},{4,0},{5,1},{8,4},{9,5},{12,9},{13,8},{14,13},{15,12},... | collective-permute-start | bytes 405512 | tf_op jit(solution)/shard_map/ppermute | solution.py:265
  3.8 6.4 %collective-permute-start.3 = (bf16[512,128]{1,0:T(8,128)(2,1)S(1)}, bf16[512,128]{1,0:T(8,128)(2,1)S(1)}, u32[]{:S(2)}, u32[]{:S(2)}) collective-permute-start(bf16[512,128]{1,0:T(8,128)(2,1)S(1)} %get-tuple-element.16), channel_id=1, source_target_pairs={{0,5},{1,4},{4,8},{5,9},{8,12},{9,13},{12,14},{13,15},{14,10},{15,... | collective-permute-start | bytes 393224 | tf_op jit(solution)/shard_map/ppermute | solution.py:265
  5.9 6.8 %collective-permute-start.1 = (bf16[512,128]{1,0:T(8,128)(2,1)S(1)}, bf16[512,128]{1,0:T(8,128)(2,1)S(1)}, u32[]{:S(2)}, u32[]{:S(2)}) collective-permute-start(bf16[512,128]{1,0:T(8,128)(2,1)S(1)} %get-tuple-element.16), channel_id=1, source_target_pairs={{0,3},{1,2},{4,0},{5,1},{8,4},{9,5},{12,9},{13,8},{14,13},{15,12},... | collective-permute-start | bytes 393224 | tf_op jit(solution)/shard_map/ppermute | solution.py:265
  7.4 5.9 %collective-permute-start.5 = (bf16[528,128]{1,0:T(8,128)(2,1)S(1)}, bf16[528,128]{1,0:T(8,128)(2,1)S(1)}, u32[]{:S(2)}, u32[]{:S(2)}) collective-permute-start(bf16[528,128]{1,0:T(8,128)(2,1)S(1)} %collective-permute-done.2.refs_3_), channel_id=1, source_target_pairs={{0,4},{1,5},{4,8},{5,9},{8,12},{9,13},{12,14},{13,15},{14,10},{15,... | collective-permute-start | bytes 405512 | tf_op jit(solution)/shard_map/ppermute | solution.py:265
  9.9 5.5 %collective-permute-start.6 = (bf16[528,128]{1,0:T(8,128)(2,1)S(1)}, bf16[528,128]{1,0:T(8,128)(2,1)S(1)}, u32[]{:S(2)}, u32[]{:S(2)}) collective-permute-start(bf16[528,128]{1,0:T(8,128)(2,1)S(1)} %collective-permute-done.refs_1_), channel_id=1, source_target_pairs={{0,2},{1,3},{4,0},{5,1},{8,4},{9,5},{12,8},{13,9},{14,12},{15,13},... | collective-permute-start | bytes 405512 | tf_op jit(solution)/shard_map/ppermute | solution.py:265
  10.2 5.9 %collective-permute-start.7 = (bf16[512,128]{1,0:T(8,128)(2,1)S(1)}, bf16[512,128]{1,0:T(8,128)(2,1)S(1)}, u32[]{:S(2)}, u32[]{:S(2)}) collective-permute-start(bf16[512,128]{1,0:T(8,128)(2,1)S(1)} %collective-permute-done.3.refs_4_), channel_id=1, source_target_pairs={{0,4},{1,5},{4,8},{5,9},{8,12},{9,13},{12,14},{13,15},{14,10},{15,... | collective-permute-start | bytes 393224 | tf_op jit(solution)/shard_map/ppermute | solution.py:265
  12.7 5.4 %collective-permute-start.8 = (bf16[512,128]{1,0:T(8,128)(2,1)S(1)}, bf16[512,128]{1,0:T(8,128)(2,1)S(1)}, u32[]{:S(2)}, u32[]{:S(2)}) collective-permute-start(bf16[512,128]{1,0:T(8,128)(2,1)S(1)} %collective-permute-done.1.refs_2_), channel_id=1, source_target_pairs={{0,2},{1,3},{4,0},{5,1},{8,4},{9,5},{12,8},{13,9},{14,12},{15,13},... | collective-permute-start | bytes 393224 | tf_op jit(solution)/shard_map/ppermute | solution.py:265
  12.8 3.3 %collective-permute-start.4 = (bf16[3,1040,128]{2,1,0:T(8,128)(2,1)S(1)}, bf16[3,1040,128]{2,1,0:T(8,128)(2,1)S(1)}, u32[]{:S(2)}, u32[]{:S(2)}) collective-permute-start(bf16[3,1040,128]{2,1,0:T(8,128)(2,1)S(1)} %bundle_kernel.1.bundle), channel_id=1, source_target_pairs={{0,1},{1,0},{4,5},{5,4},{8,9},{9,8},{12,13},{13,12},{14,15},{15,14... | collective-permute-start | bytes 2396168 | tf_op jit(solution)/shard_map/ppermute | solution.py:265
  18.6 4.0 %collective-permute-start.9 = (f32[1,256]{1,0:T(1,128)S(1)}, f32[1,256]{1,0:T(1,128)S(1)}, u32[]{:S(2)}, u32[]{:S(2)}) collective-permute-start(f32[1,256]{1,0:T(1,128)S(1)} %get-tuple-element.23), channel_id=1, source_target_pairs={{0,6},{1,7},{4,3},{5,2},{8,1},{9,0},{12,4},{13,5},{14,8},{15,9},{1... | collective-permute-start | bytes 3080 | tf_op jit(solution)/shard_map/ppermute | solution.py:265
  20.0 3.9 %collective-permute-start.10 = (f32[1,256]{1,0:T(1,128)S(1)}, f32[1,256]{1,0:T(1,128)S(1)}, u32[]{:S(2)}, u32[]{:S(2)}) collective-permute-start(f32[1,256]{1,0:T(1,128)S(1)} %get-tuple-element.24), channel_id=1, source_target_pairs={{0,8},{1,9},{4,13},{5,12},{8,15},{9,14},{12,11},{13,10},{14,7},{15... | collective-permute-start | bytes 3080 | tf_op jit(solution)/shard_map/ppermute | solution.py:265

commit v28 on v19

--- a/solution.py
+++ b/solution.py
@@ -58,12 +58,14 @@
         copy.wait()
 
 
-def pack_second_kernel(embeds, first, second, both):
+def pack_second_kernel(embeds, first, second, both, mine):
     rows, width = embeds.shape
     unit = normalised(embeds[...])
     put_unit(unit[rows // 2 :, :], second)
     put_unit(unit, both)
     put_labels(first, both)
+    own = Block(unit, labels_in(first, rows))
+    mine[...] = best_of(own, own)
 
 
 def put_labels(source, both):
@@ -157,7 +159,7 @@
     return found[0], functools.reduce(jnp.maximum, best)
 
 
-def near_kernel(own, succ_a, succ_b, prev_a, prev_b, mine, bundle):
+def near_kernel(own, succ_a, succ_b, prev_a, prev_b, self_best, mine, bundle):
     rows = mine.shape[1]
     prev, succ = whole(prev_a, prev_b, rows), whole(succ_a, succ_b, rows)
     for at, block, first in ((0, prev, prev_a), (1, succ, succ_a)):
@@ -165,7 +167,7 @@
         put_labels(first, bundle.at[at])
     bundle[2] = own[...]
     own = packed(own, rows)
-    mine[...] = best_of(own, own, prev, succ)
+    mine[...] = jnp.maximum(self_best[...], best_of(own, prev, succ))
 
 
 def far_first_kernel(bundle, back_a, ahead_a, found):
@@ -288,8 +290,8 @@
         pltpu.with_memory_space_constraint(embeds, pltpu.HBM),
         pltpu.with_memory_space_constraint(cluster.reshape(1, rows), pltpu.HBM),
     )
-    own_b, own = kernel_call(
-        pack_second_kernel, [embeds, own_a], [chunk(half, False), chunk(rows, True)], 1
+    own_b, own, mine = kernel_call(
+        pack_second_kernel, [embeds, own_a], [chunk(half, False), chunk(rows, True), line], 1
     )
     prev_a, succ_a = send(own_a, "next"), send(own_a, "prev")
     prev_b, succ_b = send(own_b, "next"), send(own_b, "prev")
@@ -298,7 +300,7 @@
     block = chunk(rows, True)
     bundle_shape = jax.ShapeDtypeStruct((3, *block.shape), jnp.bfloat16)
     mine, bundle = kernel_call(
-        near_kernel, [own, succ_a, succ_b, prev_a, prev_b], [line, bundle_shape], NEAR_COST
+        near_kernel, [own, succ_a, succ_b, prev_a, prev_b, mine], [line, bundle_shape], NEAR_COST
     )
     others = send(bundle, "sibling")
     (found,) = kernel_call(far_first_kernel, [bundle, back_a, ahead_a], [line], FIRST_COST)

time: 24.6 us -> 24.6 us (level)
  transfers between devices with their start and end apart: 11 -> 11, of which waited for: 8 -> 7; matrix products, arithmetic and copies ran while one was open for 0% -> 0% of each run, Pallas kernels for 10% -> 10%
where the time goes in v28:
time: 24.6 us; the launch traced here: 24.5 us
  starting transfers between devices  12.8 us (52%)
  waiting for transfers between devices  7.08 us (29%)
  Pallas kernels  3.92 us (16%)
  other arithmetic  0.57 us (2%)
    ppermute x11, starting transfers between devices, send(): return lax.ppermute(value, GROUP, perms[name])  12.8 us
    ppermute x11, waiting for transfers between devices, send(): return lax.ppermute(value, GROUP, perms[name])  7.08 us
    pallas_call x6, Pallas kernels, kernel_call(): pl.pallas_call(kernel, out_shape=outputs, in_specs=[vmem] * len(inputs),...  3.02 us
    pallas_call x1, Pallas kernels, on_ring(): pl.pallas_call(pack_first_kernel, out_shape=chunk(half, True), in_specs=[...  0.89 us
    max x1, other arithmetic, on_ring(): jnp.maximum(mine, jnp.maximum(send(to_back, 'home_back'), send(to_ahead,...  0.57 us
  transfers between devices with their start and end apart: 11, of which 7 were waited for; matrix products, arithmetic and copies ran while one was open for 0% of the time, Pallas kernels for 10%

profile of v28, /device:TPU:0, one launch (start us, length us, event | category | flops | bytes accessed | tf_op | source)
XLA Modules:
  0.0 24.5 jit_solution(15345671917112240900)
XLA Ops:
  0.0 0.0 copy-start
  0.0 0.9 %pack_first.1.first = bf16[528,128]{1,0:T(8,128)(2,1)S(1)} custom-call(bf16[256,512]{1,0:T(8,128)(2,1)} %embeds.3, s32[1,256]{1,0:T(1,128)} %bitcast.2), custom_call_target="tpu_custom_call" | custom-call | tf_op jit(solution)/shard_map/pack_first/pallas_call | solution.py:278
  0.9 2.5 %collective-permute-start.2 = (bf16[528,128]{1,0:T(8,128)(2,1)S(1)}, bf16[528,128]{1,0:T(8,128)(2,1)S(1)}, u32[]{:S(2)}, u32[]{:S(2)}) collective-permute-start(bf16[528,128]{1,0:T(8,128)(2,1)S(1)} %pack_first.1.first), channel_id=1, source_target_pairs={{0,5},{1,4},{4,8},{5,9},{8,12},{9,13},{12,14},{13,15},{14,10},{15,... | collective-permute-start | bytes 405512 | tf_op jit(solution)/shard_map/ppermute | solution.py:267
  3.4 0.0 collective-permute-start
  3.4 0.0 copy-done
  3.4 0.4 %pack_second_kernel.1 = (bf16[512,128]{1,0:T(8,128)(2,1)S(1)}, bf16[1040,128]{1,0:T(8,128)(2,1)S(1)}, f32[1,256]{1,0:T(1,128)S(1)}) custom-call(bf16[256,512]{1,0:T(8,128)(2,1)S(1)} %copy-done, bf16[528,128]{1,0:T(8,128)(2,1)S(1)} %pack_first.1.first), custom_call_target="tpu_custom_call" | custom-call | flops 67108864 | bytes 1048576 | tf_op jit(solution)/shard_map/pack_second_kernel/pallas_call | solution.py:248
  3.8 2.1 %collective-permute-start.3 = (bf16[512,128]{1,0:T(8,128)(2,1)S(1)}, bf16[512,128]{1,0:T(8,128)(2,1)S(1)}, u32[]{:S(2)}, u32[]{:S(2)}) collective-permute-start(bf16[512,128]{1,0:T(8,128)(2,1)S(1)} %get-tuple-element.16), channel_id=1, source_target_pairs={{0,5},{1,4},{4,8},{5,9},{8,12},{9,13},{12,14},{13,15},{14,10},{15,... | collective-permute-start | bytes 393224 | tf_op jit(solution)/shard_map/ppermute | solution.py:267
  5.9 0.3 %collective-permute-start.1 = (bf16[512,128]{1,0:T(8,128)(2,1)S(1)}, bf16[512,128]{1,0:T(8,128)(2,1)S(1)}, u32[]{:S(2)}, u32[]{:S(2)}) collective-permute-start(bf16[512,128]{1,0:T(8,128)(2,1)S(1)} %get-tuple-element.16), channel_id=1, source_target_pairs={{0,3},{1,2},{4,0},{5,1},{8,4},{9,5},{12,9},{13,8},{14,13},{15,12},... | collective-permute-start | bytes 393224 | tf_op jit(solution)/shard_map/ppermute | solution.py:267
  6.2 1.2 %collective-permute-done.2.prev_a = bf16[528,128]{1,0:T(8,128)(2,1)S(1)} collective-permute-done((bf16[528,128]{1,0:T(8,128)(2,1)S(1)}, bf16[528,128]{1,0:T(8,128)(2,1)S(1)}, u32[]{:S(2)}, u32[]{:S(2)}) %collective-permute-start.2) | collective-permute-done | bytes 135200 | tf_op jit(solution)/shard_map/ppermute | solution.py:267
  7.4 2.5 %collective-permute-start.5 = (bf16[528,128]{1,0:T(8,128)(2,1)S(1)}, bf16[528,128]{1,0:T(8,128)(2,1)S(1)}, u32[]{:S(2)}, u32[]{:S(2)}) collective-permute-start(bf16[528,128]{1,0:T(8,128)(2,1)S(1)} %collective-permute-done.2.prev_a), channel_id=1, source_target_pairs={{0,4},{1,5},{4,8},{5,9},{8,12},{9,13},{12,14},{13,15},{14,10},{15,... | collective-permute-start | bytes 405512 | tf_op jit(solution)/shard_map/ppermute | solution.py:267
  9.9 0.0 collective-permute-done.succ_a
  9.9 0.0 collective-permute-start.6
  9.9 0.3 %collective-permute-done.3.prev_b = bf16[512,128]{1,0:T(8,128)(2,1)S(1)} collective-permute-done((bf16[512,128]{1,0:T(8,128)(2,1)S(1)}, bf16[512,128]{1,0:T(8,128)(2,1)S(1)}, u32[]{:S(2)}, u32[]{:S(2)}) %collective-permute-start.3) | collective-permute-done | bytes 131104 | tf_op jit(solution)/shard_map/ppermute | solution.py:267
  10.2 2.5 %collective-permute-start.7 = (bf16[512,128]{1,0:T(8,128)(2,1)S(1)}, bf16[512,128]{1,0:T(8,128)(2,1)S(1)}, u32[]{:S(2)}, u32[]{:S(2)}) collective-permute-start(bf16[512,128]{1,0:T(8,128)(2,1)S(1)} %collective-permute-done.3.prev_b), channel_id=1, source_target_pairs={{0,4},{1,5},{4,8},{5,9},{8,12},{9,13},{12,14},{13,15},{14,10},{15,... | collective-permute-start | bytes 393224 | tf_op jit(solution)/shard_map/ppermute | solution.py:267
  12.7 0.0 collective-permute-done.1.succ_b
  12.7 0.0 collective-permute-start.8
  12.7 0.4 %near_kernel.1 = (f32[1,256]{1,0:T(1,128)S(1)}, bf16[3,1040,128]{2,1,0:T(8,128)(2,1)S(1)}) custom-call(bf16[1040,128]{1,0:T(8,128)(2,1)S(1)} %get-tuple-element.15.own, bf16[528,128]{1,0:T(8,128)(2,1)S(1)} %collective-permute-done.succ_a, bf16[512,128]{1,0:T(8,128)(2,1)S(1)} %collective-permute-done.1.succ_b, ...), custom_call_target="tpu_custom_call" | custom-call | flops 67108864 | bytes 1048576 | tf_op jit(solution)/shard_map/near_kernel/pallas_call | solution.py:248
  13.1 0.1 collective-permute-start.4
  13.2 0.1 collective-permute-done.5.back_a
  13.3 2.1 %collective-permute-done.6.ahead_a = bf16[528,128]{1,0:T(8,128)(2,1)S(1)} collective-permute-done((bf16[528,128]{1,0:T(8,128)(2,1)S(1)}, bf16[528,128]{1,0:T(8,128)(2,1)S(1)}, u32[]{:S(2)}, u32[]{:S(2)}) %collective-permute-start.6) | collective-permute-done | bytes 135200 | tf_op jit(solution)/shard_map/ppermute | solution.py:267
  15.4 0.6 %far_first_kernel.1.found = f32[1,256]{1,0:T(1,128)S(1)} custom-call(bf16[3,1040,128]{2,1,0:T(8,128)(2,1)S(1)} %get-tuple-element.18.bundle, bf16[528,128]{1,0:T(8,128)(2,1)S(1)} %collective-permute-done.5.back_a, bf16[528,128]{1,0:T(8,128)(2,1)S(1)} %collective-permute-done.6.ahead_a), custom_call_target="tpu_custom_call" | custom-call | flops 13421772800 | bytes 1048576 | tf_op jit(solution)/shard_map/far_first_kernel/pallas_call | solution.py:248
  16.0 0.0 collective-permute-done.7.back_b
  16.0 0.0 collective-permute-done.4.others
  16.0 0.6 %far_back_kernel.1 = (f32[1,256]{1,0:T(1,128)S(1)}, f32[1,128]{1,0:T(1,128)S(1)}, bf16[1040,128]{1,0:T(8,128)(2,1)S(1)}) custom-call(bf16[3,1040,128]{2,1,0:T(8,128)(2,1)S(1)} %get-tuple-element.18.bundle, bf16[3,1040,128]{2,1,0:T(8,128)(2,1)S(1)} %collective-permute-done.4.others, bf16[528,128]{1,0:T(8,128)(2,1)S(1)} %collective-permute-done.5.back_a, ...), custom_call_target="tpu_custom_call" | custom-call | flops 134217728 | bytes 1048576 | tf_op jit(solution)/shard_map/far_back_kernel/pallas_call | solution.py:248
  16.6 1.5 %collective-permute-done.8.ahead_b = bf16[512,128]{1,0:T(8,128)(2,1)S(1)} collective-permute-done((bf16[512,128]{1,0:T(8,128)(2,1)S(1)}, bf16[512,128]{1,0:T(8,128)(2,1)S(1)}, u32[]{:S(2)}, u32[]{:S(2)}) %collective-permute-start.8) | collective-permute-done | bytes 131104 | tf_op jit(solution)/shard_map/ppermute | solution.py:267
  18.1 0.5 %far_last_kernel.1 = (f32[1,256]{1,0:T(1,128)S(1)}, f32[1,256]{1,0:T(1,128)S(1)}) custom-call(bf16[3,1040,128]{2,1,0:T(8,128)(2,1)S(1)} %get-tuple-element.18.bundle, bf16[3,1040,128]{2,1,0:T(8,128)(2,1)S(1)} %collective-permute-done.4.others, bf16[1040,128]{1,0:T(8,128)(2,1)S(1)} %get-tuple-element.19.back, ...), custom_call_target="tpu_custom_call" | custom-call | flops 335544320 | bytes 1048576 | tf_op jit(solution)/shard_map/far_last_kernel/pallas_call | solution.py:248
  18.6 1.5 %collective-permute-start.9 = (f32[1,256]{1,0:T(1,128)S(1)}, f32[1,256]{1,0:T(1,128)S(1)}, u32[]{:S(2)}, u32[]{:S(2)}) collective-permute-start(f32[1,256]{1,0:T(1,128)S(1)} %get-tuple-element.23), channel_id=1, source_target_pairs={{0,6},{1,7},{4,3},{5,2},{8,1},{9,0},{12,4},{13,5},{14,8},{15,9},{1... | collective-permute-start | bytes 3080 | tf_op jit(solution)/shard_map/ppermute | solution.py:267
  20.0 1.5 %collective-permute-start.10 = (f32[1,256]{1,0:T(1,128)S(1)}, f32[1,256]{1,0:T(1,128)S(1)}, u32[]{:S(2)}, u32[]{:S(2)}) collective-permute-start(f32[1,256]{1,0:T(1,128)S(1)} %get-tuple-element.24), channel_id=1, source_target_pairs={{0,8},{1,9},{4,13},{5,12},{8,15},{9,14},{12,11},{13,10},{14,7},{15... | collective-permute-start | bytes 3080 | tf_op jit(solution)/shard_map/ppermute | solution.py:267
  21.6 0.6 %own_kernel.1 = f32[1,256]{1,0:T(1,128)S(1)} custom-call(bf16[1040,128]{1,0:T(8,128)(2,1)S(1)} %get-tuple-element.15.own, bf16[3,1040,128]{2,1,0:T(8,128)(2,1)S(1)} %collective-permute-done.4.others, bf16[1040,128]{1,0:T(8,128)(2,1)S(1)} %get-tuple-element.19.back, bf16[528,128]{1,0:T(8,128)(2,1)S(1)} %collective-permute-done.6.ahead_a, ...), custom_call_target="tpu_custom_call" | custom-call | flops 335544320 | bytes 1048576 | tf_op jit(solution)/shard_map/own_kernel/pallas_call | solution.py:248
  22.1 0.4 %collective-permute-done.9 = f32[1,256]{1,0:T(1,128)S(1)} collective-permute-done((f32[1,256]{1,0:T(1,128)S(1)}, f32[1,256]{1,0:T(1,128)S(1)}, u32[]{:S(2)}, u32[]{:S(2)}) %collective-permute-start.9) | collective-permute-done | bytes 1056 | tf_op jit(solution)/shard_map/ppermute | solution.py:267
  22.5 1.4 %collective-permute-done.10 = f32[1,256]{1,0:T(1,128)S(1)} collective-permute-done((f32[1,256]{1,0:T(1,128)S(1)}, f32[1,256]{1,0:T(1,128)S(1)}, u32[]{:S(2)}, u32[]{:S(2)}) %collective-permute-start.10) | collective-permute-done | bytes 1056 | tf_op jit(solution)/shard_map/ppermute | solution.py:267
  23.9 0.6 %maximum_maximum_fusion = f32[1,256]{1,0:T(1,128)} fusion(f32[1,256]{1,0:T(1,128)S(1)} %own_kernel.1, f32[1,256]{1,0:T(1,128)S(1)} %collective-permute-done.9, f32[1,256]{1,0:T(1,128)S(1)} %collective-permute-done.10), kind=kLoop, calls=%fused_computation | loop fusion | flops 512 | bytes 4096 | tf_op jit(solution)/shard_map/max | solution.py:318
Async XLA Ops:
  0.0 3.4 %copy-start = (bf16[256,512]{1,0:T(8,128)(2,1)S(1)}, bf16[256,512]{1,0:T(8,128)(2,1)}, u32[]{:S(2)}) copy-start(bf16[256,512]{1,0:T(8,128)(2,1)} %embeds.3) | copy-start | bytes 786436
  0.9 6.5 %collective-permute-start.2 = (bf16[528,128]{1,0:T(8,128)(2,1)S(1)}, bf16[528,128]{1,0:T(8,128)(2,1)S(1)}, u32[]{:S(2)}, u32[]{:S(2)}) collective-permute-start(bf16[528,128]{1,0:T(8,128)(2,1)S(1)} %pack_first.1.first), channel_id=1, source_target_pairs={{0,5},{1,4},{4,8},{5,9},{8,12},{9,13},{12,14},{13,15},{14,10},{15,... | collective-permute-start | bytes 405512 | tf_op jit(solution)/shard_map/ppermute | solution.py:267
  3.4 6.5 %collective-permute-start = (bf16[528,128]{1,0:T(8,128)(2,1)S(1)}, bf16[528,128]{1,0:T(8,128)(2,1)S(1)}, u32[]{:S(2)}, u32[]{:S(2)}) collective-permute-start(bf16[528,128]{1,0:T(8,128)(2,1)S(1)} %pack_first.1.first), channel_id=1, source_target_pairs={{0,3},{1,2},{4,0},{5,1},{8,4},{9,5},{12,9},{13,8},{14,13},{15,12},... | collective-permute-start | bytes 405512 | tf_op jit(solution)/shard_map/ppermute | solution.py:267
  3.8 6.4 %collective-permute-start.3 = (bf16[512,128]{1,0:T(8,128)(2,1)S(1)}, bf16[512,128]{1,0:T(8,128)(2,1)S(1)}, u32[]{:S(2)}, u32[]{:S(2)}) collective-permute-start(bf16[512,128]{1,0:T(8,128)(2,1)S(1)} %get-tuple-element.16), channel_id=1, source_target_pairs={{0,5},{1,4},{4,8},{5,9},{8,12},{9,13},{12,14},{13,15},{14,10},{15,... | collective-permute-start | bytes 393224 | tf_op jit(solution)/shard_map/ppermute | solution.py:267
  5.9 6.8 %collective-permute-start.1 = (bf16[512,128]{1,0:T(8,128)(2,1)S(1)}, bf16[512,128]{1,0:T(8,128)(2,1)S(1)}, u32[]{:S(2)}, u32[]{:S(2)}) collective-permute-start(bf16[512,128]{1,0:T(8,128)(2,1)S(1)} %get-tuple-element.16), channel_id=1, source_target_pairs={{0,3},{1,2},{4,0},{5,1},{8,4},{9,5},{12,9},{13,8},{14,13},{15,12},... | collective-permute-start | bytes 393224 | tf_op jit(solution)/shard_map/ppermute | solution.py:267
  7.4 5.9 %collective-permute-start.5 = (bf16[528,128]{1,0:T(8,128)(2,1)S(1)}, bf16[528,128]{1,0:T(8,128)(2,1)S(1)}, u32[]{:S(2)}, u32[]{:S(2)}) collective-permute-start(bf16[528,128]{1,0:T(8,128)(2,1)S(1)} %collective-permute-done.2.prev_a), channel_id=1, source_target_pairs={{0,4},{1,5},{4,8},{5,9},{8,12},{9,13},{12,14},{13,15},{14,10},{15,... | collective-permute-start | bytes 405512 | tf_op jit(solution)/shard_map/ppermute | solution.py:267
  9.9 5.5 %collective-permute-start.6 = (bf16[528,128]{1,0:T(8,128)(2,1)S(1)}, bf16[528,128]{1,0:T(8,128)(2,1)S(1)}, u32[]{:S(2)}, u32[]{:S(2)}) collective-permute-start(bf16[528,128]{1,0:T(8,128)(2,1)S(1)} %collective-permute-done.succ_a), channel_id=1, source_target_pairs={{0,2},{1,3},{4,0},{5,1},{8,4},{9,5},{12,8},{13,9},{14,12},{15,13},... | collective-permute-start | bytes 405512 | tf_op jit(solution)/shard_map/ppermute | solution.py:267
  10.2 5.8 %collective-permute-start.7 = (bf16[512,128]{1,0:T(8,128)(2,1)S(1)}, bf16[512,128]{1,0:T(8,128)(2,1)S(1)}, u32[]{:S(2)}, u32[]{:S(2)}) collective-permute-start(bf16[512,128]{1,0:T(8,128)(2,1)S(1)} %collective-permute-done.3.prev_b), channel_id=1, source_target_pairs={{0,4},{1,5},{4,8},{5,9},{8,12},{9,13},{12,14},{13,15},{14,10},{15,... | collective-permute-start | bytes 393224 | tf_op jit(solution)/shard_map/ppermute | solution.py:267
  12.7 5.4 %collective-permute-start.8 = (bf16[512,128]{1,0:T(8,128)(2,1)S(1)}, bf16[512,128]{1,0:T(8,128)(2,1)S(1)}, u32[]{:S(2)}, u32[]{:S(2)}) collective-permute-start(bf16[512,128]{1,0:T(8,128)(2,1)S(1)} %collective-permute-done.1.succ_b), channel_id=1, source_target_pairs={{0,2},{1,3},{4,0},{5,1},{8,4},{9,5},{12,8},{13,9},{14,12},{15,13},... | collective-permute-start | bytes 393224 | tf_op jit(solution)/shard_map/ppermute | solution.py:267
  13.1 2.9 %collective-permute-start.4 = (bf16[3,1040,128]{2,1,0:T(8,128)(2,1)S(1)}, bf16[3,1040,128]{2,1,0:T(8,128)(2,1)S(1)}, u32[]{:S(2)}, u32[]{:S(2)}) collective-permute-start(bf16[3,1040,128]{2,1,0:T(8,128)(2,1)S(1)} %get-tuple-element.18.bundle), channel_id=1, source_target_pairs={{0,1},{1,0},{4,5},{5,4},{8,9},{9,8},{12,13},{13,12},{14,15},{15,14... | collective-permute-start | bytes 2396168 | tf_op jit(solution)/shard_map/ppermute | solution.py:267
  18.6 4.0 %collective-permute-start.9 = (f32[1,256]{1,0:T(1,128)S(1)}, f32[1,256]{1,0:T(1,128)S(1)}, u32[]{:S(2)}, u32[]{:S(2)}) collective-permute-start(f32[1,256]{1,0:T(1,128)S(1)} %get-tuple-element.23), channel_id=1, source_target_pairs={{0,6},{1,7},{4,3},{5,2},{8,1},{9,0},{12,4},{13,5},{14,8},{15,9},{1... | collective-permute-start | bytes 3080 | tf_op jit(solution)/shard_map/ppermute | solution.py:267
  20.0 3.9 %collective-permute-start.10 = (f32[1,256]{1,0:T(1,128)S(1)}, f32[1,256]{1,0:T(1,128)S(1)}, u32[]{:S(2)}, u32[]{:S(2)}) collective-permute-start(f32[1,256]{1,0:T(1,128)S(1)} %get-tuple-element.24), channel_id=1, source_target_pairs={{0,8},{1,9},{4,13},{5,12},{8,15},{9,14},{12,11},{13,10},{14,7},{15... | collective-permute-start | bytes 3080 | tf_op jit(solution)/shard_map/ppermute | solution.py:267

commit v29 on v23

--- a/solution.py
+++ b/solution.py
@@ -166,13 +166,12 @@
     bundle[2] = own[...]
 
 
-def far_first_kernel(own, bundle, back_a, ahead_a, self_best, found, mine):
+def far_first_kernel(own, bundle, back_a, ahead_a, found):
     rows = found.shape[1]
     queries = joined(first_half(back_a, rows), first_half(ahead_a, rows))
     own = packed(own, rows)
     near = [packed(bundle.at[at], rows) for at in range(2)]
     found[...] = best_of(queries, queries, *near, own)
-    mine[...] = jnp.maximum(self_best[...], best_of(own, *near))
 
 
 def far_back_kernel(own, bundle, others, back_a, ahead_a, back_b, found, *refs):
@@ -205,9 +204,10 @@
     to_back[...] = jnp.maximum(back_found[...], best)
 
 
-def own_kernel(own, others, back, ahead_a, ahead_b, near, mine):
+def own_kernel(own, bundle, others, back, ahead_a, ahead_b, near, mine):
     rows = mine.shape[1]
-    keys = [packed(ref, rows) for ref in (others.at[at] for at in range(3))]
+    keys = [packed(others.at[at], rows) for at in range(3)]
+    keys += [packed(bundle.at[at], rows) for at in range(2)]
     keys += [packed(back, rows), whole(ahead_a, ahead_b, rows)]
     mine[...] = jnp.maximum(near[...], best_of(packed(own, rows), *keys))
 
@@ -306,9 +306,7 @@
         bundle_kernel, [own, succ_a, succ_b, prev_a, prev_b], [bundle_shape], BUNDLE_COST
     )
     others = send(bundle, "sibling")
-    found, mine = kernel_call(
-        far_first_kernel, [own, bundle, back_a, ahead_a, mine], [line] * 2, FIRST_COST
-    )
+    (found,) = kernel_call(far_first_kernel, [own, bundle, back_a, ahead_a], [line], FIRST_COST)
     *found, back = kernel_call(
         far_back_kernel,
         [own, bundle, others, back_a, ahead_a, back_b, found],
@@ -319,7 +317,7 @@
     to_back, to_ahead = kernel_call(
         far_last_kernel, [own, bundle, others, *far, *found], [line] * 2, LAST_COST
     )
-    (mine,) = kernel_call(own_kernel, [own, others, *far, mine], [line], 5)
+    (mine,) = kernel_call(own_kernel, [own, bundle, others, *far, mine], [line], 5)
     best = jnp.maximum(
         mine, jnp.maximum(send(to_back, "home_back"), send(to_ahead, "home_ahead"))
     )

time: 24.6 us -> 24.6 us (level)
  no operation moved by 1% of the time
where the time goes in v29:
time: 24.6 us; the launch traced here: 24.5 us
  starting transfers between devices  12.8 us (52%)
  waiting for transfers between devices  7.22 us (29%)
  Pallas kernels  3.77 us (15%)
  other arithmetic  0.57 us (2%)
    ppermute x11, starting transfers between devices, send(): return lax.ppermute(value, GROUP, perms[name])  12.8 us
    ppermute x11, waiting for transfers between devices, send(): return lax.ppermute(value, GROUP, perms[name])  7.22 us
    pallas_call x6, Pallas kernels, kernel_call(): pl.pallas_call(kernel, out_shape=outputs, in_specs=[vmem] * len(inputs),...  2.88 us
    pallas_call x1, Pallas kernels, on_ring(): pl.pallas_call(pack_first_kernel, out_shape=chunk(half, True), in_specs=[...  0.89 us
    max x1, other arithmetic, on_ring(): jnp.maximum(mine, jnp.maximum(send(to_back, 'home_back'), send(to_ahead,...  0.57 us
  transfers between devices with their start and end apart: 11, of which 7 were waited for; matrix products, arithmetic and copies ran while one was open for 0% of the time, Pallas kernels for 10%

profile of v29, /device:TPU:0, one launch (start us, length us, event | category | flops | bytes accessed | tf_op | source)
XLA Modules:
  0.0 24.5 jit_solution(14913505121099502519)
XLA Ops:
  0.0 0.0 copy-start
  0.0 0.9 %pack_first.1.first = bf16[528,128]{1,0:T(8,128)(2,1)S(1)} custom-call(bf16[256,512]{1,0:T(8,128)(2,1)} %embeds.3, s32[1,256]{1,0:T(1,128)} %bitcast.2), custom_call_target="tpu_custom_call" | custom-call | tf_op jit(solution)/shard_map/pack_first/pallas_call | solution.py:277
  0.9 2.5 %collective-permute-start.2 = (bf16[528,128]{1,0:T(8,128)(2,1)S(1)}, bf16[528,128]{1,0:T(8,128)(2,1)S(1)}, u32[]{:S(2)}, u32[]{:S(2)}) collective-permute-start(bf16[528,128]{1,0:T(8,128)(2,1)S(1)} %pack_first.1.first), channel_id=1, source_target_pairs={{0,5},{1,4},{4,8},{5,9},{8,12},{9,13},{12,14},{13,15},{14,10},{15,... | collective-permute-start | bytes 405512 | tf_op jit(solution)/shard_map/ppermute | solution.py:266
  3.4 0.0 collective-permute-start
  3.4 0.0 copy-done
  3.4 0.4 %pack_second_kernel.1 = (bf16[512,128]{1,0:T(8,128)(2,1)S(1)}, bf16[1040,128]{1,0:T(8,128)(2,1)S(1)}, f32[1,256]{1,0:T(1,128)S(1)}) custom-call(bf16[256,512]{1,0:T(8,128)(2,1)S(1)} %copy-done, bf16[528,128]{1,0:T(8,128)(2,1)S(1)} %pack_first.1.first), custom_call_target="tpu_custom_call" | custom-call | flops 67108864 | bytes 1048576 | tf_op jit(solution)/shard_map/pack_second_kernel/pallas_call | solution.py:247
  3.8 2.1 %collective-permute-start.3 = (bf16[512,128]{1,0:T(8,128)(2,1)S(1)}, bf16[512,128]{1,0:T(8,128)(2,1)S(1)}, u32[]{:S(2)}, u32[]{:S(2)}) collective-permute-start(bf16[512,128]{1,0:T(8,128)(2,1)S(1)} %get-tuple-element.14), channel_id=1, source_target_pairs={{0,5},{1,4},{4,8},{5,9},{8,12},{9,13},{12,14},{13,15},{14,10},{15,... | collective-permute-start | bytes 393224 | tf_op jit(solution)/shard_map/ppermute | solution.py:266
  5.9 0.3 %collective-permute-start.1 = (bf16[512,128]{1,0:T(8,128)(2,1)S(1)}, bf16[512,128]{1,0:T(8,128)(2,1)S(1)}, u32[]{:S(2)}, u32[]{:S(2)}) collective-permute-start(bf16[512,128]{1,0:T(8,128)(2,1)S(1)} %get-tuple-element.14), channel_id=1, source_target_pairs={{0,3},{1,2},{4,0},{5,1},{8,4},{9,5},{12,9},{13,8},{14,13},{15,12},... | collective-permute-start | bytes 393224 | tf_op jit(solution)/shard_map/ppermute | solution.py:266
  6.1 1.3 %collective-permute-done.2.refs_3_ = bf16[528,128]{1,0:T(8,128)(2,1)S(1)} collective-permute-done((bf16[528,128]{1,0:T(8,128)(2,1)S(1)}, bf16[528,128]{1,0:T(8,128)(2,1)S(1)}, u32[]{:S(2)}, u32[]{:S(2)}) %collective-permute-start.2) | collective-permute-done | bytes 135200 | tf_op jit(solution)/shard_map/ppermute | solution.py:266
  7.4 2.5 %collective-permute-start.5 = (bf16[528,128]{1,0:T(8,128)(2,1)S(1)}, bf16[528,128]{1,0:T(8,128)(2,1)S(1)}, u32[]{:S(2)}, u32[]{:S(2)}) collective-permute-start(bf16[528,128]{1,0:T(8,128)(2,1)S(1)} %collective-permute-done.2.refs_3_), channel_id=1, source_target_pairs={{0,4},{1,5},{4,8},{5,9},{8,12},{9,13},{12,14},{13,15},{14,10},{15,... | collective-permute-start | bytes 405512 | tf_op jit(solution)/shard_map/ppermute | solution.py:266
  9.9 0.0 collective-permute-done.refs_1_
  9.9 0.0 collective-permute-start.6
  9.9 0.3 %collective-permute-done.3.refs_4_ = bf16[512,128]{1,0:T(8,128)(2,1)S(1)} collective-permute-done((bf16[512,128]{1,0:T(8,128)(2,1)S(1)}, bf16[512,128]{1,0:T(8,128)(2,1)S(1)}, u32[]{:S(2)}, u32[]{:S(2)}) %collective-permute-start.3) | collective-permute-done | bytes 131104 | tf_op jit(solution)/shard_map/ppermute | solution.py:266
  10.2 2.5 %collective-permute-start.7 = (bf16[512,128]{1,0:T(8,128)(2,1)S(1)}, bf16[512,128]{1,0:T(8,128)(2,1)S(1)}, u32[]{:S(2)}, u32[]{:S(2)}) collective-permute-start(bf16[512,128]{1,0:T(8,128)(2,1)S(1)} %collective-permute-done.3.refs_4_), channel_id=1, source_target_pairs={{0,4},{1,5},{4,8},{5,9},{8,12},{9,13},{12,14},{13,15},{14,10},{15,... | collective-permute-start | bytes 393224 | tf_op jit(solution)/shard_map/ppermute | solution.py:266
  12.7 0.0 collective-permute-done.1.refs_2_
  12.7 0.0 collective-permute-start.8
  12.7 0.2 bundle_kernel.1.bundle
  12.8 0.1 collective-permute-start.4
  12.9 0.4 %collective-permute-done.5.back_a = bf16[528,128]{1,0:T(8,128)(2,1)S(1)} collective-permute-done((bf16[528,128]{1,0:T(8,128)(2,1)S(1)}, bf16[528,128]{1,0:T(8,128)(2,1)S(1)}, u32[]{:S(2)}, u32[]{:S(2)}) %collective-permute-start.5) | collective-permute-done | bytes 135200 | tf_op jit(solution)/shard_map/ppermute | solution.py:266
  13.3 2.1 %collective-permute-done.6.ahead_a = bf16[528,128]{1,0:T(8,128)(2,1)S(1)} collective-permute-done((bf16[528,128]{1,0:T(8,128)(2,1)S(1)}, bf16[528,128]{1,0:T(8,128)(2,1)S(1)}, u32[]{:S(2)}, u32[]{:S(2)}) %collective-permute-start.6) | collective-permute-done | bytes 135200 | tf_op jit(solution)/shard_map/ppermute | solution.py:266
  15.4 0.6 %far_first_kernel.1.found = f32[1,256]{1,0:T(1,128)S(1)} custom-call(bf16[1040,128]{1,0:T(8,128)(2,1)S(1)} %get-tuple-element.13.refs_0_.own, bf16[3,1040,128]{2,1,0:T(8,128)(2,1)S(1)} %bundle_kernel.1.bundle, bf16[528,128]{1,0:T(8,128)(2,1)S(1)} %collective-permute-done.5.back_a, bf16[528,128]{1,0:T(8,128)(2,1)S(1)} %collective-permute-done.6.ahead_a), custom_call_target="tpu_custom_call" | custom-call | flops 13421772800 | bytes 1048576 | tf_op jit(solution)/shard_map/far_first_kernel/pallas_call | solution.py:247
  16.0 0.0 collective-permute-done.7.back_b
  16.0 0.0 collective-permute-done.4.others
  16.0 0.6 %far_back_kernel.1 = (f32[1,256]{1,0:T(1,128)S(1)}, f32[1,128]{1,0:T(1,128)S(1)}, bf16[1040,128]{1,0:T(8,128)(2,1)S(1)}) custom-call(bf16[1040,128]{1,0:T(8,128)(2,1)S(1)} %get-tuple-element.13.refs_0_.own, bf16[3,1040,128]{2,1,0:T(8,128)(2,1)S(1)} %bundle_kernel.1.bundle, bf16[3,1040,128]{2,1,0:T(8,128)(2,1)S(1)} %collective-permute-done.4.others, ...), custom_call_target="tpu_custom_call" | custom-call | flops 134217728 | bytes 1048576 | tf_op jit(solution)/shard_map/far_back_kernel/pallas_call | solution.py:247
  16.6 1.5 %collective-permute-done.8.ahead_b = bf16[512,128]{1,0:T(8,128)(2,1)S(1)} collective-permute-done((bf16[512,128]{1,0:T(8,128)(2,1)S(1)}, bf16[512,128]{1,0:T(8,128)(2,1)S(1)}, u32[]{:S(2)}, u32[]{:S(2)}) %collective-permute-start.8) | collective-permute-done | bytes 131104 | tf_op jit(solution)/shard_map/ppermute | solution.py:266
  18.1 0.5 %far_last_kernel.1 = (f32[1,256]{1,0:T(1,128)S(1)}, f32[1,256]{1,0:T(1,128)S(1)}) custom-call(bf16[1040,128]{1,0:T(8,128)(2,1)S(1)} %get-tuple-element.13.refs_0_.own, bf16[3,1040,128]{2,1,0:T(8,128)(2,1)S(1)} %bundle_kernel.1.bundle, bf16[3,1040,128]{2,1,0:T(8,128)(2,1)S(1)} %collective-permute-done.4.others, bf16[1040,128]{1,0:T(8,128)(2,1)S(1)} %get-tuple-element.15.back, ...), custom_call_target="tpu_custom_call" | custom-call | flops 335544320 | bytes 1048576 | tf_op jit(solution)/shard_map/far_last_kernel/pallas_call | solution.py:247
  18.6 1.5 %collective-permute-start.9 = (f32[1,256]{1,0:T(1,128)S(1)}, f32[1,256]{1,0:T(1,128)S(1)}, u32[]{:S(2)}, u32[]{:S(2)}) collective-permute-start(f32[1,256]{1,0:T(1,128)S(1)} %get-tuple-element.19), channel_id=1, source_target_pairs={{0,6},{1,7},{4,3},{5,2},{8,1},{9,0},{12,4},{13,5},{14,8},{15,9},{1... | collective-permute-start | bytes 3080 | tf_op jit(solution)/shard_map/ppermute | solution.py:266
  20.0 1.5 %collective-permute-start.10 = (f32[1,256]{1,0:T(1,128)S(1)}, f32[1,256]{1,0:T(1,128)S(1)}, u32[]{:S(2)}, u32[]{:S(2)}) collective-permute-start(f32[1,256]{1,0:T(1,128)S(1)} %get-tuple-element.20), channel_id=1, source_target_pairs={{0,8},{1,9},{4,13},{5,12},{8,15},{9,14},{12,11},{13,10},{14,7},{15... | collective-permute-start | bytes 3080 | tf_op jit(solution)/shard_map/ppermute | solution.py:266
  21.6 0.7 %own_kernel.1 = f32[1,256]{1,0:T(1,128)S(1)} custom-call(bf16[1040,128]{1,0:T(8,128)(2,1)S(1)} %get-tuple-element.13.refs_0_.own, bf16[3,1040,128]{2,1,0:T(8,128)(2,1)S(1)} %bundle_kernel.1.bundle, bf16[3,1040,128]{2,1,0:T(8,128)(2,1)S(1)} %collective-permute-done.4.others, bf16[1040,128]{1,0:T(8,128)(2,1)S(1)} %get-tuple-element.15.back, ...), custom_call_target="tpu_custom_call" | custom-call | flops 335544320 | bytes 1048576 | tf_op jit(solution)/shard_map/own_kernel/pallas_call | solution.py:247
  22.3 0.3 %collective-permute-done.9 = f32[1,256]{1,0:T(1,128)S(1)} collective-permute-done((f32[1,256]{1,0:T(1,128)S(1)}, f32[1,256]{1,0:T(1,128)S(1)}, u32[]{:S(2)}, u32[]{:S(2)}) %collective-permute-start.9) | collective-permute-done | bytes 1056 | tf_op jit(solution)/shard_map/ppermute | solution.py:266
  22.5 1.4 %collective-permute-done.10 = f32[1,256]{1,0:T(1,128)S(1)} collective-permute-done((f32[1,256]{1,0:T(1,128)S(1)}, f32[1,256]{1,0:T(1,128)S(1)}, u32[]{:S(2)}, u32[]{:S(2)}) %collective-permute-start.10) | collective-permute-done | bytes 1056 | tf_op jit(solution)/shard_map/ppermute | solution.py:266
  23.9 0.6 %maximum_maximum_fusion = f32[1,256]{1,0:T(1,128)} fusion(f32[1,256]{1,0:T(1,128)S(1)} %own_kernel.1, f32[1,256]{1,0:T(1,128)S(1)} %collective-permute-done.9, f32[1,256]{1,0:T(1,128)S(1)} %collective-permute-done.10), kind=kLoop, calls=%fused_computation | loop fusion | flops 512 | bytes 4096 | tf_op jit(solution)/shard_map/max | solution.py:321
Async XLA Ops:
  0.0 3.4 %copy-start = (bf16[256,512]{1,0:T(8,128)(2,1)S(1)}, bf16[256,512]{1,0:T(8,128)(2,1)}, u32[]{:S(2)}) copy-start(bf16[256,512]{1,0:T(8,128)(2,1)} %embeds.3) | copy-start | bytes 786436
  0.9 6.5 %collective-permute-start.2 = (bf16[528,128]{1,0:T(8,128)(2,1)S(1)}, bf16[528,128]{1,0:T(8,128)(2,1)S(1)}, u32[]{:S(2)}, u32[]{:S(2)}) collective-permute-start(bf16[528,128]{1,0:T(8,128)(2,1)S(1)} %pack_first.1.first), channel_id=1, source_target_pairs={{0,5},{1,4},{4,8},{5,9},{8,12},{9,13},{12,14},{13,15},{14,10},{15,... | collective-permute-start | bytes 405512 | tf_op jit(solution)/shard_map/ppermute | solution.py:266
  3.4 6.5 %collective-permute-start = (bf16[528,128]{1,0:T(8,128)(2,1)S(1)}, bf16[528,128]{1,0:T(8,128)(2,1)S(1)}, u32[]{:S(2)}, u32[]{:S(2)}) collective-permute-start(bf16[528,128]{1,0:T(8,128)(2,1)S(1)} %pack_first.1.first), channel_id=1, source_target_pairs={{0,3},{1,2},{4,0},{5,1},{8,4},{9,5},{12,9},{13,8},{14,13},{15,12},... | collective-permute-start | bytes 405512 | tf_op jit(solution)/shard_map/ppermute | solution.py:266
  3.8 6.4 %collective-permute-start.3 = (bf16[512,128]{1,0:T(8,128)(2,1)S(1)}, bf16[512,128]{1,0:T(8,128)(2,1)S(1)}, u32[]{:S(2)}, u32[]{:S(2)}) collective-permute-start(bf16[512,128]{1,0:T(8,128)(2,1)S(1)} %get-tuple-element.14), channel_id=1, source_target_pairs={{0,5},{1,4},{4,8},{5,9},{8,12},{9,13},{12,14},{13,15},{14,10},{15,... | collective-permute-start | bytes 393224 | tf_op jit(solution)/shard_map/ppermute | solution.py:266
  5.9 6.8 %collective-permute-start.1 = (bf16[512,128]{1,0:T(8,128)(2,1)S(1)}, bf16[512,128]{1,0:T(8,128)(2,1)S(1)}, u32[]{:S(2)}, u32[]{:S(2)}) collective-permute-start(bf16[512,128]{1,0:T(8,128)(2,1)S(1)} %get-tuple-element.14), channel_id=1, source_target_pairs={{0,3},{1,2},{4,0},{5,1},{8,4},{9,5},{12,9},{13,8},{14,13},{15,12},... | collective-permute-start | bytes 393224 | tf_op jit(solution)/shard_map/ppermute | solution.py:266
  7.4 5.9 %collective-permute-start.5 = (bf16[528,128]{1,0:T(8,128)(2,1)S(1)}, bf16[528,128]{1,0:T(8,128)(2,1)S(1)}, u32[]{:S(2)}, u32[]{:S(2)}) collective-permute-start(bf16[528,128]{1,0:T(8,128)(2,1)S(1)} %collective-permute-done.2.refs_3_), channel_id=1, source_target_pairs={{0,4},{1,5},{4,8},{5,9},{8,12},{9,13},{12,14},{13,15},{14,10},{15,... | collective-permute-start | bytes 405512 | tf_op jit(solution)/shard_map/ppermute | solution.py:266
  9.9 5.5 %collective-permute-start.6 = (bf16[528,128]{1,0:T(8,128)(2,1)S(1)}, bf16[528,128]{1,0:T(8,128)(2,1)S(1)}, u32[]{:S(2)}, u32[]{:S(2)}) collective-permute-start(bf16[528,128]{1,0:T(8,128)(2,1)S(1)} %collective-permute-done.refs_1_), channel_id=1, source_target_pairs={{0,2},{1,3},{4,0},{5,1},{8,4},{9,5},{12,8},{13,9},{14,12},{15,13},... | collective-permute-start | bytes 405512 | tf_op jit(solution)/shard_map/ppermute | solution.py:266
  10.2 5.8 %collective-permute-start.7 = (bf16[512,128]{1,0:T(8,128)(2,1)S(1)}, bf16[512,128]{1,0:T(8,128)(2,1)S(1)}, u32[]{:S(2)}, u32[]{:S(2)}) collective-permute-start(bf16[512,128]{1,0:T(8,128)(2,1)S(1)} %collective-permute-done.3.refs_4_), channel_id=1, source_target_pairs={{0,4},{1,5},{4,8},{5,9},{8,12},{9,13},{12,14},{13,15},{14,10},{15,... | collective-permute-start | bytes 393224 | tf_op jit(solution)/shard_map/ppermute | solution.py:266
  12.7 5.4 %collective-permute-start.8 = (bf16[512,128]{1,0:T(8,128)(2,1)S(1)}, bf16[512,128]{1,0:T(8,128)(2,1)S(1)}, u32[]{:S(2)}, u32[]{:S(2)}) collective-permute-start(bf16[512,128]{1,0:T(8,128)(2,1)S(1)} %collective-permute-done.1.refs_2_), channel_id=1, source_target_pairs={{0,2},{1,3},{4,0},{5,1},{8,4},{9,5},{12,8},{13,9},{14,12},{15,13},... | collective-permute-start | bytes 393224 | tf_op jit(solution)/shard_map/ppermute | solution.py:266
  12.8 3.2 %collective-permute-start.4 = (bf16[3,1040,128]{2,1,0:T(8,128)(2,1)S(1)}, bf16[3,1040,128]{2,1,0:T(8,128)(2,1)S(1)}, u32[]{:S(2)}, u32[]{:S(2)}) collective-permute-start(bf16[3,1040,128]{2,1,0:T(8,128)(2,1)S(1)} %bundle_kernel.1.bundle), channel_id=1, source_target_pairs={{0,1},{1,0},{4,5},{5,4},{8,9},{9,8},{12,13},{13,12},{14,15},{15,14... | collective-permute-start | bytes 2396168 | tf_op jit(solution)/shard_map/ppermute | solution.py:266
  18.6 4.0 %collective-permute-start.9 = (f32[1,256]{1,0:T(1,128)S(1)}, f32[1,256]{1,0:T(1,128)S(1)}, u32[]{:S(2)}, u32[]{:S(2)}) collective-permute-start(f32[1,256]{1,0:T(1,128)S(1)} %get-tuple-element.19), channel_id=1, source_target_pairs={{0,6},{1,7},{4,3},{5,2},{8,1},{9,0},{12,4},{13,5},{14,8},{15,9},{1... | collective-permute-start | bytes 3080 | tf_op jit(solution)/shard_map/ppermute | solution.py:266
  20.0 3.9 %collective-permute-start.10 = (f32[1,256]{1,0:T(1,128)S(1)}, f32[1,256]{1,0:T(1,128)S(1)}, u32[]{:S(2)}, u32[]{:S(2)}) collective-permute-start(f32[1,256]{1,0:T(1,128)S(1)} %get-tuple-element.20), channel_id=1, source_target_pairs={{0,8},{1,9},{4,13},{5,12},{8,15},{9,14},{12,11},{13,10},{14,7},{15... | collective-permute-start | bytes 3080 | tf_op jit(solution)/shard_map/ppermute | solution.py:266

commit v30 on v29

--- a/solution.py
+++ b/solution.py
@@ -226,10 +226,10 @@
         ]
 
     def from_prev(place, core):
-        return core ^ (place % chips in (0, 1))
+        return core ^ (place % chips in (0, chips - 1))
 
     def from_next(place, core):
-        return core ^ (place % chips not in (0, 1))
+        return core ^ (place % chips not in (0, chips - 1))
 
     return {
         "sibling": perm(lambda p, k: (p, 1 - k)),

time: 24.6 us -> 24.9 us (1.012)
  waiting for transfers between devices: 7.22 us -> 8.17 us
  starting transfers between devices: 12.8 us -> 12.2 us
    ppermute x11, waiting for transfers between devices: 7.22 us -> 8.17 us  [send(): return lax.ppermute(value, GROUP, perms[name])]
    ppermute x11, starting transfers between devices: 12.8 us -> 12.2 us  [send(): return lax.ppermute(value, GROUP, perms[name])]
  transfers between devices with their start and end apart: 11 -> 11, of which waited for: 7 -> 8; matrix products, arithmetic and copies ran while one was open for 0% -> 0% of each run, Pallas kernels for 10% -> 10%
where the time goes in v30:
time: 24.9 us; the launch traced here: 24.8 us
  starting transfers between devices  12.2 us (49%)
  waiting for transfers between devices  8.17 us (33%)
  Pallas kernels  3.78 us (15%)
  other arithmetic  0.57 us (2%)
    ppermute x11, starting transfers between devices, send(): return lax.ppermute(value, GROUP, perms[name])  12.2 us
    ppermute x11, waiting for transfers between devices, send(): return lax.ppermute(value, GROUP, perms[name])  8.17 us
    pallas_call x6, Pallas kernels, kernel_call(): pl.pallas_call(kernel, out_shape=outputs, in_specs=[vmem] * len(inputs),...  2.88 us
    pallas_call x1, Pallas kernels, on_ring(): pl.pallas_call(pack_first_kernel, out_shape=chunk(half, True), in_specs=[...  0.89 us
    max x1, other arithmetic, on_ring(): jnp.maximum(mine, jnp.maximum(send(to_back, 'home_back'), send(to_ahead,...  0.57 us
  transfers between devices with their start and end apart: 11, of which 8 were waited for; matrix products, arithmetic and copies ran while one was open for 0% of the time, Pallas kernels for 10%

profile of v30, /device:TPU:0, one launch (start us, length us, event | category | flops | bytes accessed | tf_op | source)
XLA Modules:
  0.0 24.8 jit_solution(12434120829820228192)
XLA Ops:
  0.0 0.0 copy-start
  0.0 0.9 %pack_first.1.first = bf16[528,128]{1,0:T(8,128)(2,1)S(1)} custom-call(bf16[256,512]{1,0:T(8,128)(2,1)} %embeds.3, s32[1,256]{1,0:T(1,128)} %bitcast.2), custom_call_target="tpu_custom_call" | custom-call | tf_op jit(solution)/shard_map/pack_first/pallas_call | solution.py:277
  0.9 3.1 %collective-permute-start.2 = (bf16[528,128]{1,0:T(8,128)(2,1)S(1)}, bf16[528,128]{1,0:T(8,128)(2,1)S(1)}, u32[]{:S(2)}, u32[]{:S(2)}) collective-permute-start(bf16[528,128]{1,0:T(8,128)(2,1)S(1)} %pack_first.1.first), channel_id=1, source_target_pairs={{0,4},{1,5},{4,8},{5,9},{8,12},{9,13},{12,14},{13,15},{14,10},{15,... | collective-permute-start | bytes 405512 | tf_op jit(solution)/shard_map/ppermute | solution.py:266
  4.0 0.0 collective-permute-start
  4.0 0.0 copy-done
  4.0 0.4 %pack_second_kernel.1 = (bf16[512,128]{1,0:T(8,128)(2,1)S(1)}, bf16[1040,128]{1,0:T(8,128)(2,1)S(1)}, f32[1,256]{1,0:T(1,128)S(1)}) custom-call(bf16[256,512]{1,0:T(8,128)(2,1)S(1)} %copy-done, bf16[528,128]{1,0:T(8,128)(2,1)S(1)} %pack_first.1.first), custom_call_target="tpu_custom_call" | custom-call | flops 67108864 | bytes 1048576 | tf_op jit(solution)/shard_map/pack_second_kernel/pallas_call | solution.py:247
  4.4 2.1 %collective-permute-start.3 = (bf16[512,128]{1,0:T(8,128)(2,1)S(1)}, bf16[512,128]{1,0:T(8,128)(2,1)S(1)}, u32[]{:S(2)}, u32[]{:S(2)}) collective-permute-start(bf16[512,128]{1,0:T(8,128)(2,1)S(1)} %get-tuple-element.14), channel_id=1, source_target_pairs={{0,4},{1,5},{4,8},{5,9},{8,12},{9,13},{12,14},{13,15},{14,10},{15,... | collective-permute-start | bytes 393224 | tf_op jit(solution)/shard_map/ppermute | solution.py:266
  6.4 0.0 collective-permute-start.1
  6.4 1.4 %collective-permute-done.2.refs_3_ = bf16[528,128]{1,0:T(8,128)(2,1)S(1)} collective-permute-done((bf16[528,128]{1,0:T(8,128)(2,1)S(1)}, bf16[528,128]{1,0:T(8,128)(2,1)S(1)}, u32[]{:S(2)}, u32[]{:S(2)}) %collective-permute-start.2) | collective-permute-done | bytes 135200 | tf_op jit(solution)/shard_map/ppermute | solution.py:266
  7.9 2.5 %collective-permute-start.5 = (bf16[528,128]{1,0:T(8,128)(2,1)S(1)}, bf16[528,128]{1,0:T(8,128)(2,1)S(1)}, u32[]{:S(2)}, u32[]{:S(2)}) collective-permute-start(bf16[528,128]{1,0:T(8,128)(2,1)S(1)} %collective-permute-done.2.refs_3_), channel_id=1, source_target_pairs={{0,4},{1,5},{4,8},{5,9},{8,12},{9,13},{12,14},{13,15},{14,10},{15,... | collective-permute-start | bytes 405512 | tf_op jit(solution)/shard_map/ppermute | solution.py:266
  10.3 0.0 collective-permute-done.refs_1_
  10.3 0.0 collective-permute-start.6
  10.3 0.3 %collective-permute-done.3.refs_4_ = bf16[512,128]{1,0:T(8,128)(2,1)S(1)} collective-permute-done((bf16[512,128]{1,0:T(8,128)(2,1)S(1)}, bf16[512,128]{1,0:T(8,128)(2,1)S(1)}, u32[]{:S(2)}, u32[]{:S(2)}) %collective-permute-start.3) | collective-permute-done | bytes 131104 | tf_op jit(solution)/shard_map/ppermute | solution.py:266
  10.7 2.5 %collective-permute-start.7 = (bf16[512,128]{1,0:T(8,128)(2,1)S(1)}, bf16[512,128]{1,0:T(8,128)(2,1)S(1)}, u32[]{:S(2)}, u32[]{:S(2)}) collective-permute-start(bf16[512,128]{1,0:T(8,128)(2,1)S(1)} %collective-permute-done.3.refs_4_), channel_id=1, source_target_pairs={{0,4},{1,5},{4,8},{5,9},{8,12},{9,13},{12,14},{13,15},{14,10},{15,... | collective-permute-start | bytes 393224 | tf_op jit(solution)/shard_map/ppermute | solution.py:266
  13.1 0.0 collective-permute-done.1.refs_2_
  13.2 0.0 collective-permute-start.8
  13.2 0.2 bundle_kernel.1.bundle
  13.3 0.1 collective-permute-start.4
  13.4 0.7 %collective-permute-done.5.back_a = bf16[528,128]{1,0:T(8,128)(2,1)S(1)} collective-permute-done((bf16[528,128]{1,0:T(8,128)(2,1)S(1)}, bf16[528,128]{1,0:T(8,128)(2,1)S(1)}, u32[]{:S(2)}, u32[]{:S(2)}) %collective-permute-start.5) | collective-permute-done | bytes 135200 | tf_op jit(solution)/shard_map/ppermute | solution.py:266
  14.1 1.6 %collective-permute-done.6.ahead_a = bf16[528,128]{1,0:T(8,128)(2,1)S(1)} collective-permute-done((bf16[528,128]{1,0:T(8,128)(2,1)S(1)}, bf16[528,128]{1,0:T(8,128)(2,1)S(1)}, u32[]{:S(2)}, u32[]{:S(2)}) %collective-permute-start.6) | collective-permute-done | bytes 135200 | tf_op jit(solution)/shard_map/ppermute | solution.py:266
  15.6 0.6 %far_first_kernel.1.found = f32[1,256]{1,0:T(1,128)S(1)} custom-call(bf16[1040,128]{1,0:T(8,128)(2,1)S(1)} %get-tuple-element.13.refs_0_.own, bf16[3,1040,128]{2,1,0:T(8,128)(2,1)S(1)} %bundle_kernel.1.bundle, bf16[528,128]{1,0:T(8,128)(2,1)S(1)} %collective-permute-done.5.back_a, bf16[528,128]{1,0:T(8,128)(2,1)S(1)} %collective-permute-done.6.ahead_a), custom_call_target="tpu_custom_call" | custom-call | flops 13421772800 | bytes 1048576 | tf_op jit(solution)/shard_map/far_first_kernel/pallas_call | solution.py:247
  16.2 0.4 %collective-permute-done.7.back_b = bf16[512,128]{1,0:T(8,128)(2,1)S(1)} collective-permute-done((bf16[512,128]{1,0:T(8,128)(2,1)S(1)}, bf16[512,128]{1,0:T(8,128)(2,1)S(1)}, u32[]{:S(2)}, u32[]{:S(2)}) %collective-permute-start.7) | collective-permute-done | bytes 131104 | tf_op jit(solution)/shard_map/ppermute | solution.py:266
  16.6 0.0 collective-permute-done.4.others
  16.6 0.6 %far_back_kernel.1 = (f32[1,256]{1,0:T(1,128)S(1)}, f32[1,128]{1,0:T(1,128)S(1)}, bf16[1040,128]{1,0:T(8,128)(2,1)S(1)}) custom-call(bf16[1040,128]{1,0:T(8,128)(2,1)S(1)} %get-tuple-element.13.refs_0_.own, bf16[3,1040,128]{2,1,0:T(8,128)(2,1)S(1)} %bundle_kernel.1.bundle, bf16[3,1040,128]{2,1,0:T(8,128)(2,1)S(1)} %collective-permute-done.4.others, ...), custom_call_target="tpu_custom_call" | custom-call | flops 134217728 | bytes 1048576 | tf_op jit(solution)/shard_map/far_back_kernel/pallas_call | solution.py:247
  17.2 1.0 %collective-permute-done.8.ahead_b = bf16[512,128]{1,0:T(8,128)(2,1)S(1)} collective-permute-done((bf16[512,128]{1,0:T(8,128)(2,1)S(1)}, bf16[512,128]{1,0:T(8,128)(2,1)S(1)}, u32[]{:S(2)}, u32[]{:S(2)}) %collective-permute-start.8) | collective-permute-done | bytes 131104 | tf_op jit(solution)/shard_map/ppermute | solution.py:266
  18.2 0.5 %far_last_kernel.1 = (f32[1,256]{1,0:T(1,128)S(1)}, f32[1,256]{1,0:T(1,128)S(1)}) custom-call(bf16[1040,128]{1,0:T(8,128)(2,1)S(1)} %get-tuple-element.13.refs_0_.own, bf16[3,1040,128]{2,1,0:T(8,128)(2,1)S(1)} %bundle_kernel.1.bundle, bf16[3,1040,128]{2,1,0:T(8,128)(2,1)S(1)} %collective-permute-done.4.others, bf16[1040,128]{1,0:T(8,128)(2,1)S(1)} %get-tuple-element.15.back, ...), custom_call_target="tpu_custom_call" | custom-call | flops 335544320 | bytes 1048576 | tf_op jit(solution)/shard_map/far_last_kernel/pallas_call | solution.py:247
  18.7 1.0 %collective-permute-start.9 = (f32[1,256]{1,0:T(1,128)S(1)}, f32[1,256]{1,0:T(1,128)S(1)}, u32[]{:S(2)}, u32[]{:S(2)}) collective-permute-start(f32[1,256]{1,0:T(1,128)S(1)} %get-tuple-element.19), channel_id=1, source_target_pairs={{0,7},{1,6},{4,3},{5,2},{8,0},{9,1},{12,4},{13,5},{14,8},{15,9},{1... | collective-permute-start | bytes 3080 | tf_op jit(solution)/shard_map/ppermute | solution.py:266
  19.7 1.0 %collective-permute-start.10 = (f32[1,256]{1,0:T(1,128)S(1)}, f32[1,256]{1,0:T(1,128)S(1)}, u32[]{:S(2)}, u32[]{:S(2)}) collective-permute-start(f32[1,256]{1,0:T(1,128)S(1)} %get-tuple-element.20), channel_id=1, source_target_pairs={{0,9},{1,8},{4,13},{5,12},{8,15},{9,14},{12,11},{13,10},{14,7},{15... | collective-permute-start | bytes 3080 | tf_op jit(solution)/shard_map/ppermute | solution.py:266
  20.7 0.7 %own_kernel.1 = f32[1,256]{1,0:T(1,128)S(1)} custom-call(bf16[1040,128]{1,0:T(8,128)(2,1)S(1)} %get-tuple-element.13.refs_0_.own, bf16[3,1040,128]{2,1,0:T(8,128)(2,1)S(1)} %bundle_kernel.1.bundle, bf16[3,1040,128]{2,1,0:T(8,128)(2,1)S(1)} %collective-permute-done.4.others, bf16[1040,128]{1,0:T(8,128)(2,1)S(1)} %get-tuple-element.15.back, ...), custom_call_target="tpu_custom_call" | custom-call | flops 335544320 | bytes 1048576 | tf_op jit(solution)/shard_map/own_kernel/pallas_call | solution.py:247
  21.4 1.9 %collective-permute-done.9 = f32[1,256]{1,0:T(1,128)S(1)} collective-permute-done((f32[1,256]{1,0:T(1,128)S(1)}, f32[1,256]{1,0:T(1,128)S(1)}, u32[]{:S(2)}, u32[]{:S(2)}) %collective-permute-start.9) | collective-permute-done | bytes 1056 | tf_op jit(solution)/shard_map/ppermute | solution.py:266
  23.2 1.0 %collective-permute-done.10 = f32[1,256]{1,0:T(1,128)S(1)} collective-permute-done((f32[1,256]{1,0:T(1,128)S(1)}, f32[1,256]{1,0:T(1,128)S(1)}, u32[]{:S(2)}, u32[]{:S(2)}) %collective-permute-start.10) | collective-permute-done | bytes 1056 | tf_op jit(solution)/shard_map/ppermute | solution.py:266
  24.2 0.6 %maximum_maximum_fusion = f32[1,256]{1,0:T(1,128)} fusion(f32[1,256]{1,0:T(1,128)S(1)} %own_kernel.1, f32[1,256]{1,0:T(1,128)S(1)} %collective-permute-done.9, f32[1,256]{1,0:T(1,128)S(1)} %collective-permute-done.10), kind=kLoop, calls=%fused_computation | loop fusion | flops 512 | bytes 4096 | tf_op jit(solution)/shard_map/max | solution.py:321
Async XLA Ops:
  0.0 4.0 %copy-start = (bf16[256,512]{1,0:T(8,128)(2,1)S(1)}, bf16[256,512]{1,0:T(8,128)(2,1)}, u32[]{:S(2)}) copy-start(bf16[256,512]{1,0:T(8,128)(2,1)} %embeds.3) | copy-start | bytes 786436
  0.9 7.0 %collective-permute-start.2 = (bf16[528,128]{1,0:T(8,128)(2,1)S(1)}, bf16[528,128]{1,0:T(8,128)(2,1)S(1)}, u32[]{:S(2)}, u32[]{:S(2)}) collective-permute-start(bf16[528,128]{1,0:T(8,128)(2,1)S(1)} %pack_first.1.first), channel_id=1, source_target_pairs={{0,4},{1,5},{4,8},{5,9},{8,12},{9,13},{12,14},{13,15},{14,10},{15,... | collective-permute-start | bytes 405512 | tf_op jit(solution)/shard_map/ppermute | solution.py:266
  4.0 6.4 %collective-permute-start = (bf16[528,128]{1,0:T(8,128)(2,1)S(1)}, bf16[528,128]{1,0:T(8,128)(2,1)S(1)}, u32[]{:S(2)}, u32[]{:S(2)}) collective-permute-start(bf16[528,128]{1,0:T(8,128)(2,1)S(1)} %pack_first.1.first), channel_id=1, source_target_pairs={{0,2},{1,3},{4,0},{5,1},{8,5},{9,4},{12,9},{13,8},{14,13},{15,12},... | collective-permute-start | bytes 405512 | tf_op jit(solution)/shard_map/ppermute | solution.py:266
  4.4 6.3 %collective-permute-start.3 = (bf16[512,128]{1,0:T(8,128)(2,1)S(1)}, bf16[512,128]{1,0:T(8,128)(2,1)S(1)}, u32[]{:S(2)}, u32[]{:S(2)}) collective-permute-start(bf16[512,128]{1,0:T(8,128)(2,1)S(1)} %get-tuple-element.14), channel_id=1, source_target_pairs={{0,4},{1,5},{4,8},{5,9},{8,12},{9,13},{12,14},{13,15},{14,10},{15,... | collective-permute-start | bytes 393224 | tf_op jit(solution)/shard_map/ppermute | solution.py:266
  6.4 6.7 %collective-permute-start.1 = (bf16[512,128]{1,0:T(8,128)(2,1)S(1)}, bf16[512,128]{1,0:T(8,128)(2,1)S(1)}, u32[]{:S(2)}, u32[]{:S(2)}) collective-permute-start(bf16[512,128]{1,0:T(8,128)(2,1)S(1)} %get-tuple-element.14), channel_id=1, source_target_pairs={{0,2},{1,3},{4,0},{5,1},{8,5},{9,4},{12,9},{13,8},{14,13},{15,12},... | collective-permute-start | bytes 393224 | tf_op jit(solution)/shard_map/ppermute | solution.py:266
  7.9 6.2 %collective-permute-start.5 = (bf16[528,128]{1,0:T(8,128)(2,1)S(1)}, bf16[528,128]{1,0:T(8,128)(2,1)S(1)}, u32[]{:S(2)}, u32[]{:S(2)}) collective-permute-start(bf16[528,128]{1,0:T(8,128)(2,1)S(1)} %collective-permute-done.2.refs_3_), channel_id=1, source_target_pairs={{0,4},{1,5},{4,8},{5,9},{8,12},{9,13},{12,14},{13,15},{14,10},{15,... | collective-permute-start | bytes 405512 | tf_op jit(solution)/shard_map/ppermute | solution.py:266
  10.3 5.3 %collective-permute-start.6 = (bf16[528,128]{1,0:T(8,128)(2,1)S(1)}, bf16[528,128]{1,0:T(8,128)(2,1)S(1)}, u32[]{:S(2)}, u32[]{:S(2)}) collective-permute-start(bf16[528,128]{1,0:T(8,128)(2,1)S(1)} %collective-permute-done.refs_1_), channel_id=1, source_target_pairs={{0,2},{1,3},{4,0},{5,1},{8,4},{9,5},{12,8},{13,9},{14,12},{15,13},... | collective-permute-start | bytes 405512 | tf_op jit(solution)/shard_map/ppermute | solution.py:266
  10.7 5.9 %collective-permute-start.7 = (bf16[512,128]{1,0:T(8,128)(2,1)S(1)}, bf16[512,128]{1,0:T(8,128)(2,1)S(1)}, u32[]{:S(2)}, u32[]{:S(2)}) collective-permute-start(bf16[512,128]{1,0:T(8,128)(2,1)S(1)} %collective-permute-done.3.refs_4_), channel_id=1, source_target_pairs={{0,4},{1,5},{4,8},{5,9},{8,12},{9,13},{12,14},{13,15},{14,10},{15,... | collective-permute-start | bytes 393224 | tf_op jit(solution)/shard_map/ppermute | solution.py:266
  13.2 5.1 %collective-permute-start.8 = (bf16[512,128]{1,0:T(8,128)(2,1)S(1)}, bf16[512,128]{1,0:T(8,128)(2,1)S(1)}, u32[]{:S(2)}, u32[]{:S(2)}) collective-permute-start(bf16[512,128]{1,0:T(8,128)(2,1)S(1)} %collective-permute-done.1.refs_2_), channel_id=1, source_target_pairs={{0,2},{1,3},{4,0},{5,1},{8,4},{9,5},{12,8},{13,9},{14,12},{15,13},... | collective-permute-start | bytes 393224 | tf_op jit(solution)/shard_map/ppermute | solution.py:266
  13.3 3.3 %collective-permute-start.4 = (bf16[3,1040,128]{2,1,0:T(8,128)(2,1)S(1)}, bf16[3,1040,128]{2,1,0:T(8,128)(2,1)S(1)}, u32[]{:S(2)}, u32[]{:S(2)}) collective-permute-start(bf16[3,1040,128]{2,1,0:T(8,128)(2,1)S(1)} %bundle_kernel.1.bundle), channel_id=1, source_target_pairs={{0,1},{1,0},{4,5},{5,4},{8,9},{9,8},{12,13},{13,12},{14,15},{15,14... | collective-permute-start | bytes 2396168 | tf_op jit(solution)/shard_map/ppermute | solution.py:266
  18.7 4.5 %collective-permute-start.9 = (f32[1,256]{1,0:T(1,128)S(1)}, f32[1,256]{1,0:T(1,128)S(1)}, u32[]{:S(2)}, u32[]{:S(2)}) collective-permute-start(f32[1,256]{1,0:T(1,128)S(1)} %get-tuple-element.19), channel_id=1, source_target_pairs={{0,7},{1,6},{4,3},{5,2},{8,0},{9,1},{12,4},{13,5},{14,8},{15,9},{1... | collective-permute-start | bytes 3080 | tf_op jit(solution)/shard_map/ppermute | solution.py:266
  19.7 4.5 %collective-permute-start.10 = (f32[1,256]{1,0:T(1,128)S(1)}, f32[1,256]{1,0:T(1,128)S(1)}, u32[]{:S(2)}, u32[]{:S(2)}) collective-permute-start(f32[1,256]{1,0:T(1,128)S(1)} %get-tuple-element.20), channel_id=1, source_target_pairs={{0,9},{1,8},{4,13},{5,12},{8,15},{9,14},{12,11},{13,10},{14,7},{15... | collective-permute-start | bytes 3080 | tf_op jit(solution)/shard_map/ppermute | solution.py:266
